TPU v7x, 128 devices: a whole 4x4x4 slice. The times are simulated.
128 devices in a mesh: dp: 4 (over z), tensor: 32 (over y, x, core).
Axes of the slice: x: 4, y: 4, z: 4, core: 2. Of those that a mesh axis runs over, the one named last changes fastest.
Arguments:
- queries: bfloat16 [128, 576, 128], P(('dp', 'tensor')), may hold values from -40 to 40
- cache_pool: bfloat16 [1024, 576, 128], P(('dp', 'tensor')), may hold values from -6 to 6
- holder: int32 [128, 32], P(None, 'tensor'), may hold values from 0 to 3, as said below
- slot_ids: int32 [128, 32], P(None, 'tensor'), may hold values from 0 to 7
- lengths: int32 [128], replicated, may hold values from 1 to 4096, as said below
- residual: bfloat16 [128, 7168], P('dp'), may hold values from -6 to 6
- w_value: bfloat16 [128, 512, 128], P('tensor'), may hold values from -1 to 1
- w_out: bfloat16 [16384, 7168], P('tensor'), may hold values from -0.09375 to 0.09375
- norm_gain: float32 [7168], replicated, may hold values from 0.1 to 1.9
- w_gate: bfloat16 [7168, 12288], P(None, 'tensor'), may hold values from -0.0625 to 0.0625
- w_up: bfloat16 [7168, 12288], P(None, 'tensor'), may hold values from -0.0625 to 0.0625
- w_down: bfloat16 [12288, 7168], P('tensor'), may hold values from -0.0546875 to 0.0546875
Outputs:
- layer_out: float32 [128, 7168], P(('dp', 'tensor'))
Inputs may be any that keep to these rules, and one draw needn't show every extreme that they name: `holder`: among the 32 entries of the requests of one data-parallel rank at the block positions of one tensor index, no rank is named more than 12 times, and one rank exactly 12 times. `lengths`: some request has 4096 tokens and some has 1.
All inputs are finite; a program needn't handle non-finite values.
Results may differ from a plain program's by a relative error of at most 0.011.
Values may be sent and summed in bfloat16 or wider, within the bound.
No kernel may reach another device: no remote copies, remote signals or barrier semaphores. Data moves between devices by JAX's collectives and lax.ppermute only.
A program may use at most 576 MiB of HBM per device.

v0:
```python
import jax
import jax.numpy as jnp
from jax import lax
from jax.sharding import PartitionSpec as P

score_scale = 192.0 ** (-0.5)
norm_eps = 1e-06
far_below = -1e30


def pick_slots(wanted, capacity):
    item_count = wanted.shape[-1]
    order_rank = jnp.cumsum(wanted.astype(jnp.int32), axis=-1) - 1
    places = jnp.arange(capacity, dtype=jnp.int32)
    matches = wanted[:, None, :] & (order_rank[:, None, :] == places[None, :, None])
    item_ids = jnp.arange(item_count, dtype=jnp.int32)
    item_index = jnp.sum(jnp.where(matches, item_ids[None, None, :], 0), axis=-1)
    return (item_index, jnp.any(matches, axis=-1))


def rms_norm(values, norm_gain):
    scale_inv = lax.rsqrt(jnp.mean(values * values, axis=1, keepdims=True) + norm_eps)
    return (values * scale_inv * norm_gain[None, :]).astype(jnp.bfloat16)


def body(
    queries,
    cache_pool,
    holder,
    slot_ids,
    lengths,
    residual,
    w_value,
    w_out,
    norm_gain,
    w_gate,
    w_up,
    w_down,
):
    rank_count = lax.axis_size("dp")
    tensor_count = lax.axis_size("tensor")
    my_rank = lax.axis_index("dp")
    column = lax.axis_index("tensor")
    group_size = residual.shape[0]
    per_column = holder.shape[1]
    item_count = group_size * per_column
    capacity = item_count * 3 // 8
    width_all = cache_pool.shape[1]
    block_len = cache_pool.shape[2]
    latent = w_value.shape[1]
    head_total = queries.shape[2]
    head_local = w_value.shape[0]
    rows_dev = group_size // tensor_count
    owners = holder.reshape(rank_count, item_count)
    slot_rows = slot_ids.reshape(rank_count, item_count)
    send_index, send_valid = pick_slots(owners == my_rank, capacity)
    send_slots = jnp.where(send_valid, jnp.take_along_axis(slot_rows, send_index, axis=1), 0)
    outgoing = jnp.take(cache_pool, send_slots.reshape(-1), axis=0).reshape(
        rank_count, capacity, width_all, block_len
    )
    arrived = lax.all_to_all(outgoing, "dp", split_axis=0, concat_axis=0, tiled=True)
    key_block = arrived.reshape(-1, width_all, block_len)
    own_holders = lax.dynamic_index_in_dim(owners, my_rank, 0, keepdims=False)
    sources = jnp.arange(rank_count, dtype=jnp.int32)
    recv_index, recv_valid = pick_slots(own_holders[None, :] == sources[:, None], capacity)
    recv_index = recv_index.reshape(-1)
    recv_valid = recv_valid.reshape(-1)
    request = recv_index // per_column
    position = column * per_column + recv_index % per_column
    group_lengths = lax.dynamic_slice_in_dim(lengths, my_rank * group_size, group_size)
    limit_len = jnp.take(group_lengths, request)
    token_pos = position[:, None] * block_len + jnp.arange(block_len, dtype=jnp.int32)[None, :]
    live_mask = recv_valid[:, None] & (token_pos < limit_len[:, None])
    group_queries = lax.all_gather(queries, "tensor", axis=0, tiled=True)
    chosen = jnp.take(group_queries, request, axis=0)
    scores = (
        jnp.einsum("xeh,xet->xht", chosen, key_block, preferred_element_type=jnp.float32)
        * score_scale
    )
    masked = jnp.where(live_mask[:, None, :], scores, far_below)
    slot_top = jnp.max(masked, axis=2)
    belongs = request[None, :] == jnp.arange(group_size, dtype=jnp.int32)[:, None]
    row_top = jnp.max(jnp.where(belongs[:, :, None], slot_top[None, :, :], far_below), axis=1)
    slot_ref = jnp.take(row_top, request, axis=0)
    weights = jnp.where(live_mask[:, None, :], jnp.exp(masked - slot_ref[:, :, None]), 0.0)
    slot_sums = jnp.sum(weights, axis=2)
    mixed = jnp.einsum(
        "xht,xdt->xhd",
        weights.astype(jnp.bfloat16),
        key_block[:, :latent, :],
        preferred_element_type=jnp.float32,
    )
    onehot = belongs.astype(jnp.float32)
    partial_value = jnp.dot(
        onehot, mixed.reshape(mixed.shape[0], -1), precision=lax.Precision.HIGHEST
    ).reshape(group_size, head_total, latent)
    totals = jnp.dot(onehot, slot_sums, precision=lax.Precision.HIGHEST)
    top_parts, sum_parts, out_parts = (
        lax.all_to_all(row_top, "tensor", split_axis=1, concat_axis=0, tiled=True),
        lax.all_to_all(totals, "tensor", split_axis=1, concat_axis=0, tiled=True),
        lax.all_to_all(partial_value, "tensor", split_axis=1, concat_axis=0, tiled=True),
    )
    top_parts = top_parts.reshape(tensor_count, group_size, head_local)
    sum_parts = sum_parts.reshape(tensor_count, group_size, head_local)
    out_parts = out_parts.reshape(tensor_count, group_size, head_local, latent)
    peak_value = jnp.max(top_parts, axis=0)
    factor = jnp.exp(top_parts - peak_value[None])
    sum_mine = jnp.sum(sum_parts * factor, axis=0)
    out_mine = jnp.sum(out_parts * factor[..., None], axis=0)
    attended = (out_mine / sum_mine[..., None]).astype(jnp.bfloat16)
    per_head = jnp.einsum(
        "ghd,hdv->ghv", attended, w_value, preferred_element_type=jnp.float32
    ).astype(jnp.bfloat16)
    flat_heads = per_head.reshape(group_size, -1)
    row_first = column * rows_dev
    attention = lax.psum(jnp.dot(flat_heads, w_out, preferred_element_type=jnp.float32), "tensor")
    residual_sum = residual.astype(jnp.float32) + attention
    normed = rms_norm(residual_sum, norm_gain)
    gate_val = jnp.dot(normed, w_gate, preferred_element_type=jnp.float32)
    up_val = jnp.dot(normed, w_up, preferred_element_type=jnp.float32)
    activated = (jax.nn.silu(gate_val) * up_val).astype(jnp.bfloat16)
    own_sum = lax.dynamic_slice_in_dim(residual_sum, row_first, rows_dev, 0)
    down_rows = lax.psum_scatter(
        jnp.dot(activated, w_down, preferred_element_type=jnp.float32),
        "tensor",
        scatter_dimension=0,
        tiled=True,
    )
    return own_sum + down_rows


def solution(mesh):
    in_specs = (
        P(("dp", "tensor"), None, None),
        P(("dp", "tensor"), None, None),
        P(None, "tensor"),
        P(None, "tensor"),
        P(),
        P("dp", None),
        P("tensor", None, None),
        P("tensor", None),
        P(),
        P(None, "tensor"),
        P(None, "tensor"),
        P("tensor", None),
    )
    out_specs = P(("dp", "tensor"), None)
    return jax.shard_map(body, mesh=mesh, in_specs=in_specs, out_specs=out_specs, check_vma=False)
```

profile of v0, /device:TPU:1, one launch (start us, length us, event | category | flops | bytes accessed | tf_op | source)
XLA Modules:
  0.0 515.2 jit_solution(2362443499939414078)
XLA Ops:
  6.5 0.7 all-gather.2.cloned.1.call-update
  7.8 1.3 reduce.6
  10.0 1.3 reduce.7
  11.9 1.1 gather_fusion.4
  13.3 5.3 %gather_fusion.2 = bf16[48,576,128]{2,1,0:T(8,128)(2,1)} fusion(bf16[8,576,128]{2,1,0:T(8,128)(2,1)S(1)} %copy-done, s32[1024]{0:T(1024)S(1)} %pad_clamp_fusion), kind=kCustom, calls=%fused_computation.2 | custom fusion | bytes 14155968 | tf_op jit(solution)/shard_map/jit(_take)/gather | solution.py:58
  18.6 6.7 %broadcast_select_fusion = bf16[4,12,576,128]{3,2,1,0:T(8,128)(2,1)} fusion(bf16[4,12,576,128]{3,2,1,0:T(8,128)(2,1)} %bitcast.71, pred[4,12]{1,0:T(4,128)(4,1)S(1)} %copy.39), kind=kLoop, calls=%fused_computation.12 | loop fusion | flops 3538944 | bytes 14155824 | tf_op jit(solution)/shard_map/jit(_take)/select_n | solution.py:58
  25.3 6.1 %all-to-all-start = ((bf16[4,12,576,128]{3,2,1,0:T(8,128)(2,1)}), bf16[4,12,576,128]{3,2,1,0:T(8,128)(2,1)}, u32[]{:S(2)}, u32[]{:S(2)}) async-start(bf16[4,12,576,128]{3,2,1,0:T(8,128)(2,1)} %broadcast_select_fusion), calls=%async_computation | async-start | bytes 14155776 | tf_op jit(solution)/shard_map/all_to_all | solution.py:61
  32.7 0.8 gather_fusion
  33.6 26.4 %all-gather.2.cloned.1.call-done = bf16[32,576,128]{2,1,0:T(8,128)(2,1)} async-done(((bf16[1,576,128]{2,1,0:T(8,128)(2,1)}), bf16[32,576,128]{2,1,0:T(8,128)(2,1)}) %all-gather.2.cloned.1.call-update) | async-done | bytes 4718608 | tf_op jit(solution)/shard_map/all_gather | solution.py:74
  60.0 7.7 %gather_fusion.1 = bf16[48,576,128]{2,1,0:T(8,128)(2,1)} fusion(bf16[32,576,128]{2,1,0:T(8,128)(2,1)} %all-gather.2.cloned.1.call-done, s32[1024]{0:T(1024)S(1)} %pad_clamp_fusion.1), kind=kCustom, calls=%fused_computation.1 | custom fusion | bytes 14155968 | tf_op jit(solution)/shard_map/jit(_take)/gather | solution.py:75
  67.6 44.2 %all-to-all-done = bf16[4,12,576,128]{3,2,1,0:T(8,128)(2,1)} async-done(((bf16[4,12,576,128]{3,2,1,0:T(8,128)(2,1)}), bf16[4,12,576,128]{3,2,1,0:T(8,128)(2,1)}, u32[]{:S(2)}, u32[]{:S(2)}) %all-to-all-start) | async-done | bytes 7077920 | tf_op jit(solution)/shard_map/all_to_all | solution.py:61
  111.8 8.0 %fusion.9 = (f32[48,128]{1,0:T(8,128)S(1)}, f32[48,128,128]{1,2,0:T(8,128)}) fusion(pred[48,128]{1,0:T(8,128)(4,1)S(1)} %fusion.36, bf16[48,576,128]{2,1,0:T(8,128)(2,1)} %bitcast.7, bf16[48,576,128]{2,1,0:T(8,128)(2,1)} %gather_fusion.1, pred[48]{0:T(512)(128)(4,1)S(1)} %get-tuple-element.10), kind=kOutput, calls=%fused_computation.18 | convolution fusion | flops 911861760 | bytes 17332272 | tf_op jit(solution)/shard_map/xeh,xet->xht/dot_general | solution.py:77
  120.8 3.4 fusion.10
  124.7 0.7 reshape.398
  125.4 8.5 %all-to-all-start.3 = ((f32[32,1,128]{2,1,0:T(1,128)}), f32[32,1,128]{2,1,0:T(1,128)S(1)}, u32[]{:S(2)}, u32[]{:S(2)}) async-start(f32[32,1,128]{2,1,0:T(1,128)} %reshape.398), calls=%async_computation.3 | async-start | bytes 32768 | tf_op jit(solution)/shard_map/all_to_all | solution.py:100
  133.9 8.4 %fusion.6 = f32[48,128,512]{2,1,0:T(8,128)} fusion(bf16[48,576,128]{2,1,0:T(8,128)(2,1)} %bitcast.7, f32[48,128,128]{1,2,0:T(8,128)} %get-tuple-element.16, f32[48,128]{1,0:T(8,128)S(1)} %broadcast_select_fusion.1, pred[48,128]{1,0:T(8,128)(4,1)S(1)} %fusion.36), kind=kOutput, calls=%fused_computation.13 | convolution fusion | flops 809238528 | bytes 22050816 | tf_op jit(solution)/shard_map/xht,xdt->xhd/dot_general | solution.py:87
  142.4 0.7 reshape.396
  143.1 7.4 %all-to-all-start.2 = ((f32[32,1,128]{2,1,0:T(1,128)}), f32[32,1,128]{2,1,0:T(1,128)S(1)}, u32[]{:S(2)}, u32[]{:S(2)}) async-start(f32[32,1,128]{2,1,0:T(1,128)} %reshape.396), calls=%async_computation.2 | async-start | bytes 32768 | tf_op jit(solution)/shard_map/all_to_all | solution.py:99
  150.5 18.6 %fusion = f32[32,128,512]{2,0,1:T(8,128)} fusion(s32[48]{0:T(128)S(1)} %eq.91, f32[6,8,128,512]{3,2,1,0:T(8,128)} %bitcast.70), kind=kOutput, calls=%fused_computation.5 | convolution fusion | flops 1207961088 | bytes 20971712 | tf_op jit(solution)/shard_map/dot_general | solution.py:94
  169.1 7.4 %all-to-all-start.1 = ((f32[32,128,512]{2,0,1:T(8,128)}), f32[32,128,512]{2,0,1:T(8,128)}, u32[]{:S(2)}, u32[]{:S(2)}) async-start(f32[32,128,512]{2,0,1:T(8,128)} %fusion), calls=%async_computation.1 | async-start | bytes 16777216 | tf_op jit(solution)/shard_map/all_to_all | solution.py:101
  177.2 0.7 reduce.9
  178.0 0.7 reduce.8
  178.8 97.5 %all-to-all-done.1 = f32[32,128,512]{2,0,1:T(8,128)} async-done(((f32[32,128,512]{2,0,1:T(8,128)}), f32[32,128,512]{2,0,1:T(8,128)}, u32[]{:S(2)}, u32[]{:S(2)}) %all-to-all-start.1) | async-done | bytes 8388640 | tf_op jit(solution)/shard_map/all_to_all | solution.py:101
  276.3 3.8 multiply_reduce_fusion
  280.5 5.5 %fusion.31 = f32[32,7168]{1,0:T(8,128)} fusion(bf16[512,7168]{1,0:T(8,128)(2,1)} %param.19, bf16[4,4,8,128]{3,2,1,0:T(8,128)(2,1)S(1)} %fusion.19), kind=kOutput, calls=%fused_computation.49 | convolution fusion | flops 234881024 | bytes 8290304 | tf_op jit(solution)/shard_map/dot_general | solution.py:116
  286.2 103.9 %all-reduce.4.cloned.1.call-done = f32[32,7168]{1,0:T(8,128)} async-done(((f32[32,7168]{1,0:T(8,128)}), f32[32,7168]{1,0:T(8,128)}) %all-reduce.4.cloned.1.call-update) | async-done | bytes 917520 | tf_op jit(solution)/shard_map/psum | solution.py:116
  390.2 1.4 multiply_reduce_fusion.1
  391.6 3.6 fusion.56
  395.2 7.5 %fusion.20 = f32[32,7168]{1,0:T(8,128)} fusion(bf16[384,7168]{1,0:T(8,128)(2,1)} %param.23, bf16[7168,384]{1,0:T(8,128)(2,1)} %param.22, f32[32,384]{1,0:T(8,128)S(1)} %fusion.56, f32[32,7168]{1,0:T(8,128)S(1)} %get-tuple-element.6, f32[7168]{0:T(1024)S(1)} %copy-done.3, f32[32]{0:T(128)S(1)} %add_rsqrt_fusion), kind=kOutput, calls=%fused_computation.30 | convolution fusion | flops 353083392 | bytes 12923008 | tf_op jit(solution)/shard_map/dot_general | solution.py:124
  402.8 0.6 dynamic-slice
  403.4 103.1 %all-reduce.6.cloned.1.call-done = f32[32,7168]{1,0:T(8,128)} async-done(((f32[32,7168]{1,0:T(8,128)}), f32[32,7168]{1,0:T(8,128)}) %all-reduce.6.cloned.1.call-update) | async-done | bytes 917520
  506.5 2.2 dynamic-slice_add_fusion
  (72 shorter events, 6.7 us)
Async XLA Ops:
  6.5 6.7 %copy-start = (bf16[8,576,128]{2,1,0:T(8,128)(2,1)S(1)}, bf16[8,576,128]{2,1,0:T(8,128)(2,1)}, u32[]{:S(2)}) copy-start(bf16[8,576,128]{2,1,0:T(8,128)(2,1)} %param.13) | copy-start | bytes 3538948
  6.5 53.4 %all-gather.2.cloned.1.call-start = ((), (), s32[]{:S(2)}) async-start(), calls=%async_computation.4 | async-start | bytes 4866048 | tf_op jit(solution)/shard_map/all_gather | solution.py:74
  25.3 7.3 %copy-start.5 = (s32[128]{0:T(128)S(1)}, s32[128]{0:T(128)}, u32[]{:S(2)}) copy-start(s32[128]{0:T(128)} %param.16) | copy-start | bytes 1540
  25.3 86.6 %all-to-all-start = ((bf16[4,12,576,128]{3,2,1,0:T(8,128)(2,1)}), bf16[4,12,576,128]{3,2,1,0:T(8,128)(2,1)}, u32[]{:S(2)}, u32[]{:S(2)}) async-start(bf16[4,12,576,128]{3,2,1,0:T(8,128)(2,1)} %broadcast_select_fusion), calls=%async_computation | async-start | bytes 14155776 | tf_op jit(solution)/shard_map/all_to_all | solution.py:61
  125.4 17.8 %all-to-all-start.3 = ((f32[32,1,128]{2,1,0:T(1,128)}), f32[32,1,128]{2,1,0:T(1,128)S(1)}, u32[]{:S(2)}, u32[]{:S(2)}) async-start(f32[32,1,128]{2,1,0:T(1,128)} %reshape.398), calls=%async_computation.3 | async-start | bytes 32768 | tf_op jit(solution)/shard_map/all_to_all | solution.py:100
  143.1 26.0 %all-to-all-start.2 = ((f32[32,1,128]{2,1,0:T(1,128)}), f32[32,1,128]{2,1,0:T(1,128)S(1)}, u32[]{:S(2)}, u32[]{:S(2)}) async-start(f32[32,1,128]{2,1,0:T(1,128)} %reshape.396), calls=%async_computation.2 | async-start | bytes 32768 | tf_op jit(solution)/shard_map/all_to_all | solution.py:99
  169.1 107.2 %all-to-all-start.1 = ((f32[32,128,512]{2,0,1:T(8,128)}), f32[32,128,512]{2,0,1:T(8,128)}, u32[]{:S(2)}, u32[]{:S(2)}) async-start(f32[32,128,512]{2,0,1:T(8,128)} %fusion), calls=%async_computation.1 | async-start | bytes 16777216 | tf_op jit(solution)/shard_map/all_to_all | solution.py:101
  176.6 103.6 %copy-start.4 = (bf16[4,512,128]{2,1,0:T(8,128)(2,1)S(1)}, bf16[4,512,128]{2,1,0:T(8,128)(2,1)}, u32[]{:S(2)}) copy-start(bf16[4,512,128]{2,1,0:T(8,128)(2,1)} %param.18) | copy-start | bytes 1572868
  176.6 213.6 %all-reduce.4.cloned.1.call-start = ((), (), s32[]{:S(2)}) async-start(), calls=%async_computation.5 | async-start | bytes 1835008 | tf_op jit(solution)/shard_map/psum | solution.py:116
  280.4 109.7 %copy-start.2 = (bf16[32,7168]{1,0:T(8,128)(2,1)S(1)}, bf16[32,7168]{1,0:T(8,128)(2,1)}, u32[]{:S(2)}) copy-start(bf16[32,7168]{1,0:T(8,128)(2,1)} %param.17) | copy-start | bytes 1376260
  280.4 111.1 %copy-start.3 = (f32[7168]{0:T(1024)S(1)}, f32[7168]{0:T(1024)}, u32[]{:S(2)}) copy-start(f32[7168]{0:T(1024)} %param.20) | copy-start | bytes 86020
  286.0 220.6 %all-reduce.6.cloned.1.call-start = ((), (), s32[]{:S(2)}) async-start(), calls=%async_computation.6 | async-start | bytes 1835008
  391.6 117.1 %copy-start.1 = (bf16[8,576,128]{2,1,0:T(8,128)(2,1)S(1)}, bf16[8,576,128]{2,1,0:T(8,128)(2,1)}, u32[]{:S(2)}) copy-start(bf16[8,576,128]{2,1,0:T(8,128)(2,1)} %param.13) | copy-start | bytes 3538948
  395.2 7.6 %copy-start.6 = (u32[128]{0:T(128)S(1)}, u32[128]{0:T(128)}, u32[]{:S(2)}) copy-start(u32[128]{0:T(128)} %constant.160) | copy-start | bytes 1540
Sparse Core Ops, SparseCore 0:
  9.6 50.3 all-gather.1
  286.1 104.0 all-reduce.3
  402.9 103.5 all-reduce.5
where the time goes:
time: 516 us; the launch traced here: 515 us
  waiting for transfers between devices  376 us (73%)
  matrix products  52.1 us (10%)
  starting transfers between devices  29.7 us (6%)
  other arithmetic  23.7 us (5%)
  local copies, waits for them, and re-layouts  20.4 us (4%)
  between operations  13.4 us (3%)
    psum x1, waiting for transfers between devices, body(): lax.psum(jnp.dot(flat_heads, w_out, preferred_element_type=jnp.float32),...  104 us
    unnamed x4, waiting for transfers between devices  104 us
    all_to_all x1, waiting for transfers between devices, body(): lax.all_to_all(partial_value, 'tensor', split_axis=1, concat_axis=0, tile...  97.5 us
    all_to_all x1, waiting for transfers between devices, body(): lax.all_to_all(outgoing, 'dp', split_axis=0, concat_axis=0, tiled=True)  44.2 us
    all_gather x1, waiting for transfers between devices, body(): group_queries = lax.all_gather(queries, 'tensor', axis=0, tiled=True)  26.4 us
    dot_general x1, matrix products, body(): jnp.dot(onehot, mixed.reshape(mixed.shape[0], -1), precision=lax.Precisio...  18.6 us
  transfers between devices with their start and end apart: 7, of which 5 were waited for; matrix products, arithmetic and copies ran while one was open for 11% of the time, Pallas kernels for 0%

commit v1 on v0

v1 whole, which is shorter than its diff:
```python
import functools

import jax
import jax.numpy as jnp
from jax import lax
from jax.experimental import pallas as pl
from jax.experimental.pallas import tpu as pltpu
from jax.sharding import PartitionSpec as P

score_scale = 192.0 ** (-0.5)
norm_eps = 1e-06
far_below = -1e30
CORES = 2
LANES = 128


def attend_kernel(heads, group, latent, head_local, scal_ref, *refs):
    q_hbm = refs[0]
    pieces = refs[1:15]
    out_ref, kbuf, qbuf, acc, lse_buf, sems = refs[15:]
    width = kbuf.shape[2]
    block_len = kbuf.shape[3]
    owners = heads // head_local
    copies = [pltpu.make_async_copy(q_hbm, qbuf, sems.at[14])]
    half = pieces[1].shape[0]
    spots = [(0, 2 * half), (2 * half, half), (3 * half, half), (6 * half, half), (7 * half, half), (4 * half, half), (5 * half, half)]
    for side in range(2):
        for at, (first, count) in enumerate(spots):
            copies.append(
                pltpu.make_async_copy(
                    pieces[side * 7 + at],
                    kbuf.at[side, pl.ds(first, count)],
                    sems.at[side * 7 + at],
                )
            )
    for one in copies:
        one.start()
    lse_buf[...] = jnp.zeros_like(lse_buf)
    for one in copies:
        one.wait()
    base_own = scal_ref[3, 0]
    base_other = scal_ref[3, 1]
    token = lax.broadcasted_iota(jnp.int32, (heads, 2 * block_len), 1)
    position = jnp.where(token < block_len, token + base_own, token - block_len + base_other)
    lane = lax.broadcasted_iota(jnp.int32, (heads, LANES), 1)

    def four(step, carry):
        parts = []
        for i in range(4):
            r = step * 4 + i
            keys = jnp.concatenate([kbuf[0, scal_ref[0, r]], kbuf[1, scal_ref[1, r]]], axis=1)
            scores = jnp.dot(qbuf[r], keys, preferred_element_type=jnp.float32) * score_scale
            live = position < scal_ref[2, r]
            masked = jnp.where(live, scores, far_below)
            top = jnp.max(masked, axis=1, keepdims=True)
            weights = jnp.where(live, jnp.exp(masked - top), 0.0)
            total = jnp.sum(weights, axis=1, keepdims=True)
            mixed = lax.dot_general(
                weights.astype(jnp.bfloat16),
                keys[:latent],
                (((1,), (1,)), ((), ())),
                preferred_element_type=jnp.float32,
            )
            some = total > 0.0
            safe = jnp.where(some, total, 1.0)
            mixed = mixed * jnp.where(some, 1.0 / safe, 0.0)
            lse = jnp.where(some, top + jnp.log(safe), far_below)
            lse_buf[...] = jnp.where(lane == r, lse, lse_buf[...])
            parts.append(mixed)
        rows_at = pl.ds(pl.multiple_of(step * 4 * head_local, 4 * head_local), 4 * head_local)
        for k in range(owners):
            acc[k, rows_at, :] = jnp.concatenate(
                [one[k * head_local : (k + 1) * head_local] for one in parts], axis=0
            )
        return carry

    lax.fori_loop(0, group // 4, four, 0)
    rows = group * head_local
    for piece in range(latent // LANES):
        out_ref[:, piece * rows : (piece + 1) * rows, :] = acc[
            :, :, piece * LANES : (piece + 1) * LANES
        ].astype(jnp.bfloat16)
    lse_all = lse_buf[...]
    high = lse_all.astype(jnp.bfloat16).astype(jnp.float32)
    mid = (lse_all - high).astype(jnp.bfloat16).astype(jnp.float32)
    low = lse_all - high - mid
    tail = latent // LANES * rows
    for k in range(owners):
        own = slice(k * head_local, (k + 1) * head_local)
        out_ref[k, tail:, :] = jnp.concatenate(
            [high[own], mid[own], low[own], jnp.zeros_like(low[own])], axis=0
        ).astype(jnp.bfloat16)


def attend(scalars, q_all, pieces, latent, head_local):
    group, heads, width = q_all.shape
    slots, _, block_len = pieces[0].shape
    owners = heads // head_local
    rows = group * head_local
    out_rows = latent // LANES * rows + 16
    any_spec = pl.BlockSpec(memory_space=pl.ANY)
    return pl.pallas_call(
        functools.partial(attend_kernel, heads, group, latent, head_local),
        out_shape=jax.ShapeDtypeStruct((owners, out_rows, LANES), jnp.bfloat16),
        in_specs=[pl.BlockSpec(memory_space=pltpu.SMEM)] + [any_spec] * 15,
        out_specs=pl.BlockSpec(memory_space=pltpu.VMEM),
        scratch_shapes=[
            pltpu.VMEM((2, 4 * slots, width, block_len), jnp.bfloat16),
            pltpu.VMEM((group, heads, width), jnp.bfloat16),
            pltpu.VMEM((owners, rows, latent), jnp.float32),
            pltpu.VMEM((heads, LANES), jnp.float32),
            pltpu.SemaphoreType.DMA((15,)),
        ],
        compiler_params=pltpu.CompilerParams(vmem_limit_bytes=40 * 1024 * 1024),
        name="attend",
    )(scalars, q_all, *pieces)


def body(
    queries,
    cache_pool,
    holder,
    slot_ids,
    lengths,
    residual,
    w_value,
    w_out,
    norm_gain,
    w_gate,
    w_up,
    w_down,
):
    ranks = lax.axis_size("dp")
    tensors = lax.axis_size("tensor")
    my_rank = lax.axis_index("dp")
    column = lax.axis_index("tensor")
    core = column % CORES
    chips = tensors // CORES
    group = residual.shape[0]
    slots, width, block_len = cache_pool.shape
    head_local, latent, value_width = w_value.shape
    heads = head_local * chips
    features = residual.shape[1]
    tiles = features // LANES
    swap = [(i, i ^ 1) for i in range(tensors)]
    same_core = [[c + CORES * k for k in range(chips)] for c in range(CORES)]
    from_next = [((i + 1) % ranks, i) for i in range(ranks)]
    from_prev = [((i - 1) % ranks, i) for i in range(ranks)]

    def swapped(value):
        return lax.ppermute(value, "tensor", swap)

    half = slots // 2
    lo, hi = cache_pool[:half], cache_pool[half:]
    next_lo = lax.ppermute(lo, "dp", from_next)
    prev_hi = lax.ppermute(hi, "dp", from_prev)
    next_hi = lax.ppermute(hi, "dp", from_next)
    prev_lo = lax.ppermute(lo, "dp", from_prev)
    far_lo = lax.ppermute(next_lo, "dp", from_next)
    far_hi = lax.ppermute(prev_hi, "dp", from_prev)
    mine = [cache_pool, next_lo, next_hi, prev_lo, prev_hi, far_lo, far_hi]
    others = [swapped(one) for one in mine]

    want = jnp.arange(2 * heads, dtype=jnp.int32)
    side, rest = want // heads, want % heads
    chosen_core = jnp.where(side == 0, core, 1 - core)
    head_id = (rest // head_local) * (CORES * head_local) + chosen_core * head_local + rest % head_local
    select = (head_id[:, None] == jnp.arange(2 * heads, dtype=jnp.int32)[None, :]).astype(jnp.bfloat16)
    turned = lax.dot_general(
        select, queries[0], (((1,), (1,)), ((), ())), preferred_element_type=jnp.float32
    ).astype(jnp.bfloat16)
    q_keep, q_send = turned[:heads], turned[heads:]
    q_got = swapped(q_send)
    q_pair = jnp.stack([jnp.where(core == 0, q_keep, q_got), jnp.where(core == 0, q_got, q_keep)])
    q_all = lax.all_gather(q_pair, "tensor", axis=0, tiled=True, axis_index_groups=same_core)

    first = my_rank * group
    own_holder = lax.dynamic_slice_in_dim(holder[:, 0], first, group)
    own_slots = lax.dynamic_slice_in_dim(slot_ids[:, 0], first, group)
    place = ((own_holder - my_rank) % ranks) * slots + own_slots
    place_other = swapped(place)
    group_lengths = lax.dynamic_slice_in_dim(lengths, first, group)
    bases = jnp.zeros((group,), jnp.int32).at[0].set(column * block_len).at[1].set((column ^ 1) * block_len)
    scalars = jnp.stack([place, place_other, group_lengths, bases])

    partial = attend(scalars, q_all, mine + others, latent, head_local)
    parts = lax.all_to_all(
        partial, "tensor", split_axis=0, concat_axis=0, tiled=True, axis_index_groups=same_core
    )
    rows = group * head_local
    pieces = latent // LANES
    lse3 = parts[:, pieces * rows :, :group].astype(jnp.float32).reshape(chips, 4, head_local, group)
    lse = lse3[:, 0] + lse3[:, 1] + lse3[:, 2]
    share = jnp.exp(lse - jnp.max(lse, axis=0, keepdims=True))
    share = share / jnp.sum(share, axis=0, keepdims=True)
    share = jnp.transpose(share, (0, 2, 1)).reshape(chips, 1, rows, 1)
    latents = parts[:, : pieces * rows].astype(jnp.float32).reshape(chips, pieces, rows, LANES)
    attended = jnp.sum(latents * share, axis=0).astype(jnp.bfloat16)
    attended = attended.reshape(pieces, group, head_local, LANES)
    per_head = jnp.einsum(
        "prhd,hpdv->rhv",
        attended,
        w_value.reshape(head_local, pieces, LANES, value_width),
        preferred_element_type=jnp.float32,
    ).astype(jnp.bfloat16)

    def to_rows(value):
        sent = value.astype(jnp.bfloat16).reshape(group, tiles, LANES)
        got = lax.all_to_all(sent, "tensor", split_axis=0, concat_axis=0, tiled=True)
        return jnp.sum(got.astype(jnp.float32), axis=0)

    attention = to_rows(
        jnp.dot(per_head.reshape(group, -1), w_out, preferred_element_type=jnp.float32)
    )
    own_residual = lax.dynamic_index_in_dim(residual, column, 0, keepdims=False)
    residual_sum = own_residual.astype(jnp.float32).reshape(tiles, LANES) + attention
    scale_inv = lax.rsqrt(jnp.mean(residual_sum * residual_sum) + norm_eps)
    normed = (residual_sum * scale_inv * norm_gain.reshape(tiles, LANES)).astype(jnp.bfloat16)
    normed_all = lax.all_to_all(
        jnp.broadcast_to(normed[None], (group, tiles, LANES)),
        "tensor",
        split_axis=0,
        concat_axis=0,
        tiled=True,
    ).reshape(group, features)
    gate_val = jnp.dot(normed_all, w_gate, preferred_element_type=jnp.float32)
    up_val = jnp.dot(normed_all, w_up, preferred_element_type=jnp.float32)
    activated = (jax.nn.silu(gate_val) * up_val).astype(jnp.bfloat16)
    down = to_rows(jnp.dot(activated, w_down, preferred_element_type=jnp.float32))
    return (residual_sum + down).reshape(1, features)


def solution(mesh):
    in_specs = (
        P(("dp", "tensor"), None, None),
        P(("dp", "tensor"), None, None),
        P(None, "tensor"),
        P(None, "tensor"),
        P(),
        P("dp", None),
        P("tensor", None, None),
        P("tensor", None),
        P(),
        P(None, "tensor"),
        P(None, "tensor"),
        P("tensor", None),
    )
    out_specs = P(("dp", "tensor"), None)
    return jax.shard_map(body, mesh=mesh, in_specs=in_specs, out_specs=out_specs, check_vma=False)
```

time: 516 us -> 193 us (0.37)
  waiting for transfers between devices: 376 us -> 42.5 us
  blocking collectives: 0 us -> 63.9 us
  matrix products: 52.1 us -> 15.9 us
  other arithmetic: 23.7 us -> 7.66 us
  Pallas kernels: 0 us -> 13.7 us
  local copies, waits for them, and re-layouts: 20.4 us -> 12.5 us
  starting transfers between devices: 29.7 us -> 21.8 us
    all_to_all x4 -> x1, waiting for transfers between devices: 142 us -> 11 us  [to_rows(): lax.all_to_all(sent, 'tensor', split_axis=0, concat_axis=0, tiled=True)]
    psum x1 -> x0, waiting for transfers between devices: 104 us -> none  [body(): lax.psum(jnp.dot(flat_heads, w_out, preferred_element_type=jnp.float32),...]
    unnamed x4 -> x1, waiting for transfers between devices: 104 us -> 0.02 us
    all_to_all x0 -> x3, blocking collectives: none -> 63.9 us  [the longest x1 34.8 us: body(): lax.all_to_all(partial, 'tensor', split_axis=0, concat_axis=0, tiled=True...]
    dot_general x7 -> x4, matrix products: 44.6 us -> 9.36 us  [the longest x1 4.45 us: body(): jnp.dot(per_head.reshape(group, -1), w_out, preferred_element_type=jnp.fl...]
    ppermute x0 -> x15, waiting for transfers between devices: none -> 31.5 us  [the longest x1 11.4 us: body(): prev_lo = lax.ppermute(lo, 'dp', from_prev)]
    all_gather x1, waiting for transfers between devices: 26.4 us -> 0.01 us  [body(): lax.all_gather(q_pair, 'tensor', axis=0, tiled=True, axis_index_groups=sa...]
    all_to_all x4 -> x1, starting transfers between devices: 29.4 us -> 5.34 us  [to_rows(): lax.all_to_all(sent, 'tensor', split_axis=0, concat_axis=0, tiled=True)]
  transfers between devices with their start and end apart: 7 -> 17, of which waited for: 5 -> 8; matrix products, arithmetic and copies ran while one was open for 11% -> 2% of each run, Pallas kernels for 0% -> 0%
where the time goes in v1:
time: 193 us; the launch traced here: 192 us
  blocking collectives  63.9 us (33%)
  waiting for transfers between devices  42.5 us (22%)
  starting transfers between devices  21.8 us (11%)
  matrix products  15.9 us (8%)
  between operations  14.3 us (7%)
  Pallas kernels  13.7 us (7%)
  local copies, waits for them, and re-layouts  12.5 us (6%)
  other arithmetic  7.66 us (4%)
    all_to_all x1, blocking collectives, body(): lax.all_to_all(partial, 'tensor', split_axis=0, concat_axis=0, tiled=True...  34.8 us
    all_to_all x1, blocking collectives, body(): lax.all_to_all(jnp.broadcast_to(normed[None], (group, tiles, LANES)), 'te...  14.5 us
    all_to_all x1, blocking collectives, to_rows(): lax.all_to_all(sent, 'tensor', split_axis=0, concat_axis=0, tiled=True)  14.5 us
    pallas_call x1, Pallas kernels, attend(): pl.pallas_call(functools.partial(attend_kernel, heads, group, latent, hea...  13.7 us
    ppermute x1, waiting for transfers between devices, body(): prev_lo = lax.ppermute(lo, 'dp', from_prev)  11.4 us
    all_to_all x1, waiting for transfers between devices, to_rows(): lax.all_to_all(sent, 'tensor', split_axis=0, concat_axis=0, tiled=True)  11 us
    unnamed x24, local copies, waits for them, and re-layouts  8.22 us
    ppermute x9, starting transfers between devices, swapped(): return lax.ppermute(value, 'tensor', swap)  8.12 us
  transfers between devices with their start and end apart: 17, of which 8 were waited for; matrix products, arithmetic and copies ran while one was open for 2% of the time, Pallas kernels for 0%

profile of v1, /device:TPU:1, one launch (start us, length us, event | category | flops | bytes accessed | tf_op | source)
XLA Modules:
  0.0 192.2 jit_solution(2487150905524481189)
XLA Ops:
  6.6 1.3 convolution_convert_fusion.2
  8.0 1.5 collective-permute-start.1
  9.5 1.0 collective-permute-done.1
  11.4 2.4 %fusion.42 = (bf16[4,576,128]{2,1,0:T(8,128)(2,1)}, bf16[4,576,128]{2,1,0:T(8,128)(2,1)}) fusion(bf16[8,576,128]{2,1,0:T(8,128)(2,1)} %refs_1_.1), kind=kLoop, calls=%fused_computation.78 | loop fusion | bytes 2359296 | tf_op jit(solution)/shard_map/slice | solution.py:154
  13.8 1.7 collective-permute-start.5
  15.6 2.1 %collective-permute-start.3 = (bf16[4,576,128]{2,1,0:T(8,128)(2,1)}, bf16[4,576,128]{2,1,0:T(8,128)(2,1)}, u32[]{:S(2)}, u32[]{:S(2)}) collective-permute-start(bf16[4,576,128]{2,1,0:T(8,128)(2,1)} %get-tuple-element.34), channel_id=1, source_target_pairs={{32,0},{64,32},{96,64},{0,96},{33,1},{65,33},{97,65},{1,97},{34,2}... | collective-permute-start | bytes 1769480 | tf_op jit(solution)/shard_map/ppermute | solution.py:157
  17.7 2.7 %collective-permute-start.2 = (bf16[4,576,128]{2,1,0:T(8,128)(2,1)}, bf16[4,576,128]{2,1,0:T(8,128)(2,1)}, u32[]{:S(2)}, u32[]{:S(2)}) collective-permute-start(bf16[4,576,128]{2,1,0:T(8,128)(2,1)} %get-tuple-element.35), channel_id=1, source_target_pairs={{32,0},{64,32},{96,64},{0,96},{33,1},{65,33},{97,65},{1,97},{34,2}... | collective-permute-start | bytes 1769480 | tf_op jit(solution)/shard_map/ppermute | solution.py:155
  21.1 1.2 collective-permute-start
  23.5 7.8 %collective-permute-done.5.refs_5_ = bf16[4,576,128]{2,1,0:T(8,128)(2,1)S(1)} collective-permute-done((bf16[4,576,128]{2,1,0:T(8,128)(2,1)}, bf16[4,576,128]{2,1,0:T(8,128)(2,1)S(1)}, u32[]{:S(2)}, u32[]{:S(2)}) %collective-permute-start.5) | collective-permute-done | bytes 589856 | tf_op jit(solution)/shard_map/ppermute | solution.py:156
  31.3 1.4 collective-permute-start.12
  32.6 11.4 %collective-permute-done.4.refs_4_ = bf16[4,576,128]{2,1,0:T(8,128)(2,1)} collective-permute-done((bf16[4,576,128]{2,1,0:T(8,128)(2,1)}, bf16[4,576,128]{2,1,0:T(8,128)(2,1)}, u32[]{:S(2)}, u32[]{:S(2)}) %collective-permute-start.4) | collective-permute-done | bytes 589856 | tf_op jit(solution)/shard_map/ppermute | solution.py:158
  44.0 1.4 collective-permute-start.10
  45.4 1.8 collective-permute-start.6
  48.7 7.9 %collective-permute-done.7.refs_7_ = bf16[4,576,128]{2,1,0:T(8,128)(2,1)} collective-permute-done((bf16[4,576,128]{2,1,0:T(8,128)(2,1)S(1)}, bf16[4,576,128]{2,1,0:T(8,128)(2,1)}, u32[]{:S(2)}, u32[]{:S(2)}) %collective-permute-start.7) | collective-permute-done | bytes 589856 | tf_op jit(solution)/shard_map/ppermute | solution.py:160
  56.7 0.9 collective-permute-start.11
  57.6 0.9 copy-done.5
  58.4 2.2 %collective-permute-done.6.refs_6_ = bf16[4,576,128]{2,1,0:T(8,128)(2,1)} collective-permute-done((bf16[4,576,128]{2,1,0:T(8,128)(2,1)}, bf16[4,576,128]{2,1,0:T(8,128)(2,1)}, u32[]{:S(2)}, u32[]{:S(2)}) %collective-permute-start.6) | collective-permute-done | bytes 589856 | tf_op jit(solution)/shard_map/ppermute | solution.py:159
  63.4 1.7 copy-done.2
  65.2 1.1 copy-done.4
  66.2 1.1 copy-done.6
  67.3 13.7 %attend.1 = bf16[16,528,128]{2,1,0:T(8,128)(2,1)S(1)} custom-call(s32[4,32]{1,0:T(4,128)S(1)} %pad_add_fusion.scal_ref, bf16[32,64,576]{2,1,0:T(8,128)(2,1)S(1)} %copy-done.2, bf16[8,576,128]{2,1,0:T(8,128)(2,1)S(1)} %copy-done.1, bf16[4,576,128]{2,1,0:T(8,128)(2,1)} %collective-permute-done.2.refs_2_, bf16[4,576,128]{2,1,0:T(8,128)(2,1)} %collective-permute-done.3.refs_3_, ...), custom_call_target="tpu_custom_call" | custom-call | tf_op jit(solution)/shard_map/attend/pallas_call | solution.py:102
  81.0 34.8 %all_to_all.20 = bf16[16,528,128]{2,1,0:T(8,128)(2,1)S(1)} all-to-all(bf16[16,528,128]{2,1,0:T(8,128)(2,1)S(1)} %attend.1), channel_id=1, replica_groups={{0,2,4,6,8,10,12,14,16,18,20,22,24,26,28,30},{1,3,5,7,9,11,13,15,17,19,..., dimensions={0} | all-to-all | bytes 4325376 | tf_op jit(solution)/shard_map/all_to_all | solution.py:187
  115.9 1.4 copy-done.7
  118.1 3.2 %multiply_reduce_fusion = bf16[512,128]{1,0:T(8,128)(2,1)S(1)} fusion(bf16[16,528,128]{2,1,0:T(8,128)(2,1)} %copy-done.7, f32[16,512]{1,0:T(8,128)S(1)} %bitcast.85), kind=kLoop, calls=%fused_computation.3 | loop fusion | flops 3080192 | bytes 2260992 | tf_op jit(solution)/shard_map/reduce_sum | solution.py:198
  121.6 4.5 %fusion.1 = bf16[4,8,56,128]{3,1,2,0:T(8,128)(2,1)S(1)} fusion(bf16[512,7168]{1,0:T(8,128)(2,1)} %param.23, bf16[4,4,8,128]{3,2,1,0:T(8,128)(2,1)S(1)} %fusion.6), kind=kOutput, calls=%fused_computation.4 | convolution fusion | flops 235110400 | bytes 7831552 | tf_op jit(solution)/shard_map/dot_general | solution.py:213
  126.9 5.3 %all-to-all-start.1 = ((bf16[32,56,128]{2,1,0:T(8,128)(2,1)}), bf16[32,56,128]{2,1,0:T(8,128)(2,1)S(1)}, u32[]{:S(2)}, u32[]{:S(2)}) async-start(bf16[32,56,128]{2,1,0:T(8,128)(2,1)} %bitcast.32), calls=%async_computation.1 | async-start | bytes 917504 | tf_op jit(solution)/shard_map/all_to_all | solution.py:209
  132.2 11.0 %all-to-all-done.1 = bf16[32,56,128]{2,1,0:T(8,128)(2,1)S(1)} async-done(((bf16[32,56,128]{2,1,0:T(8,128)(2,1)}), bf16[32,56,128]{2,1,0:T(8,128)(2,1)S(1)}, u32[]{:S(2)}, u32[]{:S(2)}) %all-to-all-start.1) | async-done | bytes 458784 | tf_op jit(solution)/shard_map/all_to_all | solution.py:209
  143.2 1.6 multiply_reduce_fusion.1
  145.6 14.5 %all_to_all.21 = bf16[32,56,128]{2,1,0:T(8,128)(2,1)S(1)} all-to-all(bf16[32,56,128]{2,1,0:T(8,128)(2,1)S(1)} %broadcast_in_dim.12), channel_id=1, replica_groups=mesh['dp'=4,'tensor'=32] {'tensor'}, dimensions={0} | all-to-all | bytes 917504 | tf_op jit(solution)/shard_map/all_to_all | solution.py:219
  160.1 3.4 %fusion.9 = f32[32,384]{1,0:T(8,128)S(1)} fusion(bf16[7168,384]{1,0:T(8,128)(2,1)} %param.25, bf16[4,8,56,128]{3,2,1,0:T(8,128)(2,1)S(1)} %bitcast.79), kind=kOutput, calls=%fused_computation.16 | convolution fusion | flops 176160768 | bytes 6012928 | tf_op jit(solution)/shard_map/dot_general | solution.py:226
  163.6 6.5 %fusion.2 = bf16[4,8,56,128]{3,1,2,0:T(8,128)(2,1)S(1)} fusion(bf16[384,7168]{1,0:T(8,128)(2,1)} %param.27, bf16[7168,384]{1,0:T(8,128)(2,1)} %param.26, bf16[4,8,56,128]{3,2,1,0:T(8,128)(2,1)S(1)} %bitcast.80, f32[32,384]{1,0:T(8,128)S(1)} %fusion.9), kind=kOutput, calls=%fused_computation.5 | convolution fusion | flops 352624640 | bytes 11976704 | tf_op jit(solution)/shard_map/dot_general | solution.py:229
  170.2 14.5 %all_to_all.22 = bf16[32,56,128]{2,1,0:T(8,128)(2,1)S(1)} all-to-all(bf16[32,56,128]{2,1,0:T(8,128)(2,1)S(1)} %bitcast.81), channel_id=1, replica_groups=mesh['dp'=4,'tensor'=32] {'tensor'}, dimensions={0} | all-to-all | bytes 917504 | tf_op jit(solution)/shard_map/all_to_all | solution.py:209
  (61 shorter events, 10.1 us)
Async XLA Ops:
  6.5 114.8 %copy-start = (bf16[4,512,128]{2,1,0:T(8,128)(2,1)S(1)}, bf16[4,512,128]{2,1,0:T(8,128)(2,1)}, u32[]{:S(2)}) copy-start(bf16[4,512,128]{2,1,0:T(8,128)(2,1)} %param.22) | copy-start | bytes 1572868
  6.5 56.9 %copy-start.1 = (bf16[8,576,128]{2,1,0:T(8,128)(2,1)S(1)}, bf16[8,576,128]{2,1,0:T(8,128)(2,1)}, u32[]{:S(2)}) copy-start(bf16[8,576,128]{2,1,0:T(8,128)(2,1)} %refs_1_.1) | copy-start | bytes 3538948
  6.5 56.9 %all-gather.2.cloned.1.call-start = ((), (), s32[]{:S(2)}) async-start(), calls=%async_computation.4 | async-start | bytes 2785280 | tf_op jit(solution)/shard_map/all_gather | solution.py:175
  8.0 2.5 %collective-permute-start.1 = (bf16[64,576]{0,1:T(8,128)(2,1)S(1)}, bf16[64,576]{0,1:T(8,128)(2,1)S(1)}, u32[]{:S(2)}, u32[]{:S(2)}) collective-permute-start(bf16[64,576]{0,1:T(8,128)(2,1)S(1)} %slice.56), channel_id=1, source_target_pairs={{0,1},{1,0},{2,3},{3,2},{4,5},{5,4},{6,7},{7,6},{8,9},{9,8},{10,11... | collective-permute-start | bytes 221192 | tf_op jit(solution)/shard_map/ppermute | solution.py:151
  13.8 17.5 %collective-permute-start.5 = (bf16[4,576,128]{2,1,0:T(8,128)(2,1)}, bf16[4,576,128]{2,1,0:T(8,128)(2,1)S(1)}, u32[]{:S(2)}, u32[]{:S(2)}) collective-permute-start(bf16[4,576,128]{2,1,0:T(8,128)(2,1)} %get-tuple-element.34), channel_id=1, source_target_pairs={{96,0},{0,32},{32,64},{64,96},{97,1},{1,33},{33,65},{65,97},{98,2}... | collective-permute-start | bytes 1769480 | tf_op jit(solution)/shard_map/ppermute | solution.py:156
  15.6 17.1 %collective-permute-start.3 = (bf16[4,576,128]{2,1,0:T(8,128)(2,1)}, bf16[4,576,128]{2,1,0:T(8,128)(2,1)}, u32[]{:S(2)}, u32[]{:S(2)}) collective-permute-start(bf16[4,576,128]{2,1,0:T(8,128)(2,1)} %get-tuple-element.34), channel_id=1, source_target_pairs={{32,0},{64,32},{96,64},{0,96},{33,1},{65,33},{97,65},{1,97},{34,2}... | collective-permute-start | bytes 1769480 | tf_op jit(solution)/shard_map/ppermute | solution.py:157
  17.7 26.4 %collective-permute-start.4 = (bf16[4,576,128]{2,1,0:T(8,128)(2,1)}, bf16[4,576,128]{2,1,0:T(8,128)(2,1)}, u32[]{:S(2)}, u32[]{:S(2)}) collective-permute-start(bf16[4,576,128]{2,1,0:T(8,128)(2,1)} %get-tuple-element.35), channel_id=1, source_target_pairs={{96,0},{0,32},{32,64},{64,96},{97,1},{1,33},{33,65},{65,97},{98,2}... | collective-permute-start | bytes 1769480 | tf_op jit(solution)/shard_map/ppermute | solution.py:158
  17.7 27.7 %collective-permute-start.2 = (bf16[4,576,128]{2,1,0:T(8,128)(2,1)}, bf16[4,576,128]{2,1,0:T(8,128)(2,1)}, u32[]{:S(2)}, u32[]{:S(2)}) collective-permute-start(bf16[4,576,128]{2,1,0:T(8,128)(2,1)} %get-tuple-element.35), channel_id=1, source_target_pairs={{32,0},{64,32},{96,64},{0,96},{33,1},{65,33},{97,65},{1,97},{34,2}... | collective-permute-start | bytes 1769480 | tf_op jit(solution)/shard_map/ppermute | solution.py:155
  21.1 2.1 %collective-permute-start = (s32[32]{0:T(128)S(1)}, s32[32]{0:T(128)S(1)}, u32[]{:S(2)}, u32[]{:S(2)}) collective-permute-start(s32[32]{0:T(128)S(1)} %fusion.35), channel_id=1, source_target_pairs={{0,1},{1,0},{2,3},{3,2},{4,5},{5,4},{6,7},{7,6},{8,9},{9,8},{10,11... | collective-permute-start | bytes 392 | tf_op jit(solution)/shard_map/ppermute | solution.py:151
  23.2 39.9 %collective-permute-start.8 = (bf16[8,576,128]{2,1,0:T(8,128)(2,1)}, bf16[8,576,128]{2,1,0:T(8,128)(2,1)S(1)}, u32[]{:S(2)}, u32[]{:S(2)}) collective-permute-start(bf16[8,576,128]{2,1,0:T(8,128)(2,1)} %refs_1_.1), channel_id=1, source_target_pairs={{0,1},{1,0},{2,3},{3,2},{4,5},{5,4},{6,7},{7,6},{8,9},{9,8},{10,11... | collective-permute-start | bytes 3538952 | tf_op jit(solution)/shard_map/ppermute | solution.py:151
  31.3 15.9 %collective-permute-start.12 = (bf16[4,576,128]{2,1,0:T(8,128)(2,1)S(1)}, bf16[4,576,128]{2,1,0:T(8,128)(2,1)S(1)}, u32[]{:S(2)}, u32[]{:S(2)}) collective-permute-start(bf16[4,576,128]{2,1,0:T(8,128)(2,1)S(1)} %collective-permute-done.5.refs_5_), channel_id=1, source_target_pairs={{0,1},{1,0},{2,3},{3,2},{4,5},{5,4},{6,7},{7,6},{8,9},{9,8},{10,11... | collective-permute-start | bytes 1769480 | tf_op jit(solution)/shard_map/ppermute | solution.py:151
  32.6 24.0 %collective-permute-start.7 = (bf16[4,576,128]{2,1,0:T(8,128)(2,1)S(1)}, bf16[4,576,128]{2,1,0:T(8,128)(2,1)}, u32[]{:S(2)}, u32[]{:S(2)}) collective-permute-start(bf16[4,576,128]{2,1,0:T(8,128)(2,1)S(1)} %collective-permute-done.5.refs_5_), channel_id=1, source_target_pairs={{96,0},{0,32},{32,64},{64,96},{97,1},{1,33},{33,65},{65,97},{98,2}... | collective-permute-start | bytes 1769480 | tf_op jit(solution)/shard_map/ppermute | solution.py:160
  44.0 13.5 %collective-permute-start.10 = (bf16[4,576,128]{2,1,0:T(8,128)(2,1)}, bf16[4,576,128]{2,1,0:T(8,128)(2,1)S(1)}, u32[]{:S(2)}, u32[]{:S(2)}) collective-permute-start(bf16[4,576,128]{2,1,0:T(8,128)(2,1)} %collective-permute-done.3.refs_3_), channel_id=1, source_target_pairs={{0,1},{1,0},{2,3},{3,2},{4,5},{5,4},{6,7},{7,6},{8,9},{9,8},{10,11... | collective-permute-start | bytes 1769480 | tf_op jit(solution)/shard_map/ppermute | solution.py:151
  45.4 15.3 %collective-permute-start.6 = (bf16[4,576,128]{2,1,0:T(8,128)(2,1)}, bf16[4,576,128]{2,1,0:T(8,128)(2,1)}, u32[]{:S(2)}, u32[]{:S(2)}) collective-permute-start(bf16[4,576,128]{2,1,0:T(8,128)(2,1)} %collective-permute-done.2.refs_2_), channel_id=1, source_target_pairs={{32,0},{64,32},{96,64},{0,96},{33,1},{65,33},{97,65},{1,97},{34,2}... | collective-permute-start | bytes 1769480 | tf_op jit(solution)/shard_map/ppermute | solution.py:159
  47.2 0.9 copy-start.3
  48.0 15.0 %collective-permute-start.9 = (bf16[4,576,128]{2,1,0:T(8,128)(2,1)}, bf16[4,576,128]{2,1,0:T(8,128)(2,1)}, u32[]{:S(2)}, u32[]{:S(2)}) collective-permute-start(bf16[4,576,128]{2,1,0:T(8,128)(2,1)} %collective-permute-done.2.refs_2_), channel_id=1, source_target_pairs={{0,1},{1,0},{2,3},{3,2},{4,5},{5,4},{6,7},{7,6},{8,9},{9,8},{10,11... | collective-permute-start | bytes 1769480 | tf_op jit(solution)/shard_map/ppermute | solution.py:151
  56.7 6.4 %collective-permute-start.11 = (bf16[4,576,128]{2,1,0:T(8,128)(2,1)}, bf16[4,576,128]{2,1,0:T(8,128)(2,1)}, u32[]{:S(2)}, u32[]{:S(2)}) collective-permute-start(bf16[4,576,128]{2,1,0:T(8,128)(2,1)} %collective-permute-done.4.refs_4_), channel_id=1, source_target_pairs={{0,1},{1,0},{2,3},{3,2},{4,5},{5,4},{6,7},{7,6},{8,9},{9,8},{10,11... | collective-permute-start | bytes 1769480 | tf_op jit(solution)/shard_map/ppermute | solution.py:151
  57.6 0.9 copy-start.5
  58.4 4.7 %collective-permute-start.14 = (bf16[4,576,128]{2,1,0:T(8,128)(2,1)}, bf16[4,576,128]{2,1,0:T(8,128)(2,1)}, u32[]{:S(2)}, u32[]{:S(2)}) collective-permute-start(bf16[4,576,128]{2,1,0:T(8,128)(2,1)} %collective-permute-done.7.refs_7_), channel_id=1, source_target_pairs={{0,1},{1,0},{2,3},{3,2},{4,5},{5,4},{6,7},{7,6},{8,9},{9,8},{10,11... | collective-permute-start | bytes 1769480 | tf_op jit(solution)/shard_map/ppermute | solution.py:151
  60.7 2.8 %collective-permute-start.13 = (bf16[4,576,128]{2,1,0:T(8,128)(2,1)}, bf16[4,576,128]{2,1,0:T(8,128)(2,1)}, u32[]{:S(2)}, u32[]{:S(2)}) collective-permute-start(bf16[4,576,128]{2,1,0:T(8,128)(2,1)} %collective-permute-done.6.refs_6_), channel_id=1, source_target_pairs={{0,1},{1,0},{2,3},{3,2},{4,5},{5,4},{6,7},{7,6},{8,9},{9,8},{10,11... | collective-permute-start | bytes 1769480 | tf_op jit(solution)/shard_map/ppermute | solution.py:151
  63.4 1.7 copy-start.2
  65.2 1.1 copy-start.4
  66.2 1.1 copy-start.6
  115.9 1.4 copy-start.7
  121.5 24.0 %copy-start.8 = (f32[7168]{0:T(1024)S(1)}, f32[7168]{0:T(1024)}, u32[]{:S(2)}) copy-start(f32[7168]{0:T(1024)} %param.24) | copy-start | bytes 86020
  126.9 16.3 %all-to-all-start.1 = ((bf16[32,56,128]{2,1,0:T(8,128)(2,1)}), bf16[32,56,128]{2,1,0:T(8,128)(2,1)S(1)}, u32[]{:S(2)}, u32[]{:S(2)}) async-start(bf16[32,56,128]{2,1,0:T(8,128)(2,1)} %bitcast.32), calls=%async_computation.1 | async-start | bytes 917504 | tf_op jit(solution)/shard_map/all_to_all | solution.py:209
Sparse Core Ops, SparseCore 0:
  11.6 47.9 all-gather.1

commit v2 on v0

v2 whole, which is shorter than its diff:
```python
import functools

import jax
import jax.numpy as jnp
from jax import lax
from jax.experimental import pallas as pl
from jax.experimental.pallas import tpu as pltpu
from jax.sharding import PartitionSpec as P

score_scale = 192.0 ** (-0.5)
norm_eps = 1e-06
far_below = -1e30
CORES = 2
LANES = 128
MIB = 1024 * 1024
hbm_spec = pl.BlockSpec(memory_space=pl.ANY)
vmem_spec = pl.BlockSpec(memory_space=pltpu.VMEM)
smem_spec = pl.BlockSpec(memory_space=pltpu.SMEM)


def in_vmem(value):
    return pltpu.with_memory_space_constraint(value, pltpu.VMEM)


def in_hbm(value):
    return pltpu.with_memory_space_constraint(value, pltpu.HBM)


def split_kernel(pool, low, high, sems):
    half = low.shape[0]
    copies = [
        pltpu.make_async_copy(pool.at[pl.ds(i * half, half)], one, sems.at[i])
        for i, one in enumerate((low, high))
    ]
    for one in copies:
        one.start()
    for one in copies:
        one.wait()


def split_pool(pool):
    half = (pool.shape[0] // 2,) + pool.shape[1:]
    return pl.pallas_call(
        split_kernel,
        out_shape=(pltpu.VMEM(half, pool.dtype), pltpu.VMEM(half, pool.dtype)),
        in_specs=[hbm_spec],
        out_specs=(vmem_spec, vmem_spec),
        scratch_shapes=[pltpu.SemaphoreType.DMA((2,))],
        compiler_params=pltpu.CompilerParams(vmem_limit_bytes=4 * MIB),
        name="split_pool",
    )(in_hbm(pool))


def stage_kernel(count, *refs):
    copies = [
        pltpu.make_async_copy(refs[i], refs[count + i], refs[2 * count].at[i]) for i in range(count)
    ]
    for one in copies:
        one.start()
    for one in copies:
        one.wait()


def stage(*weights):
    count = len(weights)
    size = sum(one.size * one.dtype.itemsize for one in weights)
    return pl.pallas_call(
        functools.partial(stage_kernel, count),
        out_shape=tuple(pltpu.VMEM(one.shape, one.dtype) for one in weights),
        in_specs=[hbm_spec] * count,
        out_specs=(vmem_spec,) * count,
        scratch_shapes=[pltpu.SemaphoreType.DMA((count,))],
        compiler_params=pltpu.CompilerParams(vmem_limit_bytes=4 * MIB),
        cost_estimate=pl.CostEstimate(flops=0, bytes_accessed=2 * size, transcendentals=0),
        name="stage",
    )(*[in_hbm(one) for one in weights])


QUERY_PARTS = 4
UNROLL = 8


def attend_kernel(dims, code_own, code_other, lengths, q_hbm, *refs):
    slots, ranks, head_local, latent, piece_count = dims
    pieces = refs[:piece_count]
    out_ref, kbuf, qraw, qbuf, lse_buf, sems = refs[piece_count:]
    group = q_hbm.shape[0]
    portion, heads, _ = qbuf.shape
    block_len = kbuf.shape[2]
    owners = heads // head_local
    my_rank = lax.axis_index("dp")
    column = lax.axis_index("tensor")
    core = column % CORES
    first = my_rank * group
    q_copies = [
        pltpu.make_async_copy(
            q_hbm.at[pl.ds(i * portion, portion)],
            qraw.at[i % 2],
            sems.at[piece_count + i],
        )
        for i in range(QUERY_PARTS)
    ]
    copies = []
    at = 0
    for i, one in enumerate(pieces):
        copies.append(pltpu.make_async_copy(one, kbuf.at[pl.ds(at, one.shape[0])], sems.at[i]))
        at += one.shape[0]
    for one in q_copies[:2] + copies:
        one.start()
    row = lax.broadcasted_iota(jnp.int32, (heads, CORES * heads), 0)
    wanted = (row // head_local) * (CORES * head_local) + core * head_local + row % head_local
    hit = lax.broadcasted_iota(jnp.int32, (heads, CORES * heads), 1) == wanted
    select = jnp.where(hit, 1.0, 0.0).astype(jnp.bfloat16)
    token = lax.broadcasted_iota(jnp.int32, (1, 2 * block_len), 1)
    partner = column + 1 - 2 * core
    position = jnp.where(
        token < block_len, token + column * block_len, token - block_len + partner * block_len
    )
    lane = lax.broadcasted_iota(jnp.int32, (heads, LANES), 1)
    lse_buf[...] = jnp.zeros_like(lse_buf)
    for one in copies:
        one.wait()

    def place(codes, r):
        code = codes[0, first + r]
        return ((code // slots - my_rank + ranks) % ranks) * slots + code % slots

    def turn(slot, step, carry):
        for i in range(UNROLL):
            r = step * UNROLL + i
            qbuf[r] = lax.dot_general(
                select, qraw[slot, r], (((1,), (1,)), ((), ())), preferred_element_type=jnp.float32
            ).astype(jnp.bfloat16)
        return carry

    def several(step, carry):
        rs = [step * UNROLL + i for i in range(UNROLL)]
        keys = [
            jnp.concatenate(
                [kbuf[place(code_own, r)], kbuf[ranks * slots + place(code_other, r)]], axis=1
            )
            for r in rs
        ]
        scores = [
            jnp.dot(qbuf[r % portion], key, preferred_element_type=jnp.float32) * score_scale
            for r, key in zip(rs, keys)
        ]
        weights, scales, lses = [], [], []
        for r, score in zip(rs, scores):
            live = position < lengths[0, first + r]
            masked = jnp.where(live, score, far_below)
            top = jnp.max(masked, axis=1, keepdims=True)
            weight = jnp.where(live, jnp.exp(masked - top), 0.0)
            total = jnp.sum(weight, axis=1, keepdims=True)
            some = total > 0.0
            safe = jnp.where(some, total, 1.0)
            weights.append(weight.astype(jnp.bfloat16))
            scales.append(jnp.where(some, 1.0 / safe, 0.0))
            lses.append(jnp.where(some, top + jnp.log(safe), far_below))
        mixed = [
            lax.dot_general(
                weight, key[:latent], (((1,), (1,)), ((), ())), preferred_element_type=jnp.float32
            )
            * scale
            for weight, key, scale in zip(weights, keys, scales)
        ]
        lse_all = lse_buf[...]
        for r, lse in zip(rs, lses):
            lse_all = jnp.where(lane == r, lse, lse_all)
        lse_buf[...] = lse_all
        count = UNROLL * head_local
        for k in range(owners):
            both = jnp.concatenate(
                [one[k * head_local : (k + 1) * head_local] for one in mixed], axis=0
            ).astype(jnp.bfloat16)
            for p in range(latent // LANES):
                rows_at = pl.multiple_of(p * group * head_local + step * count, count)
                out_ref[k, pl.ds(rows_at, count), :] = both[:, p * LANES : (p + 1) * LANES]
        return carry

    for i in range(QUERY_PARTS):
        q_copies[i].wait()
        steps = portion // UNROLL
        lax.fori_loop(0, steps, functools.partial(turn, i % 2), 0)
        if i + 2 < QUERY_PARTS:
            q_copies[i + 2].start()
        lax.fori_loop(i * steps, (i + 1) * steps, several, 0)
    lse_all = lse_buf[...]
    high = lse_all.astype(jnp.bfloat16).astype(jnp.float32)
    mid = (lse_all - high).astype(jnp.bfloat16).astype(jnp.float32)
    low = lse_all - high - mid
    tail = latent // LANES * group * head_local
    for k in range(owners):
        own = slice(k * head_local, (k + 1) * head_local)
        out_ref[k, tail:, :] = jnp.concatenate(
            [high[own], mid[own], low[own], jnp.zeros_like(low[own])], axis=0
        ).astype(jnp.bfloat16)


def attend(code_own, code_other, lengths, q_all, pieces, ranks, latent, head_local):
    group, width, head_total = q_all.shape
    heads = head_total // CORES
    block_len = pieces[0].shape[2]
    blocks = sum(one.shape[0] for one in pieces)
    owners = heads // head_local
    rows = group * head_local
    out_rows = latent // LANES * rows + 16
    count = len(pieces)
    dims = (blocks // ranks // CORES, ranks, head_local, latent, count)
    return pl.pallas_call(
        functools.partial(attend_kernel, dims),
        out_shape=pltpu.VMEM((owners, out_rows, LANES), jnp.bfloat16),
        in_specs=[smem_spec] * 3 + [hbm_spec] + [vmem_spec] * count,
        out_specs=vmem_spec,
        scratch_shapes=[
            pltpu.VMEM((blocks, width, block_len), jnp.bfloat16),
            pltpu.VMEM((2, group // QUERY_PARTS, width, head_total), jnp.bfloat16),
            pltpu.VMEM((group // QUERY_PARTS, heads, width), jnp.bfloat16),
            pltpu.VMEM((heads, LANES), jnp.float32),
            pltpu.SemaphoreType.DMA((count + QUERY_PARTS,)),
        ],
        compiler_params=pltpu.CompilerParams(vmem_limit_bytes=24 * MIB),
        name="attend",
    )(code_own, code_other, lengths, in_hbm(q_all), *[in_vmem(one) for one in pieces])


def scatter_tiles(flat, value, first_tile, group, tiles):
    for n in range(value.shape[1] // LANES):
        flat[pl.ds(first_tile + n, group, stride=tiles), :] = value[:, n * LANES : (n + 1) * LANES]


def project_kernel(dims, parts, w_value, w_out, sent, att_buf, flat):
    group, head_local, latent, chunk = dims
    sources = parts.shape[0]
    rows = group * head_local
    pieces = latent // LANES
    tiles = w_out.shape[1] // LANES
    tail = pieces * rows
    lses = []
    for s in range(sources):
        three = parts[s, tail:, :].astype(jnp.float32)
        lses.append(
            three[:head_local]
            + three[head_local : 2 * head_local]
            + three[2 * head_local : 3 * head_local]
        )
    peak = functools.reduce(jnp.maximum, lses)
    shares = [jnp.exp(one - peak) for one in lses]
    inverse = 1.0 / functools.reduce(jnp.add, shares)
    share_all = jnp.concatenate([one * inverse for one in shares], axis=0)
    count = sources * head_local
    pick_request = jnp.where(
        lax.broadcasted_iota(jnp.int32, (rows, LANES), 0) // head_local
        == lax.broadcasted_iota(jnp.int32, (rows, LANES), 1),
        1.0,
        0.0,
    )
    valid = lax.broadcasted_iota(jnp.int32, (count, LANES), 1) < group
    spread = lax.dot_general(
        pick_request,
        jnp.where(valid, share_all, 0.0),
        (((1,), (1,)), ((), ())),
        precision=lax.Precision.HIGHEST,
        preferred_element_type=jnp.float32,
    )
    own_head = (
        lax.broadcasted_iota(jnp.int32, (rows, count), 0) % head_local
        == lax.broadcasted_iota(jnp.int32, (rows, count), 1) % head_local
    )
    pick_source = jnp.where(
        lax.broadcasted_iota(jnp.int32, (count, LANES), 0) // head_local
        == lax.broadcasted_iota(jnp.int32, (count, LANES), 1),
        1.0,
        0.0,
    )
    share = jnp.dot(
        jnp.where(own_head, spread, 0.0),
        pick_source,
        precision=lax.Precision.HIGHEST,
        preferred_element_type=jnp.float32,
    )
    totals = [None] * pieces
    for s in range(sources):
        factor = jnp.broadcast_to(share[:, s : s + 1], (rows, LANES))
        for p in range(pieces):
            term = parts[s, p * rows : (p + 1) * rows, :].astype(jnp.float32) * factor
            totals[p] = term if s == 0 else totals[p] + term
    for p in range(pieces):
        att_buf[p] = totals[p]
    heads = []
    for j in range(head_local):
        attended = jnp.concatenate(
            [att_buf[p, pl.ds(j, group, stride=head_local), :] for p in range(pieces)], axis=1
        ).astype(jnp.bfloat16)
        heads.append(
            jnp.dot(attended, w_value[j], preferred_element_type=jnp.float32).astype(jnp.bfloat16)
        )
    per_head = jnp.concatenate(heads, axis=1)
    for c in range(w_out.shape[1] // chunk):
        value = jnp.dot(
            per_head, w_out[:, c * chunk : (c + 1) * chunk], preferred_element_type=jnp.float32
        )
        scatter_tiles(flat, value, c * chunk // LANES, group, tiles)
    for r in range(group):
        sent[r] = flat[r * tiles : (r + 1) * tiles, :].astype(jnp.bfloat16)


def project(parts, w_value, w_out, group):
    head_local, latent, _ = w_value.shape
    features = w_out.shape[1]
    tiles = features // LANES
    dims = (group, head_local, latent, features // 7)
    return pl.pallas_call(
        functools.partial(project_kernel, dims),
        out_shape=pltpu.VMEM((group, tiles, LANES), jnp.bfloat16),
        in_specs=[vmem_spec] * 3,
        out_specs=vmem_spec,
        scratch_shapes=[
            pltpu.VMEM((latent // LANES, group * head_local, LANES), jnp.float32),
            pltpu.VMEM((group * tiles, LANES), jnp.float32),
        ],
        compiler_params=pltpu.CompilerParams(vmem_limit_bytes=12 * MIB),
        name="project",
    )(in_vmem(parts), w_value, w_out)


def norm_kernel(got, residual, gain, kept, normed):
    total = residual[...]
    for s in range(got.shape[0]):
        total = total + got[s].astype(jnp.float32)
    kept[...] = total
    mean = jnp.sum(total * total) * (1.0 / total.size)
    value = (total * lax.rsqrt(mean + norm_eps) * gain[...]).astype(jnp.bfloat16)
    for s in range(normed.shape[0]):
        normed[s] = value


def norm(got, residual, gain):
    return pl.pallas_call(
        norm_kernel,
        out_shape=(pltpu.VMEM(residual.shape, jnp.float32), pltpu.VMEM(got.shape, got.dtype)),
        in_specs=[vmem_spec] * 3,
        out_specs=(vmem_spec, vmem_spec),
        compiler_params=pltpu.CompilerParams(vmem_limit_bytes=8 * MIB),
        name="norm",
    )(in_vmem(got), in_vmem(residual), in_vmem(gain))


def ffn_kernel(chunk, normed, w_gate, w_up, w_down, sent, flat, wide):
    group, tiles, _ = normed.shape
    for r in range(group):
        flat[r * tiles : (r + 1) * tiles, :] = normed[r].astype(jnp.float32)
    for n in range(tiles):
        wide[:, n * LANES : (n + 1) * LANES] = flat[pl.ds(n, group, stride=tiles), :].astype(
            jnp.bfloat16
        )
    gate = jnp.dot(wide[...], w_gate[...], preferred_element_type=jnp.float32)
    up = jnp.dot(wide[...], w_up[...], preferred_element_type=jnp.float32)
    activated = (gate / (1.0 + jnp.exp(-gate)) * up).astype(jnp.bfloat16)
    for c in range(w_down.shape[1] // chunk):
        value = jnp.dot(
            activated, w_down[:, c * chunk : (c + 1) * chunk], preferred_element_type=jnp.float32
        )
        scatter_tiles(flat, value, c * chunk // LANES, group, tiles)
    for r in range(group):
        sent[r] = flat[r * tiles : (r + 1) * tiles, :].astype(jnp.bfloat16)


def ffn(normed, w_gate, w_up, w_down):
    group, tiles, _ = normed.shape
    features = tiles * LANES
    return pl.pallas_call(
        functools.partial(ffn_kernel, features // 7),
        out_shape=pltpu.VMEM(normed.shape, jnp.bfloat16),
        in_specs=[vmem_spec] * 4,
        out_specs=vmem_spec,
        scratch_shapes=[
            pltpu.VMEM((group * tiles, LANES), jnp.float32),
            pltpu.VMEM((group, features), jnp.bfloat16),
        ],
        compiler_params=pltpu.CompilerParams(vmem_limit_bytes=12 * MIB),
        name="ffn",
    )(in_vmem(normed), w_gate, w_up, w_down)


def body(
    queries,
    cache_pool,
    holder,
    slot_ids,
    lengths,
    residual,
    w_value,
    w_out,
    norm_gain,
    w_gate,
    w_up,
    w_down,
):
    ranks = lax.axis_size("dp")
    tensors = lax.axis_size("tensor")
    column = lax.axis_index("tensor")
    chips = tensors // CORES
    group = residual.shape[0]
    slots = cache_pool.shape[0]
    head_local, latent, _ = w_value.shape
    features = residual.shape[1]
    tiles = features // LANES
    requests = lengths.shape[0]
    swap = [(i, i ^ 1) for i in range(tensors)]
    same_core = [[c + CORES * k for k in range(chips)] for c in range(CORES)]
    from_next = [((i + 1) % ranks, i) for i in range(ranks)]
    from_prev = [((i - 1) % ranks, i) for i in range(ranks)]

    def swapped(value):
        return lax.ppermute(value, "tensor", swap)

    q_all = lax.all_gather(queries, "tensor", axis=0, tiled=True)
    low, high = split_pool(cache_pool)
    next_low = lax.ppermute(low, "dp", from_next)
    prev_high = lax.ppermute(high, "dp", from_prev)
    next_high = lax.ppermute(high, "dp", from_next)
    prev_low = lax.ppermute(low, "dp", from_prev)
    far_low = lax.ppermute(next_low, "dp", from_next)
    far_high = lax.ppermute(prev_high, "dp", from_prev)
    mine = [low, high, next_low, next_high, far_low, far_high, prev_low, prev_high]
    code = (holder * slots + slot_ids).reshape(1, requests)
    code_other = swapped(code)
    own_residual = (
        lax.dynamic_index_in_dim(residual, column, 0, keepdims=False)
        .astype(jnp.float32)
        .reshape(tiles, LANES)
    )
    gain = norm_gain.reshape(tiles, LANES)
    w_value, w_out, w_gate, w_up, w_down = [
        in_vmem(one) for one in (w_value, w_out, w_gate, w_up, w_down)
    ]
    others = [swapped(one) for one in mine]

    q_all, own_residual, gain = lax.optimization_barrier((q_all, own_residual, gain))
    partial = attend(
        code, code_other, lengths.reshape(1, requests), q_all, mine + others, ranks, latent, head_local
    )
    parts = lax.all_to_all(
        partial, "tensor", split_axis=0, concat_axis=0, tiled=True, axis_index_groups=same_core
    )

    def exchange(value):
        return lax.all_to_all(value, "tensor", split_axis=0, concat_axis=0, tiled=True)

    residual_sum, normed = norm(exchange(project(parts, w_value, w_out, group)), own_residual, gain)
    down = exchange(ffn(exchange(normed), w_gate, w_up, w_down))
    return (residual_sum + jnp.sum(down.astype(jnp.float32), axis=0)).reshape(1, features)


def solution(mesh):
    in_specs = (
        P(("dp", "tensor"), None, None),
        P(("dp", "tensor"), None, None),
        P(None, "tensor"),
        P(None, "tensor"),
        P(),
        P("dp", None),
        P("tensor", None, None),
        P("tensor", None),
        P(),
        P(None, "tensor"),
        P(None, "tensor"),
        P("tensor", None),
    )
    out_specs = P(("dp", "tensor"), None)
    return jax.shard_map(body, mesh=mesh, in_specs=in_specs, out_specs=out_specs, check_vma=False)
```

time: 516 us -> 169 us (0.33)
  waiting for transfers between devices: 376 us -> 33.1 us
  blocking collectives: 0 us -> 80 us
  matrix products: 52.1 us -> 0 us
  other arithmetic: 23.7 us -> 2.29 us
  Pallas kernels: 0 us -> 20.3 us
  local copies, waits for them, and re-layouts: 20.4 us -> 4.45 us
  starting transfers between devices: 29.7 us -> 15.3 us
    all_to_all x4 -> x0, waiting for transfers between devices: 142 us -> none  [the longest x1 97.5 us: body(): lax.all_to_all(partial_value, 'tensor', split_axis=1, concat_axis=0, tile...]
    psum x1 -> x0, waiting for transfers between devices: 104 us -> none  [body(): lax.psum(jnp.dot(flat_heads, w_out, preferred_element_type=jnp.float32),...]
    unnamed x4 -> x1, waiting for transfers between devices: 104 us -> 0.71 us
    all_to_all x0 -> x4, blocking collectives: none -> 80 us  [the longest x3 44.9 us: exchange(): lax.all_to_all(value, 'tensor', split_axis=0, concat_axis=0, tiled=True)]
    dot_general x8 -> x0, matrix products: 52.1 us -> none  [the longest x1 18.6 us: body(): jnp.dot(onehot, mixed.reshape(mixed.shape[0], -1), precision=lax.Precisio...]
    ppermute x0 -> x15, waiting for transfers between devices: none -> 31.5 us  [the longest x1 10.7 us: body(): far_low = lax.ppermute(next_low, 'dp', from_next)]
    all_to_all x4 -> x0, starting transfers between devices: 29.4 us -> none  [the longest x1 8.53 us: body(): lax.all_to_all(totals, 'tensor', split_axis=1, concat_axis=0, tiled=True)]
    all_gather x1, waiting for transfers between devices: 26.4 us -> 0.89 us  [body(): q_all = lax.all_gather(queries, 'tensor', axis=0, tiled=True)]
  transfers between devices with their start and end apart: 7 -> 16, of which waited for: 5 -> 7; matrix products, arithmetic and copies ran while one was open for 11% -> 1% of each run, Pallas kernels for 0% -> 1%
where the time goes in v2:
time: 169 us
  blocking collectives  80 us (47%)
  waiting for transfers between devices  33.1 us (20%)
  Pallas kernels  20.3 us (12%)
  starting transfers between devices  15.3 us (9%)
  between operations  13.6 us (8%)
  local copies, waits for them, and re-layouts  4.45 us (3%)
  other arithmetic  2.29 us (1%)
    all_to_all x3, blocking collectives, exchange(): lax.all_to_all(value, 'tensor', split_axis=0, concat_axis=0, tiled=True)  44.9 us
    all_to_all x1, blocking collectives, body(): lax.all_to_all(partial, 'tensor', split_axis=0, concat_axis=0, tiled=True...  35.1 us
    pallas_call x1, Pallas kernels, attend(): pl.pallas_call(functools.partial(attend_kernel, dims), out_shape=pltpu.VM...  12.3 us
    ppermute x1, waiting for transfers between devices, body(): far_low = lax.ppermute(next_low, 'dp', from_next)  10.7 us
    ppermute x1, waiting for transfers between devices, body(): prev_high = lax.ppermute(high, 'dp', from_prev)  10 us
    ppermute x1, waiting for transfers between devices, body(): prev_low = lax.ppermute(low, 'dp', from_prev)  6.9 us
    ppermute x9, starting transfers between devices, swapped(): return lax.ppermute(value, 'tensor', swap)  6.86 us
    unnamed x28, local copies, waits for them, and re-layouts  4.45 us
  transfers between devices with their start and end apart: 16, of which 7 were waited for; matrix products, arithmetic and copies ran while one was open for 1% of the time, Pallas kernels for 1%

profile of v2, /device:TPU:1, one launch (start us, length us, event | category | flops | bytes accessed | tf_op | source)
XLA Modules:
  0.0 169.0 jit_solution(11505572806132337304)
XLA Ops:
  6.5 0.7 all-gather.2.cloned.1.call-update
  7.3 2.3 %split_pool.1 = (bf16[4,576,128]{2,1,0:T(8,128)(2,1)S(1)}, bf16[4,576,128]{2,1,0:T(8,128)(2,1)}) custom-call(bf16[8,576,128]{2,1,0:T(8,128)(2,1)} %pool.1), custom_call_target="tpu_custom_call" | custom-call | tf_op jit(solution)/shard_map/split_pool/pallas_call | solution.py:43
  9.5 1.5 collective-permute-start.7
  11.0 1.7 %collective-permute-start.6 = (bf16[4,576,128]{2,1,0:T(8,128)(2,1)S(1)}, bf16[4,576,128]{2,1,0:T(8,128)(2,1)}, u32[]{:S(2)}, u32[]{:S(2)}) collective-permute-start(bf16[4,576,128]{2,1,0:T(8,128)(2,1)S(1)} %get-tuple-element.13.refs_0_), channel_id=1, source_target_pairs={{96,0},{0,32},{32,64},{64,96},{97,1},{1,33},{33,65},{65,97},{98,2}... | collective-permute-start | bytes 1769480 | tf_op jit(solution)/shard_map/ppermute | solution.py:423
  12.8 2.1 %collective-permute-start.1 = (bf16[4,576,128]{2,1,0:T(8,128)(2,1)S(1)}, bf16[4,576,128]{2,1,0:T(8,128)(2,1)}, u32[]{:S(2)}, u32[]{:S(2)}) collective-permute-start(bf16[4,576,128]{2,1,0:T(8,128)(2,1)S(1)} %get-tuple-element.13.refs_0_), channel_id=1, source_target_pairs={{32,0},{64,32},{96,64},{0,96},{33,1},{65,33},{97,65},{1,97},{34,2}... | collective-permute-start | bytes 1769480 | tf_op jit(solution)/shard_map/ppermute | solution.py:420
  14.9 0.8 copy-done.1
  15.7 0.7 add_bitcast_fusion.code_own
  16.8 0.8 collective-permute-done.code_other
  17.9 0.8 copy-done.3
  18.7 3.0 %collective-permute-start.2 = (bf16[4,576,128]{2,1,0:T(8,128)(2,1)}, bf16[4,576,128]{2,1,0:T(8,128)(2,1)}, u32[]{:S(2)}, u32[]{:S(2)}) collective-permute-start(bf16[4,576,128]{2,1,0:T(8,128)(2,1)} %get-tuple-element.14.refs_1_), channel_id=1, source_target_pairs={{32,0},{64,32},{96,64},{0,96},{33,1},{65,33},{97,65},{1,97},{34,2}... | collective-permute-start | bytes 1769480 | tf_op jit(solution)/shard_map/ppermute | solution.py:422
  21.7 6.9 %collective-permute-done.6.refs_6_ = bf16[4,576,128]{2,1,0:T(8,128)(2,1)} collective-permute-done((bf16[4,576,128]{2,1,0:T(8,128)(2,1)S(1)}, bf16[4,576,128]{2,1,0:T(8,128)(2,1)}, u32[]{:S(2)}, u32[]{:S(2)}) %collective-permute-start.6) | collective-permute-done | bytes 589856 | tf_op jit(solution)/shard_map/ppermute | solution.py:423
  28.6 0.9 collective-permute-start.13
  29.5 1.7 collective-permute-start.3
  31.2 10.0 %collective-permute-done.4.refs_7_ = bf16[4,576,128]{2,1,0:T(8,128)(2,1)} collective-permute-done((bf16[4,576,128]{2,1,0:T(8,128)(2,1)}, bf16[4,576,128]{2,1,0:T(8,128)(2,1)}, u32[]{:S(2)}, u32[]{:S(2)}) %collective-permute-start.4) | collective-permute-done | bytes 589856 | tf_op jit(solution)/shard_map/ppermute | solution.py:421
  41.2 0.7 collective-permute-start.9
  42.4 10.7 %collective-permute-done.3.refs_4_ = bf16[4,576,128]{2,1,0:T(8,128)(2,1)} collective-permute-done((bf16[4,576,128]{2,1,0:T(8,128)(2,1)}, bf16[4,576,128]{2,1,0:T(8,128)(2,1)}, u32[]{:S(2)}, u32[]{:S(2)}) %collective-permute-start.3) | collective-permute-done | bytes 589856 | tf_op jit(solution)/shard_map/ppermute | solution.py:424
  53.1 1.0 collective-permute-start.11
  54.1 2.9 %collective-permute-done.5.refs_5_ = bf16[4,576,128]{2,1,0:T(8,128)(2,1)} collective-permute-done((bf16[4,576,128]{2,1,0:T(8,128)(2,1)}, bf16[4,576,128]{2,1,0:T(8,128)(2,1)}, u32[]{:S(2)}, u32[]{:S(2)}) %collective-permute-start.5) | collective-permute-done | bytes 589856 | tf_op jit(solution)/shard_map/ppermute | solution.py:425
  57.0 1.5 collective-permute-start.12
  58.5 0.9 dynamic-slice_convert_fusion
  59.4 0.9 all-gather.2.cloned.1.call-done.q_hbm
  60.5 1.1 copy-done.2
  61.5 1.1 copy-done.4
  62.6 0.7 copy-done.7
  63.3 12.3 %attend.1 = bf16[16,528,128]{2,1,0:T(8,128)(2,1)S(1)} custom-call(s32[1,128]{1,0:T(1,128)S(1)} %add_bitcast_fusion.code_own, s32[1,128]{1,0:T(1,128)S(1)} %collective-permute-done.code_other, s32[1,128]{1,0:T(1,128)S(1)} %bitcast.14, bf16[32,576,128]{2,1,0:T(8,128)(2,1)} %all-gather.2.cloned.1.call-done.q_hbm, bf16[4,576,128]{2,1,0:T(8,128)(2,1)S(1)} %copy-done.2, ...), custom_call_target="tpu_custom_call" | custom-call | tf_op jit(solution)/shard_map/attend/pallas_call | solution.py:210
  75.6 35.1 %all_to_all.20.parts = bf16[16,528,128]{2,1,0:T(8,128)(2,1)S(1)} all-to-all(bf16[16,528,128]{2,1,0:T(8,128)(2,1)S(1)} %attend.1), channel_id=1, replica_groups={{0,2,4,6,8,10,12,14,16,18,20,22,24,26,28,30},{1,3,5,7,9,11,13,15,17,19,..., dimensions={0} | all-to-all | bytes 4325376 | tf_op jit(solution)/shard_map/all_to_all | solution.py:444
  110.7 2.6 %project.1 = bf16[32,56,128]{2,1,0:T(8,128)(2,1)S(1)} custom-call(bf16[16,528,128]{2,1,0:T(8,128)(2,1)S(1)} %all_to_all.20.parts, bf16[4,512,128]{2,1,0:T(8,128)(2,1)S(1)} %copy-done.5, bf16[512,7168]{1,0:T(8,128)(2,1)S(1)} %bitcast.7), custom_call_target="tpu_custom_call" | custom-call | tf_op jit(solution)/shard_map/project/pallas_call | solution.py:313
  113.4 15.8 %all_to_all.21.got = bf16[32,56,128]{2,1,0:T(8,128)(2,1)S(1)} all-to-all(bf16[32,56,128]{2,1,0:T(8,128)(2,1)S(1)} %project.1), channel_id=1, replica_groups=mesh['dp'=4,'tensor'=32] {'tensor'}, dimensions={0} | all-to-all | bytes 917504 | tf_op jit(solution)/shard_map/all_to_all | solution.py:449
  129.5 14.5 %all_to_all.22.normed = bf16[32,56,128]{2,1,0:T(8,128)(2,1)S(1)} all-to-all(bf16[32,56,128]{2,1,0:T(8,128)(2,1)S(1)} %get-tuple-element.18), channel_id=1, replica_groups=mesh['dp'=4,'tensor'=32] {'tensor'}, dimensions={0} | all-to-all | bytes 917504 | tf_op jit(solution)/shard_map/all_to_all | solution.py:449
  144.1 2.9 %ffn.1 = bf16[32,56,128]{2,1,0:T(8,128)(2,1)S(1)} custom-call(bf16[32,56,128]{2,1,0:T(8,128)(2,1)S(1)} %all_to_all.22.normed, bf16[7168,384]{1,0:T(8,128)(2,1)S(1)} %bitcast.9, bf16[7168,384]{1,0:T(8,128)(2,1)S(1)} %bitcast.11, bf16[384,7168]{1,0:T(8,128)(2,1)S(1)} %copy-done), custom_call_target="tpu_custom_call" | custom-call | tf_op jit(solution)/shard_map/ffn/pallas_call | solution.py:372
  146.9 14.5 %all_to_all.23 = bf16[32,56,128]{2,1,0:T(8,128)(2,1)S(1)} all-to-all(bf16[32,56,128]{2,1,0:T(8,128)(2,1)S(1)} %ffn.1), channel_id=1, replica_groups=mesh['dp'=4,'tensor'=32] {'tensor'}, dimensions={0} | all-to-all | bytes 917504 | tf_op jit(solution)/shard_map/all_to_all | solution.py:449
  161.5 0.6 add.12
  (45 shorter events, 1.8 us)
Async XLA Ops:
  6.5 53.8 %all-gather.2.cloned.1.call-start = ((), (), s32[]{:S(2)}) async-start(), calls=%async_computation.4 | async-start | bytes 4866048 | tf_op jit(solution)/shard_map/all_gather | solution.py:418
  7.3 103.4 %slice-start = ((s8[7340032]{0:T(1024)(128)(4,1)}), s8[3145728]{0:T(1024)(128)(4,1)S(1)}, s32[]{:S(2)}) async-start(s8[7340032]{0:T(1024)(128)(4,1)} %bitcast.6), calls=%async_computation.5 | async-start | bytes 6291456
  9.5 8.4 %collective-permute-start.7 = (bf16[4,576,128]{2,1,0:T(8,128)(2,1)S(1)}, bf16[4,576,128]{2,1,0:T(8,128)(2,1)S(1)}, u32[]{:S(2)}, u32[]{:S(2)}) collective-permute-start(bf16[4,576,128]{2,1,0:T(8,128)(2,1)S(1)} %get-tuple-element.13.refs_0_), channel_id=1, source_target_pairs={{0,1},{1,0},{2,3},{3,2},{4,5},{5,4},{6,7},{7,6},{8,9},{9,8},{10,11... | collective-permute-start | bytes 1769480 | tf_op jit(solution)/shard_map/ppermute | solution.py:416
  11.0 17.6 %collective-permute-start.6 = (bf16[4,576,128]{2,1,0:T(8,128)(2,1)S(1)}, bf16[4,576,128]{2,1,0:T(8,128)(2,1)}, u32[]{:S(2)}, u32[]{:S(2)}) collective-permute-start(bf16[4,576,128]{2,1,0:T(8,128)(2,1)S(1)} %get-tuple-element.13.refs_0_), channel_id=1, source_target_pairs={{96,0},{0,32},{32,64},{64,96},{97,1},{1,33},{33,65},{65,97},{98,2}... | collective-permute-start | bytes 1769480 | tf_op jit(solution)/shard_map/ppermute | solution.py:423
  12.8 16.8 %collective-permute-start.1 = (bf16[4,576,128]{2,1,0:T(8,128)(2,1)S(1)}, bf16[4,576,128]{2,1,0:T(8,128)(2,1)}, u32[]{:S(2)}, u32[]{:S(2)}) collective-permute-start(bf16[4,576,128]{2,1,0:T(8,128)(2,1)S(1)} %get-tuple-element.13.refs_0_), channel_id=1, source_target_pairs={{32,0},{64,32},{96,64},{0,96},{33,1},{65,33},{97,65},{1,97},{34,2}... | collective-permute-start | bytes 1769480 | tf_op jit(solution)/shard_map/ppermute | solution.py:420
  14.9 0.8 copy-start.1
  15.7 25.5 %collective-permute-start.4 = (bf16[4,576,128]{2,1,0:T(8,128)(2,1)}, bf16[4,576,128]{2,1,0:T(8,128)(2,1)}, u32[]{:S(2)}, u32[]{:S(2)}) collective-permute-start(bf16[4,576,128]{2,1,0:T(8,128)(2,1)} %get-tuple-element.14.refs_1_), channel_id=1, source_target_pairs={{96,0},{0,32},{32,64},{64,96},{97,1},{1,33},{33,65},{65,97},{98,2}... | collective-permute-start | bytes 1769480 | tf_op jit(solution)/shard_map/ppermute | solution.py:421
  16.4 1.3 collective-permute-start
  17.6 23.6 %collective-permute-start.8 = (bf16[4,576,128]{2,1,0:T(8,128)(2,1)}, bf16[4,576,128]{2,1,0:T(8,128)(2,1)}, u32[]{:S(2)}, u32[]{:S(2)}) collective-permute-start(bf16[4,576,128]{2,1,0:T(8,128)(2,1)} %get-tuple-element.14.refs_1_), channel_id=1, source_target_pairs={{0,1},{1,0},{2,3},{3,2},{4,5},{5,4},{6,7},{7,6},{8,9},{9,8},{10,11... | collective-permute-start | bytes 1769480 | tf_op jit(solution)/shard_map/ppermute | solution.py:416
  17.9 0.8 copy-start.3
  18.7 23.2 %collective-permute-start.2 = (bf16[4,576,128]{2,1,0:T(8,128)(2,1)}, bf16[4,576,128]{2,1,0:T(8,128)(2,1)}, u32[]{:S(2)}, u32[]{:S(2)}) collective-permute-start(bf16[4,576,128]{2,1,0:T(8,128)(2,1)} %get-tuple-element.14.refs_1_), channel_id=1, source_target_pairs={{32,0},{64,32},{96,64},{0,96},{33,1},{65,33},{97,65},{1,97},{34,2}... | collective-permute-start | bytes 1769480 | tf_op jit(solution)/shard_map/ppermute | solution.py:422
  28.6 13.4 %collective-permute-start.13 = (bf16[4,576,128]{2,1,0:T(8,128)(2,1)}, bf16[4,576,128]{2,1,0:T(8,128)(2,1)}, u32[]{:S(2)}, u32[]{:S(2)}) collective-permute-start(bf16[4,576,128]{2,1,0:T(8,128)(2,1)} %collective-permute-done.6.refs_6_), channel_id=1, source_target_pairs={{0,1},{1,0},{2,3},{3,2},{4,5},{5,4},{6,7},{7,6},{8,9},{9,8},{10,11... | collective-permute-start | bytes 1769480 | tf_op jit(solution)/shard_map/ppermute | solution.py:416
  29.5 23.6 %collective-permute-start.3 = (bf16[4,576,128]{2,1,0:T(8,128)(2,1)}, bf16[4,576,128]{2,1,0:T(8,128)(2,1)}, u32[]{:S(2)}, u32[]{:S(2)}) collective-permute-start(bf16[4,576,128]{2,1,0:T(8,128)(2,1)} %collective-permute-done.1.refs_2_), channel_id=1, source_target_pairs={{32,0},{64,32},{96,64},{0,96},{33,1},{65,33},{97,65},{1,97},{34,2}... | collective-permute-start | bytes 1769480 | tf_op jit(solution)/shard_map/ppermute | solution.py:424
  41.2 15.7 %collective-permute-start.5 = (bf16[4,576,128]{2,1,0:T(8,128)(2,1)}, bf16[4,576,128]{2,1,0:T(8,128)(2,1)}, u32[]{:S(2)}, u32[]{:S(2)}) collective-permute-start(bf16[4,576,128]{2,1,0:T(8,128)(2,1)} %collective-permute-done.4.refs_7_), channel_id=1, source_target_pairs={{96,0},{0,32},{32,64},{64,96},{97,1},{1,33},{33,65},{65,97},{98,2}... | collective-permute-start | bytes 1769480 | tf_op jit(solution)/shard_map/ppermute | solution.py:425
  41.2 19.1 %collective-permute-start.9 = (bf16[4,576,128]{2,1,0:T(8,128)(2,1)}, bf16[4,576,128]{2,1,0:T(8,128)(2,1)}, u32[]{:S(2)}, u32[]{:S(2)}) collective-permute-start(bf16[4,576,128]{2,1,0:T(8,128)(2,1)} %collective-permute-done.1.refs_2_), channel_id=1, source_target_pairs={{0,1},{1,0},{2,3},{3,2},{4,5},{5,4},{6,7},{7,6},{8,9},{9,8},{10,11... | collective-permute-start | bytes 1769480 | tf_op jit(solution)/shard_map/ppermute | solution.py:416
  41.9 18.4 %collective-permute-start.14 = (bf16[4,576,128]{2,1,0:T(8,128)(2,1)}, bf16[4,576,128]{2,1,0:T(8,128)(2,1)}, u32[]{:S(2)}, u32[]{:S(2)}) collective-permute-start(bf16[4,576,128]{2,1,0:T(8,128)(2,1)} %collective-permute-done.4.refs_7_), channel_id=1, source_target_pairs={{0,1},{1,0},{2,3},{3,2},{4,5},{5,4},{6,7},{7,6},{8,9},{9,8},{10,11... | collective-permute-start | bytes 1769480 | tf_op jit(solution)/shard_map/ppermute | solution.py:416
  42.0 18.3 %collective-permute-start.10 = (bf16[4,576,128]{2,1,0:T(8,128)(2,1)}, bf16[4,576,128]{2,1,0:T(8,128)(2,1)}, u32[]{:S(2)}, u32[]{:S(2)}) collective-permute-start(bf16[4,576,128]{2,1,0:T(8,128)(2,1)} %collective-permute-done.2.refs_3_), channel_id=1, source_target_pairs={{0,1},{1,0},{2,3},{3,2},{4,5},{5,4},{6,7},{7,6},{8,9},{9,8},{10,11... | collective-permute-start | bytes 1769480 | tf_op jit(solution)/shard_map/ppermute | solution.py:416
  53.1 7.2 %collective-permute-start.11 = (bf16[4,576,128]{2,1,0:T(8,128)(2,1)}, bf16[4,576,128]{2,1,0:T(8,128)(2,1)}, u32[]{:S(2)}, u32[]{:S(2)}) collective-permute-start(bf16[4,576,128]{2,1,0:T(8,128)(2,1)} %collective-permute-done.3.refs_4_), channel_id=1, source_target_pairs={{0,1},{1,0},{2,3},{3,2},{4,5},{5,4},{6,7},{7,6},{8,9},{9,8},{10,11... | collective-permute-start | bytes 1769480 | tf_op jit(solution)/shard_map/ppermute | solution.py:416
  57.0 3.5 %collective-permute-start.12 = (bf16[4,576,128]{2,1,0:T(8,128)(2,1)}, bf16[4,576,128]{2,1,0:T(8,128)(2,1)}, u32[]{:S(2)}, u32[]{:S(2)}) collective-permute-start(bf16[4,576,128]{2,1,0:T(8,128)(2,1)} %collective-permute-done.5.refs_5_), channel_id=1, source_target_pairs={{0,1},{1,0},{2,3},{3,2},{4,5},{5,4},{6,7},{7,6},{8,9},{9,8},{10,11... | collective-permute-start | bytes 1769480 | tf_op jit(solution)/shard_map/ppermute | solution.py:416
  60.5 1.1 copy-start.2
  61.5 1.1 copy-start.4
  62.6 0.7 copy-start.7
  63.3 47.4 %slice-start.1 = ((s8[7340032]{0:T(1024)(128)(4,1)}), s8[4194304]{0:T(1024)(128)(4,1)S(1)}, s32[]{:S(2)}) async-start(s8[7340032]{0:T(1024)(128)(4,1)} %bitcast.6), calls=%async_computation.6 | async-start | bytes 8388608
  63.3 47.4 %copy-start.5 = (bf16[4,512,128]{2,1,0:T(8,128)(2,1)S(1)}, bf16[4,512,128]{2,1,0:T(8,128)(2,1)}, u32[]{:S(2)}) copy-start(bf16[4,512,128]{2,1,0:T(8,128)(2,1)} %w_value.1) | copy-start | bytes 1572868
  75.6 53.7 %copy-start.6 = (f32[7168]{0:T(1024)S(1)}, f32[7168]{0:T(1024)}, u32[]{:S(2)}) copy-start(f32[7168]{0:T(1024)} %param.20) | copy-start | bytes 86020
  75.6 68.5 %slice-start.2 = ((s8[5505024]{0:T(1024)(128)(4,1)}), s8[4194304]{0:T(1024)(128)(4,1)S(1)}, s32[]{:S(2)}) async-start(s8[5505024]{0:T(1024)(128)(4,1)} %bitcast.8), calls=%async_computation.7 | async-start | bytes 8388608
  75.6 68.4 %slice-start.4 = ((s8[5505024]{0:T(1024)(128)(4,1)}), s8[4194304]{0:T(1024)(128)(4,1)S(1)}, s32[]{:S(2)}) async-start(s8[5505024]{0:T(1024)(128)(4,1)} %bitcast.10), calls=%async_computation.9 | async-start | bytes 8388608
  110.7 33.3 %slice-start.3 = ((s8[5505024]{0:T(1024)(128)(4,1)}), s8[1310720]{0:T(1024)(128)(4,1)S(1)}, s32[]{:S(2)}) async-start(s8[5505024]{0:T(1024)(128)(4,1)} %bitcast.8), calls=%async_computation.8 | async-start | bytes 2621440
  110.7 33.3 %slice-start.5 = ((s8[5505024]{0:T(1024)(128)(4,1)}), s8[1310720]{0:T(1024)(128)(4,1)S(1)}, s32[]{:S(2)}) async-start(s8[5505024]{0:T(1024)(128)(4,1)} %bitcast.10), calls=%async_computation.10 | async-start | bytes 2621440
  110.7 33.3 %copy-start = (bf16[384,7168]{1,0:T(8,128)(2,1)S(1)}, bf16[384,7168]{1,0:T(8,128)(2,1)}, u32[]{:S(2)}) copy-start(bf16[384,7168]{1,0:T(8,128)(2,1)} %w_down.1) | copy-start | bytes 16515076
Sparse Core Ops, SparseCore 0:
  9.6 50.6 all-gather.1

commit v3 on v2

--- a/solution.py
+++ b/solution.py
@@ -12,6 +12,9 @@
 far_below = -1e30
 CORES = 2
 LANES = 128
+HEAD_LOCAL = 4
+QUERY_PARTS = 4
+QUERY_ROWS = (576,)
 MIB = 1024 * 1024
 hbm_spec = pl.BlockSpec(memory_space=pl.ANY)
 vmem_spec = pl.BlockSpec(memory_space=pltpu.VMEM)
@@ -26,7 +29,8 @@
     return pltpu.with_memory_space_constraint(value, pltpu.HBM)
 
 
-def split_kernel(pool, low, high, sems):
+def split_kernel(pool, *refs):
+    low, high, sems = refs[-3:]
     half = low.shape[0]
     copies = [
         pltpu.make_async_copy(pool.at[pl.ds(i * half, half)], one, sems.at[i])
@@ -38,79 +42,100 @@
         one.wait()
 
 
-def split_pool(pool):
+def split(pool, *after):
     half = (pool.shape[0] // 2,) + pool.shape[1:]
     return pl.pallas_call(
         split_kernel,
         out_shape=(pltpu.VMEM(half, pool.dtype), pltpu.VMEM(half, pool.dtype)),
-        in_specs=[hbm_spec],
+        in_specs=[hbm_spec] * (1 + len(after)),
         out_specs=(vmem_spec, vmem_spec),
         scratch_shapes=[pltpu.SemaphoreType.DMA((2,))],
+        compiler_params=pltpu.CompilerParams(vmem_limit_bytes=12 * MIB),
+        name="split",
+    )(in_hbm(pool), *after)
+
+
+def turn_kernel(own, other, *outs):
+    width, head_total = own.shape
+    heads = head_total // CORES
+    head_local, tail = HEAD_LOCAL, width // LANES * LANES
+    core = lax.axis_index("tensor") % CORES
+    row = lax.broadcasted_iota(jnp.int32, (heads, head_total), 0)
+    wanted = (row // head_local) * (CORES * head_local) + core * head_local + row % head_local
+    hit = lax.broadcasted_iota(jnp.int32, (heads, head_total), 1) == wanted
+    select = jnp.where(hit, 1.0, 0.0).astype(jnp.bfloat16)
+    turned = [
+        lax.dot_general(select, one[...], (((1,), (1,)), ((), ())), preferred_element_type=jnp.float32)
+        for one in (own, other)
+    ]
+    pair = [
+        jnp.where(core == 0, turned[0], turned[1]).astype(jnp.bfloat16),
+        jnp.where(core == 0, turned[1], turned[0]).astype(jnp.bfloat16),
+    ]
+    rows = [
+        pair[i][:, p * LANES : (p + 1) * LANES] for p in range(tail // LANES) for i in range(CORES)
+    ]
+    rows = jnp.concatenate(
+        rows + [jnp.concatenate([one[:, tail:] for one in pair], axis=1)], axis=0
+    )
+    at = 0
+    for out in outs:
+        out[0] = rows[at : at + out.shape[1], :]
+        at += out.shape[1]
+
+
+def turn(own, other):
+    return pl.pallas_call(
+        turn_kernel,
+        out_shape=tuple(
+            jax.ShapeDtypeStruct((1, rows, own.shape[1]), own.dtype) for rows in QUERY_ROWS
+        ),
+        in_specs=[vmem_spec] * 2,
+        out_specs=(vmem_spec,) * len(QUERY_ROWS),
         compiler_params=pltpu.CompilerParams(vmem_limit_bytes=4 * MIB),
-        name="split_pool",
-    )(in_hbm(pool))
-
-
-def stage_kernel(count, *refs):
-    copies = [
-        pltpu.make_async_copy(refs[i], refs[count + i], refs[2 * count].at[i]) for i in range(count)
-    ]
-    for one in copies:
-        one.start()
-    for one in copies:
-        one.wait()
-
-
-def stage(*weights):
-    count = len(weights)
-    size = sum(one.size * one.dtype.itemsize for one in weights)
-    return pl.pallas_call(
-        functools.partial(stage_kernel, count),
-        out_shape=tuple(pltpu.VMEM(one.shape, one.dtype) for one in weights),
-        in_specs=[hbm_spec] * count,
-        out_specs=(vmem_spec,) * count,
-        scratch_shapes=[pltpu.SemaphoreType.DMA((count,))],
-        compiler_params=pltpu.CompilerParams(vmem_limit_bytes=4 * MIB),
-        cost_estimate=pl.CostEstimate(flops=0, bytes_accessed=2 * size, transcendentals=0),
-        name="stage",
-    )(*[in_hbm(one) for one in weights])
-
-
-QUERY_PARTS = 4
-UNROLL = 8
-
-
-def attend_kernel(dims, code_own, code_other, lengths, q_hbm, *refs):
-    slots, ranks, head_local, latent, piece_count = dims
-    pieces = refs[:piece_count]
-    out_ref, kbuf, qraw, qbuf, lse_buf, sems = refs[piece_count:]
-    group = q_hbm.shape[0]
-    portion, heads, _ = qbuf.shape
+        name="turn",
+    )(own, other)
+
+
+def attend_kernel(dims, code_own, code_other, lengths, *refs):
+    slots, ranks, head_local, latent, count = dims
+    q_refs = refs[: len(QUERY_ROWS)]
+    pieces = refs[len(QUERY_ROWS) : len(QUERY_ROWS) + count]
+    out_ref, kbuf, qbuf, lse_buf, sems = refs[len(QUERY_ROWS) + count :]
+    pairs, width, _ = qbuf.shape
+    group = CORES * pairs
+    heads = lse_buf.shape[0]
     block_len = kbuf.shape[2]
     owners = heads // head_local
     my_rank = lax.axis_index("dp")
     column = lax.axis_index("tensor")
     core = column % CORES
     first = my_rank * group
-    q_copies = [
-        pltpu.make_async_copy(
-            q_hbm.at[pl.ds(i * portion, portion)],
-            qraw.at[i % 2],
-            sems.at[piece_count + i],
-        )
-        for i in range(QUERY_PARTS)
-    ]
-    copies = []
-    at = 0
+    portion = pairs // QUERY_PARTS
+
+    def q_copies(step):
+        made, at = [], 0
+        for i, one in enumerate(q_refs):
+            rows = one.shape[1]
+            made.append(
+                pltpu.make_async_copy(
+                    one.at[pl.ds(step * portion, portion)],
+                    qbuf.at[pl.ds(step * portion, portion), pl.ds(at, rows)],
+                    sems.at[count + step * len(q_refs) + i],
+                )
+            )
+            at += rows
+        return made
+
+    copies, at = [], 0
     for i, one in enumerate(pieces):
         copies.append(pltpu.make_async_copy(one, kbuf.at[pl.ds(at, one.shape[0])], sems.at[i]))
         at += one.shape[0]
-    for one in q_copies[:2] + copies:
+    for one in q_copies(0) + copies:
         one.start()
-    row = lax.broadcasted_iota(jnp.int32, (heads, CORES * heads), 0)
-    wanted = (row // head_local) * (CORES * head_local) + core * head_local + row % head_local
-    hit = lax.broadcasted_iota(jnp.int32, (heads, CORES * heads), 1) == wanted
-    select = jnp.where(hit, 1.0, 0.0).astype(jnp.bfloat16)
+    for step in range(1, QUERY_PARTS):
+        for one in q_copies(step):
+            one.start()
     token = lax.broadcasted_iota(jnp.int32, (1, 2 * block_len), 1)
     partner = column + 1 - 2 * core
     position = jnp.where(
@@ -125,25 +150,37 @@
         code = codes[0, first + r]
         return ((code // slots - my_rank + ranks) % ranks) * slots + code % slots
 
-    def turn(slot, step, carry):
-        for i in range(UNROLL):
-            r = step * UNROLL + i
-            qbuf[r] = lax.dot_general(
-                select, qraw[slot, r], (((1,), (1,)), ((), ())), preferred_element_type=jnp.float32
-            ).astype(jnp.bfloat16)
-        return carry
-
-    def several(step, carry):
-        rs = [step * UNROLL + i for i in range(UNROLL)]
+    unroll = CORES * portion
+
+    def several(step):
+        rs = [step * unroll + i for i in range(unroll)]
         keys = [
             jnp.concatenate(
                 [kbuf[place(code_own, r)], kbuf[ranks * slots + place(code_other, r)]], axis=1
             )
             for r in rs
         ]
+        asked = []
+        for i in range(unroll):
+            at = step * portion + i // CORES
+            side = i % CORES
+            rotary = qbuf[at, latent:, :]
+            mine = (lane < LANES // CORES) if side == 0 else (lane >= LANES // CORES)
+            rows = [
+                qbuf[at, (p * CORES + side) * heads : (p * CORES + side + 1) * heads, :]
+                for p in range(latent // LANES)
+            ]
+            asked.append(
+                jnp.concatenate(rows + [jnp.where(mine, rotary, jnp.zeros_like(rotary))], axis=1)
+            )
         scores = [
-            jnp.dot(qbuf[r % portion], key, preferred_element_type=jnp.float32) * score_scale
-            for r, key in zip(rs, keys)
+            jnp.dot(
+                q,
+                jnp.concatenate([key, key[latent:]], axis=0),
+                preferred_element_type=jnp.float32,
+            )
+            * score_scale
+            for q, key in zip(asked, keys)
         ]
         weights, scales, lses = [], [], []
         for r, score in zip(rs, scores):
@@ -168,23 +205,22 @@
         for r, lse in zip(rs, lses):
             lse_all = jnp.where(lane == r, lse, lse_all)
         lse_buf[...] = lse_all
-        count = UNROLL * head_local
+        rows_count = unroll * head_local
         for k in range(owners):
             both = jnp.concatenate(
                 [one[k * head_local : (k + 1) * head_local] for one in mixed], axis=0
             ).astype(jnp.bfloat16)
             for p in range(latent // LANES):
-                rows_at = pl.multiple_of(p * group * head_local + step * count, count)
-                out_ref[k, pl.ds(rows_at, count), :] = both[:, p * LANES : (p + 1) * LANES]
+                rows_at = pl.multiple_of(p * group * head_local + step * rows_count, rows_count)
+                out_ref[k, pl.ds(rows_at, rows_count), :] = both[:, p * LANES : (p + 1) * LANES]
+
+    def one_step(step, carry):
+        for one in q_copies(step):
+            one.wait()
+        several(step)
         return carry
 
-    for i in range(QUERY_PARTS):
-        q_copies[i].wait()
-        steps = portion // UNROLL
-        lax.fori_loop(0, steps, functools.partial(turn, i % 2), 0)
-        if i + 2 < QUERY_PARTS:
-            q_copies[i + 2].start()
-        lax.fori_loop(i * steps, (i + 1) * steps, several, 0)
+    lax.fori_loop(0, QUERY_PARTS, one_step, 0)
     lse_all = lse_buf[...]
     high = lse_all.astype(jnp.bfloat16).astype(jnp.float32)
     mid = (lse_all - high).astype(jnp.bfloat16).astype(jnp.float32)
@@ -198,30 +234,28 @@
 
 
 def attend(code_own, code_other, lengths, q_all, pieces, ranks, latent, head_local):
-    group, width, head_total = q_all.shape
+    pairs, _, head_total = q_all[0].shape
+    width, block_len = pieces[0].shape[1:]
     heads = head_total // CORES
-    block_len = pieces[0].shape[2]
     blocks = sum(one.shape[0] for one in pieces)
     owners = heads // head_local
-    rows = group * head_local
-    out_rows = latent // LANES * rows + 16
+    out_rows = latent // LANES * pairs * CORES * head_local + 16
     count = len(pieces)
     dims = (blocks // ranks // CORES, ranks, head_local, latent, count)
     return pl.pallas_call(
         functools.partial(attend_kernel, dims),
         out_shape=pltpu.VMEM((owners, out_rows, LANES), jnp.bfloat16),
-        in_specs=[smem_spec] * 3 + [hbm_spec] + [vmem_spec] * count,
+        in_specs=[smem_spec] * 3 + [hbm_spec] * (len(q_all) + count),
         out_specs=vmem_spec,
         scratch_shapes=[
             pltpu.VMEM((blocks, width, block_len), jnp.bfloat16),
-            pltpu.VMEM((2, group // QUERY_PARTS, width, head_total), jnp.bfloat16),
-            pltpu.VMEM((group // QUERY_PARTS, heads, width), jnp.bfloat16),
+            pltpu.VMEM((pairs, width, head_total), jnp.bfloat16),
             pltpu.VMEM((heads, LANES), jnp.float32),
-            pltpu.SemaphoreType.DMA((count + QUERY_PARTS,)),
+            pltpu.SemaphoreType.DMA((count + QUERY_PARTS * len(q_all),)),
         ],
-        compiler_params=pltpu.CompilerParams(vmem_limit_bytes=24 * MIB),
+        compiler_params=pltpu.CompilerParams(vmem_limit_bytes=20 * MIB),
         name="attend",
-    )(code_own, code_other, lengths, in_hbm(q_all), *[in_vmem(one) for one in pieces])
+    )(code_own, code_other, lengths, *[in_hbm(one) for one in q_all], *pieces)
 
 
 def scatter_tiles(flat, value, first_tile, group, tiles):
@@ -415,31 +449,42 @@
     def swapped(value):
         return lax.ppermute(value, "tensor", swap)
 
-    q_all = lax.all_gather(queries, "tensor", axis=0, tiled=True)
-    low, high = split_pool(cache_pool)
+    own_queries = queries[0]
+    (q_pair,) = turn(own_queries, swapped(own_queries))
+    q_gather = lax.all_gather(q_pair, "tensor", axis=0, tiled=True, axis_index_groups=same_core)
+    low, high = split(cache_pool)
     next_low = lax.ppermute(low, "dp", from_next)
     prev_high = lax.ppermute(high, "dp", from_prev)
+    low, high = split(cache_pool, q_pair)
     next_high = lax.ppermute(high, "dp", from_next)
     prev_low = lax.ppermute(low, "dp", from_prev)
-    far_low = lax.ppermute(next_low, "dp", from_next)
-    far_high = lax.ppermute(prev_high, "dp", from_prev)
-    mine = [low, high, next_low, next_high, far_low, far_high, prev_low, prev_high]
-    code = (holder * slots + slot_ids).reshape(1, requests)
-    code_other = swapped(code)
     own_residual = (
         lax.dynamic_index_in_dim(residual, column, 0, keepdims=False)
         .astype(jnp.float32)
         .reshape(tiles, LANES)
     )
+    far_low = lax.ppermute(next_low, "dp", from_next)
+    far_high = lax.ppermute(prev_high, "dp", from_prev)
+    mine = [next_low, next_high, far_low, far_high, prev_low, prev_high]
+    moved = [in_vmem(swapped(one)) for one in mine]
+    mine = [in_vmem(one) for one in mine]
+    pieces = [in_hbm(cache_pool)] + mine + [in_hbm(swapped(cache_pool))] + moved
+    code = (holder * slots + slot_ids).reshape(1, requests)
+    code_other = swapped(code)
     gain = norm_gain.reshape(tiles, LANES)
+    q_gather, own_residual, gain = lax.optimization_barrier((q_gather, own_residual, gain))
     w_value, w_out, w_gate, w_up, w_down = [
         in_vmem(one) for one in (w_value, w_out, w_gate, w_up, w_down)
     ]
-    others = [swapped(one) for one in mine]
-
-    q_all, own_residual, gain = lax.optimization_barrier((q_all, own_residual, gain))
     partial = attend(
-        code, code_other, lengths.reshape(1, requests), q_all, mine + others, ranks, latent, head_local
+        code,
+        code_other,
+        lengths.reshape(1, requests),
+        (q_gather,),
+        pieces,
+        ranks,
+        latent,
+        head_local,
     )
     parts = lax.all_to_all(
         partial, "tensor", split_axis=0, concat_axis=0, tiled=True, axis_index_groups=same_core

time: 169 us -> 165 us (0.976)
  starting transfers between devices: 15.3 us -> 21 us
  waiting for transfers between devices: 33.1 us -> 28.3 us
  local copies, waits for them, and re-layouts: 4.45 us -> 0.97 us
    ppermute x1, waiting for transfers between devices: 10 us -> 0.01 us  [body(): prev_high = lax.ppermute(high, 'dp', from_prev)]
    ppermute x1, waiting for transfers between devices: 0.01 us -> 6.91 us  [body(): next_low = lax.ppermute(low, 'dp', from_next)]
    ppermute x1, waiting for transfers between devices: 0.01 us -> 6.85 us  [body(): next_high = lax.ppermute(high, 'dp', from_next)]
    ppermute x1, waiting for transfers between devices: 6.9 us -> 2.66 us  [body(): prev_low = lax.ppermute(low, 'dp', from_prev)]
    unnamed x28 -> x26, local copies, waits for them, and re-layouts: 4.45 us -> 0.97 us
    ppermute x9, starting transfers between devices: 6.86 us -> 10.3 us  [swapped(): return lax.ppermute(value, 'tensor', swap)]
    ppermute x1, waiting for transfers between devices: 10.7 us -> 8.04 us  [body(): far_low = lax.ppermute(next_low, 'dp', from_next)]
    pallas_call x1, Pallas kernels: 12.3 us -> 9.86 us  [attend(): pl.pallas_call(functools.partial(attend_kernel, dims), out_shape=pltpu.VM...]
  transfers between devices with their start and end apart: 16 -> 16, of which waited for: 7 -> 7; matrix products, arithmetic and copies ran while one was open for 1% -> 1% of each run, Pallas kernels for 1% -> 2%
where the time goes in v3:
time: 165 us
  blocking collectives  80.1 us (49%)
  waiting for transfers between devices  28.3 us (17%)
  starting transfers between devices  21 us (13%)
  Pallas kernels  19.2 us (12%)
  between operations  13.6 us (8%)
    all_to_all x3, blocking collectives, exchange(): lax.all_to_all(value, 'tensor', split_axis=0, concat_axis=0, tiled=True)  45 us
    all_to_all x1, blocking collectives, body(): lax.all_to_all(partial, 'tensor', split_axis=0, concat_axis=0, tiled=True...  35.1 us
    ppermute x9, starting transfers between devices, swapped(): return lax.ppermute(value, 'tensor', swap)  10.3 us
    pallas_call x1, Pallas kernels, attend(): pl.pallas_call(functools.partial(attend_kernel, dims), out_shape=pltpu.VM...  9.86 us
    ppermute x1, waiting for transfers between devices, body(): far_low = lax.ppermute(next_low, 'dp', from_next)  8.04 us
    ppermute x1, waiting for transfers between devices, body(): next_low = lax.ppermute(low, 'dp', from_next)  6.91 us
    ppermute x1, waiting for transfers between devices, body(): next_high = lax.ppermute(high, 'dp', from_next)  6.85 us
    ppermute x1, starting transfers between devices, body(): next_low = lax.ppermute(low, 'dp', from_next)  3.92 us
  transfers between devices with their start and end apart: 16, of which 7 were waited for; matrix products, arithmetic and copies ran while one was open for 1% of the time, Pallas kernels for 2%

profile of v3, /device:TPU:1, one launch (start us, length us, event | category | flops | bytes accessed | tf_op | source)
XLA Modules:
  0.0 164.8 jit_solution(11626947852026158363)
XLA Ops:
  6.5 1.5 collective-permute-start.1
  8.0 1.2 collective-permute-done.1.other
  9.3 0.9 copy-done.2
  10.2 0.9 turn.1.refs_0_
  11.1 1.3 split.2
  12.4 3.9 %collective-permute-start.2 = (bf16[4,576,128]{2,1,0:T(8,128)(2,1)S(1)}, bf16[4,576,128]{2,1,0:T(8,128)(2,1)}, u32[]{:S(2)}, u32[]{:S(2)}) collective-permute-start(bf16[4,576,128]{2,1,0:T(8,128)(2,1)S(1)} %get-tuple-element.15), channel_id=1, source_target_pairs={{32,0},{64,32},{96,64},{0,96},{33,1},{65,33},{97,65},{1,97},{34,2}... | collective-permute-start | bytes 1769480 | tf_op jit(solution)/shard_map/ppermute | solution.py:456
  16.3 1.4 split.3
  17.8 2.7 %collective-permute-start.3 = (bf16[4,576,128]{2,1,0:T(8,128)(2,1)S(1)}, bf16[4,576,128]{2,1,0:T(8,128)(2,1)}, u32[]{:S(2)}, u32[]{:S(2)}) collective-permute-start(bf16[4,576,128]{2,1,0:T(8,128)(2,1)S(1)} %get-tuple-element.16), channel_id=1, source_target_pairs={{32,0},{64,32},{96,64},{0,96},{33,1},{65,33},{97,65},{1,97},{34,2}... | collective-permute-start | bytes 1769480 | tf_op jit(solution)/shard_map/ppermute | solution.py:459
  20.5 1.3 collective-permute-start
  21.8 6.9 %collective-permute-done.2.refs_2_ = bf16[4,576,128]{2,1,0:T(8,128)(2,1)} collective-permute-done((bf16[4,576,128]{2,1,0:T(8,128)(2,1)S(1)}, bf16[4,576,128]{2,1,0:T(8,128)(2,1)}, u32[]{:S(2)}, u32[]{:S(2)}) %collective-permute-start.2) | collective-permute-done | bytes 589856 | tf_op jit(solution)/shard_map/ppermute | solution.py:456
  28.7 2.0 %collective-permute-start.9 = (bf16[4,576,128]{2,1,0:T(8,128)(2,1)}, bf16[4,576,128]{2,1,0:T(8,128)(2,1)}, u32[]{:S(2)}, u32[]{:S(2)}) collective-permute-start(bf16[4,576,128]{2,1,0:T(8,128)(2,1)} %collective-permute-done.2.refs_2_), channel_id=1, source_target_pairs={{0,1},{1,0},{2,3},{3,2},{4,5},{5,4},{6,7},{7,6},{8,9},{9,8},{10,11... | collective-permute-start | bytes 1769480 | tf_op jit(solution)/shard_map/ppermute | solution.py:450
  30.7 3.5 %collective-permute-start.4 = (bf16[4,576,128]{2,1,0:T(8,128)(2,1)}, bf16[4,576,128]{2,1,0:T(8,128)(2,1)}, u32[]{:S(2)}, u32[]{:S(2)}) collective-permute-start(bf16[4,576,128]{2,1,0:T(8,128)(2,1)} %collective-permute-done.2.refs_2_), channel_id=1, source_target_pairs={{32,0},{64,32},{96,64},{0,96},{33,1},{65,33},{97,65},{1,97},{34,2}... | collective-permute-start | bytes 1769480 | tf_op jit(solution)/shard_map/ppermute | solution.py:466
  34.2 0.3 collective-permute-start.14
  34.5 6.8 %collective-permute-done.3.refs_3_ = bf16[4,576,128]{2,1,0:T(8,128)(2,1)} collective-permute-done((bf16[4,576,128]{2,1,0:T(8,128)(2,1)S(1)}, bf16[4,576,128]{2,1,0:T(8,128)(2,1)}, u32[]{:S(2)}, u32[]{:S(2)}) %collective-permute-start.3) | collective-permute-done | bytes 589856 | tf_op jit(solution)/shard_map/ppermute | solution.py:459
  41.3 0.5 collective-permute-start.6
  41.9 2.7 %collective-permute-done.7.refs_6_ = bf16[4,576,128]{2,1,0:T(8,128)(2,1)} collective-permute-done((bf16[4,576,128]{2,1,0:T(8,128)(2,1)S(1)}, bf16[4,576,128]{2,1,0:T(8,128)(2,1)}, u32[]{:S(2)}, u32[]{:S(2)}) %collective-permute-start.7) | collective-permute-done | bytes 589856 | tf_op jit(solution)/shard_map/ppermute | solution.py:460
  44.5 1.5 collective-permute-start.8
  46.0 8.0 %collective-permute-done.4.refs_4_ = bf16[4,576,128]{2,1,0:T(8,128)(2,1)} collective-permute-done((bf16[4,576,128]{2,1,0:T(8,128)(2,1)}, bf16[4,576,128]{2,1,0:T(8,128)(2,1)}, u32[]{:S(2)}, u32[]{:S(2)}) %collective-permute-start.4) | collective-permute-done | bytes 589856 | tf_op jit(solution)/shard_map/ppermute | solution.py:466
  54.1 1.2 collective-permute-start.13
  55.3 1.6 collective-permute-done.6.refs_5_
  56.8 2.6 %collective-permute-start.12 = (bf16[4,576,128]{2,1,0:T(8,128)(2,1)}, bf16[4,576,128]{2,1,0:T(8,128)(2,1)}, u32[]{:S(2)}, u32[]{:S(2)}) collective-permute-start(bf16[4,576,128]{2,1,0:T(8,128)(2,1)} %collective-permute-done.6.refs_5_), channel_id=1, source_target_pairs={{0,1},{1,0},{2,3},{3,2},{4,5},{5,4},{6,7},{7,6},{8,9},{9,8},{10,11... | collective-permute-start | bytes 1769480 | tf_op jit(solution)/shard_map/ppermute | solution.py:450
  59.4 0.9 dynamic-slice_convert_fusion
  60.4 1.0 collective-permute-done.12.refs_12_
  61.4 9.9 %attend.1 = bf16[16,528,128]{2,1,0:T(8,128)(2,1)S(1)} custom-call(s32[1,128]{1,0:T(1,128)S(1)} %add_bitcast_fusion.code_own, s32[1,128]{1,0:T(1,128)S(1)} %collective-permute-done.code_other, s32[1,128]{1,0:T(1,128)S(1)} %bitcast.17, bf16[16,576,128]{2,1,0:T(8,128)(2,1)} %all-gather.2.cloned.1.call-done.refs_0_, bf16[8,576,128]{2,1,0:T(8,128)(2,1)} %refs_1_.1, ...), custom_call_target="tpu_custom_call" | custom-call | tf_op jit(solution)/shard_map/attend/pallas_call | solution.py:245
  71.3 35.1 %all_to_all.20.parts = bf16[16,528,128]{2,1,0:T(8,128)(2,1)S(1)} all-to-all(bf16[16,528,128]{2,1,0:T(8,128)(2,1)S(1)} %attend.1), channel_id=1, replica_groups={{0,2,4,6,8,10,12,14,16,18,20,22,24,26,28,30},{1,3,5,7,9,11,13,15,17,19,..., dimensions={0} | all-to-all | bytes 4325376 | tf_op jit(solution)/shard_map/all_to_all | solution.py:489
  106.5 2.6 %project.1 = bf16[32,56,128]{2,1,0:T(8,128)(2,1)S(1)} custom-call(bf16[16,528,128]{2,1,0:T(8,128)(2,1)S(1)} %all_to_all.20.parts, bf16[4,512,128]{2,1,0:T(8,128)(2,1)S(1)} %copy-done.1, bf16[512,7168]{1,0:T(8,128)(2,1)S(1)} %bitcast.8), custom_call_target="tpu_custom_call" | custom-call | tf_op jit(solution)/shard_map/project/pallas_call | solution.py:347
  109.1 16.0 %all_to_all.21.got = bf16[32,56,128]{2,1,0:T(8,128)(2,1)S(1)} all-to-all(bf16[32,56,128]{2,1,0:T(8,128)(2,1)S(1)} %project.1), channel_id=1, replica_groups=mesh['dp'=4,'tensor'=32] {'tensor'}, dimensions={0} | all-to-all | bytes 917504 | tf_op jit(solution)/shard_map/all_to_all | solution.py:494
  125.1 0.3 norm.1
  125.3 14.5 %all_to_all.22.normed = bf16[32,56,128]{2,1,0:T(8,128)(2,1)S(1)} all-to-all(bf16[32,56,128]{2,1,0:T(8,128)(2,1)S(1)} %get-tuple-element.22), channel_id=1, replica_groups=mesh['dp'=4,'tensor'=32] {'tensor'}, dimensions={0} | all-to-all | bytes 917504 | tf_op jit(solution)/shard_map/all_to_all | solution.py:494
  139.9 2.9 %ffn.1 = bf16[32,56,128]{2,1,0:T(8,128)(2,1)S(1)} custom-call(bf16[32,56,128]{2,1,0:T(8,128)(2,1)S(1)} %all_to_all.22.normed, bf16[7168,384]{1,0:T(8,128)(2,1)S(1)} %bitcast.10, bf16[7168,384]{1,0:T(8,128)(2,1)S(1)} %bitcast.12, bf16[384,7168]{1,0:T(8,128)(2,1)S(1)} %copy-done), custom_call_target="tpu_custom_call" | custom-call | tf_op jit(solution)/shard_map/ffn/pallas_call | solution.py:406
  142.8 14.5 %all_to_all.23 = bf16[32,56,128]{2,1,0:T(8,128)(2,1)S(1)} all-to-all(bf16[32,56,128]{2,1,0:T(8,128)(2,1)S(1)} %ffn.1), channel_id=1, replica_groups=mesh['dp'=4,'tensor'=32] {'tensor'}, dimensions={0} | all-to-all | bytes 917504 | tf_op jit(solution)/shard_map/all_to_all | solution.py:494
  157.4 0.6 add.12
  (45 shorter events, 0.2 us)
Async XLA Ops:
  6.5 14.0 %copy-start.5 = (s32[128,1]{0,1:T(1,128)S(1)}, s32[128,1]{0,1:T(1,128)}, u32[]{:S(2)}) copy-start(s32[128,1]{0,1:T(1,128)} %param.15) | copy-start | bytes 1540
  6.5 14.0 %copy-start.6 = (s32[128,1]{0,1:T(1,128)S(1)}, s32[128,1]{0,1:T(1,128)}, u32[]{:S(2)}) copy-start(s32[128,1]{0,1:T(1,128)} %param.14) | copy-start | bytes 1540
  6.5 54.9 %copy-start.4 = (s32[128]{0:T(128)S(1)}, s32[128]{0:T(128)}, u32[]{:S(2)}) copy-start(s32[128]{0:T(128)} %param.16) | copy-start | bytes 1540
  6.5 53.9 %all-gather.2.cloned.1.call-start = ((), (), s32[]{:S(2)}) async-start(), calls=%async_computation.4 | async-start | bytes 2506752 | tf_op jit(solution)/shard_map/all_gather | solution.py:454
  6.5 2.7 %collective-permute-start.1 = (bf16[576,128]{1,0:T(8,128)(2,1)}, bf16[576,128]{1,0:T(8,128)(2,1)S(1)}, u32[]{:S(2)}, u32[]{:S(2)}) collective-permute-start(bf16[576,128]{1,0:T(8,128)(2,1)} %bitcast.13), channel_id=1, source_target_pairs={{0,1},{1,0},{2,3},{3,2},{4,5},{5,4},{6,7},{7,6},{8,9},{9,8},{10,11... | collective-permute-start | bytes 442376 | tf_op jit(solution)/shard_map/ppermute | solution.py:450
  9.3 0.9 copy-start.2
  12.4 16.3 %collective-permute-start.2 = (bf16[4,576,128]{2,1,0:T(8,128)(2,1)S(1)}, bf16[4,576,128]{2,1,0:T(8,128)(2,1)}, u32[]{:S(2)}, u32[]{:S(2)}) collective-permute-start(bf16[4,576,128]{2,1,0:T(8,128)(2,1)S(1)} %get-tuple-element.15), channel_id=1, source_target_pairs={{32,0},{64,32},{96,64},{0,96},{33,1},{65,33},{97,65},{1,97},{34,2}... | collective-permute-start | bytes 1769480 | tf_op jit(solution)/shard_map/ppermute | solution.py:456
  16.3 17.8 %collective-permute-start.5 = (bf16[4,576,128]{2,1,0:T(8,128)(2,1)S(1)}, bf16[4,576,128]{2,1,0:T(8,128)(2,1)}, u32[]{:S(2)}, u32[]{:S(2)}) collective-permute-start(bf16[4,576,128]{2,1,0:T(8,128)(2,1)S(1)} %get-tuple-element.17), channel_id=1, source_target_pairs={{96,0},{0,32},{32,64},{64,96},{97,1},{1,33},{33,65},{65,97},{98,2}... | collective-permute-start | bytes 1769480 | tf_op jit(solution)/shard_map/ppermute | solution.py:457
  16.3 90.1 %slice-start = ((s8[7340032]{0:T(1024)(128)(4,1)}), s8[3145728]{0:T(1024)(128)(4,1)S(1)}, s32[]{:S(2)}) async-start(s8[7340032]{0:T(1024)(128)(4,1)} %bitcast.7), calls=%async_computation.5 | async-start | bytes 6291456
  17.8 23.6 %collective-permute-start.3 = (bf16[4,576,128]{2,1,0:T(8,128)(2,1)S(1)}, bf16[4,576,128]{2,1,0:T(8,128)(2,1)}, u32[]{:S(2)}, u32[]{:S(2)}) collective-permute-start(bf16[4,576,128]{2,1,0:T(8,128)(2,1)S(1)} %get-tuple-element.16), channel_id=1, source_target_pairs={{32,0},{64,32},{96,64},{0,96},{33,1},{65,33},{97,65},{1,97},{34,2}... | collective-permute-start | bytes 1769480 | tf_op jit(solution)/shard_map/ppermute | solution.py:459
  20.5 24.0 %collective-permute-start.7 = (bf16[4,576,128]{2,1,0:T(8,128)(2,1)S(1)}, bf16[4,576,128]{2,1,0:T(8,128)(2,1)}, u32[]{:S(2)}, u32[]{:S(2)}) collective-permute-start(bf16[4,576,128]{2,1,0:T(8,128)(2,1)S(1)} %get-tuple-element.18), channel_id=1, source_target_pairs={{96,0},{0,32},{32,64},{64,96},{97,1},{1,33},{33,65},{65,97},{98,2}... | collective-permute-start | bytes 1769480 | tf_op jit(solution)/shard_map/ppermute | solution.py:460
  20.5 10.1 %collective-permute-start = (s32[1,128]{1,0:T(1,128)S(1)}, s32[1,128]{1,0:T(1,128)S(1)}, u32[]{:S(2)}, u32[]{:S(2)}) collective-permute-start(s32[1,128]{1,0:T(1,128)S(1)} %add_bitcast_fusion.code_own), channel_id=1, source_target_pairs={{0,1},{1,0},{2,3},{3,2},{4,5},{5,4},{6,7},{7,6},{8,9},{9,8},{10,11... | collective-permute-start | bytes 1544 | tf_op jit(solution)/shard_map/ppermute | solution.py:450
  28.7 17.3 %collective-permute-start.9 = (bf16[4,576,128]{2,1,0:T(8,128)(2,1)}, bf16[4,576,128]{2,1,0:T(8,128)(2,1)}, u32[]{:S(2)}, u32[]{:S(2)}) collective-permute-start(bf16[4,576,128]{2,1,0:T(8,128)(2,1)} %collective-permute-done.2.refs_2_), channel_id=1, source_target_pairs={{0,1},{1,0},{2,3},{3,2},{4,5},{5,4},{6,7},{7,6},{8,9},{9,8},{10,11... | collective-permute-start | bytes 1769480 | tf_op jit(solution)/shard_map/ppermute | solution.py:450
  30.7 23.4 %collective-permute-start.4 = (bf16[4,576,128]{2,1,0:T(8,128)(2,1)}, bf16[4,576,128]{2,1,0:T(8,128)(2,1)}, u32[]{:S(2)}, u32[]{:S(2)}) collective-permute-start(bf16[4,576,128]{2,1,0:T(8,128)(2,1)} %collective-permute-done.2.refs_2_), channel_id=1, source_target_pairs={{32,0},{64,32},{96,64},{0,96},{33,1},{65,33},{97,65},{1,97},{34,2}... | collective-permute-start | bytes 1769480 | tf_op jit(solution)/shard_map/ppermute | solution.py:466
  34.2 21.1 %collective-permute-start.14 = (bf16[4,576,128]{2,1,0:T(8,128)(2,1)}, bf16[4,576,128]{2,1,0:T(8,128)(2,1)}, u32[]{:S(2)}, u32[]{:S(2)}) collective-permute-start(bf16[4,576,128]{2,1,0:T(8,128)(2,1)} %collective-permute-done.5.refs_7_), channel_id=1, source_target_pairs={{0,1},{1,0},{2,3},{3,2},{4,5},{5,4},{6,7},{7,6},{8,9},{9,8},{10,11... | collective-permute-start | bytes 1769480 | tf_op jit(solution)/shard_map/ppermute | solution.py:450
  41.3 15.5 %collective-permute-start.6 = (bf16[4,576,128]{2,1,0:T(8,128)(2,1)}, bf16[4,576,128]{2,1,0:T(8,128)(2,1)}, u32[]{:S(2)}, u32[]{:S(2)}) collective-permute-start(bf16[4,576,128]{2,1,0:T(8,128)(2,1)} %collective-permute-done.5.refs_7_), channel_id=1, source_target_pairs={{96,0},{0,32},{32,64},{64,96},{97,1},{1,33},{33,65},{65,97},{98,2}... | collective-permute-start | bytes 1769480 | tf_op jit(solution)/shard_map/ppermute | solution.py:467
  44.5 15.9 %collective-permute-start.8 = (bf16[8,576,128]{2,1,0:T(8,128)(2,1)}, bf16[8,576,128]{2,1,0:T(8,128)(2,1)}, u32[]{:S(2)}, u32[]{:S(2)}) collective-permute-start(bf16[8,576,128]{2,1,0:T(8,128)(2,1)} %refs_1_.1), channel_id=1, source_target_pairs={{0,1},{1,0},{2,3},{3,2},{4,5},{5,4},{6,7},{7,6},{8,9},{9,8},{10,11... | collective-permute-start | bytes 3538952 | tf_op jit(solution)/shard_map/ppermute | solution.py:450
  46.0 14.4 %collective-permute-start.10 = (bf16[4,576,128]{2,1,0:T(8,128)(2,1)}, bf16[4,576,128]{2,1,0:T(8,128)(2,1)}, u32[]{:S(2)}, u32[]{:S(2)}) collective-permute-start(bf16[4,576,128]{2,1,0:T(8,128)(2,1)} %collective-permute-done.3.refs_3_), channel_id=1, source_target_pairs={{0,1},{1,0},{2,3},{3,2},{4,5},{5,4},{6,7},{7,6},{8,9},{9,8},{10,11... | collective-permute-start | bytes 1769480 | tf_op jit(solution)/shard_map/ppermute | solution.py:450
  54.1 6.3 %collective-permute-start.13 = (bf16[4,576,128]{2,1,0:T(8,128)(2,1)}, bf16[4,576,128]{2,1,0:T(8,128)(2,1)}, u32[]{:S(2)}, u32[]{:S(2)}) collective-permute-start(bf16[4,576,128]{2,1,0:T(8,128)(2,1)} %collective-permute-done.7.refs_6_), channel_id=1, source_target_pairs={{0,1},{1,0},{2,3},{3,2},{4,5},{5,4},{6,7},{7,6},{8,9},{9,8},{10,11... | collective-permute-start | bytes 1769480 | tf_op jit(solution)/shard_map/ppermute | solution.py:450
  55.3 5.2 %collective-permute-start.11 = (bf16[4,576,128]{2,1,0:T(8,128)(2,1)}, bf16[4,576,128]{2,1,0:T(8,128)(2,1)}, u32[]{:S(2)}, u32[]{:S(2)}) collective-permute-start(bf16[4,576,128]{2,1,0:T(8,128)(2,1)} %collective-permute-done.4.refs_4_), channel_id=1, source_target_pairs={{0,1},{1,0},{2,3},{3,2},{4,5},{5,4},{6,7},{7,6},{8,9},{9,8},{10,11... | collective-permute-start | bytes 1769480 | tf_op jit(solution)/shard_map/ppermute | solution.py:450
  56.8 4.6 %collective-permute-start.12 = (bf16[4,576,128]{2,1,0:T(8,128)(2,1)}, bf16[4,576,128]{2,1,0:T(8,128)(2,1)}, u32[]{:S(2)}, u32[]{:S(2)}) collective-permute-start(bf16[4,576,128]{2,1,0:T(8,128)(2,1)} %collective-permute-done.6.refs_5_), channel_id=1, source_target_pairs={{0,1},{1,0},{2,3},{3,2},{4,5},{5,4},{6,7},{7,6},{8,9},{9,8},{10,11... | collective-permute-start | bytes 1769480 | tf_op jit(solution)/shard_map/ppermute | solution.py:450
  61.4 45.0 %slice-start.1 = ((s8[7340032]{0:T(1024)(128)(4,1)}), s8[4194304]{0:T(1024)(128)(4,1)S(1)}, s32[]{:S(2)}) async-start(s8[7340032]{0:T(1024)(128)(4,1)} %bitcast.7), calls=%async_computation.6 | async-start | bytes 8388608
  61.4 45.0 %copy-start.1 = (bf16[4,512,128]{2,1,0:T(8,128)(2,1)S(1)}, bf16[4,512,128]{2,1,0:T(8,128)(2,1)}, u32[]{:S(2)}) copy-start(bf16[4,512,128]{2,1,0:T(8,128)(2,1)} %w_value.1) | copy-start | bytes 1572868
  71.3 53.8 %copy-start.3 = (f32[7168]{0:T(1024)S(1)}, f32[7168]{0:T(1024)}, u32[]{:S(2)}) copy-start(f32[7168]{0:T(1024)} %param.20) | copy-start | bytes 86020
  71.3 68.6 %slice-start.2 = ((s8[5505024]{0:T(1024)(128)(4,1)}), s8[1310720]{0:T(1024)(128)(4,1)S(1)}, s32[]{:S(2)}) async-start(s8[5505024]{0:T(1024)(128)(4,1)} %bitcast.9), calls=%async_computation.7 | async-start | bytes 2621440
  71.3 68.5 %slice-start.4 = ((s8[5505024]{0:T(1024)(128)(4,1)}), s8[4194304]{0:T(1024)(128)(4,1)S(1)}, s32[]{:S(2)}) async-start(s8[5505024]{0:T(1024)(128)(4,1)} %bitcast.11), calls=%async_computation.9 | async-start | bytes 8388608
  106.4 33.4 %slice-start.3 = ((s8[5505024]{0:T(1024)(128)(4,1)}), s8[4194304]{0:T(1024)(128)(4,1)S(1)}, s32[]{:S(2)}) async-start(s8[5505024]{0:T(1024)(128)(4,1)} %bitcast.9), calls=%async_computation.8 | async-start | bytes 8388608
  106.4 33.4 %slice-start.5 = ((s8[5505024]{0:T(1024)(128)(4,1)}), s8[1310720]{0:T(1024)(128)(4,1)S(1)}, s32[]{:S(2)}) async-start(s8[5505024]{0:T(1024)(128)(4,1)} %bitcast.11), calls=%async_computation.10 | async-start | bytes 2621440
  106.5 33.4 %copy-start = (bf16[384,7168]{1,0:T(8,128)(2,1)S(1)}, bf16[384,7168]{1,0:T(8,128)(2,1)}, u32[]{:S(2)}) copy-start(bf16[384,7168]{1,0:T(8,128)(2,1)} %w_down.1) | copy-start | bytes 16515076
Sparse Core Ops, SparseCore 0:
  11.3 46.7 all-gather.1

commit v4 on v3

--- a/solution.py
+++ b/solution.py
@@ -13,8 +13,7 @@
 CORES = 2
 LANES = 128
 HEAD_LOCAL = 4
-QUERY_PARTS = 4
-QUERY_ROWS = (576,)
+SIDE = 4
 MIB = 1024 * 1024
 hbm_spec = pl.BlockSpec(memory_space=pl.ANY)
 vmem_spec = pl.BlockSpec(memory_space=pltpu.VMEM)
@@ -55,7 +54,7 @@
     )(in_hbm(pool), *after)
 
 
-def turn_kernel(own, other, *outs):
+def turn_kernel(own, other, out):
     width, head_total = own.shape
     heads = head_total // CORES
     head_local, tail = HEAD_LOCAL, width // LANES * LANES
@@ -75,67 +74,90 @@
     rows = [
         pair[i][:, p * LANES : (p + 1) * LANES] for p in range(tail // LANES) for i in range(CORES)
     ]
-    rows = jnp.concatenate(
+    out[0] = jnp.concatenate(
         rows + [jnp.concatenate([one[:, tail:] for one in pair], axis=1)], axis=0
     )
-    at = 0
-    for out in outs:
-        out[0] = rows[at : at + out.shape[1], :]
-        at += out.shape[1]
 
 
 def turn(own, other):
     return pl.pallas_call(
         turn_kernel,
-        out_shape=tuple(
-            jax.ShapeDtypeStruct((1, rows, own.shape[1]), own.dtype) for rows in QUERY_ROWS
-        ),
+        out_shape=jax.ShapeDtypeStruct((1,) + own.shape, own.dtype),
         in_specs=[vmem_spec] * 2,
-        out_specs=(vmem_spec,) * len(QUERY_ROWS),
+        out_specs=vmem_spec,
         compiler_params=pltpu.CompilerParams(vmem_limit_bytes=4 * MIB),
         name="turn",
     )(own, other)
 
 
+def join_kernel(*refs):
+    count = len(refs) - 2
+    out, sems = refs[count:]
+    copies = [
+        pltpu.make_async_copy(one, out.at[pl.ds(i, 1)], sems.at[i])
+        for i, one in enumerate(refs[:count])
+    ]
+    for one in copies:
+        one.start()
+    for one in copies:
+        one.wait()
+
+
+def join(pieces):
+    count = len(pieces)
+    return pl.pallas_call(
+        join_kernel,
+        out_shape=jax.ShapeDtypeStruct((count,) + pieces[0].shape[1:], pieces[0].dtype),
+        in_specs=[hbm_spec] * count,
+        out_specs=hbm_spec,
+        scratch_shapes=[pltpu.SemaphoreType.DMA((count,))],
+        compiler_params=pltpu.CompilerParams(vmem_limit_bytes=4 * MIB),
+        name="join",
+    )(*pieces)
+
+
+def by_core(core, chip):
+    x, y = chip % SIDE, chip // SIDE
+    return jnp.where(core == 0, x, y), jnp.where(core == 0, y, x)
+
+
+def shifts(tensors, first, distance):
+    pairs = []
+    for i in range(tensors):
+        core, chip = i % CORES, i // CORES
+        x, y = chip % SIDE, chip // SIDE
+        if (core == 0) == first:
+            x = (x + distance) % SIDE
+        else:
+            y = (y + distance) % SIDE
+        pairs.append((i, (y * SIDE + x) * CORES + core))
+    return pairs
+
+
 def attend_kernel(dims, code_own, code_other, lengths, *refs):
     slots, ranks, head_local, latent, count = dims
-    q_refs = refs[: len(QUERY_ROWS)]
-    pieces = refs[len(QUERY_ROWS) : len(QUERY_ROWS) + count]
-    out_ref, kbuf, qbuf, lse_buf, sems = refs[len(QUERY_ROWS) + count :]
-    pairs, width, _ = qbuf.shape
-    group = CORES * pairs
+    q_refs, pieces = refs[:SIDE], refs[SIDE : SIDE + count]
+    outs = refs[SIDE + count : 2 * SIDE + count]
+    kbuf, qbuf, obuf, lse_buf, sems = refs[2 * SIDE + count :]
+    group = CORES * SIDE * SIDE
     heads = lse_buf.shape[0]
     block_len = kbuf.shape[2]
     owners = heads // head_local
     my_rank = lax.axis_index("dp")
     column = lax.axis_index("tensor")
     core = column % CORES
+    own_first, own_second = by_core(core, column // CORES)
     first = my_rank * group
-    portion = pairs // QUERY_PARTS
-
-    def q_copies(step):
-        made, at = [], 0
-        for i, one in enumerate(q_refs):
-            rows = one.shape[1]
-            made.append(
-                pltpu.make_async_copy(
-                    one.at[pl.ds(step * portion, portion)],
-                    qbuf.at[pl.ds(step * portion, portion), pl.ds(at, rows)],
-                    sems.at[count + step * len(q_refs) + i],
-                )
-            )
-            at += rows
-        return made
-
+    q_copies = [
+        pltpu.make_async_copy(one, qbuf.at[pl.ds(e * SIDE, SIDE)], sems.at[count + e])
+        for e, one in enumerate(q_refs)
+    ]
     copies, at = [], 0
     for i, one in enumerate(pieces):
         copies.append(pltpu.make_async_copy(one, kbuf.at[pl.ds(at, one.shape[0])], sems.at[i]))
         at += one.shape[0]
-    for one in q_copies(0) + copies:
+    for one in q_copies + copies:
         one.start()
-    for step in range(1, QUERY_PARTS):
-        for one in q_copies(step):
-            one.start()
     token = lax.broadcasted_iota(jnp.int32, (1, 2 * block_len), 1)
     partner = column + 1 - 2 * core
     position = jnp.where(
@@ -143,36 +165,46 @@
     )
     lane = lax.broadcasted_iota(jnp.int32, (heads, LANES), 1)
     lse_buf[...] = jnp.zeros_like(lse_buf)
-    for one in copies:
+    spots = []
+    for k in range(owners):
+        k_first, k_second = by_core(core, k)
+        spots.append(
+            (k_first - own_first + SIDE) % SIDE * SIDE + (k_second - own_second + SIDE) % SIDE
+        )
+    for one in q_copies + copies:
         one.wait()
 
     def place(codes, r):
         code = codes[0, first + r]
         return ((code // slots - my_rank + ranks) % ranks) * slots + code % slots
 
-    unroll = CORES * portion
-
-    def several(step):
-        rs = [step * unroll + i for i in range(unroll)]
+    unroll = CORES * SIDE
+
+    def several(e, carry):
+        second = (own_second - e + SIDE) % SIDE
+        rs, asked = [], []
+        for i in range(SIDE):
+            chip = jnp.where(core == 0, second * SIDE + i, i * SIDE + second)
+            at = e * SIDE + (own_first - i + SIDE) % SIDE
+            for side in range(CORES):
+                rs.append(chip * CORES + side)
+                rotary = qbuf[at, latent:, :]
+                mine = (lane < LANES // CORES) if side == 0 else (lane >= LANES // CORES)
+                rows = [
+                    qbuf[at, (p * CORES + side) * heads : (p * CORES + side + 1) * heads, :]
+                    for p in range(latent // LANES)
+                ]
+                asked.append(
+                    jnp.concatenate(
+                        rows + [jnp.where(mine, rotary, jnp.zeros_like(rotary))], axis=1
+                    )
+                )
         keys = [
             jnp.concatenate(
                 [kbuf[place(code_own, r)], kbuf[ranks * slots + place(code_other, r)]], axis=1
             )
             for r in rs
         ]
-        asked = []
-        for i in range(unroll):
-            at = step * portion + i // CORES
-            side = i % CORES
-            rotary = qbuf[at, latent:, :]
-            mine = (lane < LANES // CORES) if side == 0 else (lane >= LANES // CORES)
-            rows = [
-                qbuf[at, (p * CORES + side) * heads : (p * CORES + side + 1) * heads, :]
-                for p in range(latent // LANES)
-            ]
-            asked.append(
-                jnp.concatenate(rows + [jnp.where(mine, rotary, jnp.zeros_like(rotary))], axis=1)
-            )
         scores = [
             jnp.dot(
                 q,
@@ -202,8 +234,8 @@
             for weight, key, scale in zip(weights, keys, scales)
         ]
         lse_all = lse_buf[...]
-        for r, lse in zip(rs, lses):
-            lse_all = jnp.where(lane == r, lse, lse_all)
+        for i, lse in enumerate(lses):
+            lse_all = jnp.where(lane == second * unroll + i, lse, lse_all)
         lse_buf[...] = lse_all
         rows_count = unroll * head_local
         for k in range(owners):
@@ -211,78 +243,72 @@
                 [one[k * head_local : (k + 1) * head_local] for one in mixed], axis=0
             ).astype(jnp.bfloat16)
             for p in range(latent // LANES):
-                rows_at = pl.multiple_of(p * group * head_local + step * rows_count, rows_count)
-                out_ref[k, pl.ds(rows_at, rows_count), :] = both[:, p * LANES : (p + 1) * LANES]
-
-    def one_step(step, carry):
-        for one in q_copies(step):
-            one.wait()
-        several(step)
+                rows_at = pl.multiple_of(p * group * head_local + second * rows_count, rows_count)
+                obuf[spots[k], pl.ds(rows_at, rows_count), :] = both[:, p * LANES : (p + 1) * LANES]
         return carry
 
-    lax.fori_loop(0, QUERY_PARTS, one_step, 0)
-    lse_all = lse_buf[...]
-    high = lse_all.astype(jnp.bfloat16).astype(jnp.float32)
-    mid = (lse_all - high).astype(jnp.bfloat16).astype(jnp.float32)
-    low = lse_all - high - mid
+    lax.fori_loop(0, SIDE, several, 0)
     tail = latent // LANES * group * head_local
+    parts = lse_parts(lse_buf[...])
     for k in range(owners):
         own = slice(k * head_local, (k + 1) * head_local)
-        out_ref[k, tail:, :] = jnp.concatenate(
-            [high[own], mid[own], low[own], jnp.zeros_like(low[own])], axis=0
+        obuf[spots[k], tail:, :] = jnp.concatenate(
+            [one[own] for one in parts] + [jnp.zeros_like(parts[0][own])], axis=0
         ).astype(jnp.bfloat16)
+    copies = [
+        pltpu.make_async_copy(obuf.at[pl.ds(d * SIDE, SIDE)], outs[d], sems.at[d])
+        for d in range(SIDE)
+    ]
+    for one in copies:
+        one.start()
+    for one in copies:
+        one.wait()
+
+
+def lse_parts(value):
+    high = value.astype(jnp.bfloat16).astype(jnp.float32)
+    mid = (value - high).astype(jnp.bfloat16).astype(jnp.float32)
+    return [high, mid, value - high - mid]
 
 
 def attend(code_own, code_other, lengths, q_all, pieces, ranks, latent, head_local):
-    pairs, _, head_total = q_all[0].shape
+    per, _, head_total = q_all[0].shape
     width, block_len = pieces[0].shape[1:]
     heads = head_total // CORES
     blocks = sum(one.shape[0] for one in pieces)
-    owners = heads // head_local
-    out_rows = latent // LANES * pairs * CORES * head_local + 16
+    chips = SIDE * SIDE
+    out_rows = latent // LANES * chips * CORES * head_local + 16
     count = len(pieces)
     dims = (blocks // ranks // CORES, ranks, head_local, latent, count)
     return pl.pallas_call(
         functools.partial(attend_kernel, dims),
-        out_shape=pltpu.VMEM((owners, out_rows, LANES), jnp.bfloat16),
-        in_specs=[smem_spec] * 3 + [hbm_spec] * (len(q_all) + count),
-        out_specs=vmem_spec,
+        out_shape=(pltpu.VMEM((SIDE, out_rows, LANES), jnp.bfloat16),) * SIDE,
+        in_specs=[smem_spec] * 3 + [hbm_spec] * (SIDE + count),
+        out_specs=(vmem_spec,) * SIDE,
         scratch_shapes=[
             pltpu.VMEM((blocks, width, block_len), jnp.bfloat16),
-            pltpu.VMEM((pairs, width, head_total), jnp.bfloat16),
+            pltpu.VMEM((chips, width, head_total), jnp.bfloat16),
+            pltpu.VMEM((chips, out_rows, LANES), jnp.bfloat16),
             pltpu.VMEM((heads, LANES), jnp.float32),
-            pltpu.SemaphoreType.DMA((count + QUERY_PARTS * len(q_all),)),
+            pltpu.SemaphoreType.DMA((count + SIDE,)),
         ],
-        compiler_params=pltpu.CompilerParams(vmem_limit_bytes=20 * MIB),
+        compiler_params=pltpu.CompilerParams(vmem_limit_bytes=22 * MIB),
         name="attend",
     )(code_own, code_other, lengths, *[in_hbm(one) for one in q_all], *pieces)
 
 
-def scatter_tiles(flat, value, first_tile, group, tiles):
-    for n in range(value.shape[1] // LANES):
-        flat[pl.ds(first_tile + n, group, stride=tiles), :] = value[:, n * LANES : (n + 1) * LANES]
-
-
-def project_kernel(dims, parts, w_value, w_out, sent, att_buf, flat):
-    group, head_local, latent, chunk = dims
-    sources = parts.shape[0]
-    rows = group * head_local
-    pieces = latent // LANES
-    tiles = w_out.shape[1] // LANES
-    tail = pieces * rows
-    lses = []
-    for s in range(sources):
-        three = parts[s, tail:, :].astype(jnp.float32)
-        lses.append(
-            three[:head_local]
-            + three[head_local : 2 * head_local]
-            + three[2 * head_local : 3 * head_local]
-        )
-    peak = functools.reduce(jnp.maximum, lses)
-    shares = [jnp.exp(one - peak) for one in lses]
-    inverse = 1.0 / functools.reduce(jnp.add, shares)
-    share_all = jnp.concatenate([one * inverse for one in shares], axis=0)
-    count = sources * head_local
+def combine_shares(lses, sets, rows, group, head_local):
+    merged, scaled = [], [None] * len(lses)
+    for one_set in sets:
+        peak = functools.reduce(jnp.maximum, [lses[s] for s in one_set])
+        shares = [jnp.exp(lses[s] - peak) for s in one_set]
+        total = functools.reduce(jnp.add, shares)
+        merged.append(peak + jnp.log(total))
+        inverse = 1.0 / total
+        for s, share in zip(one_set, shares):
+            scaled[s] = share * inverse
+    share_all = jnp.concatenate(scaled, axis=0)
+    count = len(lses) * head_local
     pick_request = jnp.where(
         lax.broadcasted_iota(jnp.int32, (rows, LANES), 0) // head_local
         == lax.broadcasted_iota(jnp.int32, (rows, LANES), 1),
@@ -313,11 +339,73 @@
         precision=lax.Precision.HIGHEST,
         preferred_element_type=jnp.float32,
     )
+    return share, merged
+
+
+def read_lse(tile, head_local):
+    three = tile.astype(jnp.float32)
+    return functools.reduce(
+        jnp.add, [three[i * head_local : (i + 1) * head_local] for i in range(3)]
+    )
+
+
+def merge_kernel(dims, *refs):
+    group, head_local, latent = dims
+    ins, outs = refs[:SIDE], refs[SIDE:]
+    rows = group * head_local
+    pieces = latent // LANES
+    tail = pieces * rows
+    lses = [read_lse(one[e, tail:, :], head_local) for e in range(SIDE) for one in ins]
+    sets = [[e * SIDE + s for s in range(SIDE)] for e in range(SIDE)]
+    share, merged = combine_shares(lses, sets, rows, group, head_local)
+    for e in range(SIDE):
+        totals = [None] * pieces
+        for s in range(SIDE):
+            at = e * SIDE + s
+            factor = jnp.broadcast_to(share[:, at : at + 1], (rows, LANES))
+            for p in range(pieces):
+                term = ins[s][e, p * rows : (p + 1) * rows, :].astype(jnp.float32) * factor
+                totals[p] = term if s == 0 else totals[p] + term
+        for p in range(pieces):
+            outs[e][p * rows : (p + 1) * rows, :] = totals[p].astype(jnp.bfloat16)
+        parts = lse_parts(merged[e])
+        outs[e][tail:, :] = jnp.concatenate(parts + [jnp.zeros_like(parts[0])], axis=0).astype(
+            jnp.bfloat16
+        )
+
+
+def merge(arrived, group, head_local, latent):
+    shape = arrived[0].shape[1:]
+    return pl.pallas_call(
+        functools.partial(merge_kernel, (group, head_local, latent)),
+        out_shape=(pltpu.VMEM(shape, jnp.bfloat16),) * SIDE,
+        in_specs=[vmem_spec] * SIDE,
+        out_specs=(vmem_spec,) * SIDE,
+        compiler_params=pltpu.CompilerParams(vmem_limit_bytes=8 * MIB),
+        name="merge",
+    )(*[in_vmem(one) for one in arrived])
+
+
+def scatter_tiles(flat, value, first_tile, group, tiles):
+    for n in range(value.shape[1] // LANES):
+        flat[pl.ds(first_tile + n, group, stride=tiles), :] = value[:, n * LANES : (n + 1) * LANES]
+
+
+def project_kernel(dims, *refs):
+    group, head_local, latent, chunk = dims
+    parts = refs[:SIDE]
+    w_value, w_out, sent, att_buf, flat = refs[SIDE:]
+    rows = group * head_local
+    pieces = latent // LANES
+    tiles = w_out.shape[1] // LANES
+    tail = pieces * rows
+    lses = [read_lse(one[tail:, :], head_local) for one in parts]
+    share, _ = combine_shares(lses, [list(range(SIDE))], rows, group, head_local)
     totals = [None] * pieces
-    for s in range(sources):
+    for s in range(SIDE):
         factor = jnp.broadcast_to(share[:, s : s + 1], (rows, LANES))
         for p in range(pieces):
-            term = parts[s, p * rows : (p + 1) * rows, :].astype(jnp.float32) * factor
+            term = parts[s][p * rows : (p + 1) * rows, :].astype(jnp.float32) * factor
             totals[p] = term if s == 0 else totals[p] + term
     for p in range(pieces):
         att_buf[p] = totals[p]
@@ -335,8 +423,12 @@
             per_head, w_out[:, c * chunk : (c + 1) * chunk], preferred_element_type=jnp.float32
         )
         scatter_tiles(flat, value, c * chunk // LANES, group, tiles)
-    for r in range(group):
-        sent[r] = flat[r * tiles : (r + 1) * tiles, :].astype(jnp.bfloat16)
+    core = lax.axis_index("tensor") % CORES
+    for i in range(group):
+        pair, side = i // CORES, i % CORES
+        second, place = pair // SIDE, pair % SIDE
+        r = jnp.where(core == 0, pair, place * SIDE + second) * CORES + side
+        sent[r] = flat[i * tiles : (i + 1) * tiles, :].astype(jnp.bfloat16)
 
 
 def project(parts, w_value, w_out, group):
@@ -347,7 +439,7 @@
     return pl.pallas_call(
         functools.partial(project_kernel, dims),
         out_shape=pltpu.VMEM((group, tiles, LANES), jnp.bfloat16),
-        in_specs=[vmem_spec] * 3,
+        in_specs=[vmem_spec] * (SIDE + 2),
         out_specs=vmem_spec,
         scratch_shapes=[
             pltpu.VMEM((latent // LANES, group * head_local, LANES), jnp.float32),
@@ -355,7 +447,7 @@
         ],
         compiler_params=pltpu.CompilerParams(vmem_limit_bytes=12 * MIB),
         name="project",
-    )(in_vmem(parts), w_value, w_out)
+    )(*[in_vmem(one) for one in parts], w_value, w_out)
 
 
 def norm_kernel(got, residual, gain, kept, normed):
@@ -434,7 +526,6 @@
     ranks = lax.axis_size("dp")
     tensors = lax.axis_size("tensor")
     column = lax.axis_index("tensor")
-    chips = tensors // CORES
     group = residual.shape[0]
     slots = cache_pool.shape[0]
     head_local, latent, _ = w_value.shape
@@ -442,16 +533,17 @@
     tiles = features // LANES
     requests = lengths.shape[0]
     swap = [(i, i ^ 1) for i in range(tensors)]
-    same_core = [[c + CORES * k for k in range(chips)] for c in range(CORES)]
     from_next = [((i + 1) % ranks, i) for i in range(ranks)]
     from_prev = [((i - 1) % ranks, i) for i in range(ranks)]
 
     def swapped(value):
         return lax.ppermute(value, "tensor", swap)
 
+    def along(value, first, distance):
+        return lax.ppermute(value, "tensor", shifts(tensors, first, distance))
+
     own_queries = queries[0]
-    (q_pair,) = turn(own_queries, swapped(own_queries))
-    q_gather = lax.all_gather(q_pair, "tensor", axis=0, tiled=True, axis_index_groups=same_core)
+    q_pair = turn(own_queries, swapped(own_queries))
     low, high = split(cache_pool)
     next_low = lax.ppermute(low, "dp", from_next)
     prev_high = lax.ppermute(high, "dp", from_prev)
@@ -463,6 +555,8 @@
         .astype(jnp.float32)
         .reshape(tiles, LANES)
     )
+    q_line = join([q_pair] + [along(q_pair, True, d) for d in range(1, SIDE)])
+    q_all = [q_line] + [along(q_line, False, e) for e in range(1, SIDE)]
     far_low = lax.ppermute(next_low, "dp", from_next)
     far_high = lax.ppermute(prev_high, "dp", from_prev)
     mine = [next_low, next_high, far_low, far_high, prev_low, prev_high]
@@ -472,7 +566,7 @@
     code = (holder * slots + slot_ids).reshape(1, requests)
     code_other = swapped(code)
     gain = norm_gain.reshape(tiles, LANES)
-    q_gather, own_residual, gain = lax.optimization_barrier((q_gather, own_residual, gain))
+    q_all, own_residual, gain = lax.optimization_barrier((q_all, own_residual, gain))
     w_value, w_out, w_gate, w_up, w_down = [
         in_vmem(one) for one in (w_value, w_out, w_gate, w_up, w_down)
     ]
@@ -480,15 +574,15 @@
         code,
         code_other,
         lengths.reshape(1, requests),
-        (q_gather,),
+        q_all,
         pieces,
         ranks,
         latent,
         head_local,
     )
-    parts = lax.all_to_all(
-        partial, "tensor", split_axis=0, concat_axis=0, tiled=True, axis_index_groups=same_core
-    )
+    arrived = [partial[0]] + [along(partial[d], True, d) for d in range(1, SIDE)]
+    merged = merge(arrived, group, head_local, latent)
+    parts = [merged[0]] + [along(merged[e], False, e) for e in range(1, SIDE)]
 
     def exchange(value):
         return lax.all_to_all(value, "tensor", split_axis=0, concat_axis=0, tiled=True)

time: 165 us -> 150 us (0.909)
  blocking collectives: 80.1 us -> 48.4 us
  starting transfers between devices: 21 us -> 36.7 us
  between operations: 13.6 us -> 0.24 us
  waiting for transfers between devices: 28.3 us -> 40.8 us
    all_to_all x1 -> x0, blocking collectives: 35.1 us -> none  [body(): lax.all_to_all(partial, 'tensor', split_axis=0, concat_axis=0, tiled=True...]
    ppermute x0 -> x12, waiting for transfers between devices: none -> 20.2 us  [along(): return lax.ppermute(value, 'tensor', shifts(tensors, first, distance))]
    ppermute x0 -> x12, starting transfers between devices: none -> 16.5 us  [along(): return lax.ppermute(value, 'tensor', shifts(tensors, first, distance))]
    ppermute x1, waiting for transfers between devices: 6.91 us -> 0.01 us  [body(): next_low = lax.ppermute(low, 'dp', from_next)]
    ppermute x1, waiting for transfers between devices: 1.58 us -> 5.19 us  [body(): far_high = lax.ppermute(prev_high, 'dp', from_prev)]
    all_to_all x3, blocking collectives: 45 us -> 48.4 us  [exchange(): lax.all_to_all(value, 'tensor', split_axis=0, concat_axis=0, tiled=True)]
    ppermute x1, waiting for transfers between devices: 8.04 us -> 5.67 us  [body(): far_low = lax.ppermute(next_low, 'dp', from_next)]
    pallas_call x2 -> x4, Pallas kernels: 10.8 us -> 11.7 us  [the longest x1 9.6 us: attend(): pl.pallas_call(functools.partial(attend_kernel, dims), out_shape=(pltpu.V...]
  transfers between devices with their start and end apart: 16 -> 27, of which waited for: 7 -> 13; matrix products, arithmetic and copies ran while one was open for 1% -> 1% of each run, Pallas kernels for 2% -> 2%
where the time goes in v4:
time: 150 us
  blocking collectives  48.4 us (32%)
  waiting for transfers between devices  40.8 us (27%)
  starting transfers between devices  36.7 us (24%)
  Pallas kernels  19.5 us (13%)
  other arithmetic  2.29 us (2%)
  local copies, waits for them, and re-layouts  1.77 us (1%)
    all_to_all x3, blocking collectives, exchange(): lax.all_to_all(value, 'tensor', split_axis=0, concat_axis=0, tiled=True)  48.4 us
    ppermute x12, waiting for transfers between devices, along(): return lax.ppermute(value, 'tensor', shifts(tensors, first, distance))  20.2 us
    ppermute x12, starting transfers between devices, along(): return lax.ppermute(value, 'tensor', shifts(tensors, first, distance))  16.5 us
    ppermute x9, starting transfers between devices, swapped(): return lax.ppermute(value, 'tensor', swap)  10.2 us
    pallas_call x1, Pallas kernels, attend(): pl.pallas_call(functools.partial(attend_kernel, dims), out_shape=(pltpu.V...  9.6 us
    ppermute x1, waiting for transfers between devices, body(): next_high = lax.ppermute(high, 'dp', from_next)  6.53 us
    ppermute x1, waiting for transfers between devices, body(): far_low = lax.ppermute(next_low, 'dp', from_next)  5.67 us
    ppermute x1, waiting for transfers between devices, body(): far_high = lax.ppermute(prev_high, 'dp', from_prev)  5.19 us
  transfers between devices with their start and end apart: 27, of which 13 were waited for; matrix products, arithmetic and copies ran while one was open for 1% of the time, Pallas kernels for 2%

profile of v4, /device:TPU:1, one launch (start us, length us, event | category | flops | bytes accessed | tf_op | source)
XLA Modules:
  0.0 149.8 jit_solution(8976709126626982404)
XLA Ops:
  0.0 1.3 split.2
  1.3 4.7 %collective-permute-start.8 = (bf16[4,576,128]{2,1,0:T(8,128)(2,1)S(1)}, bf16[4,576,128]{2,1,0:T(8,128)(2,1)S(1)}, u32[]{:S(2)}, u32[]{:S(2)}) collective-permute-start(bf16[4,576,128]{2,1,0:T(8,128)(2,1)S(1)} %get-tuple-element.29), channel_id=1, source_target_pairs={{32,0},{64,32},{96,64},{0,96},{33,1},{65,33},{97,65},{1,97},{34,2}... | collective-permute-start | bytes 1769480 | tf_op jit(solution)/shard_map/ppermute | solution.py:548
  6.9 1.2 collective-permute-done.1.other
  9.3 2.8 %collective-permute-start.4 = (bf16[1,576,128]{2,1,0:T(8,128)(2,1)S(1)}, bf16[1,576,128]{2,1,0:T(8,128)(2,1)S(1)}, u32[]{:S(2)}, u32[]{:S(2)}) collective-permute-start(bf16[1,576,128]{2,1,0:T(8,128)(2,1)S(1)} %turn.1.refs_0_), channel_id=1, source_target_pairs={{0,6},{1,25},{2,0},{3,27},{4,2},{5,29},{6,4},{7,31},{8,14},{9,1},{... | collective-permute-start | bytes 442376 | tf_op jit(solution)/shard_map/ppermute | solution.py:543
  13.8 2.0 %collective-permute-done.4.refs_3_ = bf16[1,576,128]{2,1,0:T(8,128)(2,1)S(1)} collective-permute-done((bf16[1,576,128]{2,1,0:T(8,128)(2,1)S(1)}, bf16[1,576,128]{2,1,0:T(8,128)(2,1)S(1)}, u32[]{:S(2)}, u32[]{:S(2)}) %collective-permute-start.4) | collective-permute-done | bytes 147488 | tf_op jit(solution)/shard_map/ppermute | solution.py:543
  15.7 1.0 collective-permute-start
  16.7 1.3 split.3
  18.0 3.0 %collective-permute-start.9 = (bf16[4,576,128]{2,1,0:T(8,128)(2,1)S(1)}, bf16[4,576,128]{2,1,0:T(8,128)(2,1)S(1)}, u32[]{:S(2)}, u32[]{:S(2)}) collective-permute-start(bf16[4,576,128]{2,1,0:T(8,128)(2,1)S(1)} %get-tuple-element.30), channel_id=1, source_target_pairs={{32,0},{64,32},{96,64},{0,96},{33,1},{65,33},{97,65},{1,97},{34,2}... | collective-permute-start | bytes 1769480 | tf_op jit(solution)/shard_map/ppermute | solution.py:551
  21.8 3.4 %collective-permute-start.7 = (bf16[4,576,128]{2,1,0:T(8,128)(2,1)S(1)}, bf16[4,576,128]{2,1,0:T(8,128)(2,1)S(1)}, u32[]{:S(2)}, u32[]{:S(2)}) collective-permute-start(bf16[4,576,128]{2,1,0:T(8,128)(2,1)S(1)} %join.1.refs_0_), channel_id=1, source_target_pairs={{0,24},{1,7},{2,26},{3,1},{4,28},{5,3},{6,30},{7,5},{8,0},{9,15},{... | collective-permute-start | bytes 1769480 | tf_op jit(solution)/shard_map/ppermute | solution.py:543
  26.0 6.5 %collective-permute-done.9.refs_6_ = bf16[4,576,128]{2,1,0:T(8,128)(2,1)S(1)} collective-permute-done((bf16[4,576,128]{2,1,0:T(8,128)(2,1)S(1)}, bf16[4,576,128]{2,1,0:T(8,128)(2,1)S(1)}, u32[]{:S(2)}, u32[]{:S(2)}) %collective-permute-start.9) | collective-permute-done | bytes 589856 | tf_op jit(solution)/shard_map/ppermute | solution.py:551
  32.5 2.1 %collective-permute-start.15 = (bf16[4,576,128]{2,1,0:T(8,128)(2,1)S(1)}, bf16[4,576,128]{2,1,0:T(8,128)(2,1)S(1)}, u32[]{:S(2)}, u32[]{:S(2)}) collective-permute-start(bf16[4,576,128]{2,1,0:T(8,128)(2,1)S(1)} %collective-permute-done.8.refs_5_), channel_id=1, source_target_pairs={{0,1},{1,0},{2,3},{3,2},{4,5},{5,4},{6,7},{7,6},{8,9},{9,8},{10,11... | collective-permute-start | bytes 1769480 | tf_op jit(solution)/shard_map/ppermute | solution.py:540
  34.6 1.1 collective-permute-done.13.refs_9_
  35.6 2.3 %collective-permute-start.10 = (bf16[4,576,128]{2,1,0:T(8,128)(2,1)S(1)}, bf16[4,576,128]{2,1,0:T(8,128)(2,1)}, u32[]{:S(2)}, u32[]{:S(2)}) collective-permute-start(bf16[4,576,128]{2,1,0:T(8,128)(2,1)S(1)} %collective-permute-done.8.refs_5_), channel_id=1, source_target_pairs={{32,0},{64,32},{96,64},{0,96},{33,1},{65,33},{97,65},{1,97},{34,2}... | collective-permute-start | bytes 1769480 | tf_op jit(solution)/shard_map/ppermute | solution.py:560
  38.4 1.6 %collective-permute-start.20 = (bf16[4,576,128]{2,1,0:T(8,128)(2,1)S(1)}, bf16[4,576,128]{2,1,0:T(8,128)(2,1)}, u32[]{:S(2)}, u32[]{:S(2)}) collective-permute-start(bf16[4,576,128]{2,1,0:T(8,128)(2,1)S(1)} %collective-permute-done.11.refs_10_), channel_id=1, source_target_pairs={{0,1},{1,0},{2,3},{3,2},{4,5},{5,4},{6,7},{7,6},{8,9},{9,8},{10,11... | collective-permute-start | bytes 1769480 | tf_op jit(solution)/shard_map/ppermute | solution.py:540
  40.1 1.9 %collective-permute-done.5.refs_1_ = bf16[4,576,128]{2,1,0:T(8,128)(2,1)S(1)} collective-permute-done((bf16[4,576,128]{2,1,0:T(8,128)(2,1)S(1)}, bf16[4,576,128]{2,1,0:T(8,128)(2,1)S(1)}, u32[]{:S(2)}, u32[]{:S(2)}) %collective-permute-start.5) | collective-permute-done | bytes 589856 | tf_op jit(solution)/shard_map/ppermute | solution.py:543
  41.9 2.1 %collective-permute-start.14 = (bf16[8,576,128]{2,1,0:T(8,128)(2,1)}, bf16[8,576,128]{2,1,0:T(8,128)(2,1)}, u32[]{:S(2)}, u32[]{:S(2)}) collective-permute-start(bf16[8,576,128]{2,1,0:T(8,128)(2,1)} %refs_4_.2), channel_id=1, source_target_pairs={{0,1},{1,0},{2,3},{3,2},{4,5},{5,4},{6,7},{7,6},{8,9},{9,8},{10,11... | collective-permute-start | bytes 3538952 | tf_op jit(solution)/shard_map/ppermute | solution.py:540
  44.9 5.7 %collective-permute-done.10.refs_7_ = bf16[4,576,128]{2,1,0:T(8,128)(2,1)} collective-permute-done((bf16[4,576,128]{2,1,0:T(8,128)(2,1)S(1)}, bf16[4,576,128]{2,1,0:T(8,128)(2,1)}, u32[]{:S(2)}, u32[]{:S(2)}) %collective-permute-start.10) | collective-permute-done | bytes 589856 | tf_op jit(solution)/shard_map/ppermute | solution.py:560
  50.6 1.0 collective-permute-start.19
  51.5 5.2 %collective-permute-done.12.refs_8_ = bf16[4,576,128]{2,1,0:T(8,128)(2,1)} collective-permute-done((bf16[4,576,128]{2,1,0:T(8,128)(2,1)S(1)}, bf16[4,576,128]{2,1,0:T(8,128)(2,1)}, u32[]{:S(2)}, u32[]{:S(2)}) %collective-permute-start.12) | collective-permute-done | bytes 589856 | tf_op jit(solution)/shard_map/ppermute | solution.py:561
  60.0 9.6 %attend.1 = (bf16[4,528,128]{2,1,0:T(8,128)(2,1)S(1)}, bf16[4,528,128]{2,1,0:T(8,128)(2,1)S(1)}, bf16[4,528,128]{2,1,0:T(8,128)(2,1)S(1)}, bf16[4,528,128]{2,1,0:T(8,128)(2,1)S(1)}) custom-call(s32[1,128]{1,0:T(1,128)S(1)} %add_bitcast_fusion.code_own, s32[1,128]{1,0:T(1,128)S(1)} %collective-permute-done.code_other, s32[1,128]{1,0:T(1,128)S(1)} %bitcast.17, ...), custom_call_target="tpu_custom_call" | custom-call | tf_op jit(solution)/shard_map/attend/pallas_call | solution.py:283
  69.7 4.6 %collective-permute-start.22 = (bf16[4,528,128]{2,1,0:T(8,128)(2,1)S(1)}, bf16[4,528,128]{2,1,0:T(8,128)(2,1)S(1)}, u32[]{:S(2)}, u32[]{:S(2)}) collective-permute-start(bf16[4,528,128]{2,1,0:T(8,128)(2,1)S(1)} %get-tuple-element.35), channel_id=1, source_target_pairs={{0,4},{1,17},{2,6},{3,19},{4,0},{5,21},{6,2},{7,23},{8,12},{9,25},... | collective-permute-start | bytes 1622024 | tf_op jit(solution)/shard_map/ppermute | solution.py:543
  74.3 5.9 %collective-permute-done.21.refs_1_ = bf16[4,528,128]{2,1,0:T(8,128)(2,1)S(1)} collective-permute-done((bf16[4,528,128]{2,1,0:T(8,128)(2,1)S(1)}, bf16[4,528,128]{2,1,0:T(8,128)(2,1)S(1)}, u32[]{:S(2)}, u32[]{:S(2)}) %collective-permute-start.21) | collective-permute-done | bytes 540704 | tf_op jit(solution)/shard_map/ppermute | solution.py:543
  80.2 6.7 %collective-permute-done.22.refs_2_ = bf16[4,528,128]{2,1,0:T(8,128)(2,1)S(1)} collective-permute-done((bf16[4,528,128]{2,1,0:T(8,128)(2,1)S(1)}, bf16[4,528,128]{2,1,0:T(8,128)(2,1)S(1)}, u32[]{:S(2)}, u32[]{:S(2)}) %collective-permute-start.22) | collective-permute-done | bytes 540704 | tf_op jit(solution)/shard_map/ppermute | solution.py:543
  86.9 1.1 merge.1
  88.3 3.2 %collective-permute-start.25 = (bf16[528,128]{1,0:T(8,128)(2,1)S(1)}, bf16[528,128]{1,0:T(8,128)(2,1)S(1)}, u32[]{:S(2)}, u32[]{:S(2)}) collective-permute-start(bf16[528,128]{1,0:T(8,128)(2,1)S(1)} %get-tuple-element.39), channel_id=1, source_target_pairs={{0,16},{1,5},{2,18},{3,7},{4,20},{5,1},{6,22},{7,3},{8,24},{9,13},... | collective-permute-start | bytes 405512 | tf_op jit(solution)/shard_map/ppermute | solution.py:543
  91.9 1.5 collective-permute-done.24.refs_1_
  93.4 1.9 %collective-permute-done.25.refs_2_ = bf16[528,128]{1,0:T(8,128)(2,1)S(1)} collective-permute-done((bf16[528,128]{1,0:T(8,128)(2,1)S(1)}, bf16[528,128]{1,0:T(8,128)(2,1)S(1)}, u32[]{:S(2)}, u32[]{:S(2)}) %collective-permute-start.25) | collective-permute-done | bytes 135200 | tf_op jit(solution)/shard_map/ppermute | solution.py:543
  95.3 2.1 %project.1 = bf16[32,56,128]{2,1,0:T(8,128)(2,1)S(1)} custom-call(bf16[528,128]{1,0:T(8,128)(2,1)S(1)} %get-tuple-element.37.refs_0_, bf16[528,128]{1,0:T(8,128)(2,1)S(1)} %collective-permute-done.24.refs_1_, bf16[528,128]{1,0:T(8,128)(2,1)S(1)} %collective-permute-done.25.refs_2_, bf16[528,128]{1,0:T(8,128)(2,1)S(1)} %collective-permute-done.26.refs_3_, ...), custom_call_target="tpu_custom_call" | custom-call | tf_op jit(solution)/shard_map/project/pallas_call | solution.py:439
  97.5 19.4 %all_to_all.15.got = bf16[32,56,128]{2,1,0:T(8,128)(2,1)S(1)} all-to-all(bf16[32,56,128]{2,1,0:T(8,128)(2,1)S(1)} %project.1), channel_id=1, replica_groups=mesh['dp'=4,'tensor'=32] {'tensor'}, dimensions={0} | all-to-all | bytes 917504 | tf_op jit(solution)/shard_map/all_to_all | solution.py:588
  117.1 14.5 %all_to_all.16.normed = bf16[32,56,128]{2,1,0:T(8,128)(2,1)S(1)} all-to-all(bf16[32,56,128]{2,1,0:T(8,128)(2,1)S(1)} %get-tuple-element.44), channel_id=1, replica_groups=mesh['dp'=4,'tensor'=32] {'tensor'}, dimensions={0} | all-to-all | bytes 917504 | tf_op jit(solution)/shard_map/all_to_all | solution.py:588
  131.7 2.9 %ffn.1 = bf16[32,56,128]{2,1,0:T(8,128)(2,1)S(1)} custom-call(bf16[32,56,128]{2,1,0:T(8,128)(2,1)S(1)} %all_to_all.16.normed, bf16[7168,384]{1,0:T(8,128)(2,1)S(1)} %bitcast.10, bf16[7168,384]{1,0:T(8,128)(2,1)S(1)} %bitcast.12, bf16[384,7168]{1,0:T(8,128)(2,1)S(1)} %copy-done), custom_call_target="tpu_custom_call" | custom-call | tf_op jit(solution)/shard_map/ffn/pallas_call | solution.py:498
  134.6 14.5 %all_to_all.17 = bf16[32,56,128]{2,1,0:T(8,128)(2,1)S(1)} all-to-all(bf16[32,56,128]{2,1,0:T(8,128)(2,1)S(1)} %ffn.1), channel_id=1, replica_groups=mesh['dp'=4,'tensor'=32] {'tensor'}, dimensions={0} | all-to-all | bytes 917504 | tf_op jit(solution)/shard_map/all_to_all | solution.py:588
  (71 shorter events, 11.8 us)
Async XLA Ops:
  1.3 24.0 %collective-permute-start.8 = (bf16[4,576,128]{2,1,0:T(8,128)(2,1)S(1)}, bf16[4,576,128]{2,1,0:T(8,128)(2,1)S(1)}, u32[]{:S(2)}, u32[]{:S(2)}) collective-permute-start(bf16[4,576,128]{2,1,0:T(8,128)(2,1)S(1)} %get-tuple-element.29), channel_id=1, source_target_pairs={{32,0},{64,32},{96,64},{0,96},{33,1},{65,33},{97,65},{1,97},{34,2}... | collective-permute-start | bytes 1769480 | tf_op jit(solution)/shard_map/ppermute | solution.py:548
  5.9 19.4 %collective-permute-start.11 = (bf16[4,576,128]{2,1,0:T(8,128)(2,1)S(1)}, bf16[4,576,128]{2,1,0:T(8,128)(2,1)S(1)}, u32[]{:S(2)}, u32[]{:S(2)}) collective-permute-start(bf16[4,576,128]{2,1,0:T(8,128)(2,1)S(1)} %get-tuple-element.31), channel_id=1, source_target_pairs={{96,0},{0,32},{32,64},{64,96},{97,1},{1,33},{33,65},{65,97},{98,2}... | collective-permute-start | bytes 1769480 | tf_op jit(solution)/shard_map/ppermute | solution.py:549
  5.9 2.2 %collective-permute-start.1 = (bf16[576,128]{1,0:T(8,128)(2,1)}, bf16[576,128]{1,0:T(8,128)(2,1)S(1)}, u32[]{:S(2)}, u32[]{:S(2)}) collective-permute-start(bf16[576,128]{1,0:T(8,128)(2,1)} %bitcast.13), channel_id=1, source_target_pairs={{0,1},{1,0},{2,3},{3,2},{4,5},{5,4},{6,7},{7,6},{8,9},{9,8},{10,11... | collective-permute-start | bytes 442376 | tf_op jit(solution)/shard_map/ppermute | solution.py:540
  9.3 6.4 %collective-permute-start.4 = (bf16[1,576,128]{2,1,0:T(8,128)(2,1)S(1)}, bf16[1,576,128]{2,1,0:T(8,128)(2,1)S(1)}, u32[]{:S(2)}, u32[]{:S(2)}) collective-permute-start(bf16[1,576,128]{2,1,0:T(8,128)(2,1)S(1)} %turn.1.refs_0_), channel_id=1, source_target_pairs={{0,6},{1,25},{2,0},{3,27},{4,2},{5,29},{6,4},{7,31},{8,14},{9,1},{... | collective-permute-start | bytes 442376 | tf_op jit(solution)/shard_map/ppermute | solution.py:543
  12.1 5.9 %collective-permute-start.3 = (bf16[1,576,128]{2,1,0:T(8,128)(2,1)S(1)}, bf16[1,576,128]{2,1,0:T(8,128)(2,1)S(1)}, u32[]{:S(2)}, u32[]{:S(2)}) collective-permute-start(bf16[1,576,128]{2,1,0:T(8,128)(2,1)S(1)} %turn.1.refs_0_), channel_id=1, source_target_pairs={{0,4},{1,17},{2,6},{3,19},{4,0},{5,21},{6,2},{7,23},{8,12},{9,25},... | collective-permute-start | bytes 442376 | tf_op jit(solution)/shard_map/ppermute | solution.py:543
  12.4 8.6 %collective-permute-start.2 = (bf16[1,576,128]{2,1,0:T(8,128)(2,1)S(1)}, bf16[1,576,128]{2,1,0:T(8,128)(2,1)S(1)}, u32[]{:S(2)}, u32[]{:S(2)}) collective-permute-start(bf16[1,576,128]{2,1,0:T(8,128)(2,1)S(1)} %turn.1.refs_0_), channel_id=1, source_target_pairs={{0,2},{1,9},{2,4},{3,11},{4,6},{5,13},{6,0},{7,15},{8,10},{9,17},{... | collective-permute-start | bytes 442376 | tf_op jit(solution)/shard_map/ppermute | solution.py:543
  15.7 6.1 %collective-permute-start = (s32[1,128]{1,0:T(1,128)S(1)}, s32[1,128]{1,0:T(1,128)S(1)}, u32[]{:S(2)}, u32[]{:S(2)}) collective-permute-start(s32[1,128]{1,0:T(1,128)S(1)} %add_bitcast_fusion.code_own), channel_id=1, source_target_pairs={{0,1},{1,0},{2,3},{3,2},{4,5},{5,4},{6,7},{7,6},{8,9},{9,8},{10,11... | collective-permute-start | bytes 1544 | tf_op jit(solution)/shard_map/ppermute | solution.py:540
  18.0 14.5 %collective-permute-start.9 = (bf16[4,576,128]{2,1,0:T(8,128)(2,1)S(1)}, bf16[4,576,128]{2,1,0:T(8,128)(2,1)S(1)}, u32[]{:S(2)}, u32[]{:S(2)}) collective-permute-start(bf16[4,576,128]{2,1,0:T(8,128)(2,1)S(1)} %get-tuple-element.30), channel_id=1, source_target_pairs={{32,0},{64,32},{96,64},{0,96},{33,1},{65,33},{97,65},{1,97},{34,2}... | collective-permute-start | bytes 1769480 | tf_op jit(solution)/shard_map/ppermute | solution.py:551
  21.0 14.6 %collective-permute-start.13 = (bf16[4,576,128]{2,1,0:T(8,128)(2,1)S(1)}, bf16[4,576,128]{2,1,0:T(8,128)(2,1)S(1)}, u32[]{:S(2)}, u32[]{:S(2)}) collective-permute-start(bf16[4,576,128]{2,1,0:T(8,128)(2,1)S(1)} %get-tuple-element.32), channel_id=1, source_target_pairs={{96,0},{0,32},{32,64},{64,96},{97,1},{1,33},{33,65},{65,97},{98,2}... | collective-permute-start | bytes 1769480 | tf_op jit(solution)/shard_map/ppermute | solution.py:552
  21.8 37.4 %copy-start.1 = (bf16[4,576,128]{2,1,0:T(8,128)(2,1)}, bf16[4,576,128]{2,1,0:T(8,128)(2,1)S(1)}, u32[]{:S(2)}) copy-start(bf16[4,576,128]{2,1,0:T(8,128)(2,1)S(1)} %join.1.refs_0_) | copy-start | bytes 1769476
  21.8 16.6 %collective-permute-start.7 = (bf16[4,576,128]{2,1,0:T(8,128)(2,1)S(1)}, bf16[4,576,128]{2,1,0:T(8,128)(2,1)S(1)}, u32[]{:S(2)}, u32[]{:S(2)}) collective-permute-start(bf16[4,576,128]{2,1,0:T(8,128)(2,1)S(1)} %join.1.refs_0_), channel_id=1, source_target_pairs={{0,24},{1,7},{2,26},{3,1},{4,28},{5,3},{6,30},{7,5},{8,0},{9,15},{... | collective-permute-start | bytes 1769480 | tf_op jit(solution)/shard_map/ppermute | solution.py:543
  25.3 14.8 %collective-permute-start.6 = (bf16[4,576,128]{2,1,0:T(8,128)(2,1)S(1)}, bf16[4,576,128]{2,1,0:T(8,128)(2,1)S(1)}, u32[]{:S(2)}, u32[]{:S(2)}) collective-permute-start(bf16[4,576,128]{2,1,0:T(8,128)(2,1)S(1)} %join.1.refs_0_), channel_id=1, source_target_pairs={{0,16},{1,5},{2,18},{3,7},{4,20},{5,1},{6,22},{7,3},{8,24},{9,13},... | collective-permute-start | bytes 1769480 | tf_op jit(solution)/shard_map/ppermute | solution.py:543
  25.3 16.6 %collective-permute-start.5 = (bf16[4,576,128]{2,1,0:T(8,128)(2,1)S(1)}, bf16[4,576,128]{2,1,0:T(8,128)(2,1)S(1)}, u32[]{:S(2)}, u32[]{:S(2)}) collective-permute-start(bf16[4,576,128]{2,1,0:T(8,128)(2,1)S(1)} %join.1.refs_0_), channel_id=1, source_target_pairs={{0,8},{1,3},{2,10},{3,5},{4,12},{5,7},{6,14},{7,1},{8,16},{9,11},{... | collective-permute-start | bytes 1769480 | tf_op jit(solution)/shard_map/ppermute | solution.py:543
  32.5 11.6 %collective-permute-start.15 = (bf16[4,576,128]{2,1,0:T(8,128)(2,1)S(1)}, bf16[4,576,128]{2,1,0:T(8,128)(2,1)S(1)}, u32[]{:S(2)}, u32[]{:S(2)}) collective-permute-start(bf16[4,576,128]{2,1,0:T(8,128)(2,1)S(1)} %collective-permute-done.8.refs_5_), channel_id=1, source_target_pairs={{0,1},{1,0},{2,3},{3,2},{4,5},{5,4},{6,7},{7,6},{8,9},{9,8},{10,11... | collective-permute-start | bytes 1769480 | tf_op jit(solution)/shard_map/ppermute | solution.py:540
  35.6 14.9 %collective-permute-start.10 = (bf16[4,576,128]{2,1,0:T(8,128)(2,1)S(1)}, bf16[4,576,128]{2,1,0:T(8,128)(2,1)}, u32[]{:S(2)}, u32[]{:S(2)}) collective-permute-start(bf16[4,576,128]{2,1,0:T(8,128)(2,1)S(1)} %collective-permute-done.8.refs_5_), channel_id=1, source_target_pairs={{32,0},{64,32},{96,64},{0,96},{33,1},{65,33},{97,65},{1,97},{34,2}... | collective-permute-start | bytes 1769480 | tf_op jit(solution)/shard_map/ppermute | solution.py:560
  38.4 13.1 %collective-permute-start.20 = (bf16[4,576,128]{2,1,0:T(8,128)(2,1)S(1)}, bf16[4,576,128]{2,1,0:T(8,128)(2,1)}, u32[]{:S(2)}, u32[]{:S(2)}) collective-permute-start(bf16[4,576,128]{2,1,0:T(8,128)(2,1)S(1)} %collective-permute-done.11.refs_10_), channel_id=1, source_target_pairs={{0,1},{1,0},{2,3},{3,2},{4,5},{5,4},{6,7},{7,6},{8,9},{9,8},{10,11... | collective-permute-start | bytes 1769480 | tf_op jit(solution)/shard_map/ppermute | solution.py:540
  40.1 16.6 %collective-permute-start.12 = (bf16[4,576,128]{2,1,0:T(8,128)(2,1)S(1)}, bf16[4,576,128]{2,1,0:T(8,128)(2,1)}, u32[]{:S(2)}, u32[]{:S(2)}) collective-permute-start(bf16[4,576,128]{2,1,0:T(8,128)(2,1)S(1)} %collective-permute-done.11.refs_10_), channel_id=1, source_target_pairs={{96,0},{0,32},{32,64},{64,96},{97,1},{1,33},{33,65},{65,97},{98,2}... | collective-permute-start | bytes 1769480 | tf_op jit(solution)/shard_map/ppermute | solution.py:561
  41.9 16.4 %collective-permute-start.14 = (bf16[8,576,128]{2,1,0:T(8,128)(2,1)}, bf16[8,576,128]{2,1,0:T(8,128)(2,1)}, u32[]{:S(2)}, u32[]{:S(2)}) collective-permute-start(bf16[8,576,128]{2,1,0:T(8,128)(2,1)} %refs_4_.2), channel_id=1, source_target_pairs={{0,1},{1,0},{2,3},{3,2},{4,5},{5,4},{6,7},{7,6},{8,9},{9,8},{10,11... | collective-permute-start | bytes 3538952 | tf_op jit(solution)/shard_map/ppermute | solution.py:540
  44.1 14.3 %collective-permute-start.16 = (bf16[4,576,128]{2,1,0:T(8,128)(2,1)S(1)}, bf16[4,576,128]{2,1,0:T(8,128)(2,1)S(1)}, u32[]{:S(2)}, u32[]{:S(2)}) collective-permute-start(bf16[4,576,128]{2,1,0:T(8,128)(2,1)S(1)} %collective-permute-done.9.refs_6_), channel_id=1, source_target_pairs={{0,1},{1,0},{2,3},{3,2},{4,5},{5,4},{6,7},{7,6},{8,9},{9,8},{10,11... | collective-permute-start | bytes 1769480 | tf_op jit(solution)/shard_map/ppermute | solution.py:540
  50.6 7.8 %collective-permute-start.19 = (bf16[4,576,128]{2,1,0:T(8,128)(2,1)S(1)}, bf16[4,576,128]{2,1,0:T(8,128)(2,1)S(1)}, u32[]{:S(2)}, u32[]{:S(2)}) collective-permute-start(bf16[4,576,128]{2,1,0:T(8,128)(2,1)S(1)} %collective-permute-done.13.refs_9_), channel_id=1, source_target_pairs={{0,1},{1,0},{2,3},{3,2},{4,5},{5,4},{6,7},{7,6},{8,9},{9,8},{10,11... | collective-permute-start | bytes 1769480 | tf_op jit(solution)/shard_map/ppermute | solution.py:540
  51.5 6.8 %collective-permute-start.17 = (bf16[4,576,128]{2,1,0:T(8,128)(2,1)}, bf16[4,576,128]{2,1,0:T(8,128)(2,1)S(1)}, u32[]{:S(2)}, u32[]{:S(2)}) collective-permute-start(bf16[4,576,128]{2,1,0:T(8,128)(2,1)} %collective-permute-done.10.refs_7_), channel_id=1, source_target_pairs={{0,1},{1,0},{2,3},{3,2},{4,5},{5,4},{6,7},{7,6},{8,9},{9,8},{10,11... | collective-permute-start | bytes 1769480 | tf_op jit(solution)/shard_map/ppermute | solution.py:540
  56.7 2.5 %collective-permute-start.18 = (bf16[4,576,128]{2,1,0:T(8,128)(2,1)}, bf16[4,576,128]{2,1,0:T(8,128)(2,1)S(1)}, u32[]{:S(2)}, u32[]{:S(2)}) collective-permute-start(bf16[4,576,128]{2,1,0:T(8,128)(2,1)} %collective-permute-done.12.refs_8_), channel_id=1, source_target_pairs={{0,1},{1,0},{2,3},{3,2},{4,5},{5,4},{6,7},{7,6},{8,9},{9,8},{10,11... | collective-permute-start | bytes 1769480 | tf_op jit(solution)/shard_map/ppermute | solution.py:540
  60.0 71.6 %slice-start.4 = ((s8[5505024]{0:T(1024)(128)(4,1)}), s8[4194304]{0:T(1024)(128)(4,1)S(1)}, s32[]{:S(2)}) async-start(s8[5505024]{0:T(1024)(128)(4,1)} %bitcast.11), calls=%async_computation.7 | async-start | bytes 8388608
  69.6 10.5 %collective-permute-start.21 = (bf16[4,528,128]{2,1,0:T(8,128)(2,1)S(1)}, bf16[4,528,128]{2,1,0:T(8,128)(2,1)S(1)}, u32[]{:S(2)}, u32[]{:S(2)}) collective-permute-start(bf16[4,528,128]{2,1,0:T(8,128)(2,1)S(1)} %get-tuple-element.34), channel_id=1, source_target_pairs={{0,2},{1,9},{2,4},{3,11},{4,6},{5,13},{6,0},{7,15},{8,10},{9,17},{... | collective-permute-start | bytes 1622024 | tf_op jit(solution)/shard_map/ppermute | solution.py:543
  69.7 17.1 %collective-permute-start.22 = (bf16[4,528,128]{2,1,0:T(8,128)(2,1)S(1)}, bf16[4,528,128]{2,1,0:T(8,128)(2,1)S(1)}, u32[]{:S(2)}, u32[]{:S(2)}) collective-permute-start(bf16[4,528,128]{2,1,0:T(8,128)(2,1)S(1)} %get-tuple-element.35), channel_id=1, source_target_pairs={{0,4},{1,17},{2,6},{3,19},{4,0},{5,21},{6,2},{7,23},{8,12},{9,25},... | collective-permute-start | bytes 1622024 | tf_op jit(solution)/shard_map/ppermute | solution.py:543
  74.3 12.5 %collective-permute-start.23 = (bf16[4,528,128]{2,1,0:T(8,128)(2,1)S(1)}, bf16[4,528,128]{2,1,0:T(8,128)(2,1)S(1)}, u32[]{:S(2)}, u32[]{:S(2)}) collective-permute-start(bf16[4,528,128]{2,1,0:T(8,128)(2,1)S(1)} %get-tuple-element.36), channel_id=1, source_target_pairs={{0,6},{1,25},{2,0},{3,27},{4,2},{5,29},{6,4},{7,31},{8,14},{9,1},{... | collective-permute-start | bytes 1622024 | tf_op jit(solution)/shard_map/ppermute | solution.py:543
  86.9 44.8 %slice-start.5 = ((s8[5505024]{0:T(1024)(128)(4,1)}), s8[1310720]{0:T(1024)(128)(4,1)S(1)}, s32[]{:S(2)}) async-start(s8[5505024]{0:T(1024)(128)(4,1)} %bitcast.11), calls=%async_computation.8 | async-start | bytes 2621440
  87.9 5.4 %collective-permute-start.24 = (bf16[528,128]{1,0:T(8,128)(2,1)S(1)}, bf16[528,128]{1,0:T(8,128)(2,1)S(1)}, u32[]{:S(2)}, u32[]{:S(2)}) collective-permute-start(bf16[528,128]{1,0:T(8,128)(2,1)S(1)} %get-tuple-element.38), channel_id=1, source_target_pairs={{0,8},{1,3},{2,10},{3,5},{4,12},{5,7},{6,14},{7,1},{8,16},{9,11},{... | collective-permute-start | bytes 405512 | tf_op jit(solution)/shard_map/ppermute | solution.py:543
  88.3 7.0 %collective-permute-start.25 = (bf16[528,128]{1,0:T(8,128)(2,1)S(1)}, bf16[528,128]{1,0:T(8,128)(2,1)S(1)}, u32[]{:S(2)}, u32[]{:S(2)}) collective-permute-start(bf16[528,128]{1,0:T(8,128)(2,1)S(1)} %get-tuple-element.39), channel_id=1, source_target_pairs={{0,16},{1,5},{2,18},{3,7},{4,20},{5,1},{6,22},{7,3},{8,24},{9,13},... | collective-permute-start | bytes 405512 | tf_op jit(solution)/shard_map/ppermute | solution.py:543
  91.4 3.9 %collective-permute-start.26 = (bf16[528,128]{1,0:T(8,128)(2,1)S(1)}, bf16[528,128]{1,0:T(8,128)(2,1)S(1)}, u32[]{:S(2)}, u32[]{:S(2)}) collective-permute-start(bf16[528,128]{1,0:T(8,128)(2,1)S(1)} %get-tuple-element.40), channel_id=1, source_target_pairs={{0,24},{1,7},{2,26},{3,1},{4,28},{5,3},{6,30},{7,5},{8,0},{9,15},{... | collective-permute-start | bytes 405512 | tf_op jit(solution)/shard_map/ppermute | solution.py:543
  95.3 36.4 %slice-start.2 = ((s8[5505024]{0:T(1024)(128)(4,1)}), s8[4194304]{0:T(1024)(128)(4,1)S(1)}, s32[]{:S(2)}) async-start(s8[5505024]{0:T(1024)(128)(4,1)} %bitcast.9), calls=%async_computation.5 | async-start | bytes 8388608
  95.3 36.3 %slice-start.3 = ((s8[5505024]{0:T(1024)(128)(4,1)}), s8[1310720]{0:T(1024)(128)(4,1)S(1)}, s32[]{:S(2)}) async-start(s8[5505024]{0:T(1024)(128)(4,1)} %bitcast.9), calls=%async_computation.6 | async-start | bytes 2621440
  (10 other events, 184.3 us)

commit v5 on v4

--- a/solution.py
+++ b/solution.py
@@ -28,12 +28,11 @@
     return pltpu.with_memory_space_constraint(value, pltpu.HBM)
 
 
-def split_kernel(pool, *refs):
-    low, high, sems = refs[-3:]
+def split_kernel(following, previous, low, high, sems):
     half = low.shape[0]
     copies = [
-        pltpu.make_async_copy(pool.at[pl.ds(i * half, half)], one, sems.at[i])
-        for i, one in enumerate((low, high))
+        pltpu.make_async_copy(following.at[pl.ds(0, half)], low, sems.at[0]),
+        pltpu.make_async_copy(previous.at[pl.ds(half, half)], high, sems.at[1]),
     ]
     for one in copies:
         one.start()
@@ -41,17 +40,17 @@
         one.wait()
 
 
-def split(pool, *after):
-    half = (pool.shape[0] // 2,) + pool.shape[1:]
+def split(following, previous):
+    half = (following.shape[0] // 2,) + following.shape[1:]
     return pl.pallas_call(
         split_kernel,
-        out_shape=(pltpu.VMEM(half, pool.dtype), pltpu.VMEM(half, pool.dtype)),
-        in_specs=[hbm_spec] * (1 + len(after)),
+        out_shape=(pltpu.VMEM(half, following.dtype), pltpu.VMEM(half, following.dtype)),
+        in_specs=[hbm_spec] * 2,
         out_specs=(vmem_spec, vmem_spec),
         scratch_shapes=[pltpu.SemaphoreType.DMA((2,))],
         compiler_params=pltpu.CompilerParams(vmem_limit_bytes=12 * MIB),
         name="split",
-    )(in_hbm(pool), *after)
+    )(following, previous)
 
 
 def turn_kernel(own, other, out):
@@ -543,28 +542,26 @@
         return lax.ppermute(value, "tensor", shifts(tensors, first, distance))
 
     own_queries = queries[0]
-    q_pair = turn(own_queries, swapped(own_queries))
-    low, high = split(cache_pool)
-    next_low = lax.ppermute(low, "dp", from_next)
-    prev_high = lax.ppermute(high, "dp", from_prev)
-    low, high = split(cache_pool, q_pair)
-    next_high = lax.ppermute(high, "dp", from_next)
-    prev_low = lax.ppermute(low, "dp", from_prev)
-    own_residual = (
-        lax.dynamic_index_in_dim(residual, column, 0, keepdims=False)
-        .astype(jnp.float32)
-        .reshape(tiles, LANES)
-    )
+    other_queries = swapped(own_queries)
+    q_pair = turn(own_queries, other_queries)
+    following = lax.ppermute(cache_pool, "dp", from_next)
+    previous = lax.ppermute(cache_pool, "dp", from_prev)
     q_line = join([q_pair] + [along(q_pair, True, d) for d in range(1, SIDE)])
     q_all = [q_line] + [along(q_line, False, e) for e in range(1, SIDE)]
-    far_low = lax.ppermute(next_low, "dp", from_next)
-    far_high = lax.ppermute(prev_high, "dp", from_prev)
-    mine = [next_low, next_high, far_low, far_high, prev_low, prev_high]
+    passed = split(following, previous)
+    far_low = lax.ppermute(passed[0], "dp", from_next)
+    far_high = lax.ppermute(passed[1], "dp", from_prev)
+    mine = [following, far_low, far_high, previous]
     moved = [in_vmem(swapped(one)) for one in mine]
     mine = [in_vmem(one) for one in mine]
     pieces = [in_hbm(cache_pool)] + mine + [in_hbm(swapped(cache_pool))] + moved
     code = (holder * slots + slot_ids).reshape(1, requests)
     code_other = swapped(code)
+    own_residual = (
+        lax.dynamic_index_in_dim(residual, column, 0, keepdims=False)
+        .astype(jnp.float32)
+        .reshape(tiles, LANES)
+    )
     gain = norm_gain.reshape(tiles, LANES)
     q_all, own_residual, gain = lax.optimization_barrier((q_all, own_residual, gain))
     w_value, w_out, w_gate, w_up, w_down = [

time: 150 us -> 144 us (0.960)
  starting transfers between devices: 36.7 us -> 33.8 us
    ppermute x6 -> x4, starting transfers between devices: 10 us -> 6.2 us  [the longest x1 2.47 us: body(): previous = lax.ppermute(cache_pool, 'dp', from_prev)]
    ppermute x6 -> x4, waiting for transfers between devices: 18.5 us -> 15.4 us  [the longest x1 7.83 us: body(): previous = lax.ppermute(cache_pool, 'dp', from_prev)]
    ppermute x12, waiting for transfers between devices: 20.2 us -> 22.2 us  [along(): return lax.ppermute(value, 'tensor', shifts(tensors, first, distance))]
    ppermute x9 -> x7, starting transfers between devices: 10.2 us -> 10.5 us  [swapped(): return lax.ppermute(value, 'tensor', swap)]
  transfers between devices with their start and end apart: 27 -> 23, of which waited for: 13 -> 14; matrix products, arithmetic and copies ran while one was open for 1% -> 1% of each run, Pallas kernels for 2% -> 2%
where the time goes in v5:
time: 144 us
  blocking collectives  49.6 us (34%)
  waiting for transfers between devices  39.7 us (28%)
  starting transfers between devices  33.8 us (23%)
  Pallas kernels  18.1 us (13%)
  other arithmetic  1.62 us (1%)
    all_to_all x3, blocking collectives, exchange(): lax.all_to_all(value, 'tensor', split_axis=0, concat_axis=0, tiled=True)  49.6 us
    ppermute x12, waiting for transfers between devices, along(): return lax.ppermute(value, 'tensor', shifts(tensors, first, distance))  22.2 us
    ppermute x12, starting transfers between devices, along(): return lax.ppermute(value, 'tensor', shifts(tensors, first, distance))  17.1 us
    ppermute x7, starting transfers between devices, swapped(): return lax.ppermute(value, 'tensor', swap)  10.5 us
    pallas_call x1, Pallas kernels, attend(): pl.pallas_call(functools.partial(attend_kernel, dims), out_shape=(pltpu.V...  9.49 us
    ppermute x1, waiting for transfers between devices, body(): previous = lax.ppermute(cache_pool, 'dp', from_prev)  7.83 us
    ppermute x1, waiting for transfers between devices, body(): far_low = lax.ppermute(passed[0], 'dp', from_next)  7.35 us
    pallas_call x1, Pallas kernels, ffn(): pl.pallas_call(functools.partial(ffn_kernel, features // 7), out_shape=pl...  2.88 us
  transfers between devices with their start and end apart: 23, of which 14 were waited for; matrix products, arithmetic and copies ran while one was open for 1% of the time, Pallas kernels for 2%

profile of v5, /device:TPU:1, one launch (start us, length us, event | category | flops | bytes accessed | tf_op | source)
XLA Modules:
  0.0 144.0 jit_solution(9844337064410555754)
XLA Ops:
  0.0 2.5 %collective-permute-start.9 = (bf16[8,576,128]{2,1,0:T(8,128)(2,1)}, bf16[8,576,128]{2,1,0:T(8,128)(2,1)S(1)}, u32[]{:S(2)}, u32[]{:S(2)}) collective-permute-start(bf16[8,576,128]{2,1,0:T(8,128)(2,1)} %refs_4_.2), channel_id=1, source_target_pairs={{96,0},{0,32},{32,64},{64,96},{97,1},{1,33},{33,65},{65,97},{98,2}... | collective-permute-start | bytes 3538952 | tf_op jit(solution)/shard_map/ppermute | solution.py:548
  2.5 2.2 %collective-permute-start.8 = (bf16[8,576,128]{2,1,0:T(8,128)(2,1)}, bf16[8,576,128]{2,1,0:T(8,128)(2,1)S(1)}, u32[]{:S(2)}, u32[]{:S(2)}) collective-permute-start(bf16[8,576,128]{2,1,0:T(8,128)(2,1)} %refs_4_.2), channel_id=1, source_target_pairs={{32,0},{64,32},{96,64},{0,96},{33,1},{65,33},{97,65},{1,97},{34,2}... | collective-permute-start | bytes 3538952 | tf_op jit(solution)/shard_map/ppermute | solution.py:547
  5.6 1.2 collective-permute-done.1.other
  8.0 2.8 %collective-permute-start.4 = (bf16[1,576,128]{2,1,0:T(8,128)(2,1)S(1)}, bf16[1,576,128]{2,1,0:T(8,128)(2,1)S(1)}, u32[]{:S(2)}, u32[]{:S(2)}) collective-permute-start(bf16[1,576,128]{2,1,0:T(8,128)(2,1)S(1)} %turn.1.refs_0_), channel_id=1, source_target_pairs={{0,6},{1,25},{2,0},{3,27},{4,2},{5,29},{6,4},{7,31},{8,14},{9,1},{... | collective-permute-start | bytes 442376 | tf_op jit(solution)/shard_map/ppermute | solution.py:542
  11.8 2.6 %collective-permute-done.4.refs_3_ = bf16[1,576,128]{2,1,0:T(8,128)(2,1)S(1)} collective-permute-done((bf16[1,576,128]{2,1,0:T(8,128)(2,1)S(1)}, bf16[1,576,128]{2,1,0:T(8,128)(2,1)S(1)}, u32[]{:S(2)}, u32[]{:S(2)}) %collective-permute-start.4) | collective-permute-done | bytes 147488 | tf_op jit(solution)/shard_map/ppermute | solution.py:542
  14.5 2.1 %collective-permute-done.3.refs_2_ = bf16[1,576,128]{2,1,0:T(8,128)(2,1)S(1)} collective-permute-done((bf16[1,576,128]{2,1,0:T(8,128)(2,1)S(1)}, bf16[1,576,128]{2,1,0:T(8,128)(2,1)S(1)}, u32[]{:S(2)}, u32[]{:S(2)}) %collective-permute-start.3) | collective-permute-done | bytes 147488 | tf_op jit(solution)/shard_map/ppermute | solution.py:542
  16.6 1.6 %collective-permute-done.2.refs_1_ = bf16[1,576,128]{2,1,0:T(8,128)(2,1)S(1)} collective-permute-done((bf16[1,576,128]{2,1,0:T(8,128)(2,1)S(1)}, bf16[1,576,128]{2,1,0:T(8,128)(2,1)S(1)}, u32[]{:S(2)}, u32[]{:S(2)}) %collective-permute-start.2) | collective-permute-done | bytes 147488 | tf_op jit(solution)/shard_map/ppermute | solution.py:542
  19.0 2.5 %collective-permute-start.7 = (bf16[4,576,128]{2,1,0:T(8,128)(2,1)S(1)}, bf16[4,576,128]{2,1,0:T(8,128)(2,1)S(1)}, u32[]{:S(2)}, u32[]{:S(2)}) collective-permute-start(bf16[4,576,128]{2,1,0:T(8,128)(2,1)S(1)} %join.1.refs_0_), channel_id=1, source_target_pairs={{0,24},{1,7},{2,26},{3,1},{4,28},{5,3},{6,30},{7,5},{8,0},{9,15},{... | collective-permute-start | bytes 1769480 | tf_op jit(solution)/shard_map/ppermute | solution.py:542
  22.7 7.8 %collective-permute-done.9.previous.refs_8_ = bf16[8,576,128]{2,1,0:T(8,128)(2,1)S(1)} collective-permute-done((bf16[8,576,128]{2,1,0:T(8,128)(2,1)}, bf16[8,576,128]{2,1,0:T(8,128)(2,1)S(1)}, u32[]{:S(2)}, u32[]{:S(2)}) %collective-permute-start.9) | collective-permute-done | bytes 1179680 | tf_op jit(solution)/shard_map/ppermute | solution.py:548
  30.5 1.2 collective-permute-start
  31.7 1.3 split.1
  33.0 1.5 %collective-permute-start.10 = (bf16[4,576,128]{2,1,0:T(8,128)(2,1)}, bf16[4,576,128]{2,1,0:T(8,128)(2,1)}, u32[]{:S(2)}, u32[]{:S(2)}) collective-permute-start(bf16[4,576,128]{2,1,0:T(8,128)(2,1)} %get-tuple-element.27), channel_id=1, source_target_pairs={{32,0},{64,32},{96,64},{0,96},{33,1},{65,33},{97,65},{1,97},{34,2}... | collective-permute-start | bytes 1769480 | tf_op jit(solution)/shard_map/ppermute | solution.py:552
  34.7 2.4 %collective-permute-start.12 = (bf16[8,576,128]{2,1,0:T(8,128)(2,1)}, bf16[8,576,128]{2,1,0:T(8,128)(2,1)}, u32[]{:S(2)}, u32[]{:S(2)}) collective-permute-start(bf16[8,576,128]{2,1,0:T(8,128)(2,1)} %refs_4_.2), channel_id=1, source_target_pairs={{0,1},{1,0},{2,3},{3,2},{4,5},{5,4},{6,7},{7,6},{8,9},{9,8},{10,11... | collective-permute-start | bytes 3538952 | tf_op jit(solution)/shard_map/ppermute | solution.py:539
  37.1 1.3 collective-permute-done.5.refs_1_
  38.4 2.6 %collective-permute-start.13 = (bf16[8,576,128]{2,1,0:T(8,128)(2,1)S(1)}, bf16[8,576,128]{2,1,0:T(8,128)(2,1)S(1)}, u32[]{:S(2)}, u32[]{:S(2)}) collective-permute-start(bf16[8,576,128]{2,1,0:T(8,128)(2,1)S(1)} %collective-permute-done.8.following.refs_5_), channel_id=1, source_target_pairs={{0,1},{1,0},{2,3},{3,2},{4,5},{5,4},{6,7},{7,6},{8,9},{9,8},{10,11... | collective-permute-start | bytes 3538952 | tf_op jit(solution)/shard_map/ppermute | solution.py:539
  41.0 7.3 %collective-permute-done.10.refs_6_ = bf16[4,576,128]{2,1,0:T(8,128)(2,1)} collective-permute-done((bf16[4,576,128]{2,1,0:T(8,128)(2,1)}, bf16[4,576,128]{2,1,0:T(8,128)(2,1)}, u32[]{:S(2)}, u32[]{:S(2)}) %collective-permute-start.10) | collective-permute-done | bytes 589856 | tf_op jit(solution)/shard_map/ppermute | solution.py:552
  49.3 2.5 %collective-permute-start.15 = (bf16[4,576,128]{2,1,0:T(8,128)(2,1)}, bf16[4,576,128]{2,1,0:T(8,128)(2,1)S(1)}, u32[]{:S(2)}, u32[]{:S(2)}) collective-permute-start(bf16[4,576,128]{2,1,0:T(8,128)(2,1)} %collective-permute-done.11.refs_7_), channel_id=1, source_target_pairs={{0,1},{1,0},{2,3},{3,2},{4,5},{5,4},{6,7},{7,6},{8,9},{9,8},{10,11... | collective-permute-start | bytes 1769480 | tf_op jit(solution)/shard_map/ppermute | solution.py:539
  53.7 9.5 %attend.1 = (bf16[4,528,128]{2,1,0:T(8,128)(2,1)S(1)}, bf16[4,528,128]{2,1,0:T(8,128)(2,1)S(1)}, bf16[4,528,128]{2,1,0:T(8,128)(2,1)S(1)}, bf16[4,528,128]{2,1,0:T(8,128)(2,1)S(1)}) custom-call(s32[1,128]{1,0:T(1,128)S(1)} %add_bitcast_fusion.code_own, s32[1,128]{1,0:T(1,128)S(1)} %collective-permute-done.code_other, s32[1,128]{1,0:T(1,128)S(1)} %bitcast.17, ...), custom_call_target="tpu_custom_call" | custom-call | tf_op jit(solution)/shard_map/attend/pallas_call | solution.py:282
  63.2 1.4 collective-permute-start.17
  64.6 2.6 %collective-permute-start.18 = (bf16[4,528,128]{2,1,0:T(8,128)(2,1)S(1)}, bf16[4,528,128]{2,1,0:T(8,128)(2,1)S(1)}, u32[]{:S(2)}, u32[]{:S(2)}) collective-permute-start(bf16[4,528,128]{2,1,0:T(8,128)(2,1)S(1)} %get-tuple-element.31), channel_id=1, source_target_pairs={{0,4},{1,17},{2,6},{3,19},{4,0},{5,21},{6,2},{7,23},{8,12},{9,25},... | collective-permute-start | bytes 1622024 | tf_op jit(solution)/shard_map/ppermute | solution.py:542
  67.2 1.1 collective-permute-start.19
  68.2 4.8 %collective-permute-done.17.refs_1_ = bf16[4,528,128]{2,1,0:T(8,128)(2,1)S(1)} collective-permute-done((bf16[4,528,128]{2,1,0:T(8,128)(2,1)S(1)}, bf16[4,528,128]{2,1,0:T(8,128)(2,1)S(1)}, u32[]{:S(2)}, u32[]{:S(2)}) %collective-permute-start.17) | collective-permute-done | bytes 540704 | tf_op jit(solution)/shard_map/ppermute | solution.py:542
  73.0 7.0 %collective-permute-done.18.refs_2_ = bf16[4,528,128]{2,1,0:T(8,128)(2,1)S(1)} collective-permute-done((bf16[4,528,128]{2,1,0:T(8,128)(2,1)S(1)}, bf16[4,528,128]{2,1,0:T(8,128)(2,1)S(1)}, u32[]{:S(2)}, u32[]{:S(2)}) %collective-permute-start.18) | collective-permute-done | bytes 540704 | tf_op jit(solution)/shard_map/ppermute | solution.py:542
  80.0 1.0 merge.1
  82.0 2.5 %collective-permute-start.21 = (bf16[528,128]{1,0:T(8,128)(2,1)S(1)}, bf16[528,128]{1,0:T(8,128)(2,1)S(1)}, u32[]{:S(2)}, u32[]{:S(2)}) collective-permute-start(bf16[528,128]{1,0:T(8,128)(2,1)S(1)} %get-tuple-element.35), channel_id=1, source_target_pairs={{0,16},{1,5},{2,18},{3,7},{4,20},{5,1},{6,22},{7,3},{8,24},{9,13},... | collective-permute-start | bytes 405512 | tf_op jit(solution)/shard_map/ppermute | solution.py:542
  84.5 1.1 collective-permute-start.22
  86.5 1.9 %collective-permute-done.21.refs_2_ = bf16[528,128]{1,0:T(8,128)(2,1)S(1)} collective-permute-done((bf16[528,128]{1,0:T(8,128)(2,1)S(1)}, bf16[528,128]{1,0:T(8,128)(2,1)S(1)}, u32[]{:S(2)}, u32[]{:S(2)}) %collective-permute-start.21) | collective-permute-done | bytes 135200 | tf_op jit(solution)/shard_map/ppermute | solution.py:542
  88.4 2.1 %project.1 = bf16[32,56,128]{2,1,0:T(8,128)(2,1)S(1)} custom-call(bf16[528,128]{1,0:T(8,128)(2,1)S(1)} %get-tuple-element.33.refs_0_, bf16[528,128]{1,0:T(8,128)(2,1)S(1)} %collective-permute-done.20.refs_1_, bf16[528,128]{1,0:T(8,128)(2,1)S(1)} %collective-permute-done.21.refs_2_, bf16[528,128]{1,0:T(8,128)(2,1)S(1)} %collective-permute-done.22.refs_3_, ...), custom_call_target="tpu_custom_call" | custom-call | tf_op jit(solution)/shard_map/project/pallas_call | solution.py:438
  90.5 20.5 %all_to_all.15.got = bf16[32,56,128]{2,1,0:T(8,128)(2,1)S(1)} all-to-all(bf16[32,56,128]{2,1,0:T(8,128)(2,1)S(1)} %project.1), channel_id=1, replica_groups=mesh['dp'=4,'tensor'=32] {'tensor'}, dimensions={0} | all-to-all | bytes 917504 | tf_op jit(solution)/shard_map/all_to_all | solution.py:585
  111.3 14.5 %all_to_all.16.normed = bf16[32,56,128]{2,1,0:T(8,128)(2,1)S(1)} all-to-all(bf16[32,56,128]{2,1,0:T(8,128)(2,1)S(1)} %get-tuple-element.40), channel_id=1, replica_groups=mesh['dp'=4,'tensor'=32] {'tensor'}, dimensions={0} | all-to-all | bytes 917504 | tf_op jit(solution)/shard_map/all_to_all | solution.py:585
  125.9 2.9 %ffn.1 = bf16[32,56,128]{2,1,0:T(8,128)(2,1)S(1)} custom-call(bf16[32,56,128]{2,1,0:T(8,128)(2,1)S(1)} %all_to_all.16.normed, bf16[7168,384]{1,0:T(8,128)(2,1)S(1)} %bitcast.10, bf16[7168,384]{1,0:T(8,128)(2,1)S(1)} %bitcast.12, bf16[384,7168]{1,0:T(8,128)(2,1)S(1)} %copy-done), custom_call_target="tpu_custom_call" | custom-call | tf_op jit(solution)/shard_map/ffn/pallas_call | solution.py:497
  128.8 14.5 %all_to_all.17 = bf16[32,56,128]{2,1,0:T(8,128)(2,1)S(1)} all-to-all(bf16[32,56,128]{2,1,0:T(8,128)(2,1)S(1)} %ffn.1), channel_id=1, replica_groups=mesh['dp'=4,'tensor'=32] {'tensor'}, dimensions={0} | all-to-all | bytes 917504 | tf_op jit(solution)/shard_map/all_to_all | solution.py:585
  (66 shorter events, 11.0 us)
Async XLA Ops:
  0.0 30.5 %collective-permute-start.9 = (bf16[8,576,128]{2,1,0:T(8,128)(2,1)}, bf16[8,576,128]{2,1,0:T(8,128)(2,1)S(1)}, u32[]{:S(2)}, u32[]{:S(2)}) collective-permute-start(bf16[8,576,128]{2,1,0:T(8,128)(2,1)} %refs_4_.2), channel_id=1, source_target_pairs={{96,0},{0,32},{32,64},{64,96},{97,1},{1,33},{33,65},{65,97},{98,2}... | collective-permute-start | bytes 3538952 | tf_op jit(solution)/shard_map/ppermute | solution.py:548
  2.5 29.3 %collective-permute-start.8 = (bf16[8,576,128]{2,1,0:T(8,128)(2,1)}, bf16[8,576,128]{2,1,0:T(8,128)(2,1)S(1)}, u32[]{:S(2)}, u32[]{:S(2)}) collective-permute-start(bf16[8,576,128]{2,1,0:T(8,128)(2,1)} %refs_4_.2), channel_id=1, source_target_pairs={{32,0},{64,32},{96,64},{0,96},{33,1},{65,33},{97,65},{1,97},{34,2}... | collective-permute-start | bytes 3538952 | tf_op jit(solution)/shard_map/ppermute | solution.py:547
  4.7 2.2 %collective-permute-start.1 = (bf16[576,128]{1,0:T(8,128)(2,1)}, bf16[576,128]{1,0:T(8,128)(2,1)S(1)}, u32[]{:S(2)}, u32[]{:S(2)}) collective-permute-start(bf16[576,128]{1,0:T(8,128)(2,1)} %bitcast.13), channel_id=1, source_target_pairs={{0,1},{1,0},{2,3},{3,2},{4,5},{5,4},{6,7},{7,6},{8,9},{9,8},{10,11... | collective-permute-start | bytes 442376 | tf_op jit(solution)/shard_map/ppermute | solution.py:539
  8.0 6.4 %collective-permute-start.4 = (bf16[1,576,128]{2,1,0:T(8,128)(2,1)S(1)}, bf16[1,576,128]{2,1,0:T(8,128)(2,1)S(1)}, u32[]{:S(2)}, u32[]{:S(2)}) collective-permute-start(bf16[1,576,128]{2,1,0:T(8,128)(2,1)S(1)} %turn.1.refs_0_), channel_id=1, source_target_pairs={{0,6},{1,25},{2,0},{3,27},{4,2},{5,29},{6,4},{7,31},{8,14},{9,1},{... | collective-permute-start | bytes 442376 | tf_op jit(solution)/shard_map/ppermute | solution.py:542
  10.8 5.8 %collective-permute-start.3 = (bf16[1,576,128]{2,1,0:T(8,128)(2,1)S(1)}, bf16[1,576,128]{2,1,0:T(8,128)(2,1)S(1)}, u32[]{:S(2)}, u32[]{:S(2)}) collective-permute-start(bf16[1,576,128]{2,1,0:T(8,128)(2,1)S(1)} %turn.1.refs_0_), channel_id=1, source_target_pairs={{0,4},{1,17},{2,6},{3,19},{4,0},{5,21},{6,2},{7,23},{8,12},{9,25},... | collective-permute-start | bytes 442376 | tf_op jit(solution)/shard_map/ppermute | solution.py:542
  11.1 7.0 %collective-permute-start.2 = (bf16[1,576,128]{2,1,0:T(8,128)(2,1)S(1)}, bf16[1,576,128]{2,1,0:T(8,128)(2,1)S(1)}, u32[]{:S(2)}, u32[]{:S(2)}) collective-permute-start(bf16[1,576,128]{2,1,0:T(8,128)(2,1)S(1)} %turn.1.refs_0_), channel_id=1, source_target_pairs={{0,2},{1,9},{2,4},{3,11},{4,6},{5,13},{6,0},{7,15},{8,10},{9,17},{... | collective-permute-start | bytes 442376 | tf_op jit(solution)/shard_map/ppermute | solution.py:542
  19.0 15.7 %collective-permute-start.7 = (bf16[4,576,128]{2,1,0:T(8,128)(2,1)S(1)}, bf16[4,576,128]{2,1,0:T(8,128)(2,1)S(1)}, u32[]{:S(2)}, u32[]{:S(2)}) collective-permute-start(bf16[4,576,128]{2,1,0:T(8,128)(2,1)S(1)} %join.1.refs_0_), channel_id=1, source_target_pairs={{0,24},{1,7},{2,26},{3,1},{4,28},{5,3},{6,30},{7,5},{8,0},{9,15},{... | collective-permute-start | bytes 1769480 | tf_op jit(solution)/shard_map/ppermute | solution.py:542
  21.5 15.5 %collective-permute-start.6 = (bf16[4,576,128]{2,1,0:T(8,128)(2,1)S(1)}, bf16[4,576,128]{2,1,0:T(8,128)(2,1)S(1)}, u32[]{:S(2)}, u32[]{:S(2)}) collective-permute-start(bf16[4,576,128]{2,1,0:T(8,128)(2,1)S(1)} %join.1.refs_0_), channel_id=1, source_target_pairs={{0,16},{1,5},{2,18},{3,7},{4,20},{5,1},{6,22},{7,3},{8,24},{9,13},... | collective-permute-start | bytes 1769480 | tf_op jit(solution)/shard_map/ppermute | solution.py:542
  22.0 16.3 %collective-permute-start.5 = (bf16[4,576,128]{2,1,0:T(8,128)(2,1)S(1)}, bf16[4,576,128]{2,1,0:T(8,128)(2,1)S(1)}, u32[]{:S(2)}, u32[]{:S(2)}) collective-permute-start(bf16[4,576,128]{2,1,0:T(8,128)(2,1)S(1)} %join.1.refs_0_), channel_id=1, source_target_pairs={{0,8},{1,3},{2,10},{3,5},{4,12},{5,7},{6,14},{7,1},{8,16},{9,11},{... | collective-permute-start | bytes 1769480 | tf_op jit(solution)/shard_map/ppermute | solution.py:542
  22.6 31.0 %copy-start.5 = (s32[128]{0:T(128)S(1)}, s32[128]{0:T(128)}, u32[]{:S(2)}) copy-start(s32[128]{0:T(128)} %param.16) | copy-start | bytes 1540
  30.5 4.0 %collective-permute-start = (s32[1,128]{1,0:T(1,128)S(1)}, s32[1,128]{1,0:T(1,128)S(1)}, u32[]{:S(2)}, u32[]{:S(2)}) collective-permute-start(s32[1,128]{1,0:T(1,128)S(1)} %add_bitcast_fusion.code_own), channel_id=1, source_target_pairs={{0,1},{1,0},{2,3},{3,2},{4,5},{5,4},{6,7},{7,6},{8,9},{9,8},{10,11... | collective-permute-start | bytes 1544 | tf_op jit(solution)/shard_map/ppermute | solution.py:539
  33.0 15.3 %collective-permute-start.10 = (bf16[4,576,128]{2,1,0:T(8,128)(2,1)}, bf16[4,576,128]{2,1,0:T(8,128)(2,1)}, u32[]{:S(2)}, u32[]{:S(2)}) collective-permute-start(bf16[4,576,128]{2,1,0:T(8,128)(2,1)} %get-tuple-element.27), channel_id=1, source_target_pairs={{32,0},{64,32},{96,64},{0,96},{33,1},{65,33},{97,65},{1,97},{34,2}... | collective-permute-start | bytes 1769480 | tf_op jit(solution)/shard_map/ppermute | solution.py:552
  34.5 14.8 %collective-permute-start.11 = (bf16[4,576,128]{2,1,0:T(8,128)(2,1)}, bf16[4,576,128]{2,1,0:T(8,128)(2,1)}, u32[]{:S(2)}, u32[]{:S(2)}) collective-permute-start(bf16[4,576,128]{2,1,0:T(8,128)(2,1)} %get-tuple-element.28), channel_id=1, source_target_pairs={{96,0},{0,32},{32,64},{64,96},{97,1},{1,33},{33,65},{65,97},{98,2}... | collective-permute-start | bytes 1769480 | tf_op jit(solution)/shard_map/ppermute | solution.py:553
  34.7 18.1 %collective-permute-start.12 = (bf16[8,576,128]{2,1,0:T(8,128)(2,1)}, bf16[8,576,128]{2,1,0:T(8,128)(2,1)}, u32[]{:S(2)}, u32[]{:S(2)}) collective-permute-start(bf16[8,576,128]{2,1,0:T(8,128)(2,1)} %refs_4_.2), channel_id=1, source_target_pairs={{0,1},{1,0},{2,3},{3,2},{4,5},{5,4},{6,7},{7,6},{8,9},{9,8},{10,11... | collective-permute-start | bytes 3538952 | tf_op jit(solution)/shard_map/ppermute | solution.py:539
  37.0 15.7 %collective-permute-start.16 = (bf16[8,576,128]{2,1,0:T(8,128)(2,1)S(1)}, bf16[8,576,128]{2,1,0:T(8,128)(2,1)}, u32[]{:S(2)}, u32[]{:S(2)}) collective-permute-start(bf16[8,576,128]{2,1,0:T(8,128)(2,1)S(1)} %collective-permute-done.9.previous.refs_8_), channel_id=1, source_target_pairs={{0,1},{1,0},{2,3},{3,2},{4,5},{5,4},{6,7},{7,6},{8,9},{9,8},{10,11... | collective-permute-start | bytes 3538952 | tf_op jit(solution)/shard_map/ppermute | solution.py:539
  38.4 15.3 %collective-permute-start.13 = (bf16[8,576,128]{2,1,0:T(8,128)(2,1)S(1)}, bf16[8,576,128]{2,1,0:T(8,128)(2,1)S(1)}, u32[]{:S(2)}, u32[]{:S(2)}) collective-permute-start(bf16[8,576,128]{2,1,0:T(8,128)(2,1)S(1)} %collective-permute-done.8.following.refs_5_), channel_id=1, source_target_pairs={{0,1},{1,0},{2,3},{3,2},{4,5},{5,4},{6,7},{7,6},{8,9},{9,8},{10,11... | collective-permute-start | bytes 3538952 | tf_op jit(solution)/shard_map/ppermute | solution.py:539
  48.4 4.4 %collective-permute-start.14 = (bf16[4,576,128]{2,1,0:T(8,128)(2,1)}, bf16[4,576,128]{2,1,0:T(8,128)(2,1)S(1)}, u32[]{:S(2)}, u32[]{:S(2)}) collective-permute-start(bf16[4,576,128]{2,1,0:T(8,128)(2,1)} %collective-permute-done.10.refs_6_), channel_id=1, source_target_pairs={{0,1},{1,0},{2,3},{3,2},{4,5},{5,4},{6,7},{7,6},{8,9},{9,8},{10,11... | collective-permute-start | bytes 1769480 | tf_op jit(solution)/shard_map/ppermute | solution.py:539
  49.3 4.3 %collective-permute-start.15 = (bf16[4,576,128]{2,1,0:T(8,128)(2,1)}, bf16[4,576,128]{2,1,0:T(8,128)(2,1)S(1)}, u32[]{:S(2)}, u32[]{:S(2)}) collective-permute-start(bf16[4,576,128]{2,1,0:T(8,128)(2,1)} %collective-permute-done.11.refs_7_), channel_id=1, source_target_pairs={{0,1},{1,0},{2,3},{3,2},{4,5},{5,4},{6,7},{7,6},{8,9},{9,8},{10,11... | collective-permute-start | bytes 1769480 | tf_op jit(solution)/shard_map/ppermute | solution.py:539
  53.7 34.7 %slice-start = ((s8[7340032]{0:T(1024)(128)(4,1)}), s8[4194304]{0:T(1024)(128)(4,1)S(1)}, s32[]{:S(2)}) async-start(s8[7340032]{0:T(1024)(128)(4,1)} %bitcast.7), calls=%async_computation.3 | async-start | bytes 8388608
  53.7 34.7 %slice-start.1 = ((s8[7340032]{0:T(1024)(128)(4,1)}), s8[3145728]{0:T(1024)(128)(4,1)S(1)}, s32[]{:S(2)}) async-start(s8[7340032]{0:T(1024)(128)(4,1)} %bitcast.7), calls=%async_computation.4 | async-start | bytes 6291456
  53.7 72.2 %slice-start.4 = ((s8[5505024]{0:T(1024)(128)(4,1)}), s8[4194304]{0:T(1024)(128)(4,1)S(1)}, s32[]{:S(2)}) async-start(s8[5505024]{0:T(1024)(128)(4,1)} %bitcast.11), calls=%async_computation.7 | async-start | bytes 8388608
  63.2 9.8 %collective-permute-start.17 = (bf16[4,528,128]{2,1,0:T(8,128)(2,1)S(1)}, bf16[4,528,128]{2,1,0:T(8,128)(2,1)S(1)}, u32[]{:S(2)}, u32[]{:S(2)}) collective-permute-start(bf16[4,528,128]{2,1,0:T(8,128)(2,1)S(1)} %get-tuple-element.30), channel_id=1, source_target_pairs={{0,2},{1,9},{2,4},{3,11},{4,6},{5,13},{6,0},{7,15},{8,10},{9,17},{... | collective-permute-start | bytes 1622024 | tf_op jit(solution)/shard_map/ppermute | solution.py:542
  64.6 15.4 %collective-permute-start.18 = (bf16[4,528,128]{2,1,0:T(8,128)(2,1)S(1)}, bf16[4,528,128]{2,1,0:T(8,128)(2,1)S(1)}, u32[]{:S(2)}, u32[]{:S(2)}) collective-permute-start(bf16[4,528,128]{2,1,0:T(8,128)(2,1)S(1)} %get-tuple-element.31), channel_id=1, source_target_pairs={{0,4},{1,17},{2,6},{3,19},{4,0},{5,21},{6,2},{7,23},{8,12},{9,25},... | collective-permute-start | bytes 1622024 | tf_op jit(solution)/shard_map/ppermute | solution.py:542
  67.2 12.8 %collective-permute-start.19 = (bf16[4,528,128]{2,1,0:T(8,128)(2,1)S(1)}, bf16[4,528,128]{2,1,0:T(8,128)(2,1)S(1)}, u32[]{:S(2)}, u32[]{:S(2)}) collective-permute-start(bf16[4,528,128]{2,1,0:T(8,128)(2,1)S(1)} %get-tuple-element.32), channel_id=1, source_target_pairs={{0,6},{1,25},{2,0},{3,27},{4,2},{5,29},{6,4},{7,31},{8,14},{9,1},{... | collective-permute-start | bytes 1622024 | tf_op jit(solution)/shard_map/ppermute | solution.py:542
  80.0 31.0 %copy-start.4 = (f32[7168]{0:T(1024)S(1)}, f32[7168]{0:T(1024)}, u32[]{:S(2)}) copy-start(f32[7168]{0:T(1024)} %param.20) | copy-start | bytes 86020
  80.0 45.8 %slice-start.5 = ((s8[5505024]{0:T(1024)(128)(4,1)}), s8[1310720]{0:T(1024)(128)(4,1)S(1)}, s32[]{:S(2)}) async-start(s8[5505024]{0:T(1024)(128)(4,1)} %bitcast.11), calls=%async_computation.8 | async-start | bytes 2621440
  81.0 5.4 %collective-permute-start.20 = (bf16[528,128]{1,0:T(8,128)(2,1)S(1)}, bf16[528,128]{1,0:T(8,128)(2,1)S(1)}, u32[]{:S(2)}, u32[]{:S(2)}) collective-permute-start(bf16[528,128]{1,0:T(8,128)(2,1)S(1)} %get-tuple-element.34), channel_id=1, source_target_pairs={{0,8},{1,3},{2,10},{3,5},{4,12},{5,7},{6,14},{7,1},{8,16},{9,11},{... | collective-permute-start | bytes 405512 | tf_op jit(solution)/shard_map/ppermute | solution.py:542
  82.0 6.3 %collective-permute-start.21 = (bf16[528,128]{1,0:T(8,128)(2,1)S(1)}, bf16[528,128]{1,0:T(8,128)(2,1)S(1)}, u32[]{:S(2)}, u32[]{:S(2)}) collective-permute-start(bf16[528,128]{1,0:T(8,128)(2,1)S(1)} %get-tuple-element.35), channel_id=1, source_target_pairs={{0,16},{1,5},{2,18},{3,7},{4,20},{5,1},{6,22},{7,3},{8,24},{9,13},... | collective-permute-start | bytes 405512 | tf_op jit(solution)/shard_map/ppermute | solution.py:542
  84.5 3.9 %collective-permute-start.22 = (bf16[528,128]{1,0:T(8,128)(2,1)S(1)}, bf16[528,128]{1,0:T(8,128)(2,1)S(1)}, u32[]{:S(2)}, u32[]{:S(2)}) collective-permute-start(bf16[528,128]{1,0:T(8,128)(2,1)S(1)} %get-tuple-element.36), channel_id=1, source_target_pairs={{0,24},{1,7},{2,26},{3,1},{4,28},{5,3},{6,30},{7,5},{8,0},{9,15},{... | collective-permute-start | bytes 405512 | tf_op jit(solution)/shard_map/ppermute | solution.py:542
  88.3 37.5 %slice-start.2 = ((s8[5505024]{0:T(1024)(128)(4,1)}), s8[4194304]{0:T(1024)(128)(4,1)S(1)}, s32[]{:S(2)}) async-start(s8[5505024]{0:T(1024)(128)(4,1)} %bitcast.9), calls=%async_computation.5 | async-start | bytes 8388608
  88.4 37.5 %slice-start.3 = ((s8[5505024]{0:T(1024)(128)(4,1)}), s8[1310720]{0:T(1024)(128)(4,1)S(1)}, s32[]{:S(2)}) async-start(s8[5505024]{0:T(1024)(128)(4,1)} %bitcast.9), calls=%async_computation.6 | async-start | bytes 2621440
  88.4 37.5 %copy-start = (bf16[384,7168]{1,0:T(8,128)(2,1)S(1)}, bf16[384,7168]{1,0:T(8,128)(2,1)}, u32[]{:S(2)}) copy-start(bf16[384,7168]{1,0:T(8,128)(2,1)} %w_down.1) | copy-start | bytes 16515076
  (8 other events, 91.8 us)

commit v6 on v5

--- a/solution.py
+++ b/solution.py
@@ -393,7 +393,7 @@
 def project_kernel(dims, *refs):
     group, head_local, latent, chunk = dims
     parts = refs[:SIDE]
-    w_value, w_out, sent, att_buf, flat = refs[SIDE:]
+    w_value, w_out, kept, passed, att_buf, flat = refs[SIDE:]
     rows = group * head_local
     pieces = latent // LANES
     tiles = w_out.shape[1] // LANES
@@ -423,11 +423,11 @@
         )
         scatter_tiles(flat, value, c * chunk // LANES, group, tiles)
     core = lax.axis_index("tensor") % CORES
-    for i in range(group):
-        pair, side = i // CORES, i % CORES
-        second, place = pair // SIDE, pair % SIDE
-        r = jnp.where(core == 0, pair, place * SIDE + second) * CORES + side
-        sent[r] = flat[i * tiles : (i + 1) * tiles, :].astype(jnp.bfloat16)
+    for chip in range(SIDE * SIDE):
+        pair = jnp.where(core == 0, chip, chip % SIDE * SIDE + chip // SIDE)
+        for out, side in ((kept, core), (passed, 1 - core)):
+            at = pl.multiple_of((pair * CORES + side) * tiles, 8)
+            out[chip] = flat[pl.ds(at, tiles), :].astype(jnp.bfloat16)
 
 
 def project(parts, w_value, w_out, group):
@@ -437,9 +437,9 @@
     dims = (group, head_local, latent, features // 7)
     return pl.pallas_call(
         functools.partial(project_kernel, dims),
-        out_shape=pltpu.VMEM((group, tiles, LANES), jnp.bfloat16),
+        out_shape=(pltpu.VMEM((group // CORES, tiles, LANES), jnp.bfloat16),) * CORES,
         in_specs=[vmem_spec] * (SIDE + 2),
-        out_specs=vmem_spec,
+        out_specs=(vmem_spec,) * CORES,
         scratch_shapes=[
             pltpu.VMEM((latent // LANES, group * head_local, LANES), jnp.float32),
             pltpu.VMEM((group * tiles, LANES), jnp.float32),
@@ -447,6 +447,22 @@
         compiler_params=pltpu.CompilerParams(vmem_limit_bytes=12 * MIB),
         name="project",
     )(*[in_vmem(one) for one in parts], w_value, w_out)
+
+
+def add_kernel(one, other, out):
+    for s in range(out.shape[0]):
+        out[s] = (one[s].astype(jnp.float32) + other[s].astype(jnp.float32)).astype(out.dtype)
+
+
+def add(one, other):
+    return pl.pallas_call(
+        add_kernel,
+        out_shape=pltpu.VMEM(one.shape, one.dtype),
+        in_specs=[vmem_spec] * 2,
+        out_specs=vmem_spec,
+        compiler_params=pltpu.CompilerParams(vmem_limit_bytes=4 * MIB),
+        name="add",
+    )(in_vmem(one), in_vmem(other))
 
 
 def norm_kernel(got, residual, gain, kept, normed):
@@ -471,10 +487,15 @@
     )(in_vmem(got), in_vmem(residual), in_vmem(gain))
 
 
-def ffn_kernel(chunk, normed, w_gate, w_up, w_down, sent, flat, wide):
-    group, tiles, _ = normed.shape
-    for r in range(group):
-        flat[r * tiles : (r + 1) * tiles, :] = normed[r].astype(jnp.float32)
+def ffn_kernel(chunk, *refs):
+    normed, (w_gate, w_up, w_down) = refs[:CORES], refs[CORES : CORES + 3]
+    outs, (flat, wide) = refs[CORES + 3 : 2 * CORES + 3], refs[2 * CORES + 3 :]
+    half, tiles, _ = normed[0].shape
+    group = CORES * half
+    for c in range(CORES):
+        for r in range(half):
+            at = (c * half + r) * tiles
+            flat[at : at + tiles, :] = normed[c][r].astype(jnp.float32)
     for n in range(tiles):
         wide[:, n * LANES : (n + 1) * LANES] = flat[pl.ds(n, group, stride=tiles), :].astype(
             jnp.bfloat16
@@ -487,25 +508,27 @@
             activated, w_down[:, c * chunk : (c + 1) * chunk], preferred_element_type=jnp.float32
         )
         scatter_tiles(flat, value, c * chunk // LANES, group, tiles)
-    for r in range(group):
-        sent[r] = flat[r * tiles : (r + 1) * tiles, :].astype(jnp.bfloat16)
+    for c in range(CORES):
+        for r in range(half):
+            at = (c * half + r) * tiles
+            outs[c][r] = flat[at : at + tiles, :].astype(jnp.bfloat16)
 
 
 def ffn(normed, w_gate, w_up, w_down):
-    group, tiles, _ = normed.shape
-    features = tiles * LANES
+    half, tiles, _ = normed[0].shape
+    group, features = CORES * half, tiles * LANES
     return pl.pallas_call(
         functools.partial(ffn_kernel, features // 7),
-        out_shape=pltpu.VMEM(normed.shape, jnp.bfloat16),
-        in_specs=[vmem_spec] * 4,
-        out_specs=vmem_spec,
+        out_shape=(pltpu.VMEM(normed[0].shape, jnp.bfloat16),) * CORES,
+        in_specs=[vmem_spec] * (CORES + 3),
+        out_specs=(vmem_spec,) * CORES,
         scratch_shapes=[
             pltpu.VMEM((group * tiles, LANES), jnp.float32),
             pltpu.VMEM((group, features), jnp.bfloat16),
         ],
         compiler_params=pltpu.CompilerParams(vmem_limit_bytes=12 * MIB),
         name="ffn",
-    )(in_vmem(normed), w_gate, w_up, w_down)
+    )(*[in_vmem(one) for one in normed], w_gate, w_up, w_down)
 
 
 def body(
@@ -581,11 +604,22 @@
     merged = merge(arrived, group, head_local, latent)
     parts = [merged[0]] + [along(merged[e], False, e) for e in range(1, SIDE)]
 
+    chips = SIDE * SIDE
+    same_core = [[c + CORES * k for k in range(chips)] for c in range(CORES)]
+
     def exchange(value):
-        return lax.all_to_all(value, "tensor", split_axis=0, concat_axis=0, tiled=True)
-
-    residual_sum, normed = norm(exchange(project(parts, w_value, w_out, group)), own_residual, gain)
-    down = exchange(ffn(exchange(normed), w_gate, w_up, w_down))
+        return lax.all_to_all(
+            value, "tensor", split_axis=0, concat_axis=0, tiled=True, axis_index_groups=same_core
+        )
+
+    def to_rows(kept, passed):
+        return exchange(add(kept, swapped(passed)))
+
+    residual_sum, normed = norm(
+        to_rows(*project(parts, w_value, w_out, group)), own_residual, gain
+    )
+    rows = exchange(normed)
+    down = to_rows(*ffn((rows, swapped(rows)), w_gate, w_up, w_down))
     return (residual_sum + jnp.sum(down.astype(jnp.float32), axis=0)).reshape(1, features)
 
 

time: 144 us -> 141 us (0.979)
  blocking collectives: 49.6 us -> 34 us
  starting transfers between devices: 33.8 us -> 40.4 us
  waiting for transfers between devices: 39.7 us -> 43.5 us
  Pallas kernels: 18.1 us -> 19.7 us
    all_to_all x3, blocking collectives: 49.6 us -> 34 us  [exchange(): lax.all_to_all(value, 'tensor', split_axis=0, concat_axis=0, tiled=True,...]
    ppermute x7 -> x10, starting transfers between devices: 10.5 us -> 17 us  [swapped(): return lax.ppermute(value, 'tensor', swap)]
    ppermute x7 -> x10, waiting for transfers between devices: 2.12 us -> 5.46 us  [swapped(): return lax.ppermute(value, 'tensor', swap)]
    pallas_call x2 -> x4, Pallas kernels: 5.02 us -> 5.15 us  [the longest x1 2.88 us: ffn(): pl.pallas_call(functools.partial(ffn_kernel, features // 7), out_shape=(p...]
  transfers between devices with their start and end apart: 23 -> 26, of which waited for: 14 -> 16; matrix products, arithmetic and copies ran while one was open for 1% -> 1% of each run, Pallas kernels for 2% -> 2%
where the time goes in v6:
time: 141 us; the launch traced here: 140 us
  waiting for transfers between devices  43.5 us (31%)
  starting transfers between devices  40.4 us (29%)
  blocking collectives  34 us (24%)
  Pallas kernels  19.7 us (14%)
  other arithmetic  1.58 us (1%)
    all_to_all x3, blocking collectives, exchange(): lax.all_to_all(value, 'tensor', split_axis=0, concat_axis=0, tiled=True,...  34 us
    ppermute x12, waiting for transfers between devices, along(): return lax.ppermute(value, 'tensor', shifts(tensors, first, distance))  21.8 us
    ppermute x12, starting transfers between devices, along(): return lax.ppermute(value, 'tensor', shifts(tensors, first, distance))  17.1 us
    ppermute x10, starting transfers between devices, swapped(): return lax.ppermute(value, 'tensor', swap)  17 us
    pallas_call x1, Pallas kernels, attend(): pl.pallas_call(functools.partial(attend_kernel, dims), out_shape=(pltpu.V...  10.1 us
    ppermute x1, waiting for transfers between devices, body(): far_low = lax.ppermute(passed[0], 'dp', from_next)  8.29 us
    ppermute x1, waiting for transfers between devices, body(): previous = lax.ppermute(cache_pool, 'dp', from_prev)  7.83 us
    ppermute x10, waiting for transfers between devices, swapped(): return lax.ppermute(value, 'tensor', swap)  5.46 us
  transfers between devices with their start and end apart: 26, of which 16 were waited for; matrix products, arithmetic and copies ran while one was open for 1% of the time, Pallas kernels for 2%

profile of v6, /device:TPU:1, one launch (start us, length us, event | category | flops | bytes accessed | tf_op | source)
XLA Modules:
  0.0 140.3 jit_solution(18184850932475436286)
XLA Ops:
  0.0 2.5 %collective-permute-start.9 = (bf16[8,576,128]{2,1,0:T(8,128)(2,1)}, bf16[8,576,128]{2,1,0:T(8,128)(2,1)S(1)}, u32[]{:S(2)}, u32[]{:S(2)}) collective-permute-start(bf16[8,576,128]{2,1,0:T(8,128)(2,1)} %refs_4_.3), channel_id=1, source_target_pairs={{96,0},{0,32},{32,64},{64,96},{97,1},{1,33},{33,65},{65,97},{98,2}... | collective-permute-start | bytes 3538952 | tf_op jit(solution)/shard_map/ppermute | solution.py:571
  2.5 2.2 %collective-permute-start.8 = (bf16[8,576,128]{2,1,0:T(8,128)(2,1)}, bf16[8,576,128]{2,1,0:T(8,128)(2,1)}, u32[]{:S(2)}, u32[]{:S(2)}) collective-permute-start(bf16[8,576,128]{2,1,0:T(8,128)(2,1)} %refs_4_.3), channel_id=1, source_target_pairs={{32,0},{64,32},{96,64},{0,96},{33,1},{65,33},{97,65},{1,97},{34,2}... | collective-permute-start | bytes 3538952 | tf_op jit(solution)/shard_map/ppermute | solution.py:570
  5.6 1.2 collective-permute-done.1.other
  8.0 2.8 %collective-permute-start.4 = (bf16[1,576,128]{2,1,0:T(8,128)(2,1)S(1)}, bf16[1,576,128]{2,1,0:T(8,128)(2,1)S(1)}, u32[]{:S(2)}, u32[]{:S(2)}) collective-permute-start(bf16[1,576,128]{2,1,0:T(8,128)(2,1)S(1)} %turn.1.refs_0_), channel_id=1, source_target_pairs={{0,6},{1,25},{2,0},{3,27},{4,2},{5,29},{6,4},{7,31},{8,14},{9,1},{... | collective-permute-start | bytes 442376 | tf_op jit(solution)/shard_map/ppermute | solution.py:565
  11.8 2.6 %collective-permute-done.4.refs_3_ = bf16[1,576,128]{2,1,0:T(8,128)(2,1)S(1)} collective-permute-done((bf16[1,576,128]{2,1,0:T(8,128)(2,1)S(1)}, bf16[1,576,128]{2,1,0:T(8,128)(2,1)S(1)}, u32[]{:S(2)}, u32[]{:S(2)}) %collective-permute-start.4) | collective-permute-done | bytes 147488 | tf_op jit(solution)/shard_map/ppermute | solution.py:565
  14.5 2.1 %collective-permute-done.3.refs_2_ = bf16[1,576,128]{2,1,0:T(8,128)(2,1)S(1)} collective-permute-done((bf16[1,576,128]{2,1,0:T(8,128)(2,1)S(1)}, bf16[1,576,128]{2,1,0:T(8,128)(2,1)S(1)}, u32[]{:S(2)}, u32[]{:S(2)}) %collective-permute-start.3) | collective-permute-done | bytes 147488 | tf_op jit(solution)/shard_map/ppermute | solution.py:565
  16.6 1.6 %collective-permute-done.2.refs_1_ = bf16[1,576,128]{2,1,0:T(8,128)(2,1)S(1)} collective-permute-done((bf16[1,576,128]{2,1,0:T(8,128)(2,1)S(1)}, bf16[1,576,128]{2,1,0:T(8,128)(2,1)S(1)}, u32[]{:S(2)}, u32[]{:S(2)}) %collective-permute-start.2) | collective-permute-done | bytes 147488 | tf_op jit(solution)/shard_map/ppermute | solution.py:565
  19.0 2.5 %collective-permute-start.7 = (bf16[4,576,128]{2,1,0:T(8,128)(2,1)S(1)}, bf16[4,576,128]{2,1,0:T(8,128)(2,1)S(1)}, u32[]{:S(2)}, u32[]{:S(2)}) collective-permute-start(bf16[4,576,128]{2,1,0:T(8,128)(2,1)S(1)} %join.1.refs_0_), channel_id=1, source_target_pairs={{0,24},{1,7},{2,26},{3,1},{4,28},{5,3},{6,30},{7,5},{8,0},{9,15},{... | collective-permute-start | bytes 1769480 | tf_op jit(solution)/shard_map/ppermute | solution.py:565
  22.7 7.8 %collective-permute-done.9.previous.refs_8_ = bf16[8,576,128]{2,1,0:T(8,128)(2,1)S(1)} collective-permute-done((bf16[8,576,128]{2,1,0:T(8,128)(2,1)}, bf16[8,576,128]{2,1,0:T(8,128)(2,1)S(1)}, u32[]{:S(2)}, u32[]{:S(2)}) %collective-permute-start.9) | collective-permute-done | bytes 1179680 | tf_op jit(solution)/shard_map/ppermute | solution.py:571
  30.5 1.2 collective-permute-start
  31.7 2.2 %split.1 = (bf16[4,576,128]{2,1,0:T(8,128)(2,1)}, bf16[4,576,128]{2,1,0:T(8,128)(2,1)}) custom-call(bf16[8,576,128]{2,1,0:T(8,128)(2,1)} %collective-permute-done.8.following.refs_5_, bf16[8,576,128]{2,1,0:T(8,128)(2,1)S(1)} %collective-permute-done.9.previous.refs_8_), custom_call_target="tpu_custom_call" | custom-call | tf_op jit(solution)/shard_map/split/pallas_call | solution.py:45
  34.0 1.5 %collective-permute-start.10 = (bf16[4,576,128]{2,1,0:T(8,128)(2,1)}, bf16[4,576,128]{2,1,0:T(8,128)(2,1)}, u32[]{:S(2)}, u32[]{:S(2)}) collective-permute-start(bf16[4,576,128]{2,1,0:T(8,128)(2,1)} %get-tuple-element.31), channel_id=1, source_target_pairs={{32,0},{64,32},{96,64},{0,96},{33,1},{65,33},{97,65},{1,97},{34,2}... | collective-permute-start | bytes 1769480 | tf_op jit(solution)/shard_map/ppermute | solution.py:575
  35.5 1.8 %collective-permute-start.12 = (bf16[8,576,128]{2,1,0:T(8,128)(2,1)}, bf16[8,576,128]{2,1,0:T(8,128)(2,1)}, u32[]{:S(2)}, u32[]{:S(2)}) collective-permute-start(bf16[8,576,128]{2,1,0:T(8,128)(2,1)} %refs_4_.3), channel_id=1, source_target_pairs={{0,1},{1,0},{2,3},{3,2},{4,5},{5,4},{6,7},{7,6},{8,9},{9,8},{10,11... | collective-permute-start | bytes 3538952 | tf_op jit(solution)/shard_map/ppermute | solution.py:562
  38.4 2.6 %collective-permute-start.13 = (bf16[8,576,128]{2,1,0:T(8,128)(2,1)}, bf16[8,576,128]{2,1,0:T(8,128)(2,1)}, u32[]{:S(2)}, u32[]{:S(2)}) collective-permute-start(bf16[8,576,128]{2,1,0:T(8,128)(2,1)} %collective-permute-done.8.following.refs_5_), channel_id=1, source_target_pairs={{0,1},{1,0},{2,3},{3,2},{4,5},{5,4},{6,7},{7,6},{8,9},{9,8},{10,11... | collective-permute-start | bytes 3538952 | tf_op jit(solution)/shard_map/ppermute | solution.py:562
  41.0 8.3 %collective-permute-done.10.refs_6_ = bf16[4,576,128]{2,1,0:T(8,128)(2,1)} collective-permute-done((bf16[4,576,128]{2,1,0:T(8,128)(2,1)}, bf16[4,576,128]{2,1,0:T(8,128)(2,1)}, u32[]{:S(2)}, u32[]{:S(2)}) %collective-permute-start.10) | collective-permute-done | bytes 589856 | tf_op jit(solution)/shard_map/ppermute | solution.py:575
  50.2 2.6 %collective-permute-start.15 = (bf16[4,576,128]{2,1,0:T(8,128)(2,1)}, bf16[4,576,128]{2,1,0:T(8,128)(2,1)S(1)}, u32[]{:S(2)}, u32[]{:S(2)}) collective-permute-start(bf16[4,576,128]{2,1,0:T(8,128)(2,1)} %collective-permute-done.11.refs_7_), channel_id=1, source_target_pairs={{0,1},{1,0},{2,3},{3,2},{4,5},{5,4},{6,7},{7,6},{8,9},{9,8},{10,11... | collective-permute-start | bytes 1769480 | tf_op jit(solution)/shard_map/ppermute | solution.py:562
  54.6 10.1 %attend.1 = (bf16[4,528,128]{2,1,0:T(8,128)(2,1)S(1)}, bf16[4,528,128]{2,1,0:T(8,128)(2,1)S(1)}, bf16[4,528,128]{2,1,0:T(8,128)(2,1)S(1)}, bf16[4,528,128]{2,1,0:T(8,128)(2,1)S(1)}) custom-call(s32[1,128]{1,0:T(1,128)S(1)} %add_bitcast_fusion.code_own, s32[1,128]{1,0:T(1,128)S(1)} %collective-permute-done.code_other, s32[1,128]{1,0:T(1,128)S(1)} %bitcast.17, ...), custom_call_target="tpu_custom_call" | custom-call | tf_op jit(solution)/shard_map/attend/pallas_call | solution.py:282
  64.7 1.4 collective-permute-start.17
  66.1 2.6 %collective-permute-start.18 = (bf16[4,528,128]{2,1,0:T(8,128)(2,1)S(1)}, bf16[4,528,128]{2,1,0:T(8,128)(2,1)S(1)}, u32[]{:S(2)}, u32[]{:S(2)}) collective-permute-start(bf16[4,528,128]{2,1,0:T(8,128)(2,1)S(1)} %get-tuple-element.35), channel_id=1, source_target_pairs={{0,4},{1,17},{2,6},{3,19},{4,0},{5,21},{6,2},{7,23},{8,12},{9,25},... | collective-permute-start | bytes 1622024 | tf_op jit(solution)/shard_map/ppermute | solution.py:565
  69.8 4.8 %collective-permute-done.17.refs_1_ = bf16[4,528,128]{2,1,0:T(8,128)(2,1)S(1)} collective-permute-done((bf16[4,528,128]{2,1,0:T(8,128)(2,1)S(1)}, bf16[4,528,128]{2,1,0:T(8,128)(2,1)S(1)}, u32[]{:S(2)}, u32[]{:S(2)}) %collective-permute-start.17) | collective-permute-done | bytes 540704 | tf_op jit(solution)/shard_map/ppermute | solution.py:565
  74.5 7.0 %collective-permute-done.18.refs_2_ = bf16[4,528,128]{2,1,0:T(8,128)(2,1)S(1)} collective-permute-done((bf16[4,528,128]{2,1,0:T(8,128)(2,1)S(1)}, bf16[4,528,128]{2,1,0:T(8,128)(2,1)S(1)}, u32[]{:S(2)}, u32[]{:S(2)}) %collective-permute-start.18) | collective-permute-done | bytes 540704 | tf_op jit(solution)/shard_map/ppermute | solution.py:565
  83.5 2.4 %collective-permute-start.21 = (bf16[528,128]{1,0:T(8,128)(2,1)S(1)}, bf16[528,128]{1,0:T(8,128)(2,1)S(1)}, u32[]{:S(2)}, u32[]{:S(2)}) collective-permute-start(bf16[528,128]{1,0:T(8,128)(2,1)S(1)} %get-tuple-element.39), channel_id=1, source_target_pairs={{0,16},{1,5},{2,18},{3,7},{4,20},{5,1},{6,22},{7,3},{8,24},{9,13},... | collective-permute-start | bytes 405512 | tf_op jit(solution)/shard_map/ppermute | solution.py:565
  86.0 1.2 collective-permute-start.22
  88.0 1.8 %collective-permute-done.21.refs_2_ = bf16[528,128]{1,0:T(8,128)(2,1)S(1)} collective-permute-done((bf16[528,128]{1,0:T(8,128)(2,1)S(1)}, bf16[528,128]{1,0:T(8,128)(2,1)S(1)}, u32[]{:S(2)}, u32[]{:S(2)}) %collective-permute-start.21) | collective-permute-done | bytes 135200 | tf_op jit(solution)/shard_map/ppermute | solution.py:565
  89.9 2.2 %project.1 = (bf16[16,56,128]{2,1,0:T(8,128)(2,1)S(1)}, bf16[16,56,128]{2,1,0:T(8,128)(2,1)S(1)}) custom-call(bf16[528,128]{1,0:T(8,128)(2,1)S(1)} %get-tuple-element.37.refs_0_, bf16[528,128]{1,0:T(8,128)(2,1)S(1)} %collective-permute-done.20.refs_1_, bf16[528,128]{1,0:T(8,128)(2,1)S(1)} %collective-permute-done.21.refs_2_, ...), custom_call_target="tpu_custom_call" | custom-call | tf_op jit(solution)/shard_map/project/pallas_call | solution.py:438
  92.0 3.5 %collective-permute-start.23 = (bf16[16,56,128]{2,1,0:T(8,128)(2,1)S(1)}, bf16[16,56,128]{2,1,0:T(8,128)(2,1)S(1)}, u32[]{:S(2)}, u32[]{:S(2)}) collective-permute-start(bf16[16,56,128]{2,1,0:T(8,128)(2,1)S(1)} %get-tuple-element.42), channel_id=1, source_target_pairs={{0,1},{1,0},{2,3},{3,2},{4,5},{5,4},{6,7},{7,6},{8,9},{9,8},{10,11... | collective-permute-start | bytes 688136 | tf_op jit(solution)/shard_map/ppermute | solution.py:562
  95.5 1.1 collective-permute-done.23.other
  96.7 13.6 %all_to_all.15.got = bf16[16,56,128]{2,1,0:T(8,128)(2,1)S(1)} all-to-all(bf16[16,56,128]{2,1,0:T(8,128)(2,1)S(1)} %add.16), channel_id=1, replica_groups={{0,2,4,6,8,10,12,14,16,18,20,22,24,26,28,30},{1,3,5,7,9,11,13,15,17,19,..., dimensions={0} | all-to-all | bytes 458752 | tf_op jit(solution)/shard_map/all_to_all | solution.py:611
  110.5 10.0 %all_to_all.16.refs_0_ = bf16[16,56,128]{2,1,0:T(8,128)(2,1)S(1)} all-to-all(bf16[16,56,128]{2,1,0:T(8,128)(2,1)S(1)} %get-tuple-element.46), channel_id=1, replica_groups={{0,2,4,6,8,10,12,14,16,18,20,22,24,26,28,30},{1,3,5,7,9,11,13,15,17,19,..., dimensions={0} | all-to-all | bytes 458752 | tf_op jit(solution)/shard_map/all_to_all | solution.py:611
  120.5 3.0 %collective-permute-start.24 = (bf16[16,56,128]{2,1,0:T(8,128)(2,1)S(1)}, bf16[16,56,128]{2,1,0:T(8,128)(2,1)S(1)}, u32[]{:S(2)}, u32[]{:S(2)}) collective-permute-start(bf16[16,56,128]{2,1,0:T(8,128)(2,1)S(1)} %all_to_all.16.refs_0_), channel_id=1, source_target_pairs={{0,1},{1,0},{2,3},{3,2},{4,5},{5,4},{6,7},{7,6},{8,9},{9,8},{10,11... | collective-permute-start | bytes 688136 | tf_op jit(solution)/shard_map/ppermute | solution.py:562
  124.7 2.9 %ffn.1 = (bf16[16,56,128]{2,1,0:T(8,128)(2,1)S(1)}, bf16[16,56,128]{2,1,0:T(8,128)(2,1)S(1)}) custom-call(bf16[16,56,128]{2,1,0:T(8,128)(2,1)S(1)} %all_to_all.16.refs_0_, bf16[16,56,128]{2,1,0:T(8,128)(2,1)S(1)} %collective-permute-done.24.refs_1_, bf16[7168,384]{1,0:T(8,128)(2,1)S(1)} %bitcast.10, bf16[7168,384]{1,0:T(8,128)(2,1)S(1)} %bitcast.12, ...), custom_call_target="tpu_custom_call" | custom-call | tf_op jit(solution)/shard_map/ffn/pallas_call | solution.py:520
  129.2 10.4 %all_to_all.17 = bf16[16,56,128]{2,1,0:T(8,128)(2,1)S(1)} all-to-all(bf16[16,56,128]{2,1,0:T(8,128)(2,1)S(1)} %add.17), channel_id=1, replica_groups={{0,2,4,6,8,10,12,14,16,18,20,22,24,26,28,30},{1,3,5,7,9,11,13,15,17,19,..., dimensions={0} | all-to-all | bytes 458752 | tf_op jit(solution)/shard_map/all_to_all | solution.py:611
  (74 shorter events, 16.6 us)
Async XLA Ops:
  0.0 30.5 %collective-permute-start.9 = (bf16[8,576,128]{2,1,0:T(8,128)(2,1)}, bf16[8,576,128]{2,1,0:T(8,128)(2,1)S(1)}, u32[]{:S(2)}, u32[]{:S(2)}) collective-permute-start(bf16[8,576,128]{2,1,0:T(8,128)(2,1)} %refs_4_.3), channel_id=1, source_target_pairs={{96,0},{0,32},{32,64},{64,96},{97,1},{1,33},{33,65},{65,97},{98,2}... | collective-permute-start | bytes 3538952 | tf_op jit(solution)/shard_map/ppermute | solution.py:571
  2.5 29.3 %collective-permute-start.8 = (bf16[8,576,128]{2,1,0:T(8,128)(2,1)}, bf16[8,576,128]{2,1,0:T(8,128)(2,1)}, u32[]{:S(2)}, u32[]{:S(2)}) collective-permute-start(bf16[8,576,128]{2,1,0:T(8,128)(2,1)} %refs_4_.3), channel_id=1, source_target_pairs={{32,0},{64,32},{96,64},{0,96},{33,1},{65,33},{97,65},{1,97},{34,2}... | collective-permute-start | bytes 3538952 | tf_op jit(solution)/shard_map/ppermute | solution.py:570
  4.7 2.2 %collective-permute-start.1 = (bf16[576,128]{1,0:T(8,128)(2,1)}, bf16[576,128]{1,0:T(8,128)(2,1)S(1)}, u32[]{:S(2)}, u32[]{:S(2)}) collective-permute-start(bf16[576,128]{1,0:T(8,128)(2,1)} %bitcast.13), channel_id=1, source_target_pairs={{0,1},{1,0},{2,3},{3,2},{4,5},{5,4},{6,7},{7,6},{8,9},{9,8},{10,11... | collective-permute-start | bytes 442376 | tf_op jit(solution)/shard_map/ppermute | solution.py:562
  8.0 6.4 %collective-permute-start.4 = (bf16[1,576,128]{2,1,0:T(8,128)(2,1)S(1)}, bf16[1,576,128]{2,1,0:T(8,128)(2,1)S(1)}, u32[]{:S(2)}, u32[]{:S(2)}) collective-permute-start(bf16[1,576,128]{2,1,0:T(8,128)(2,1)S(1)} %turn.1.refs_0_), channel_id=1, source_target_pairs={{0,6},{1,25},{2,0},{3,27},{4,2},{5,29},{6,4},{7,31},{8,14},{9,1},{... | collective-permute-start | bytes 442376 | tf_op jit(solution)/shard_map/ppermute | solution.py:565
  10.8 5.8 %collective-permute-start.3 = (bf16[1,576,128]{2,1,0:T(8,128)(2,1)S(1)}, bf16[1,576,128]{2,1,0:T(8,128)(2,1)S(1)}, u32[]{:S(2)}, u32[]{:S(2)}) collective-permute-start(bf16[1,576,128]{2,1,0:T(8,128)(2,1)S(1)} %turn.1.refs_0_), channel_id=1, source_target_pairs={{0,4},{1,17},{2,6},{3,19},{4,0},{5,21},{6,2},{7,23},{8,12},{9,25},... | collective-permute-start | bytes 442376 | tf_op jit(solution)/shard_map/ppermute | solution.py:565
  11.1 7.0 %collective-permute-start.2 = (bf16[1,576,128]{2,1,0:T(8,128)(2,1)S(1)}, bf16[1,576,128]{2,1,0:T(8,128)(2,1)S(1)}, u32[]{:S(2)}, u32[]{:S(2)}) collective-permute-start(bf16[1,576,128]{2,1,0:T(8,128)(2,1)S(1)} %turn.1.refs_0_), channel_id=1, source_target_pairs={{0,2},{1,9},{2,4},{3,11},{4,6},{5,13},{6,0},{7,15},{8,10},{9,17},{... | collective-permute-start | bytes 442376 | tf_op jit(solution)/shard_map/ppermute | solution.py:565
  19.0 16.5 %collective-permute-start.7 = (bf16[4,576,128]{2,1,0:T(8,128)(2,1)S(1)}, bf16[4,576,128]{2,1,0:T(8,128)(2,1)S(1)}, u32[]{:S(2)}, u32[]{:S(2)}) collective-permute-start(bf16[4,576,128]{2,1,0:T(8,128)(2,1)S(1)} %join.1.refs_0_), channel_id=1, source_target_pairs={{0,24},{1,7},{2,26},{3,1},{4,28},{5,3},{6,30},{7,5},{8,0},{9,15},{... | collective-permute-start | bytes 1769480 | tf_op jit(solution)/shard_map/ppermute | solution.py:565
  21.5 15.8 %collective-permute-start.6 = (bf16[4,576,128]{2,1,0:T(8,128)(2,1)S(1)}, bf16[4,576,128]{2,1,0:T(8,128)(2,1)S(1)}, u32[]{:S(2)}, u32[]{:S(2)}) collective-permute-start(bf16[4,576,128]{2,1,0:T(8,128)(2,1)S(1)} %join.1.refs_0_), channel_id=1, source_target_pairs={{0,16},{1,5},{2,18},{3,7},{4,20},{5,1},{6,22},{7,3},{8,24},{9,13},... | collective-permute-start | bytes 1769480 | tf_op jit(solution)/shard_map/ppermute | solution.py:565
  22.0 16.3 %collective-permute-start.5 = (bf16[4,576,128]{2,1,0:T(8,128)(2,1)S(1)}, bf16[4,576,128]{2,1,0:T(8,128)(2,1)S(1)}, u32[]{:S(2)}, u32[]{:S(2)}) collective-permute-start(bf16[4,576,128]{2,1,0:T(8,128)(2,1)S(1)} %join.1.refs_0_), channel_id=1, source_target_pairs={{0,8},{1,3},{2,10},{3,5},{4,12},{5,7},{6,14},{7,1},{8,16},{9,11},{... | collective-permute-start | bytes 1769480 | tf_op jit(solution)/shard_map/ppermute | solution.py:565
  30.5 5.0 %collective-permute-start = (s32[1,128]{1,0:T(1,128)S(1)}, s32[1,128]{1,0:T(1,128)S(1)}, u32[]{:S(2)}, u32[]{:S(2)}) collective-permute-start(s32[1,128]{1,0:T(1,128)S(1)} %add_bitcast_fusion.code_own), channel_id=1, source_target_pairs={{0,1},{1,0},{2,3},{3,2},{4,5},{5,4},{6,7},{7,6},{8,9},{9,8},{10,11... | collective-permute-start | bytes 1544 | tf_op jit(solution)/shard_map/ppermute | solution.py:562
  31.7 92.9 %slice-start.4 = ((s8[5505024]{0:T(1024)(128)(4,1)}), s8[1310720]{0:T(1024)(128)(4,1)S(1)}, s32[]{:S(2)}) async-start(s8[5505024]{0:T(1024)(128)(4,1)} %bitcast.11), calls=%async_computation.7 | async-start | bytes 2621440
  34.0 15.3 %collective-permute-start.10 = (bf16[4,576,128]{2,1,0:T(8,128)(2,1)}, bf16[4,576,128]{2,1,0:T(8,128)(2,1)}, u32[]{:S(2)}, u32[]{:S(2)}) collective-permute-start(bf16[4,576,128]{2,1,0:T(8,128)(2,1)} %get-tuple-element.31), channel_id=1, source_target_pairs={{32,0},{64,32},{96,64},{0,96},{33,1},{65,33},{97,65},{1,97},{34,2}... | collective-permute-start | bytes 1769480 | tf_op jit(solution)/shard_map/ppermute | solution.py:575
  35.5 14.7 %collective-permute-start.11 = (bf16[4,576,128]{2,1,0:T(8,128)(2,1)}, bf16[4,576,128]{2,1,0:T(8,128)(2,1)}, u32[]{:S(2)}, u32[]{:S(2)}) collective-permute-start(bf16[4,576,128]{2,1,0:T(8,128)(2,1)} %get-tuple-element.32), channel_id=1, source_target_pairs={{96,0},{0,32},{32,64},{64,96},{97,1},{1,33},{33,65},{65,97},{98,2}... | collective-permute-start | bytes 1769480 | tf_op jit(solution)/shard_map/ppermute | solution.py:576
  35.5 18.2 %collective-permute-start.12 = (bf16[8,576,128]{2,1,0:T(8,128)(2,1)}, bf16[8,576,128]{2,1,0:T(8,128)(2,1)}, u32[]{:S(2)}, u32[]{:S(2)}) collective-permute-start(bf16[8,576,128]{2,1,0:T(8,128)(2,1)} %refs_4_.3), channel_id=1, source_target_pairs={{0,1},{1,0},{2,3},{3,2},{4,5},{5,4},{6,7},{7,6},{8,9},{9,8},{10,11... | collective-permute-start | bytes 3538952 | tf_op jit(solution)/shard_map/ppermute | solution.py:562
  37.3 16.4 %collective-permute-start.16 = (bf16[8,576,128]{2,1,0:T(8,128)(2,1)S(1)}, bf16[8,576,128]{2,1,0:T(8,128)(2,1)}, u32[]{:S(2)}, u32[]{:S(2)}) collective-permute-start(bf16[8,576,128]{2,1,0:T(8,128)(2,1)S(1)} %collective-permute-done.9.previous.refs_8_), channel_id=1, source_target_pairs={{0,1},{1,0},{2,3},{3,2},{4,5},{5,4},{6,7},{7,6},{8,9},{9,8},{10,11... | collective-permute-start | bytes 3538952 | tf_op jit(solution)/shard_map/ppermute | solution.py:562
  38.4 16.2 %collective-permute-start.13 = (bf16[8,576,128]{2,1,0:T(8,128)(2,1)}, bf16[8,576,128]{2,1,0:T(8,128)(2,1)}, u32[]{:S(2)}, u32[]{:S(2)}) collective-permute-start(bf16[8,576,128]{2,1,0:T(8,128)(2,1)} %collective-permute-done.8.following.refs_5_), channel_id=1, source_target_pairs={{0,1},{1,0},{2,3},{3,2},{4,5},{5,4},{6,7},{7,6},{8,9},{9,8},{10,11... | collective-permute-start | bytes 3538952 | tf_op jit(solution)/shard_map/ppermute | solution.py:562
  49.3 4.4 %collective-permute-start.14 = (bf16[4,576,128]{2,1,0:T(8,128)(2,1)}, bf16[4,576,128]{2,1,0:T(8,128)(2,1)S(1)}, u32[]{:S(2)}, u32[]{:S(2)}) collective-permute-start(bf16[4,576,128]{2,1,0:T(8,128)(2,1)} %collective-permute-done.10.refs_6_), channel_id=1, source_target_pairs={{0,1},{1,0},{2,3},{3,2},{4,5},{5,4},{6,7},{7,6},{8,9},{9,8},{10,11... | collective-permute-start | bytes 1769480 | tf_op jit(solution)/shard_map/ppermute | solution.py:562
  50.2 4.4 %collective-permute-start.15 = (bf16[4,576,128]{2,1,0:T(8,128)(2,1)}, bf16[4,576,128]{2,1,0:T(8,128)(2,1)S(1)}, u32[]{:S(2)}, u32[]{:S(2)}) collective-permute-start(bf16[4,576,128]{2,1,0:T(8,128)(2,1)} %collective-permute-done.11.refs_7_), channel_id=1, source_target_pairs={{0,1},{1,0},{2,3},{3,2},{4,5},{5,4},{6,7},{7,6},{8,9},{9,8},{10,11... | collective-permute-start | bytes 1769480 | tf_op jit(solution)/shard_map/ppermute | solution.py:562
  54.6 35.2 %slice-start = ((s8[7340032]{0:T(1024)(128)(4,1)}), s8[4194304]{0:T(1024)(128)(4,1)S(1)}, s32[]{:S(2)}) async-start(s8[7340032]{0:T(1024)(128)(4,1)} %bitcast.7), calls=%async_computation.3 | async-start | bytes 8388608
  54.6 35.2 %slice-start.1 = ((s8[7340032]{0:T(1024)(128)(4,1)}), s8[3145728]{0:T(1024)(128)(4,1)S(1)}, s32[]{:S(2)}) async-start(s8[7340032]{0:T(1024)(128)(4,1)} %bitcast.7), calls=%async_computation.4 | async-start | bytes 6291456
  54.6 70.0 %slice-start.5 = ((s8[5505024]{0:T(1024)(128)(4,1)}), s8[4194304]{0:T(1024)(128)(4,1)S(1)}, s32[]{:S(2)}) async-start(s8[5505024]{0:T(1024)(128)(4,1)} %bitcast.11), calls=%async_computation.8 | async-start | bytes 8388608
  64.7 9.8 %collective-permute-start.17 = (bf16[4,528,128]{2,1,0:T(8,128)(2,1)S(1)}, bf16[4,528,128]{2,1,0:T(8,128)(2,1)S(1)}, u32[]{:S(2)}, u32[]{:S(2)}) collective-permute-start(bf16[4,528,128]{2,1,0:T(8,128)(2,1)S(1)} %get-tuple-element.34), channel_id=1, source_target_pairs={{0,2},{1,9},{2,4},{3,11},{4,6},{5,13},{6,0},{7,15},{8,10},{9,17},{... | collective-permute-start | bytes 1622024 | tf_op jit(solution)/shard_map/ppermute | solution.py:565
  66.1 15.4 %collective-permute-start.18 = (bf16[4,528,128]{2,1,0:T(8,128)(2,1)S(1)}, bf16[4,528,128]{2,1,0:T(8,128)(2,1)S(1)}, u32[]{:S(2)}, u32[]{:S(2)}) collective-permute-start(bf16[4,528,128]{2,1,0:T(8,128)(2,1)S(1)} %get-tuple-element.35), channel_id=1, source_target_pairs={{0,4},{1,17},{2,6},{3,19},{4,0},{5,21},{6,2},{7,23},{8,12},{9,25},... | collective-permute-start | bytes 1622024 | tf_op jit(solution)/shard_map/ppermute | solution.py:565
  68.7 12.8 %collective-permute-start.19 = (bf16[4,528,128]{2,1,0:T(8,128)(2,1)S(1)}, bf16[4,528,128]{2,1,0:T(8,128)(2,1)S(1)}, u32[]{:S(2)}, u32[]{:S(2)}) collective-permute-start(bf16[4,528,128]{2,1,0:T(8,128)(2,1)S(1)} %get-tuple-element.36), channel_id=1, source_target_pairs={{0,6},{1,25},{2,0},{3,27},{4,2},{5,29},{6,4},{7,31},{8,14},{9,1},{... | collective-permute-start | bytes 1622024 | tf_op jit(solution)/shard_map/ppermute | solution.py:565
  81.5 43.1 %copy-start = (bf16[384,7168]{1,0:T(8,128)(2,1)S(1)}, bf16[384,7168]{1,0:T(8,128)(2,1)}, u32[]{:S(2)}) copy-start(bf16[384,7168]{1,0:T(8,128)(2,1)} %refs_4_.5) | copy-start | bytes 16515076
  82.5 5.4 %collective-permute-start.20 = (bf16[528,128]{1,0:T(8,128)(2,1)S(1)}, bf16[528,128]{1,0:T(8,128)(2,1)S(1)}, u32[]{:S(2)}, u32[]{:S(2)}) collective-permute-start(bf16[528,128]{1,0:T(8,128)(2,1)S(1)} %get-tuple-element.38), channel_id=1, source_target_pairs={{0,8},{1,3},{2,10},{3,5},{4,12},{5,7},{6,14},{7,1},{8,16},{9,11},{... | collective-permute-start | bytes 405512 | tf_op jit(solution)/shard_map/ppermute | solution.py:565
  83.5 6.3 %collective-permute-start.21 = (bf16[528,128]{1,0:T(8,128)(2,1)S(1)}, bf16[528,128]{1,0:T(8,128)(2,1)S(1)}, u32[]{:S(2)}, u32[]{:S(2)}) collective-permute-start(bf16[528,128]{1,0:T(8,128)(2,1)S(1)} %get-tuple-element.39), channel_id=1, source_target_pairs={{0,16},{1,5},{2,18},{3,7},{4,20},{5,1},{6,22},{7,3},{8,24},{9,13},... | collective-permute-start | bytes 405512 | tf_op jit(solution)/shard_map/ppermute | solution.py:565
  86.0 3.9 %collective-permute-start.22 = (bf16[528,128]{1,0:T(8,128)(2,1)S(1)}, bf16[528,128]{1,0:T(8,128)(2,1)S(1)}, u32[]{:S(2)}, u32[]{:S(2)}) collective-permute-start(bf16[528,128]{1,0:T(8,128)(2,1)S(1)} %get-tuple-element.40), channel_id=1, source_target_pairs={{0,24},{1,7},{2,26},{3,1},{4,28},{5,3},{6,30},{7,5},{8,0},{9,15},{... | collective-permute-start | bytes 405512 | tf_op jit(solution)/shard_map/ppermute | solution.py:565
  89.8 34.8 %slice-start.2 = ((s8[5505024]{0:T(1024)(128)(4,1)}), s8[4194304]{0:T(1024)(128)(4,1)S(1)}, s32[]{:S(2)}) async-start(s8[5505024]{0:T(1024)(128)(4,1)} %bitcast.9), calls=%async_computation.5 | async-start | bytes 8388608
  92.0 4.6 %collective-permute-start.23 = (bf16[16,56,128]{2,1,0:T(8,128)(2,1)S(1)}, bf16[16,56,128]{2,1,0:T(8,128)(2,1)S(1)}, u32[]{:S(2)}, u32[]{:S(2)}) collective-permute-start(bf16[16,56,128]{2,1,0:T(8,128)(2,1)S(1)} %get-tuple-element.42), channel_id=1, source_target_pairs={{0,1},{1,0},{2,3},{3,2},{4,5},{5,4},{6,7},{7,6},{8,9},{9,8},{10,11... | collective-permute-start | bytes 688136 | tf_op jit(solution)/shard_map/ppermute | solution.py:562
  120.5 4.1 %collective-permute-start.24 = (bf16[16,56,128]{2,1,0:T(8,128)(2,1)S(1)}, bf16[16,56,128]{2,1,0:T(8,128)(2,1)S(1)}, u32[]{:S(2)}, u32[]{:S(2)}) collective-permute-start(bf16[16,56,128]{2,1,0:T(8,128)(2,1)S(1)} %all_to_all.16.refs_0_), channel_id=1, source_target_pairs={{0,1},{1,0},{2,3},{3,2},{4,5},{5,4},{6,7},{7,6},{8,9},{9,8},{10,11... | collective-permute-start | bytes 688136 | tf_op jit(solution)/shard_map/ppermute | solution.py:562
  127.6 1.6 %collective-permute-start.25 = (bf16[16,56,128]{2,1,0:T(8,128)(2,1)S(1)}, bf16[16,56,128]{2,1,0:T(8,128)(2,1)S(1)}, u32[]{:S(2)}, u32[]{:S(2)}) collective-permute-start(bf16[16,56,128]{2,1,0:T(8,128)(2,1)S(1)} %get-tuple-element.48), channel_id=1, source_target_pairs={{0,1},{1,0},{2,3},{3,2},{4,5},{5,4},{6,7},{7,6},{8,9},{9,8},{10,11... | collective-permute-start | bytes 688136 | tf_op jit(solution)/shard_map/ppermute | solution.py:562
  (11 other events, 182.8 us)

commit v7 on v6

--- a/solution.py
+++ b/solution.py
@@ -24,33 +24,51 @@
     return pltpu.with_memory_space_constraint(value, pltpu.VMEM)
 
 
+def moves(size):
+    return pl.CostEstimate(flops=0, bytes_accessed=size, transcendentals=0)
+
+
 def in_hbm(value):
     return pltpu.with_memory_space_constraint(value, pltpu.HBM)
 
 
-def split_kernel(following, previous, low, high, sems):
-    half = low.shape[0]
-    copies = [
-        pltpu.make_async_copy(following.at[pl.ds(0, half)], low, sems.at[0]),
-        pltpu.make_async_copy(previous.at[pl.ds(half, half)], high, sems.at[1]),
-    ]
-    for one in copies:
-        one.start()
-    for one in copies:
-        one.wait()
-
-
-def split(following, previous):
-    half = (following.shape[0] // 2,) + following.shape[1:]
-    return pl.pallas_call(
-        split_kernel,
-        out_shape=(pltpu.VMEM(half, following.dtype), pltpu.VMEM(half, following.dtype)),
-        in_specs=[hbm_spec] * 2,
-        out_specs=(vmem_spec, vmem_spec),
-        scratch_shapes=[pltpu.SemaphoreType.DMA((2,))],
-        compiler_params=pltpu.CompilerParams(vmem_limit_bytes=12 * MIB),
-        name="split",
-    )(following, previous)
+def cut_kernel(first, blocks, out, sem):
+    copy = pltpu.make_async_copy(blocks.at[pl.ds(first, out.shape[0])], out, sem)
+    copy.start()
+    copy.wait()
+
+
+def cut(blocks, first):
+    half = (blocks.shape[0] // 2,) + blocks.shape[1:]
+    return pl.pallas_call(
+        functools.partial(cut_kernel, first),
+        out_shape=pltpu.VMEM(half, blocks.dtype),
+        in_specs=[hbm_spec],
+        out_specs=vmem_spec,
+        scratch_shapes=[pltpu.SemaphoreType.DMA],
+        compiler_params=pltpu.CompilerParams(vmem_limit_bytes=4 * MIB),
+        cost_estimate=moves(1200000),
+        name="cut",
+    )(blocks)
+
+
+def fetch_kernel(weight, _, out, sem):
+    copy = pltpu.make_async_copy(weight, out, sem)
+    copy.start()
+    copy.wait()
+
+
+def fetch(weight, after):
+    return pl.pallas_call(
+        fetch_kernel,
+        out_shape=pltpu.VMEM(weight.shape, weight.dtype),
+        in_specs=[hbm_spec, vmem_spec],
+        out_specs=vmem_spec,
+        scratch_shapes=[pltpu.SemaphoreType.DMA],
+        compiler_params=pltpu.CompilerParams(vmem_limit_bytes=4 * MIB),
+        cost_estimate=moves(2 * weight.size * weight.dtype.itemsize),
+        name="fetch",
+    )(in_hbm(weight), in_vmem(after))
 
 
 def turn_kernel(own, other, out):
@@ -85,6 +103,7 @@
         in_specs=[vmem_spec] * 2,
         out_specs=vmem_spec,
         compiler_params=pltpu.CompilerParams(vmem_limit_bytes=4 * MIB),
+        cost_estimate=moves(450000),
         name="turn",
     )(own, other)
 
@@ -111,6 +130,7 @@
         out_specs=hbm_spec,
         scratch_shapes=[pltpu.SemaphoreType.DMA((count,))],
         compiler_params=pltpu.CompilerParams(vmem_limit_bytes=4 * MIB),
+        cost_estimate=moves(1200000),
         name="join",
     )(*pieces)
 
@@ -292,6 +312,7 @@
             pltpu.SemaphoreType.DMA((count + SIDE,)),
         ],
         compiler_params=pltpu.CompilerParams(vmem_limit_bytes=22 * MIB),
+        cost_estimate=moves(20000000),
         name="attend",
     )(code_own, code_other, lengths, *[in_hbm(one) for one in q_all], *pieces)
 
@@ -381,6 +402,7 @@
         in_specs=[vmem_spec] * SIDE,
         out_specs=(vmem_spec,) * SIDE,
         compiler_params=pltpu.CompilerParams(vmem_limit_bytes=8 * MIB),
+        cost_estimate=moves(4500000),
         name="merge",
     )(*[in_vmem(one) for one in arrived])
 
@@ -445,6 +467,7 @@
             pltpu.VMEM((group * tiles, LANES), jnp.float32),
         ],
         compiler_params=pltpu.CompilerParams(vmem_limit_bytes=12 * MIB),
+        cost_estimate=moves(9000000),
         name="project",
     )(*[in_vmem(one) for one in parts], w_value, w_out)
 
@@ -461,6 +484,7 @@
         in_specs=[vmem_spec] * 2,
         out_specs=vmem_spec,
         compiler_params=pltpu.CompilerParams(vmem_limit_bytes=4 * MIB),
+        cost_estimate=moves(700000),
         name="add",
     )(in_vmem(one), in_vmem(other))
 
@@ -483,6 +507,7 @@
         in_specs=[vmem_spec] * 3,
         out_specs=(vmem_spec, vmem_spec),
         compiler_params=pltpu.CompilerParams(vmem_limit_bytes=8 * MIB),
+        cost_estimate=moves(700000),
         name="norm",
     )(in_vmem(got), in_vmem(residual), in_vmem(gain))
 
@@ -527,6 +552,7 @@
             pltpu.VMEM((group, features), jnp.bfloat16),
         ],
         compiler_params=pltpu.CompilerParams(vmem_limit_bytes=12 * MIB),
+        cost_estimate=moves(17000000),
         name="ffn",
     )(*[in_vmem(one) for one in normed], w_gate, w_up, w_down)
 
@@ -571,9 +597,8 @@
     previous = lax.ppermute(cache_pool, "dp", from_prev)
     q_line = join([q_pair] + [along(q_pair, True, d) for d in range(1, SIDE)])
     q_all = [q_line] + [along(q_line, False, e) for e in range(1, SIDE)]
-    passed = split(following, previous)
-    far_low = lax.ppermute(passed[0], "dp", from_next)
-    far_high = lax.ppermute(passed[1], "dp", from_prev)
+    far_low = lax.ppermute(cut(following, 0), "dp", from_next)
+    far_high = lax.ppermute(cut(previous, slots // 2), "dp", from_prev)
     mine = [following, far_low, far_high, previous]
     moved = [in_vmem(swapped(one)) for one in mine]
     mine = [in_vmem(one) for one in mine]
@@ -587,8 +612,8 @@
     )
     gain = norm_gain.reshape(tiles, LANES)
     q_all, own_residual, gain = lax.optimization_barrier((q_all, own_residual, gain))
-    w_value, w_out, w_gate, w_up, w_down = [
-        in_vmem(one) for one in (w_value, w_out, w_gate, w_up, w_down)
+    w_value, w_gate, w_up, w_down = [
+        in_vmem(one) for one in (w_value, w_gate, w_up, w_down)
     ]
     partial = attend(
         code,
@@ -600,6 +625,7 @@
         latent,
         head_local,
     )
+    w_out = fetch(w_out, partial[0])
     arrived = [partial[0]] + [along(partial[d], True, d) for d in range(1, SIDE)]
     merged = merge(arrived, group, head_local, latent)
     parts = [merged[0]] + [along(merged[e], False, e) for e in range(1, SIDE)]

time: 141 us -> 138 us (0.979)
  starting transfers between devices: 40.4 us -> 37.2 us
  Pallas kernels: 19.7 us -> 22.3 us
  waiting for transfers between devices: 43.5 us -> 41.4 us
    ppermute x10, starting transfers between devices: 17 us -> 12.6 us  [swapped(): return lax.ppermute(value, 'tensor', swap)]
    pallas_call x1 -> x3, Pallas kernels: 2.21 us -> 5.57 us  [the longest x1 3.67 us: fetch(): pl.pallas_call(fetch_kernel, out_shape=pltpu.VMEM(weight.shape, weight.dt...]
    ppermute x12, waiting for transfers between devices: 21.8 us -> 19.2 us  [along(): return lax.ppermute(value, 'tensor', shifts(tensors, first, distance))]
  transfers between devices with their start and end apart: 26 -> 26, of which waited for: 16 -> 14; matrix products, arithmetic and copies ran while one was open for 1% -> 1% of each run, Pallas kernels for 2% -> 5%
where the time goes in v7:
time: 138 us
  waiting for transfers between devices  41.4 us (30%)
  starting transfers between devices  37.2 us (27%)
  blocking collectives  33.8 us (24%)
  Pallas kernels  22.3 us (16%)
  other arithmetic  1.58 us (1%)
    all_to_all x3, blocking collectives, exchange(): lax.all_to_all(value, 'tensor', split_axis=0, concat_axis=0, tiled=True,...  33.8 us
    ppermute x12, waiting for transfers between devices, along(): return lax.ppermute(value, 'tensor', shifts(tensors, first, distance))  19.2 us
    ppermute x12, starting transfers between devices, along(): return lax.ppermute(value, 'tensor', shifts(tensors, first, distance))  17.2 us
    ppermute x10, starting transfers between devices, swapped(): return lax.ppermute(value, 'tensor', swap)  12.6 us
    pallas_call x1, Pallas kernels, attend(): pl.pallas_call(functools.partial(attend_kernel, dims), out_shape=(pltpu.V...  9.23 us
    ppermute x1, waiting for transfers between devices, body(): far_high = lax.ppermute(cut(previous, slots // 2), 'dp', from_prev)  8.26 us
    ppermute x1, waiting for transfers between devices, body(): previous = lax.ppermute(cache_pool, 'dp', from_prev)  7.85 us
    ppermute x10, waiting for transfers between devices, swapped(): return lax.ppermute(value, 'tensor', swap)  6.02 us
  transfers between devices with their start and end apart: 26, of which 14 were waited for; matrix products, arithmetic and copies ran while one was open for 1% of the time, Pallas kernels for 5%

profile of v7, /device:TPU:1, one launch (start us, length us, event | category | flops | bytes accessed | tf_op | source)
XLA Modules:
  0.0 137.7 jit_solution(8549394336424568447)
XLA Ops:
  0.0 2.5 %collective-permute-start.10 = (bf16[8,576,128]{2,1,0:T(8,128)(2,1)}, bf16[8,576,128]{2,1,0:T(8,128)(2,1)S(1)}, u32[]{:S(2)}, u32[]{:S(2)}) collective-permute-start(bf16[8,576,128]{2,1,0:T(8,128)(2,1)} %refs_4_.3), channel_id=1, source_target_pairs={{96,0},{0,32},{32,64},{64,96},{97,1},{1,33},{33,65},{65,97},{98,2}... | collective-permute-start | bytes 3538952 | tf_op jit(solution)/shard_map/ppermute | solution.py:597
  2.5 2.2 %collective-permute-start.8 = (bf16[8,576,128]{2,1,0:T(8,128)(2,1)}, bf16[8,576,128]{2,1,0:T(8,128)(2,1)S(1)}, u32[]{:S(2)}, u32[]{:S(2)}) collective-permute-start(bf16[8,576,128]{2,1,0:T(8,128)(2,1)} %refs_4_.3), channel_id=1, source_target_pairs={{32,0},{64,32},{96,64},{0,96},{33,1},{65,33},{97,65},{1,97},{34,2}... | collective-permute-start | bytes 3538952 | tf_op jit(solution)/shard_map/ppermute | solution.py:596
  5.6 1.2 collective-permute-done.1.other
  8.0 2.8 %collective-permute-start.4 = (bf16[1,576,128]{2,1,0:T(8,128)(2,1)S(1)}, bf16[1,576,128]{2,1,0:T(8,128)(2,1)S(1)}, u32[]{:S(2)}, u32[]{:S(2)}) collective-permute-start(bf16[1,576,128]{2,1,0:T(8,128)(2,1)S(1)} %turn.1.refs_0_), channel_id=1, source_target_pairs={{0,6},{1,25},{2,0},{3,27},{4,2},{5,29},{6,4},{7,31},{8,14},{9,1},{... | collective-permute-start | bytes 442376 | tf_op jit(solution)/shard_map/ppermute | solution.py:591
  11.8 2.6 %collective-permute-done.4.refs_3_ = bf16[1,576,128]{2,1,0:T(8,128)(2,1)S(1)} collective-permute-done((bf16[1,576,128]{2,1,0:T(8,128)(2,1)S(1)}, bf16[1,576,128]{2,1,0:T(8,128)(2,1)S(1)}, u32[]{:S(2)}, u32[]{:S(2)}) %collective-permute-start.4) | collective-permute-done | bytes 147488 | tf_op jit(solution)/shard_map/ppermute | solution.py:591
  14.5 2.1 %collective-permute-done.3.refs_2_ = bf16[1,576,128]{2,1,0:T(8,128)(2,1)S(1)} collective-permute-done((bf16[1,576,128]{2,1,0:T(8,128)(2,1)S(1)}, bf16[1,576,128]{2,1,0:T(8,128)(2,1)S(1)}, u32[]{:S(2)}, u32[]{:S(2)}) %collective-permute-start.3) | collective-permute-done | bytes 147488 | tf_op jit(solution)/shard_map/ppermute | solution.py:591
  16.6 1.6 %collective-permute-done.2.refs_1_ = bf16[1,576,128]{2,1,0:T(8,128)(2,1)S(1)} collective-permute-done((bf16[1,576,128]{2,1,0:T(8,128)(2,1)S(1)}, bf16[1,576,128]{2,1,0:T(8,128)(2,1)S(1)}, u32[]{:S(2)}, u32[]{:S(2)}) %collective-permute-start.2) | collective-permute-done | bytes 147488 | tf_op jit(solution)/shard_map/ppermute | solution.py:591
  19.0 2.5 %collective-permute-start.7 = (bf16[4,576,128]{2,1,0:T(8,128)(2,1)S(1)}, bf16[4,576,128]{2,1,0:T(8,128)(2,1)S(1)}, u32[]{:S(2)}, u32[]{:S(2)}) collective-permute-start(bf16[4,576,128]{2,1,0:T(8,128)(2,1)S(1)} %join.1.refs_0_), channel_id=1, source_target_pairs={{0,24},{1,7},{2,26},{3,1},{4,28},{5,3},{6,30},{7,5},{8,0},{9,15},{... | collective-permute-start | bytes 1769480 | tf_op jit(solution)/shard_map/ppermute | solution.py:591
  22.6 7.8 %collective-permute-done.10.blocks.refs_8_ = bf16[8,576,128]{2,1,0:T(8,128)(2,1)S(1)} collective-permute-done((bf16[8,576,128]{2,1,0:T(8,128)(2,1)}, bf16[8,576,128]{2,1,0:T(8,128)(2,1)S(1)}, u32[]{:S(2)}, u32[]{:S(2)}) %collective-permute-start.10) | collective-permute-done | bytes 1179680 | tf_op jit(solution)/shard_map/ppermute | solution.py:597
  30.5 1.2 collective-permute-start
  33.8 2.7 %collective-permute-start.9 = (bf16[4,576,128]{2,1,0:T(8,128)(2,1)}, bf16[4,576,128]{2,1,0:T(8,128)(2,1)}, u32[]{:S(2)}, u32[]{:S(2)}) collective-permute-start(bf16[4,576,128]{2,1,0:T(8,128)(2,1)} %cut.2), channel_id=1, source_target_pairs={{32,0},{64,32},{96,64},{0,96},{33,1},{65,33},{97,65},{1,97},{34,2}... | collective-permute-start | bytes 1769480 | tf_op jit(solution)/shard_map/ppermute | solution.py:600
  37.3 1.1 collective-permute-done.5.refs_1_
  38.5 2.5 %collective-permute-start.13 = (bf16[8,576,128]{2,1,0:T(8,128)(2,1)S(1)}, bf16[8,576,128]{2,1,0:T(8,128)(2,1)S(1)}, u32[]{:S(2)}, u32[]{:S(2)}) collective-permute-start(bf16[8,576,128]{2,1,0:T(8,128)(2,1)S(1)} %collective-permute-done.8.blocks.refs_5_), channel_id=1, source_target_pairs={{0,1},{1,0},{2,3},{3,2},{4,5},{5,4},{6,7},{7,6},{8,9},{9,8},{10,11... | collective-permute-start | bytes 3538952 | tf_op jit(solution)/shard_map/ppermute | solution.py:588
  41.0 8.3 %collective-permute-done.11.refs_7_ = bf16[4,576,128]{2,1,0:T(8,128)(2,1)} collective-permute-done((bf16[4,576,128]{2,1,0:T(8,128)(2,1)}, bf16[4,576,128]{2,1,0:T(8,128)(2,1)}, u32[]{:S(2)}, u32[]{:S(2)}) %collective-permute-start.11) | collective-permute-done | bytes 589856 | tf_op jit(solution)/shard_map/ppermute | solution.py:601
  52.7 9.2 %attend.1 = (bf16[4,528,128]{2,1,0:T(8,128)(2,1)S(1)}, bf16[4,528,128]{2,1,0:T(8,128)(2,1)S(1)}, bf16[4,528,128]{2,1,0:T(8,128)(2,1)S(1)}, bf16[4,528,128]{2,1,0:T(8,128)(2,1)S(1)}) custom-call(s32[1,128]{1,0:T(1,128)S(1)} %add_bitcast_fusion.code_own, s32[1,128]{1,0:T(1,128)S(1)} %collective-permute-done.code_other, s32[1,128]{1,0:T(1,128)S(1)} %bitcast.17, ...), custom_call_target="tpu_custom_call" | custom-call | bytes 20000000 | tf_op jit(solution)/shard_map/attend/pallas_call | solution.py:302
  62.0 1.4 collective-permute-start.17
  63.3 2.6 %collective-permute-start.18 = (bf16[4,528,128]{2,1,0:T(8,128)(2,1)S(1)}, bf16[4,528,128]{2,1,0:T(8,128)(2,1)S(1)}, u32[]{:S(2)}, u32[]{:S(2)}) collective-permute-start(bf16[4,528,128]{2,1,0:T(8,128)(2,1)S(1)} %get-tuple-element.31), channel_id=1, source_target_pairs={{0,4},{1,17},{2,6},{3,19},{4,0},{5,21},{6,2},{7,23},{8,12},{9,25},... | collective-permute-start | bytes 1622024 | tf_op jit(solution)/shard_map/ppermute | solution.py:591
  67.0 4.8 %collective-permute-done.17.refs_1_ = bf16[4,528,128]{2,1,0:T(8,128)(2,1)S(1)} collective-permute-done((bf16[4,528,128]{2,1,0:T(8,128)(2,1)S(1)}, bf16[4,528,128]{2,1,0:T(8,128)(2,1)S(1)}, u32[]{:S(2)}, u32[]{:S(2)}) %collective-permute-start.17) | collective-permute-done | bytes 540704 | tf_op jit(solution)/shard_map/ppermute | solution.py:591
  71.8 7.0 %collective-permute-done.18.refs_2_ = bf16[4,528,128]{2,1,0:T(8,128)(2,1)S(1)} collective-permute-done((bf16[4,528,128]{2,1,0:T(8,128)(2,1)S(1)}, bf16[4,528,128]{2,1,0:T(8,128)(2,1)S(1)}, u32[]{:S(2)}, u32[]{:S(2)}) %collective-permute-start.18) | collective-permute-done | bytes 540704 | tf_op jit(solution)/shard_map/ppermute | solution.py:591
  80.9 2.4 %collective-permute-start.21 = (bf16[528,128]{1,0:T(8,128)(2,1)S(1)}, bf16[528,128]{1,0:T(8,128)(2,1)S(1)}, u32[]{:S(2)}, u32[]{:S(2)}) collective-permute-start(bf16[528,128]{1,0:T(8,128)(2,1)S(1)} %get-tuple-element.35), channel_id=1, source_target_pairs={{0,16},{1,5},{2,18},{3,7},{4,20},{5,1},{6,22},{7,3},{8,24},{9,13},... | collective-permute-start | bytes 405512 | tf_op jit(solution)/shard_map/ppermute | solution.py:591
  83.3 1.2 collective-permute-start.22
  84.5 3.7 %fetch.1.refs_5_ = bf16[512,7168]{1,0:T(8,128)(2,1)S(1)} custom-call(bf16[512,7168]{1,0:T(8,128)(2,1)} %weight.1, bf16[4,528,128]{2,1,0:T(8,128)(2,1)S(1)} %get-tuple-element.29.refs_0_._), custom_call_target="tpu_custom_call" | custom-call | bytes 14680064 | tf_op jit(solution)/shard_map/fetch/pallas_call | solution.py:62
  88.3 2.2 %project.1 = (bf16[16,56,128]{2,1,0:T(8,128)(2,1)S(1)}, bf16[16,56,128]{2,1,0:T(8,128)(2,1)S(1)}) custom-call(bf16[528,128]{1,0:T(8,128)(2,1)S(1)} %get-tuple-element.33.refs_0_, bf16[528,128]{1,0:T(8,128)(2,1)S(1)} %collective-permute-done.20.refs_1_, bf16[528,128]{1,0:T(8,128)(2,1)S(1)} %collective-permute-done.21.refs_2_, ...), custom_call_target="tpu_custom_call" | custom-call | bytes 9000000 | tf_op jit(solution)/shard_map/project/pallas_call | solution.py:460
  90.5 2.6 %collective-permute-start.23 = (bf16[16,56,128]{2,1,0:T(8,128)(2,1)S(1)}, bf16[16,56,128]{2,1,0:T(8,128)(2,1)S(1)}, u32[]{:S(2)}, u32[]{:S(2)}) collective-permute-start(bf16[16,56,128]{2,1,0:T(8,128)(2,1)S(1)} %get-tuple-element.38), channel_id=1, source_target_pairs={{0,1},{1,0},{2,3},{3,2},{4,5},{5,4},{6,7},{7,6},{8,9},{9,8},{10,11... | collective-permute-start | bytes 688136 | tf_op jit(solution)/shard_map/ppermute | solution.py:588
  93.1 1.1 collective-permute-done.23.other
  94.3 13.4 %all_to_all.15.got = bf16[16,56,128]{2,1,0:T(8,128)(2,1)S(1)} all-to-all(bf16[16,56,128]{2,1,0:T(8,128)(2,1)S(1)} %add.16), channel_id=1, replica_groups={{0,2,4,6,8,10,12,14,16,18,20,22,24,26,28,30},{1,3,5,7,9,11,13,15,17,19,..., dimensions={0} | all-to-all | bytes 458752 | tf_op jit(solution)/shard_map/all_to_all | solution.py:637
  107.9 10.0 %all_to_all.16.refs_0_ = bf16[16,56,128]{2,1,0:T(8,128)(2,1)S(1)} all-to-all(bf16[16,56,128]{2,1,0:T(8,128)(2,1)S(1)} %get-tuple-element.42), channel_id=1, replica_groups={{0,2,4,6,8,10,12,14,16,18,20,22,24,26,28,30},{1,3,5,7,9,11,13,15,17,19,..., dimensions={0} | all-to-all | bytes 458752 | tf_op jit(solution)/shard_map/all_to_all | solution.py:637
  117.9 3.0 %collective-permute-start.24 = (bf16[16,56,128]{2,1,0:T(8,128)(2,1)S(1)}, bf16[16,56,128]{2,1,0:T(8,128)(2,1)S(1)}, u32[]{:S(2)}, u32[]{:S(2)}) collective-permute-start(bf16[16,56,128]{2,1,0:T(8,128)(2,1)S(1)} %all_to_all.16.refs_0_), channel_id=1, source_target_pairs={{0,1},{1,0},{2,3},{3,2},{4,5},{5,4},{6,7},{7,6},{8,9},{9,8},{10,11... | collective-permute-start | bytes 688136 | tf_op jit(solution)/shard_map/ppermute | solution.py:588
  120.9 1.1 collective-permute-done.24.refs_1_
  122.1 2.9 %ffn.1 = (bf16[16,56,128]{2,1,0:T(8,128)(2,1)S(1)}, bf16[16,56,128]{2,1,0:T(8,128)(2,1)S(1)}) custom-call(bf16[16,56,128]{2,1,0:T(8,128)(2,1)S(1)} %all_to_all.16.refs_0_, bf16[16,56,128]{2,1,0:T(8,128)(2,1)S(1)} %collective-permute-done.24.refs_1_, bf16[7168,384]{1,0:T(8,128)(2,1)S(1)} %bitcast.8, bf16[7168,384]{1,0:T(8,128)(2,1)S(1)} %bitcast.10, ...), custom_call_target="tpu_custom_call" | custom-call | bytes 17000000 | tf_op jit(solution)/shard_map/ffn/pallas_call | solution.py:545
  125.4 1.1 collective-permute-done.25.other
  126.6 10.4 %all_to_all.17 = bf16[16,56,128]{2,1,0:T(8,128)(2,1)S(1)} all-to-all(bf16[16,56,128]{2,1,0:T(8,128)(2,1)S(1)} %add.17), channel_id=1, replica_groups={{0,2,4,6,8,10,12,14,16,18,20,22,24,26,28,30},{1,3,5,7,9,11,13,15,17,19,..., dimensions={0} | all-to-all | bytes 458752 | tf_op jit(solution)/shard_map/all_to_all | solution.py:637
  (74 shorter events, 16.0 us)
Async XLA Ops:
  0.0 30.5 %collective-permute-start.10 = (bf16[8,576,128]{2,1,0:T(8,128)(2,1)}, bf16[8,576,128]{2,1,0:T(8,128)(2,1)S(1)}, u32[]{:S(2)}, u32[]{:S(2)}) collective-permute-start(bf16[8,576,128]{2,1,0:T(8,128)(2,1)} %refs_4_.3), channel_id=1, source_target_pairs={{96,0},{0,32},{32,64},{64,96},{97,1},{1,33},{33,65},{65,97},{98,2}... | collective-permute-start | bytes 3538952 | tf_op jit(solution)/shard_map/ppermute | solution.py:597
  2.5 30.2 %collective-permute-start.8 = (bf16[8,576,128]{2,1,0:T(8,128)(2,1)}, bf16[8,576,128]{2,1,0:T(8,128)(2,1)S(1)}, u32[]{:S(2)}, u32[]{:S(2)}) collective-permute-start(bf16[8,576,128]{2,1,0:T(8,128)(2,1)} %refs_4_.3), channel_id=1, source_target_pairs={{32,0},{64,32},{96,64},{0,96},{33,1},{65,33},{97,65},{1,97},{34,2}... | collective-permute-start | bytes 3538952 | tf_op jit(solution)/shard_map/ppermute | solution.py:596
  4.7 2.2 %collective-permute-start.1 = (bf16[576,128]{1,0:T(8,128)(2,1)}, bf16[576,128]{1,0:T(8,128)(2,1)S(1)}, u32[]{:S(2)}, u32[]{:S(2)}) collective-permute-start(bf16[576,128]{1,0:T(8,128)(2,1)} %bitcast.13), channel_id=1, source_target_pairs={{0,1},{1,0},{2,3},{3,2},{4,5},{5,4},{6,7},{7,6},{8,9},{9,8},{10,11... | collective-permute-start | bytes 442376 | tf_op jit(solution)/shard_map/ppermute | solution.py:588
  8.0 6.4 %collective-permute-start.4 = (bf16[1,576,128]{2,1,0:T(8,128)(2,1)S(1)}, bf16[1,576,128]{2,1,0:T(8,128)(2,1)S(1)}, u32[]{:S(2)}, u32[]{:S(2)}) collective-permute-start(bf16[1,576,128]{2,1,0:T(8,128)(2,1)S(1)} %turn.1.refs_0_), channel_id=1, source_target_pairs={{0,6},{1,25},{2,0},{3,27},{4,2},{5,29},{6,4},{7,31},{8,14},{9,1},{... | collective-permute-start | bytes 442376 | tf_op jit(solution)/shard_map/ppermute | solution.py:591
  10.8 5.8 %collective-permute-start.3 = (bf16[1,576,128]{2,1,0:T(8,128)(2,1)S(1)}, bf16[1,576,128]{2,1,0:T(8,128)(2,1)S(1)}, u32[]{:S(2)}, u32[]{:S(2)}) collective-permute-start(bf16[1,576,128]{2,1,0:T(8,128)(2,1)S(1)} %turn.1.refs_0_), channel_id=1, source_target_pairs={{0,4},{1,17},{2,6},{3,19},{4,0},{5,21},{6,2},{7,23},{8,12},{9,25},... | collective-permute-start | bytes 442376 | tf_op jit(solution)/shard_map/ppermute | solution.py:591
  11.1 7.0 %collective-permute-start.2 = (bf16[1,576,128]{2,1,0:T(8,128)(2,1)S(1)}, bf16[1,576,128]{2,1,0:T(8,128)(2,1)S(1)}, u32[]{:S(2)}, u32[]{:S(2)}) collective-permute-start(bf16[1,576,128]{2,1,0:T(8,128)(2,1)S(1)} %turn.1.refs_0_), channel_id=1, source_target_pairs={{0,2},{1,9},{2,4},{3,11},{4,6},{5,13},{6,0},{7,15},{8,10},{9,17},{... | collective-permute-start | bytes 442376 | tf_op jit(solution)/shard_map/ppermute | solution.py:591
  19.0 17.5 %collective-permute-start.7 = (bf16[4,576,128]{2,1,0:T(8,128)(2,1)S(1)}, bf16[4,576,128]{2,1,0:T(8,128)(2,1)S(1)}, u32[]{:S(2)}, u32[]{:S(2)}) collective-permute-start(bf16[4,576,128]{2,1,0:T(8,128)(2,1)S(1)} %join.1.refs_0_), channel_id=1, source_target_pairs={{0,24},{1,7},{2,26},{3,1},{4,28},{5,3},{6,30},{7,5},{8,0},{9,15},{... | collective-permute-start | bytes 1769480 | tf_op jit(solution)/shard_map/ppermute | solution.py:591
  21.5 15.6 %collective-permute-start.6 = (bf16[4,576,128]{2,1,0:T(8,128)(2,1)S(1)}, bf16[4,576,128]{2,1,0:T(8,128)(2,1)S(1)}, u32[]{:S(2)}, u32[]{:S(2)}) collective-permute-start(bf16[4,576,128]{2,1,0:T(8,128)(2,1)S(1)} %join.1.refs_0_), channel_id=1, source_target_pairs={{0,16},{1,5},{2,18},{3,7},{4,20},{5,1},{6,22},{7,3},{8,24},{9,13},... | collective-permute-start | bytes 1769480 | tf_op jit(solution)/shard_map/ppermute | solution.py:591
  22.0 16.4 %collective-permute-start.5 = (bf16[4,576,128]{2,1,0:T(8,128)(2,1)S(1)}, bf16[4,576,128]{2,1,0:T(8,128)(2,1)S(1)}, u32[]{:S(2)}, u32[]{:S(2)}) collective-permute-start(bf16[4,576,128]{2,1,0:T(8,128)(2,1)S(1)} %join.1.refs_0_), channel_id=1, source_target_pairs={{0,8},{1,3},{2,10},{3,5},{4,12},{5,7},{6,14},{7,1},{8,16},{9,11},{... | collective-permute-start | bytes 1769480 | tf_op jit(solution)/shard_map/ppermute | solution.py:591
  30.5 3.3 %collective-permute-start = (s32[1,128]{1,0:T(1,128)S(1)}, s32[1,128]{1,0:T(1,128)S(1)}, u32[]{:S(2)}, u32[]{:S(2)}) collective-permute-start(s32[1,128]{1,0:T(1,128)S(1)} %add_bitcast_fusion.code_own), channel_id=1, source_target_pairs={{0,1},{1,0},{2,3},{3,2},{4,5},{5,4},{6,7},{7,6},{8,9},{9,8},{10,11... | collective-permute-start | bytes 1544 | tf_op jit(solution)/shard_map/ppermute | solution.py:588
  32.7 16.6 %collective-permute-start.11 = (bf16[4,576,128]{2,1,0:T(8,128)(2,1)}, bf16[4,576,128]{2,1,0:T(8,128)(2,1)}, u32[]{:S(2)}, u32[]{:S(2)}) collective-permute-start(bf16[4,576,128]{2,1,0:T(8,128)(2,1)} %cut.3), channel_id=1, source_target_pairs={{96,0},{0,32},{32,64},{64,96},{97,1},{1,33},{33,65},{65,97},{98,2}... | collective-permute-start | bytes 1769480 | tf_op jit(solution)/shard_map/ppermute | solution.py:601
  33.8 16.3 %collective-permute-start.9 = (bf16[4,576,128]{2,1,0:T(8,128)(2,1)}, bf16[4,576,128]{2,1,0:T(8,128)(2,1)}, u32[]{:S(2)}, u32[]{:S(2)}) collective-permute-start(bf16[4,576,128]{2,1,0:T(8,128)(2,1)} %cut.2), channel_id=1, source_target_pairs={{32,0},{64,32},{96,64},{0,96},{33,1},{65,33},{97,65},{1,97},{34,2}... | collective-permute-start | bytes 1769480 | tf_op jit(solution)/shard_map/ppermute | solution.py:600
  36.5 14.8 %collective-permute-start.12 = (bf16[8,576,128]{2,1,0:T(8,128)(2,1)}, bf16[8,576,128]{2,1,0:T(8,128)(2,1)}, u32[]{:S(2)}, u32[]{:S(2)}) collective-permute-start(bf16[8,576,128]{2,1,0:T(8,128)(2,1)} %refs_4_.3), channel_id=1, source_target_pairs={{0,1},{1,0},{2,3},{3,2},{4,5},{5,4},{6,7},{7,6},{8,9},{9,8},{10,11... | collective-permute-start | bytes 3538952 | tf_op jit(solution)/shard_map/ppermute | solution.py:588
  37.1 14.8 %collective-permute-start.16 = (bf16[8,576,128]{2,1,0:T(8,128)(2,1)S(1)}, bf16[8,576,128]{2,1,0:T(8,128)(2,1)}, u32[]{:S(2)}, u32[]{:S(2)}) collective-permute-start(bf16[8,576,128]{2,1,0:T(8,128)(2,1)S(1)} %collective-permute-done.10.blocks.refs_8_), channel_id=1, source_target_pairs={{0,1},{1,0},{2,3},{3,2},{4,5},{5,4},{6,7},{7,6},{8,9},{9,8},{10,11... | collective-permute-start | bytes 3538952 | tf_op jit(solution)/shard_map/ppermute | solution.py:588
  38.5 14.3 %collective-permute-start.13 = (bf16[8,576,128]{2,1,0:T(8,128)(2,1)S(1)}, bf16[8,576,128]{2,1,0:T(8,128)(2,1)S(1)}, u32[]{:S(2)}, u32[]{:S(2)}) collective-permute-start(bf16[8,576,128]{2,1,0:T(8,128)(2,1)S(1)} %collective-permute-done.8.blocks.refs_5_), channel_id=1, source_target_pairs={{0,1},{1,0},{2,3},{3,2},{4,5},{5,4},{6,7},{7,6},{8,9},{9,8},{10,11... | collective-permute-start | bytes 3538952 | tf_op jit(solution)/shard_map/ppermute | solution.py:588
  49.3 2.6 %collective-permute-start.15 = (bf16[4,576,128]{2,1,0:T(8,128)(2,1)}, bf16[4,576,128]{2,1,0:T(8,128)(2,1)S(1)}, u32[]{:S(2)}, u32[]{:S(2)}) collective-permute-start(bf16[4,576,128]{2,1,0:T(8,128)(2,1)} %collective-permute-done.11.refs_7_), channel_id=1, source_target_pairs={{0,1},{1,0},{2,3},{3,2},{4,5},{5,4},{6,7},{7,6},{8,9},{9,8},{10,11... | collective-permute-start | bytes 1769480 | tf_op jit(solution)/shard_map/ppermute | solution.py:588
  50.1 2.7 %collective-permute-start.14 = (bf16[4,576,128]{2,1,0:T(8,128)(2,1)}, bf16[4,576,128]{2,1,0:T(8,128)(2,1)S(1)}, u32[]{:S(2)}, u32[]{:S(2)}) collective-permute-start(bf16[4,576,128]{2,1,0:T(8,128)(2,1)} %collective-permute-done.9.refs_6_), channel_id=1, source_target_pairs={{0,1},{1,0},{2,3},{3,2},{4,5},{5,4},{6,7},{7,6},{8,9},{9,8},{10,11... | collective-permute-start | bytes 1769480 | tf_op jit(solution)/shard_map/ppermute | solution.py:588
  62.0 9.8 %collective-permute-start.17 = (bf16[4,528,128]{2,1,0:T(8,128)(2,1)S(1)}, bf16[4,528,128]{2,1,0:T(8,128)(2,1)S(1)}, u32[]{:S(2)}, u32[]{:S(2)}) collective-permute-start(bf16[4,528,128]{2,1,0:T(8,128)(2,1)S(1)} %get-tuple-element.30), channel_id=1, source_target_pairs={{0,2},{1,9},{2,4},{3,11},{4,6},{5,13},{6,0},{7,15},{8,10},{9,17},{... | collective-permute-start | bytes 1622024 | tf_op jit(solution)/shard_map/ppermute | solution.py:591
  63.3 15.5 %collective-permute-start.18 = (bf16[4,528,128]{2,1,0:T(8,128)(2,1)S(1)}, bf16[4,528,128]{2,1,0:T(8,128)(2,1)S(1)}, u32[]{:S(2)}, u32[]{:S(2)}) collective-permute-start(bf16[4,528,128]{2,1,0:T(8,128)(2,1)S(1)} %get-tuple-element.31), channel_id=1, source_target_pairs={{0,4},{1,17},{2,6},{3,19},{4,0},{5,21},{6,2},{7,23},{8,12},{9,25},... | collective-permute-start | bytes 1622024 | tf_op jit(solution)/shard_map/ppermute | solution.py:591
  66.0 12.8 %collective-permute-start.19 = (bf16[4,528,128]{2,1,0:T(8,128)(2,1)S(1)}, bf16[4,528,128]{2,1,0:T(8,128)(2,1)S(1)}, u32[]{:S(2)}, u32[]{:S(2)}) collective-permute-start(bf16[4,528,128]{2,1,0:T(8,128)(2,1)S(1)} %get-tuple-element.32), channel_id=1, source_target_pairs={{0,6},{1,25},{2,0},{3,27},{4,2},{5,29},{6,4},{7,31},{8,14},{9,1},{... | collective-permute-start | bytes 1622024 | tf_op jit(solution)/shard_map/ppermute | solution.py:591
  79.9 8.4 %collective-permute-start.20 = (bf16[528,128]{1,0:T(8,128)(2,1)S(1)}, bf16[528,128]{1,0:T(8,128)(2,1)S(1)}, u32[]{:S(2)}, u32[]{:S(2)}) collective-permute-start(bf16[528,128]{1,0:T(8,128)(2,1)S(1)} %get-tuple-element.34), channel_id=1, source_target_pairs={{0,8},{1,3},{2,10},{3,5},{4,12},{5,7},{6,14},{7,1},{8,16},{9,11},{... | collective-permute-start | bytes 405512 | tf_op jit(solution)/shard_map/ppermute | solution.py:591
  80.9 7.4 %collective-permute-start.21 = (bf16[528,128]{1,0:T(8,128)(2,1)S(1)}, bf16[528,128]{1,0:T(8,128)(2,1)S(1)}, u32[]{:S(2)}, u32[]{:S(2)}) collective-permute-start(bf16[528,128]{1,0:T(8,128)(2,1)S(1)} %get-tuple-element.35), channel_id=1, source_target_pairs={{0,16},{1,5},{2,18},{3,7},{4,20},{5,1},{6,22},{7,3},{8,24},{9,13},... | collective-permute-start | bytes 405512 | tf_op jit(solution)/shard_map/ppermute | solution.py:591
  83.3 38.7 %slice-start.2 = ((s8[5505024]{0:T(1024)(128)(4,1)}), s8[4194304]{0:T(1024)(128)(4,1)S(1)}, s32[]{:S(2)}) async-start(s8[5505024]{0:T(1024)(128)(4,1)} %bitcast.9), calls=%async_computation.5 | async-start | bytes 8388608
  83.3 38.7 %slice-start.4 = ((s8[5505024]{0:T(1024)(128)(4,1)}), s8[4194304]{0:T(1024)(128)(4,1)S(1)}, s32[]{:S(2)}) async-start(s8[5505024]{0:T(1024)(128)(4,1)} %bitcast.11), calls=%async_computation.7 | async-start | bytes 8388608
  83.3 38.7 %slice-start.3 = ((s8[5505024]{0:T(1024)(128)(4,1)}), s8[1310720]{0:T(1024)(128)(4,1)S(1)}, s32[]{:S(2)}) async-start(s8[5505024]{0:T(1024)(128)(4,1)} %bitcast.9), calls=%async_computation.6 | async-start | bytes 2621440
  83.3 38.7 %slice-start.5 = ((s8[5505024]{0:T(1024)(128)(4,1)}), s8[1310720]{0:T(1024)(128)(4,1)S(1)}, s32[]{:S(2)}) async-start(s8[5505024]{0:T(1024)(128)(4,1)} %bitcast.11), calls=%async_computation.8 | async-start | bytes 2621440
  83.3 4.9 %collective-permute-start.22 = (bf16[528,128]{1,0:T(8,128)(2,1)S(1)}, bf16[528,128]{1,0:T(8,128)(2,1)S(1)}, u32[]{:S(2)}, u32[]{:S(2)}) collective-permute-start(bf16[528,128]{1,0:T(8,128)(2,1)S(1)} %get-tuple-element.36), channel_id=1, source_target_pairs={{0,24},{1,7},{2,26},{3,1},{4,28},{5,3},{6,30},{7,5},{8,0},{9,15},{... | collective-permute-start | bytes 405512 | tf_op jit(solution)/shard_map/ppermute | solution.py:591
  88.3 33.8 %slice-start = ((s8[5505024]{0:T(1024)(128)(4,1)}), s8[4194304]{0:T(1024)(128)(4,1)S(1)}, s32[]{:S(2)}) async-start(s8[5505024]{0:T(1024)(128)(4,1)} %bitcast.7), calls=%async_computation.3 | async-start | bytes 8388608
  88.3 33.8 %slice-start.1 = ((s8[5505024]{0:T(1024)(128)(4,1)}), s8[1310720]{0:T(1024)(128)(4,1)S(1)}, s32[]{:S(2)}) async-start(s8[5505024]{0:T(1024)(128)(4,1)} %bitcast.7), calls=%async_computation.4 | async-start | bytes 2621440
  90.5 3.7 %collective-permute-start.23 = (bf16[16,56,128]{2,1,0:T(8,128)(2,1)S(1)}, bf16[16,56,128]{2,1,0:T(8,128)(2,1)S(1)}, u32[]{:S(2)}, u32[]{:S(2)}) collective-permute-start(bf16[16,56,128]{2,1,0:T(8,128)(2,1)S(1)} %get-tuple-element.38), channel_id=1, source_target_pairs={{0,1},{1,0},{2,3},{3,2},{4,5},{5,4},{6,7},{7,6},{8,9},{9,8},{10,11... | collective-permute-start | bytes 688136 | tf_op jit(solution)/shard_map/ppermute | solution.py:588
  117.9 4.1 %collective-permute-start.24 = (bf16[16,56,128]{2,1,0:T(8,128)(2,1)S(1)}, bf16[16,56,128]{2,1,0:T(8,128)(2,1)S(1)}, u32[]{:S(2)}, u32[]{:S(2)}) collective-permute-start(bf16[16,56,128]{2,1,0:T(8,128)(2,1)S(1)} %all_to_all.16.refs_0_), channel_id=1, source_target_pairs={{0,1},{1,0},{2,3},{3,2},{4,5},{5,4},{6,7},{7,6},{8,9},{9,8},{10,11... | collective-permute-start | bytes 688136 | tf_op jit(solution)/shard_map/ppermute | solution.py:588
  125.0 1.6 %collective-permute-start.25 = (bf16[16,56,128]{2,1,0:T(8,128)(2,1)S(1)}, bf16[16,56,128]{2,1,0:T(8,128)(2,1)S(1)}, u32[]{:S(2)}, u32[]{:S(2)}) collective-permute-start(bf16[16,56,128]{2,1,0:T(8,128)(2,1)S(1)} %get-tuple-element.44), channel_id=1, source_target_pairs={{0,1},{1,0},{2,3},{3,2},{4,5},{5,4},{6,7},{7,6},{8,9},{9,8},{10,11... | collective-permute-start | bytes 688136 | tf_op jit(solution)/shard_map/ppermute | solution.py:588
  (10 other events, 110.2 us)

commit v8 on v7

--- a/solution.py
+++ b/solution.py
@@ -175,7 +175,9 @@
     for i, one in enumerate(pieces):
         copies.append(pltpu.make_async_copy(one, kbuf.at[pl.ds(at, one.shape[0])], sems.at[i]))
         at += one.shape[0]
-    for one in q_copies + copies:
+    for one in copies[:1] + copies[count // 2 : count // 2 + 1] + q_copies[:1]:
+        one.start()
+    for one in copies[1 : count // 2] + copies[count // 2 + 1 :] + q_copies[1:]:
         one.start()
     token = lax.broadcasted_iota(jnp.int32, (1, 2 * block_len), 1)
     partner = column + 1 - 2 * core
@@ -190,7 +192,7 @@
         spots.append(
             (k_first - own_first + SIDE) % SIDE * SIDE + (k_second - own_second + SIDE) % SIDE
         )
-    for one in q_copies + copies:
+    for one in copies:
         one.wait()
 
     def place(codes, r):
@@ -200,6 +202,8 @@
     unroll = CORES * SIDE
 
     def several(e, carry):
+        for i, one in enumerate(q_copies):
+            pl.when(e == i)(one.wait)
         second = (own_second - e + SIDE) % SIDE
         rs, asked = [], []
         for i in range(SIDE):
@@ -371,7 +375,7 @@
 
 def merge_kernel(dims, *refs):
     group, head_local, latent = dims
-    ins, outs = refs[:SIDE], refs[SIDE:]
+    ins, outs = refs[:SIDE], refs[SIDE + 1 :]
     rows = group * head_local
     pieces = latent // LANES
     tail = pieces * rows
@@ -394,17 +398,17 @@
         )
 
 
-def merge(arrived, group, head_local, latent):
+def merge(arrived, after, group, head_local, latent):
     shape = arrived[0].shape[1:]
     return pl.pallas_call(
         functools.partial(merge_kernel, (group, head_local, latent)),
         out_shape=(pltpu.VMEM(shape, jnp.bfloat16),) * SIDE,
-        in_specs=[vmem_spec] * SIDE,
+        in_specs=[vmem_spec] * (SIDE + 1),
         out_specs=(vmem_spec,) * SIDE,
         compiler_params=pltpu.CompilerParams(vmem_limit_bytes=8 * MIB),
         cost_estimate=moves(4500000),
         name="merge",
-    )(*[in_vmem(one) for one in arrived])
+    )(*[in_vmem(one) for one in arrived], after)
 
 
 def scatter_tiles(flat, value, first_tile, group, tiles):
@@ -626,9 +630,12 @@
         head_local,
     )
     w_out = fetch(w_out, partial[0])
-    arrived = [partial[0]] + [along(partial[d], True, d) for d in range(1, SIDE)]
-    merged = merge(arrived, group, head_local, latent)
-    parts = [merged[0]] + [along(merged[e], False, e) for e in range(1, SIDE)]
+    opposite = along(partial[2], True, 2)
+    one_on, one_back = along(partial[1], True, 1), along(partial[3], True, 3)
+    arrived = [partial[0], opposite, one_on, one_back]
+    merged = merge(arrived, w_out, group, head_local, latent)
+    opposite = along(merged[2], False, 2)
+    parts = [merged[0], opposite, along(merged[1], False, 1), along(merged[3], False, 3)]
 
     chips = SIDE * SIDE
     same_core = [[c + CORES * k for k in range(chips)] for c in range(CORES)]

time: 138 us -> 137 us (level)
  waiting for transfers between devices: 41.4 us -> 39.3 us
  starting transfers between devices: 37.2 us -> 38.9 us
    ppermute x12, waiting for transfers between devices: 19.2 us -> 17.2 us  [along(): return lax.ppermute(value, 'tensor', shifts(tensors, first, distance))]
  transfers between devices with their start and end apart: 26 -> 26, of which waited for: 14 -> 17; matrix products, arithmetic and copies ran while one was open for 1% -> 1% of each run, Pallas kernels for 5% -> 5%
where the time goes in v8:
time: 137 us
  waiting for transfers between devices  39.3 us (29%)
  starting transfers between devices  38.9 us (28%)
  blocking collectives  34.3 us (25%)
  Pallas kernels  21.4 us (16%)
  other arithmetic  1.58 us (1%)
    all_to_all x3, blocking collectives, exchange(): lax.all_to_all(value, 'tensor', split_axis=0, concat_axis=0, tiled=True,...  34.3 us
    ppermute x12, starting transfers between devices, along(): return lax.ppermute(value, 'tensor', shifts(tensors, first, distance))  18.3 us
    ppermute x12, waiting for transfers between devices, along(): return lax.ppermute(value, 'tensor', shifts(tensors, first, distance))  17.2 us
    ppermute x10, starting transfers between devices, swapped(): return lax.ppermute(value, 'tensor', swap)  13.1 us
    pallas_call x1, Pallas kernels, attend(): pl.pallas_call(functools.partial(attend_kernel, dims), out_shape=(pltpu.V...  8.75 us
    ppermute x1, waiting for transfers between devices, body(): far_high = lax.ppermute(cut(previous, slots // 2), 'dp', from_prev)  8.26 us
    ppermute x1, waiting for transfers between devices, body(): previous = lax.ppermute(cache_pool, 'dp', from_prev)  7.85 us
    ppermute x10, waiting for transfers between devices, swapped(): return lax.ppermute(value, 'tensor', swap)  6.02 us
  transfers between devices with their start and end apart: 26, of which 17 were waited for; matrix products, arithmetic and copies ran while one was open for 1% of the time, Pallas kernels for 5%

profile of v8, /device:TPU:1, one launch (start us, length us, event | category | flops | bytes accessed | tf_op | source)
XLA Modules:
  0.0 136.9 jit_solution(15446852718818280029)
XLA Ops:
  0.0 2.5 %collective-permute-start.10 = (bf16[8,576,128]{2,1,0:T(8,128)(2,1)}, bf16[8,576,128]{2,1,0:T(8,128)(2,1)S(1)}, u32[]{:S(2)}, u32[]{:S(2)}) collective-permute-start(bf16[8,576,128]{2,1,0:T(8,128)(2,1)} %refs_4_.3), channel_id=1, source_target_pairs={{96,0},{0,32},{32,64},{64,96},{97,1},{1,33},{33,65},{65,97},{98,2}... | collective-permute-start | bytes 3538952 | tf_op jit(solution)/shard_map/ppermute | solution.py:601
  2.5 2.2 %collective-permute-start.8 = (bf16[8,576,128]{2,1,0:T(8,128)(2,1)}, bf16[8,576,128]{2,1,0:T(8,128)(2,1)S(1)}, u32[]{:S(2)}, u32[]{:S(2)}) collective-permute-start(bf16[8,576,128]{2,1,0:T(8,128)(2,1)} %refs_4_.3), channel_id=1, source_target_pairs={{32,0},{64,32},{96,64},{0,96},{33,1},{65,33},{97,65},{1,97},{34,2}... | collective-permute-start | bytes 3538952 | tf_op jit(solution)/shard_map/ppermute | solution.py:600
  5.6 1.2 collective-permute-done.1.other
  8.0 2.8 %collective-permute-start.4 = (bf16[1,576,128]{2,1,0:T(8,128)(2,1)S(1)}, bf16[1,576,128]{2,1,0:T(8,128)(2,1)S(1)}, u32[]{:S(2)}, u32[]{:S(2)}) collective-permute-start(bf16[1,576,128]{2,1,0:T(8,128)(2,1)S(1)} %turn.1.refs_0_), channel_id=1, source_target_pairs={{0,6},{1,25},{2,0},{3,27},{4,2},{5,29},{6,4},{7,31},{8,14},{9,1},{... | collective-permute-start | bytes 442376 | tf_op jit(solution)/shard_map/ppermute | solution.py:595
  11.8 2.6 %collective-permute-done.4.refs_3_ = bf16[1,576,128]{2,1,0:T(8,128)(2,1)S(1)} collective-permute-done((bf16[1,576,128]{2,1,0:T(8,128)(2,1)S(1)}, bf16[1,576,128]{2,1,0:T(8,128)(2,1)S(1)}, u32[]{:S(2)}, u32[]{:S(2)}) %collective-permute-start.4) | collective-permute-done | bytes 147488 | tf_op jit(solution)/shard_map/ppermute | solution.py:595
  14.5 2.1 %collective-permute-done.3.refs_2_ = bf16[1,576,128]{2,1,0:T(8,128)(2,1)S(1)} collective-permute-done((bf16[1,576,128]{2,1,0:T(8,128)(2,1)S(1)}, bf16[1,576,128]{2,1,0:T(8,128)(2,1)S(1)}, u32[]{:S(2)}, u32[]{:S(2)}) %collective-permute-start.3) | collective-permute-done | bytes 147488 | tf_op jit(solution)/shard_map/ppermute | solution.py:595
  16.6 1.6 %collective-permute-done.2.refs_1_ = bf16[1,576,128]{2,1,0:T(8,128)(2,1)S(1)} collective-permute-done((bf16[1,576,128]{2,1,0:T(8,128)(2,1)S(1)}, bf16[1,576,128]{2,1,0:T(8,128)(2,1)S(1)}, u32[]{:S(2)}, u32[]{:S(2)}) %collective-permute-start.2) | collective-permute-done | bytes 147488 | tf_op jit(solution)/shard_map/ppermute | solution.py:595
  19.0 2.5 %collective-permute-start.7 = (bf16[4,576,128]{2,1,0:T(8,128)(2,1)S(1)}, bf16[4,576,128]{2,1,0:T(8,128)(2,1)S(1)}, u32[]{:S(2)}, u32[]{:S(2)}) collective-permute-start(bf16[4,576,128]{2,1,0:T(8,128)(2,1)S(1)} %join.1.refs_0_), channel_id=1, source_target_pairs={{0,24},{1,7},{2,26},{3,1},{4,28},{5,3},{6,30},{7,5},{8,0},{9,15},{... | collective-permute-start | bytes 1769480 | tf_op jit(solution)/shard_map/ppermute | solution.py:595
  22.6 7.8 %collective-permute-done.10.blocks.refs_8_ = bf16[8,576,128]{2,1,0:T(8,128)(2,1)S(1)} collective-permute-done((bf16[8,576,128]{2,1,0:T(8,128)(2,1)}, bf16[8,576,128]{2,1,0:T(8,128)(2,1)S(1)}, u32[]{:S(2)}, u32[]{:S(2)}) %collective-permute-start.10) | collective-permute-done | bytes 1179680 | tf_op jit(solution)/shard_map/ppermute | solution.py:601
  30.5 1.2 collective-permute-start
  33.8 2.7 %collective-permute-start.9 = (bf16[4,576,128]{2,1,0:T(8,128)(2,1)}, bf16[4,576,128]{2,1,0:T(8,128)(2,1)}, u32[]{:S(2)}, u32[]{:S(2)}) collective-permute-start(bf16[4,576,128]{2,1,0:T(8,128)(2,1)} %cut.2), channel_id=1, source_target_pairs={{32,0},{64,32},{96,64},{0,96},{33,1},{65,33},{97,65},{1,97},{34,2}... | collective-permute-start | bytes 1769480 | tf_op jit(solution)/shard_map/ppermute | solution.py:604
  37.3 1.1 collective-permute-done.5.refs_1_
  38.5 2.5 %collective-permute-start.13 = (bf16[8,576,128]{2,1,0:T(8,128)(2,1)S(1)}, bf16[8,576,128]{2,1,0:T(8,128)(2,1)S(1)}, u32[]{:S(2)}, u32[]{:S(2)}) collective-permute-start(bf16[8,576,128]{2,1,0:T(8,128)(2,1)S(1)} %collective-permute-done.8.blocks.refs_5_), channel_id=1, source_target_pairs={{0,1},{1,0},{2,3},{3,2},{4,5},{5,4},{6,7},{7,6},{8,9},{9,8},{10,11... | collective-permute-start | bytes 3538952 | tf_op jit(solution)/shard_map/ppermute | solution.py:592
  41.0 8.3 %collective-permute-done.11.refs_7_ = bf16[4,576,128]{2,1,0:T(8,128)(2,1)} collective-permute-done((bf16[4,576,128]{2,1,0:T(8,128)(2,1)}, bf16[4,576,128]{2,1,0:T(8,128)(2,1)}, u32[]{:S(2)}, u32[]{:S(2)}) %collective-permute-start.11) | collective-permute-done | bytes 589856 | tf_op jit(solution)/shard_map/ppermute | solution.py:605
  52.7 8.8 %attend.1 = (bf16[4,528,128]{2,1,0:T(8,128)(2,1)S(1)}, bf16[4,528,128]{2,1,0:T(8,128)(2,1)S(1)}, bf16[4,528,128]{2,1,0:T(8,128)(2,1)S(1)}, bf16[4,528,128]{2,1,0:T(8,128)(2,1)S(1)}) custom-call(s32[1,128]{1,0:T(1,128)S(1)} %add_bitcast_fusion.code_own, s32[1,128]{1,0:T(1,128)S(1)} %collective-permute-done.code_other, s32[1,128]{1,0:T(1,128)S(1)} %bitcast.17, ...), custom_call_target="tpu_custom_call" | custom-call | bytes 20000000 | tf_op jit(solution)/shard_map/attend/pallas_call | solution.py:306
  61.5 3.0 %collective-permute-start.17 = (bf16[4,528,128]{2,1,0:T(8,128)(2,1)S(1)}, bf16[4,528,128]{2,1,0:T(8,128)(2,1)S(1)}, u32[]{:S(2)}, u32[]{:S(2)}) collective-permute-start(bf16[4,528,128]{2,1,0:T(8,128)(2,1)S(1)} %get-tuple-element.30), channel_id=1, source_target_pairs={{0,4},{1,17},{2,6},{3,19},{4,0},{5,21},{6,2},{7,23},{8,12},{9,25},... | collective-permute-start | bytes 1622024 | tf_op jit(solution)/shard_map/ppermute | solution.py:595
  64.9 2.3 %collective-permute-start.19 = (bf16[4,528,128]{2,1,0:T(8,128)(2,1)S(1)}, bf16[4,528,128]{2,1,0:T(8,128)(2,1)S(1)}, u32[]{:S(2)}, u32[]{:S(2)}) collective-permute-start(bf16[4,528,128]{2,1,0:T(8,128)(2,1)S(1)} %get-tuple-element.32), channel_id=1, source_target_pairs={{0,6},{1,25},{2,0},{3,27},{4,2},{5,29},{6,4},{7,31},{8,14},{9,1},{... | collective-permute-start | bytes 1622024 | tf_op jit(solution)/shard_map/ppermute | solution.py:595
  67.2 3.2 %fetch.1.refs_4_.refs_5_ = bf16[512,7168]{1,0:T(8,128)(2,1)S(1)} custom-call(bf16[512,7168]{1,0:T(8,128)(2,1)} %weight.1, bf16[4,528,128]{2,1,0:T(8,128)(2,1)S(1)} %get-tuple-element.29._.refs_0_), custom_call_target="tpu_custom_call" | custom-call | bytes 14680064 | tf_op jit(solution)/shard_map/fetch/pallas_call | solution.py:62
  70.5 1.2 collective-permute-done.17.refs_1_
  71.6 5.7 %collective-permute-done.18.refs_2_ = bf16[4,528,128]{2,1,0:T(8,128)(2,1)S(1)} collective-permute-done((bf16[4,528,128]{2,1,0:T(8,128)(2,1)S(1)}, bf16[4,528,128]{2,1,0:T(8,128)(2,1)S(1)}, u32[]{:S(2)}, u32[]{:S(2)}) %collective-permute-start.18) | collective-permute-done | bytes 540704 | tf_op jit(solution)/shard_map/ppermute | solution.py:595
  78.8 2.5 %collective-permute-start.20 = (bf16[528,128]{1,0:T(8,128)(2,1)S(1)}, bf16[528,128]{1,0:T(8,128)(2,1)S(1)}, u32[]{:S(2)}, u32[]{:S(2)}) collective-permute-start(bf16[528,128]{1,0:T(8,128)(2,1)S(1)} %get-tuple-element.34), channel_id=1, source_target_pairs={{0,16},{1,5},{2,18},{3,7},{4,20},{5,1},{6,22},{7,3},{8,24},{9,13},... | collective-permute-start | bytes 405512 | tf_op jit(solution)/shard_map/ppermute | solution.py:595
  82.0 2.1 %collective-permute-start.22 = (bf16[528,128]{1,0:T(8,128)(2,1)S(1)}, bf16[528,128]{1,0:T(8,128)(2,1)S(1)}, u32[]{:S(2)}, u32[]{:S(2)}) collective-permute-start(bf16[528,128]{1,0:T(8,128)(2,1)S(1)} %get-tuple-element.36), channel_id=1, source_target_pairs={{0,24},{1,7},{2,26},{3,1},{4,28},{5,3},{6,30},{7,5},{8,0},{9,15},{... | collective-permute-start | bytes 405512 | tf_op jit(solution)/shard_map/ppermute | solution.py:595
  84.6 1.9 %collective-permute-done.21.refs_2_ = bf16[528,128]{1,0:T(8,128)(2,1)S(1)} collective-permute-done((bf16[528,128]{1,0:T(8,128)(2,1)S(1)}, bf16[528,128]{1,0:T(8,128)(2,1)S(1)}, u32[]{:S(2)}, u32[]{:S(2)}) %collective-permute-start.21) | collective-permute-done | bytes 135200 | tf_op jit(solution)/shard_map/ppermute | solution.py:595
  86.5 2.2 %project.1 = (bf16[16,56,128]{2,1,0:T(8,128)(2,1)S(1)}, bf16[16,56,128]{2,1,0:T(8,128)(2,1)S(1)}) custom-call(bf16[528,128]{1,0:T(8,128)(2,1)S(1)} %get-tuple-element.33.refs_0_, bf16[528,128]{1,0:T(8,128)(2,1)S(1)} %collective-permute-done.20.refs_1_, bf16[528,128]{1,0:T(8,128)(2,1)S(1)} %collective-permute-done.21.refs_2_, ...), custom_call_target="tpu_custom_call" | custom-call | bytes 9000000 | tf_op jit(solution)/shard_map/project/pallas_call | solution.py:464
  88.6 3.1 %collective-permute-start.23 = (bf16[16,56,128]{2,1,0:T(8,128)(2,1)S(1)}, bf16[16,56,128]{2,1,0:T(8,128)(2,1)S(1)}, u32[]{:S(2)}, u32[]{:S(2)}) collective-permute-start(bf16[16,56,128]{2,1,0:T(8,128)(2,1)S(1)} %get-tuple-element.38), channel_id=1, source_target_pairs={{0,1},{1,0},{2,3},{3,2},{4,5},{5,4},{6,7},{7,6},{8,9},{9,8},{10,11... | collective-permute-start | bytes 688136 | tf_op jit(solution)/shard_map/ppermute | solution.py:592
  91.7 1.1 collective-permute-done.23.other
  92.9 13.9 %all_to_all.15.got = bf16[16,56,128]{2,1,0:T(8,128)(2,1)S(1)} all-to-all(bf16[16,56,128]{2,1,0:T(8,128)(2,1)S(1)} %add.16), channel_id=1, replica_groups={{0,2,4,6,8,10,12,14,16,18,20,22,24,26,28,30},{1,3,5,7,9,11,13,15,17,19,..., dimensions={0} | all-to-all | bytes 458752 | tf_op jit(solution)/shard_map/all_to_all | solution.py:644
  107.1 10.0 %all_to_all.16.refs_0_ = bf16[16,56,128]{2,1,0:T(8,128)(2,1)S(1)} all-to-all(bf16[16,56,128]{2,1,0:T(8,128)(2,1)S(1)} %get-tuple-element.42), channel_id=1, replica_groups={{0,2,4,6,8,10,12,14,16,18,20,22,24,26,28,30},{1,3,5,7,9,11,13,15,17,19,..., dimensions={0} | all-to-all | bytes 458752 | tf_op jit(solution)/shard_map/all_to_all | solution.py:644
  117.0 3.0 %collective-permute-start.24 = (bf16[16,56,128]{2,1,0:T(8,128)(2,1)S(1)}, bf16[16,56,128]{2,1,0:T(8,128)(2,1)S(1)}, u32[]{:S(2)}, u32[]{:S(2)}) collective-permute-start(bf16[16,56,128]{2,1,0:T(8,128)(2,1)S(1)} %all_to_all.16.refs_0_), channel_id=1, source_target_pairs={{0,1},{1,0},{2,3},{3,2},{4,5},{5,4},{6,7},{7,6},{8,9},{9,8},{10,11... | collective-permute-start | bytes 688136 | tf_op jit(solution)/shard_map/ppermute | solution.py:592
  120.1 1.1 collective-permute-done.24.refs_1_
  121.2 2.9 %ffn.1 = (bf16[16,56,128]{2,1,0:T(8,128)(2,1)S(1)}, bf16[16,56,128]{2,1,0:T(8,128)(2,1)S(1)}) custom-call(bf16[16,56,128]{2,1,0:T(8,128)(2,1)S(1)} %all_to_all.16.refs_0_, bf16[16,56,128]{2,1,0:T(8,128)(2,1)S(1)} %collective-permute-done.24.refs_1_, bf16[7168,384]{1,0:T(8,128)(2,1)S(1)} %bitcast.8, bf16[7168,384]{1,0:T(8,128)(2,1)S(1)} %bitcast.10, ...), custom_call_target="tpu_custom_call" | custom-call | bytes 17000000 | tf_op jit(solution)/shard_map/ffn/pallas_call | solution.py:549
  125.8 10.4 %all_to_all.17 = bf16[16,56,128]{2,1,0:T(8,128)(2,1)S(1)} all-to-all(bf16[16,56,128]{2,1,0:T(8,128)(2,1)S(1)} %add.17), channel_id=1, replica_groups={{0,2,4,6,8,10,12,14,16,18,20,22,24,26,28,30},{1,3,5,7,9,11,13,15,17,19,..., dimensions={0} | all-to-all | bytes 458752 | tf_op jit(solution)/shard_map/all_to_all | solution.py:644
  (74 shorter events, 17.0 us)
Async XLA Ops:
  0.0 30.5 %collective-permute-start.10 = (bf16[8,576,128]{2,1,0:T(8,128)(2,1)}, bf16[8,576,128]{2,1,0:T(8,128)(2,1)S(1)}, u32[]{:S(2)}, u32[]{:S(2)}) collective-permute-start(bf16[8,576,128]{2,1,0:T(8,128)(2,1)} %refs_4_.3), channel_id=1, source_target_pairs={{96,0},{0,32},{32,64},{64,96},{97,1},{1,33},{33,65},{65,97},{98,2}... | collective-permute-start | bytes 3538952 | tf_op jit(solution)/shard_map/ppermute | solution.py:601
  2.5 30.2 %collective-permute-start.8 = (bf16[8,576,128]{2,1,0:T(8,128)(2,1)}, bf16[8,576,128]{2,1,0:T(8,128)(2,1)S(1)}, u32[]{:S(2)}, u32[]{:S(2)}) collective-permute-start(bf16[8,576,128]{2,1,0:T(8,128)(2,1)} %refs_4_.3), channel_id=1, source_target_pairs={{32,0},{64,32},{96,64},{0,96},{33,1},{65,33},{97,65},{1,97},{34,2}... | collective-permute-start | bytes 3538952 | tf_op jit(solution)/shard_map/ppermute | solution.py:600
  4.7 2.2 %collective-permute-start.1 = (bf16[576,128]{1,0:T(8,128)(2,1)}, bf16[576,128]{1,0:T(8,128)(2,1)S(1)}, u32[]{:S(2)}, u32[]{:S(2)}) collective-permute-start(bf16[576,128]{1,0:T(8,128)(2,1)} %bitcast.13), channel_id=1, source_target_pairs={{0,1},{1,0},{2,3},{3,2},{4,5},{5,4},{6,7},{7,6},{8,9},{9,8},{10,11... | collective-permute-start | bytes 442376 | tf_op jit(solution)/shard_map/ppermute | solution.py:592
  8.0 6.4 %collective-permute-start.4 = (bf16[1,576,128]{2,1,0:T(8,128)(2,1)S(1)}, bf16[1,576,128]{2,1,0:T(8,128)(2,1)S(1)}, u32[]{:S(2)}, u32[]{:S(2)}) collective-permute-start(bf16[1,576,128]{2,1,0:T(8,128)(2,1)S(1)} %turn.1.refs_0_), channel_id=1, source_target_pairs={{0,6},{1,25},{2,0},{3,27},{4,2},{5,29},{6,4},{7,31},{8,14},{9,1},{... | collective-permute-start | bytes 442376 | tf_op jit(solution)/shard_map/ppermute | solution.py:595
  10.8 5.8 %collective-permute-start.3 = (bf16[1,576,128]{2,1,0:T(8,128)(2,1)S(1)}, bf16[1,576,128]{2,1,0:T(8,128)(2,1)S(1)}, u32[]{:S(2)}, u32[]{:S(2)}) collective-permute-start(bf16[1,576,128]{2,1,0:T(8,128)(2,1)S(1)} %turn.1.refs_0_), channel_id=1, source_target_pairs={{0,4},{1,17},{2,6},{3,19},{4,0},{5,21},{6,2},{7,23},{8,12},{9,25},... | collective-permute-start | bytes 442376 | tf_op jit(solution)/shard_map/ppermute | solution.py:595
  11.1 7.0 %collective-permute-start.2 = (bf16[1,576,128]{2,1,0:T(8,128)(2,1)S(1)}, bf16[1,576,128]{2,1,0:T(8,128)(2,1)S(1)}, u32[]{:S(2)}, u32[]{:S(2)}) collective-permute-start(bf16[1,576,128]{2,1,0:T(8,128)(2,1)S(1)} %turn.1.refs_0_), channel_id=1, source_target_pairs={{0,2},{1,9},{2,4},{3,11},{4,6},{5,13},{6,0},{7,15},{8,10},{9,17},{... | collective-permute-start | bytes 442376 | tf_op jit(solution)/shard_map/ppermute | solution.py:595
  19.0 17.5 %collective-permute-start.7 = (bf16[4,576,128]{2,1,0:T(8,128)(2,1)S(1)}, bf16[4,576,128]{2,1,0:T(8,128)(2,1)S(1)}, u32[]{:S(2)}, u32[]{:S(2)}) collective-permute-start(bf16[4,576,128]{2,1,0:T(8,128)(2,1)S(1)} %join.1.refs_0_), channel_id=1, source_target_pairs={{0,24},{1,7},{2,26},{3,1},{4,28},{5,3},{6,30},{7,5},{8,0},{9,15},{... | collective-permute-start | bytes 1769480 | tf_op jit(solution)/shard_map/ppermute | solution.py:595
  21.5 15.6 %collective-permute-start.6 = (bf16[4,576,128]{2,1,0:T(8,128)(2,1)S(1)}, bf16[4,576,128]{2,1,0:T(8,128)(2,1)S(1)}, u32[]{:S(2)}, u32[]{:S(2)}) collective-permute-start(bf16[4,576,128]{2,1,0:T(8,128)(2,1)S(1)} %join.1.refs_0_), channel_id=1, source_target_pairs={{0,16},{1,5},{2,18},{3,7},{4,20},{5,1},{6,22},{7,3},{8,24},{9,13},... | collective-permute-start | bytes 1769480 | tf_op jit(solution)/shard_map/ppermute | solution.py:595
  22.0 16.4 %collective-permute-start.5 = (bf16[4,576,128]{2,1,0:T(8,128)(2,1)S(1)}, bf16[4,576,128]{2,1,0:T(8,128)(2,1)S(1)}, u32[]{:S(2)}, u32[]{:S(2)}) collective-permute-start(bf16[4,576,128]{2,1,0:T(8,128)(2,1)S(1)} %join.1.refs_0_), channel_id=1, source_target_pairs={{0,8},{1,3},{2,10},{3,5},{4,12},{5,7},{6,14},{7,1},{8,16},{9,11},{... | collective-permute-start | bytes 1769480 | tf_op jit(solution)/shard_map/ppermute | solution.py:595
  30.5 3.3 %collective-permute-start = (s32[1,128]{1,0:T(1,128)S(1)}, s32[1,128]{1,0:T(1,128)S(1)}, u32[]{:S(2)}, u32[]{:S(2)}) collective-permute-start(s32[1,128]{1,0:T(1,128)S(1)} %add_bitcast_fusion.code_own), channel_id=1, source_target_pairs={{0,1},{1,0},{2,3},{3,2},{4,5},{5,4},{6,7},{7,6},{8,9},{9,8},{10,11... | collective-permute-start | bytes 1544 | tf_op jit(solution)/shard_map/ppermute | solution.py:592
  32.7 16.6 %collective-permute-start.11 = (bf16[4,576,128]{2,1,0:T(8,128)(2,1)}, bf16[4,576,128]{2,1,0:T(8,128)(2,1)}, u32[]{:S(2)}, u32[]{:S(2)}) collective-permute-start(bf16[4,576,128]{2,1,0:T(8,128)(2,1)} %cut.3), channel_id=1, source_target_pairs={{96,0},{0,32},{32,64},{64,96},{97,1},{1,33},{33,65},{65,97},{98,2}... | collective-permute-start | bytes 1769480 | tf_op jit(solution)/shard_map/ppermute | solution.py:605
  33.8 16.3 %collective-permute-start.9 = (bf16[4,576,128]{2,1,0:T(8,128)(2,1)}, bf16[4,576,128]{2,1,0:T(8,128)(2,1)}, u32[]{:S(2)}, u32[]{:S(2)}) collective-permute-start(bf16[4,576,128]{2,1,0:T(8,128)(2,1)} %cut.2), channel_id=1, source_target_pairs={{32,0},{64,32},{96,64},{0,96},{33,1},{65,33},{97,65},{1,97},{34,2}... | collective-permute-start | bytes 1769480 | tf_op jit(solution)/shard_map/ppermute | solution.py:604
  36.5 14.8 %collective-permute-start.12 = (bf16[8,576,128]{2,1,0:T(8,128)(2,1)}, bf16[8,576,128]{2,1,0:T(8,128)(2,1)}, u32[]{:S(2)}, u32[]{:S(2)}) collective-permute-start(bf16[8,576,128]{2,1,0:T(8,128)(2,1)} %refs_4_.3), channel_id=1, source_target_pairs={{0,1},{1,0},{2,3},{3,2},{4,5},{5,4},{6,7},{7,6},{8,9},{9,8},{10,11... | collective-permute-start | bytes 3538952 | tf_op jit(solution)/shard_map/ppermute | solution.py:592
  37.1 14.8 %collective-permute-start.16 = (bf16[8,576,128]{2,1,0:T(8,128)(2,1)S(1)}, bf16[8,576,128]{2,1,0:T(8,128)(2,1)}, u32[]{:S(2)}, u32[]{:S(2)}) collective-permute-start(bf16[8,576,128]{2,1,0:T(8,128)(2,1)S(1)} %collective-permute-done.10.blocks.refs_8_), channel_id=1, source_target_pairs={{0,1},{1,0},{2,3},{3,2},{4,5},{5,4},{6,7},{7,6},{8,9},{9,8},{10,11... | collective-permute-start | bytes 3538952 | tf_op jit(solution)/shard_map/ppermute | solution.py:592
  38.5 14.3 %collective-permute-start.13 = (bf16[8,576,128]{2,1,0:T(8,128)(2,1)S(1)}, bf16[8,576,128]{2,1,0:T(8,128)(2,1)S(1)}, u32[]{:S(2)}, u32[]{:S(2)}) collective-permute-start(bf16[8,576,128]{2,1,0:T(8,128)(2,1)S(1)} %collective-permute-done.8.blocks.refs_5_), channel_id=1, source_target_pairs={{0,1},{1,0},{2,3},{3,2},{4,5},{5,4},{6,7},{7,6},{8,9},{9,8},{10,11... | collective-permute-start | bytes 3538952 | tf_op jit(solution)/shard_map/ppermute | solution.py:592
  49.3 2.6 %collective-permute-start.15 = (bf16[4,576,128]{2,1,0:T(8,128)(2,1)}, bf16[4,576,128]{2,1,0:T(8,128)(2,1)S(1)}, u32[]{:S(2)}, u32[]{:S(2)}) collective-permute-start(bf16[4,576,128]{2,1,0:T(8,128)(2,1)} %collective-permute-done.11.refs_7_), channel_id=1, source_target_pairs={{0,1},{1,0},{2,3},{3,2},{4,5},{5,4},{6,7},{7,6},{8,9},{9,8},{10,11... | collective-permute-start | bytes 1769480 | tf_op jit(solution)/shard_map/ppermute | solution.py:592
  50.1 2.7 %collective-permute-start.14 = (bf16[4,576,128]{2,1,0:T(8,128)(2,1)}, bf16[4,576,128]{2,1,0:T(8,128)(2,1)S(1)}, u32[]{:S(2)}, u32[]{:S(2)}) collective-permute-start(bf16[4,576,128]{2,1,0:T(8,128)(2,1)} %collective-permute-done.9.refs_6_), channel_id=1, source_target_pairs={{0,1},{1,0},{2,3},{3,2},{4,5},{5,4},{6,7},{7,6},{8,9},{9,8},{10,11... | collective-permute-start | bytes 1769480 | tf_op jit(solution)/shard_map/ppermute | solution.py:592
  61.5 10.1 %collective-permute-start.17 = (bf16[4,528,128]{2,1,0:T(8,128)(2,1)S(1)}, bf16[4,528,128]{2,1,0:T(8,128)(2,1)S(1)}, u32[]{:S(2)}, u32[]{:S(2)}) collective-permute-start(bf16[4,528,128]{2,1,0:T(8,128)(2,1)S(1)} %get-tuple-element.30), channel_id=1, source_target_pairs={{0,4},{1,17},{2,6},{3,19},{4,0},{5,21},{6,2},{7,23},{8,12},{9,25},... | collective-permute-start | bytes 1622024 | tf_op jit(solution)/shard_map/ppermute | solution.py:595
  64.5 12.9 %collective-permute-start.18 = (bf16[4,528,128]{2,1,0:T(8,128)(2,1)S(1)}, bf16[4,528,128]{2,1,0:T(8,128)(2,1)S(1)}, u32[]{:S(2)}, u32[]{:S(2)}) collective-permute-start(bf16[4,528,128]{2,1,0:T(8,128)(2,1)S(1)} %get-tuple-element.31), channel_id=1, source_target_pairs={{0,2},{1,9},{2,4},{3,11},{4,6},{5,13},{6,0},{7,15},{8,10},{9,17},{... | collective-permute-start | bytes 1622024 | tf_op jit(solution)/shard_map/ppermute | solution.py:595
  64.9 12.9 %collective-permute-start.19 = (bf16[4,528,128]{2,1,0:T(8,128)(2,1)S(1)}, bf16[4,528,128]{2,1,0:T(8,128)(2,1)S(1)}, u32[]{:S(2)}, u32[]{:S(2)}) collective-permute-start(bf16[4,528,128]{2,1,0:T(8,128)(2,1)S(1)} %get-tuple-element.32), channel_id=1, source_target_pairs={{0,6},{1,25},{2,0},{3,27},{4,2},{5,29},{6,4},{7,31},{8,14},{9,1},{... | collective-permute-start | bytes 1622024 | tf_op jit(solution)/shard_map/ppermute | solution.py:595
  67.2 54.0 %slice-start.2 = ((s8[5505024]{0:T(1024)(128)(4,1)}), s8[4194304]{0:T(1024)(128)(4,1)S(1)}, s32[]{:S(2)}) async-start(s8[5505024]{0:T(1024)(128)(4,1)} %bitcast.9), calls=%async_computation.5 | async-start | bytes 8388608
  67.2 54.0 %slice-start.4 = ((s8[5505024]{0:T(1024)(128)(4,1)}), s8[4194304]{0:T(1024)(128)(4,1)S(1)}, s32[]{:S(2)}) async-start(s8[5505024]{0:T(1024)(128)(4,1)} %bitcast.11), calls=%async_computation.7 | async-start | bytes 8388608
  70.4 50.8 %slice-start.3 = ((s8[5505024]{0:T(1024)(128)(4,1)}), s8[1310720]{0:T(1024)(128)(4,1)S(1)}, s32[]{:S(2)}) async-start(s8[5505024]{0:T(1024)(128)(4,1)} %bitcast.9), calls=%async_computation.6 | async-start | bytes 2621440
  70.4 50.8 %slice-start.5 = ((s8[5505024]{0:T(1024)(128)(4,1)}), s8[1310720]{0:T(1024)(128)(4,1)S(1)}, s32[]{:S(2)}) async-start(s8[5505024]{0:T(1024)(128)(4,1)} %bitcast.11), calls=%async_computation.8 | async-start | bytes 2621440
  78.8 5.7 %collective-permute-start.20 = (bf16[528,128]{1,0:T(8,128)(2,1)S(1)}, bf16[528,128]{1,0:T(8,128)(2,1)S(1)}, u32[]{:S(2)}, u32[]{:S(2)}) collective-permute-start(bf16[528,128]{1,0:T(8,128)(2,1)S(1)} %get-tuple-element.34), channel_id=1, source_target_pairs={{0,16},{1,5},{2,18},{3,7},{4,20},{5,1},{6,22},{7,3},{8,24},{9,13},... | collective-permute-start | bytes 405512 | tf_op jit(solution)/shard_map/ppermute | solution.py:595
  81.4 5.1 %collective-permute-start.21 = (bf16[528,128]{1,0:T(8,128)(2,1)S(1)}, bf16[528,128]{1,0:T(8,128)(2,1)S(1)}, u32[]{:S(2)}, u32[]{:S(2)}) collective-permute-start(bf16[528,128]{1,0:T(8,128)(2,1)S(1)} %get-tuple-element.35), channel_id=1, source_target_pairs={{0,8},{1,3},{2,10},{3,5},{4,12},{5,7},{6,14},{7,1},{8,16},{9,11},{... | collective-permute-start | bytes 405512 | tf_op jit(solution)/shard_map/ppermute | solution.py:595
  82.0 4.5 %collective-permute-start.22 = (bf16[528,128]{1,0:T(8,128)(2,1)S(1)}, bf16[528,128]{1,0:T(8,128)(2,1)S(1)}, u32[]{:S(2)}, u32[]{:S(2)}) collective-permute-start(bf16[528,128]{1,0:T(8,128)(2,1)S(1)} %get-tuple-element.36), channel_id=1, source_target_pairs={{0,24},{1,7},{2,26},{3,1},{4,28},{5,3},{6,30},{7,5},{8,0},{9,15},{... | collective-permute-start | bytes 405512 | tf_op jit(solution)/shard_map/ppermute | solution.py:595
  86.4 34.8 %slice-start = ((s8[5505024]{0:T(1024)(128)(4,1)}), s8[4194304]{0:T(1024)(128)(4,1)S(1)}, s32[]{:S(2)}) async-start(s8[5505024]{0:T(1024)(128)(4,1)} %bitcast.7), calls=%async_computation.3 | async-start | bytes 8388608
  86.4 34.8 %slice-start.1 = ((s8[5505024]{0:T(1024)(128)(4,1)}), s8[1310720]{0:T(1024)(128)(4,1)S(1)}, s32[]{:S(2)}) async-start(s8[5505024]{0:T(1024)(128)(4,1)} %bitcast.7), calls=%async_computation.4 | async-start | bytes 2621440
  88.6 4.2 %collective-permute-start.23 = (bf16[16,56,128]{2,1,0:T(8,128)(2,1)S(1)}, bf16[16,56,128]{2,1,0:T(8,128)(2,1)S(1)}, u32[]{:S(2)}, u32[]{:S(2)}) collective-permute-start(bf16[16,56,128]{2,1,0:T(8,128)(2,1)S(1)} %get-tuple-element.38), channel_id=1, source_target_pairs={{0,1},{1,0},{2,3},{3,2},{4,5},{5,4},{6,7},{7,6},{8,9},{9,8},{10,11... | collective-permute-start | bytes 688136 | tf_op jit(solution)/shard_map/ppermute | solution.py:592
  117.0 4.1 %collective-permute-start.24 = (bf16[16,56,128]{2,1,0:T(8,128)(2,1)S(1)}, bf16[16,56,128]{2,1,0:T(8,128)(2,1)S(1)}, u32[]{:S(2)}, u32[]{:S(2)}) collective-permute-start(bf16[16,56,128]{2,1,0:T(8,128)(2,1)S(1)} %all_to_all.16.refs_0_), channel_id=1, source_target_pairs={{0,1},{1,0},{2,3},{3,2},{4,5},{5,4},{6,7},{7,6},{8,9},{9,8},{10,11... | collective-permute-start | bytes 688136 | tf_op jit(solution)/shard_map/ppermute | solution.py:592
  124.1 1.6 %collective-permute-start.25 = (bf16[16,56,128]{2,1,0:T(8,128)(2,1)S(1)}, bf16[16,56,128]{2,1,0:T(8,128)(2,1)S(1)}, u32[]{:S(2)}, u32[]{:S(2)}) collective-permute-start(bf16[16,56,128]{2,1,0:T(8,128)(2,1)S(1)} %get-tuple-element.44), channel_id=1, source_target_pairs={{0,1},{1,0},{2,3},{3,2},{4,5},{5,4},{6,7},{7,6},{8,9},{9,8},{10,11... | collective-permute-start | bytes 688136 | tf_op jit(solution)/shard_map/ppermute | solution.py:592
  (10 other events, 122.3 us)

commit v9 on v8

--- a/solution.py
+++ b/solution.py
@@ -561,6 +561,26 @@
     )(*[in_vmem(one) for one in normed], w_gate, w_up, w_down)
 
 
+def finish_kernel(kept, got, out):
+    total = kept[...]
+    for s in range(got.shape[0]):
+        total = total + got[s].astype(jnp.float32)
+    for n in range(total.shape[0]):
+        out[:, n * LANES : (n + 1) * LANES] = total[n : n + 1, :]
+
+
+def finish(kept, got):
+    return pl.pallas_call(
+        finish_kernel,
+        out_shape=jax.ShapeDtypeStruct((1, kept.size), jnp.float32),
+        in_specs=[vmem_spec] * 2,
+        out_specs=vmem_spec,
+        compiler_params=pltpu.CompilerParams(vmem_limit_bytes=4 * MIB),
+        cost_estimate=moves(300000),
+        name="finish",
+    )(in_vmem(kept), in_vmem(got))
+
+
 def body(
     queries,
     cache_pool,
@@ -653,7 +673,7 @@
     )
     rows = exchange(normed)
     down = to_rows(*ffn((rows, swapped(rows)), w_gate, w_up, w_down))
-    return (residual_sum + jnp.sum(down.astype(jnp.float32), axis=0)).reshape(1, features)
+    return finish(residual_sum, down)
 
 
 def solution(mesh):

time: 137 us -> 137 us (level)
  no operation moved by 1% of the time
where the time goes in v9:
time: 137 us
  waiting for transfers between devices  39.3 us (29%)
  starting transfers between devices  38.9 us (28%)
  blocking collectives  34.3 us (25%)
  Pallas kernels  22 us (16%)
    all_to_all x3, blocking collectives, exchange(): lax.all_to_all(value, 'tensor', split_axis=0, concat_axis=0, tiled=True,...  34.3 us
    ppermute x12, starting transfers between devices, along(): return lax.ppermute(value, 'tensor', shifts(tensors, first, distance))  18.3 us
    ppermute x12, waiting for transfers between devices, along(): return lax.ppermute(value, 'tensor', shifts(tensors, first, distance))  17.2 us
    ppermute x10, starting transfers between devices, swapped(): return lax.ppermute(value, 'tensor', swap)  13.1 us
    pallas_call x1, Pallas kernels, attend(): pl.pallas_call(functools.partial(attend_kernel, dims), out_shape=(pltpu.V...  8.76 us
    ppermute x1, waiting for transfers between devices, body(): far_high = lax.ppermute(cut(previous, slots // 2), 'dp', from_prev)  8.27 us
    ppermute x1, waiting for transfers between devices, body(): previous = lax.ppermute(cache_pool, 'dp', from_prev)  7.85 us
    ppermute x10, waiting for transfers between devices, swapped(): return lax.ppermute(value, 'tensor', swap)  6.03 us
  transfers between devices with their start and end apart: 26, of which 17 were waited for; matrix products, arithmetic and copies ran while one was open for 1% of the time, Pallas kernels for 5%

profile of v9, /device:TPU:1, one launch (start us, length us, event | category | flops | bytes accessed | tf_op | source)
XLA Modules:
  0.0 136.9 jit_solution(734766298939199290)
XLA Ops:
  0.0 2.5 %collective-permute-start.10 = (bf16[8,576,128]{2,1,0:T(8,128)(2,1)}, bf16[8,576,128]{2,1,0:T(8,128)(2,1)S(1)}, u32[]{:S(2)}, u32[]{:S(2)}) collective-permute-start(bf16[8,576,128]{2,1,0:T(8,128)(2,1)} %refs_4_.3), channel_id=1, source_target_pairs={{96,0},{0,32},{32,64},{64,96},{97,1},{1,33},{33,65},{65,97},{98,2}... | collective-permute-start | bytes 3538952 | tf_op jit(solution)/shard_map/ppermute | solution.py:621
  2.5 2.2 %collective-permute-start.8 = (bf16[8,576,128]{2,1,0:T(8,128)(2,1)}, bf16[8,576,128]{2,1,0:T(8,128)(2,1)S(1)}, u32[]{:S(2)}, u32[]{:S(2)}) collective-permute-start(bf16[8,576,128]{2,1,0:T(8,128)(2,1)} %refs_4_.3), channel_id=1, source_target_pairs={{32,0},{64,32},{96,64},{0,96},{33,1},{65,33},{97,65},{1,97},{34,2}... | collective-permute-start | bytes 3538952 | tf_op jit(solution)/shard_map/ppermute | solution.py:620
  5.6 1.2 collective-permute-done.1.other
  8.0 2.8 %collective-permute-start.4 = (bf16[1,576,128]{2,1,0:T(8,128)(2,1)S(1)}, bf16[1,576,128]{2,1,0:T(8,128)(2,1)S(1)}, u32[]{:S(2)}, u32[]{:S(2)}) collective-permute-start(bf16[1,576,128]{2,1,0:T(8,128)(2,1)S(1)} %turn.1.refs_0_), channel_id=1, source_target_pairs={{0,6},{1,25},{2,0},{3,27},{4,2},{5,29},{6,4},{7,31},{8,14},{9,1},{... | collective-permute-start | bytes 442376 | tf_op jit(solution)/shard_map/ppermute | solution.py:615
  11.8 2.6 %collective-permute-done.4.refs_3_ = bf16[1,576,128]{2,1,0:T(8,128)(2,1)S(1)} collective-permute-done((bf16[1,576,128]{2,1,0:T(8,128)(2,1)S(1)}, bf16[1,576,128]{2,1,0:T(8,128)(2,1)S(1)}, u32[]{:S(2)}, u32[]{:S(2)}) %collective-permute-start.4) | collective-permute-done | bytes 147488 | tf_op jit(solution)/shard_map/ppermute | solution.py:615
  14.5 2.1 %collective-permute-done.3.refs_2_ = bf16[1,576,128]{2,1,0:T(8,128)(2,1)S(1)} collective-permute-done((bf16[1,576,128]{2,1,0:T(8,128)(2,1)S(1)}, bf16[1,576,128]{2,1,0:T(8,128)(2,1)S(1)}, u32[]{:S(2)}, u32[]{:S(2)}) %collective-permute-start.3) | collective-permute-done | bytes 147488 | tf_op jit(solution)/shard_map/ppermute | solution.py:615
  16.6 1.6 %collective-permute-done.2.refs_1_ = bf16[1,576,128]{2,1,0:T(8,128)(2,1)S(1)} collective-permute-done((bf16[1,576,128]{2,1,0:T(8,128)(2,1)S(1)}, bf16[1,576,128]{2,1,0:T(8,128)(2,1)S(1)}, u32[]{:S(2)}, u32[]{:S(2)}) %collective-permute-start.2) | collective-permute-done | bytes 147488 | tf_op jit(solution)/shard_map/ppermute | solution.py:615
  19.0 2.5 %collective-permute-start.7 = (bf16[4,576,128]{2,1,0:T(8,128)(2,1)S(1)}, bf16[4,576,128]{2,1,0:T(8,128)(2,1)S(1)}, u32[]{:S(2)}, u32[]{:S(2)}) collective-permute-start(bf16[4,576,128]{2,1,0:T(8,128)(2,1)S(1)} %join.1.refs_0_), channel_id=1, source_target_pairs={{0,24},{1,7},{2,26},{3,1},{4,28},{5,3},{6,30},{7,5},{8,0},{9,15},{... | collective-permute-start | bytes 1769480 | tf_op jit(solution)/shard_map/ppermute | solution.py:615
  22.6 7.8 %collective-permute-done.10.blocks.refs_8_ = bf16[8,576,128]{2,1,0:T(8,128)(2,1)S(1)} collective-permute-done((bf16[8,576,128]{2,1,0:T(8,128)(2,1)}, bf16[8,576,128]{2,1,0:T(8,128)(2,1)S(1)}, u32[]{:S(2)}, u32[]{:S(2)}) %collective-permute-start.10) | collective-permute-done | bytes 1179680 | tf_op jit(solution)/shard_map/ppermute | solution.py:621
  30.5 1.2 collective-permute-start
  33.8 2.7 %collective-permute-start.9 = (bf16[4,576,128]{2,1,0:T(8,128)(2,1)}, bf16[4,576,128]{2,1,0:T(8,128)(2,1)}, u32[]{:S(2)}, u32[]{:S(2)}) collective-permute-start(bf16[4,576,128]{2,1,0:T(8,128)(2,1)} %cut.2), channel_id=1, source_target_pairs={{32,0},{64,32},{96,64},{0,96},{33,1},{65,33},{97,65},{1,97},{34,2}... | collective-permute-start | bytes 1769480 | tf_op jit(solution)/shard_map/ppermute | solution.py:624
  37.3 1.1 collective-permute-done.5.refs_1_
  38.5 2.5 %collective-permute-start.13 = (bf16[8,576,128]{2,1,0:T(8,128)(2,1)S(1)}, bf16[8,576,128]{2,1,0:T(8,128)(2,1)S(1)}, u32[]{:S(2)}, u32[]{:S(2)}) collective-permute-start(bf16[8,576,128]{2,1,0:T(8,128)(2,1)S(1)} %collective-permute-done.8.blocks.refs_5_), channel_id=1, source_target_pairs={{0,1},{1,0},{2,3},{3,2},{4,5},{5,4},{6,7},{7,6},{8,9},{9,8},{10,11... | collective-permute-start | bytes 3538952 | tf_op jit(solution)/shard_map/ppermute | solution.py:612
  41.0 8.3 %collective-permute-done.11.refs_7_ = bf16[4,576,128]{2,1,0:T(8,128)(2,1)} collective-permute-done((bf16[4,576,128]{2,1,0:T(8,128)(2,1)}, bf16[4,576,128]{2,1,0:T(8,128)(2,1)}, u32[]{:S(2)}, u32[]{:S(2)}) %collective-permute-start.11) | collective-permute-done | bytes 589856 | tf_op jit(solution)/shard_map/ppermute | solution.py:625
  52.7 8.8 %attend.1 = (bf16[4,528,128]{2,1,0:T(8,128)(2,1)S(1)}, bf16[4,528,128]{2,1,0:T(8,128)(2,1)S(1)}, bf16[4,528,128]{2,1,0:T(8,128)(2,1)S(1)}, bf16[4,528,128]{2,1,0:T(8,128)(2,1)S(1)}) custom-call(s32[1,128]{1,0:T(1,128)S(1)} %add_bitcast_fusion.code_own, s32[1,128]{1,0:T(1,128)S(1)} %collective-permute-done.code_other, s32[1,128]{1,0:T(1,128)S(1)} %bitcast.16, ...), custom_call_target="tpu_custom_call" | custom-call | bytes 20000000 | tf_op jit(solution)/shard_map/attend/pallas_call | solution.py:306
  61.5 3.0 %collective-permute-start.17 = (bf16[4,528,128]{2,1,0:T(8,128)(2,1)S(1)}, bf16[4,528,128]{2,1,0:T(8,128)(2,1)S(1)}, u32[]{:S(2)}, u32[]{:S(2)}) collective-permute-start(bf16[4,528,128]{2,1,0:T(8,128)(2,1)S(1)} %get-tuple-element.30), channel_id=1, source_target_pairs={{0,4},{1,17},{2,6},{3,19},{4,0},{5,21},{6,2},{7,23},{8,12},{9,25},... | collective-permute-start | bytes 1622024 | tf_op jit(solution)/shard_map/ppermute | solution.py:615
  64.9 2.3 %collective-permute-start.19 = (bf16[4,528,128]{2,1,0:T(8,128)(2,1)S(1)}, bf16[4,528,128]{2,1,0:T(8,128)(2,1)S(1)}, u32[]{:S(2)}, u32[]{:S(2)}) collective-permute-start(bf16[4,528,128]{2,1,0:T(8,128)(2,1)S(1)} %get-tuple-element.32), channel_id=1, source_target_pairs={{0,6},{1,25},{2,0},{3,27},{4,2},{5,29},{6,4},{7,31},{8,14},{9,1},{... | collective-permute-start | bytes 1622024 | tf_op jit(solution)/shard_map/ppermute | solution.py:615
  67.2 3.2 %fetch.1.refs_4_.refs_5_ = bf16[512,7168]{1,0:T(8,128)(2,1)S(1)} custom-call(bf16[512,7168]{1,0:T(8,128)(2,1)} %weight.1, bf16[4,528,128]{2,1,0:T(8,128)(2,1)S(1)} %get-tuple-element.29._.refs_0_), custom_call_target="tpu_custom_call" | custom-call | bytes 14680064 | tf_op jit(solution)/shard_map/fetch/pallas_call | solution.py:62
  70.5 1.2 collective-permute-done.17.refs_1_
  71.6 5.7 %collective-permute-done.18.refs_2_ = bf16[4,528,128]{2,1,0:T(8,128)(2,1)S(1)} collective-permute-done((bf16[4,528,128]{2,1,0:T(8,128)(2,1)S(1)}, bf16[4,528,128]{2,1,0:T(8,128)(2,1)S(1)}, u32[]{:S(2)}, u32[]{:S(2)}) %collective-permute-start.18) | collective-permute-done | bytes 540704 | tf_op jit(solution)/shard_map/ppermute | solution.py:615
  78.8 2.5 %collective-permute-start.20 = (bf16[528,128]{1,0:T(8,128)(2,1)S(1)}, bf16[528,128]{1,0:T(8,128)(2,1)S(1)}, u32[]{:S(2)}, u32[]{:S(2)}) collective-permute-start(bf16[528,128]{1,0:T(8,128)(2,1)S(1)} %get-tuple-element.34), channel_id=1, source_target_pairs={{0,16},{1,5},{2,18},{3,7},{4,20},{5,1},{6,22},{7,3},{8,24},{9,13},... | collective-permute-start | bytes 405512 | tf_op jit(solution)/shard_map/ppermute | solution.py:615
  82.0 2.1 %collective-permute-start.22 = (bf16[528,128]{1,0:T(8,128)(2,1)S(1)}, bf16[528,128]{1,0:T(8,128)(2,1)S(1)}, u32[]{:S(2)}, u32[]{:S(2)}) collective-permute-start(bf16[528,128]{1,0:T(8,128)(2,1)S(1)} %get-tuple-element.36), channel_id=1, source_target_pairs={{0,24},{1,7},{2,26},{3,1},{4,28},{5,3},{6,30},{7,5},{8,0},{9,15},{... | collective-permute-start | bytes 405512 | tf_op jit(solution)/shard_map/ppermute | solution.py:615
  84.6 1.9 %collective-permute-done.21.refs_2_ = bf16[528,128]{1,0:T(8,128)(2,1)S(1)} collective-permute-done((bf16[528,128]{1,0:T(8,128)(2,1)S(1)}, bf16[528,128]{1,0:T(8,128)(2,1)S(1)}, u32[]{:S(2)}, u32[]{:S(2)}) %collective-permute-start.21) | collective-permute-done | bytes 135200 | tf_op jit(solution)/shard_map/ppermute | solution.py:615
  86.5 2.2 %project.1 = (bf16[16,56,128]{2,1,0:T(8,128)(2,1)S(1)}, bf16[16,56,128]{2,1,0:T(8,128)(2,1)S(1)}) custom-call(bf16[528,128]{1,0:T(8,128)(2,1)S(1)} %get-tuple-element.33.refs_0_, bf16[528,128]{1,0:T(8,128)(2,1)S(1)} %collective-permute-done.20.refs_1_, bf16[528,128]{1,0:T(8,128)(2,1)S(1)} %collective-permute-done.21.refs_2_, ...), custom_call_target="tpu_custom_call" | custom-call | bytes 9000000 | tf_op jit(solution)/shard_map/project/pallas_call | solution.py:464
  88.6 3.1 %collective-permute-start.23 = (bf16[16,56,128]{2,1,0:T(8,128)(2,1)S(1)}, bf16[16,56,128]{2,1,0:T(8,128)(2,1)S(1)}, u32[]{:S(2)}, u32[]{:S(2)}) collective-permute-start(bf16[16,56,128]{2,1,0:T(8,128)(2,1)S(1)} %get-tuple-element.38), channel_id=1, source_target_pairs={{0,1},{1,0},{2,3},{3,2},{4,5},{5,4},{6,7},{7,6},{8,9},{9,8},{10,11... | collective-permute-start | bytes 688136 | tf_op jit(solution)/shard_map/ppermute | solution.py:612
  91.8 1.1 collective-permute-done.23.other
  92.9 13.9 %all_to_all.15.got = bf16[16,56,128]{2,1,0:T(8,128)(2,1)S(1)} all-to-all(bf16[16,56,128]{2,1,0:T(8,128)(2,1)S(1)} %add.12), channel_id=1, replica_groups={{0,2,4,6,8,10,12,14,16,18,20,22,24,26,28,30},{1,3,5,7,9,11,13,15,17,19,..., dimensions={0} | all-to-all | bytes 458752 | tf_op jit(solution)/shard_map/all_to_all | solution.py:664
  107.1 10.0 %all_to_all.16.refs_0_ = bf16[16,56,128]{2,1,0:T(8,128)(2,1)S(1)} all-to-all(bf16[16,56,128]{2,1,0:T(8,128)(2,1)S(1)} %get-tuple-element.42), channel_id=1, replica_groups={{0,2,4,6,8,10,12,14,16,18,20,22,24,26,28,30},{1,3,5,7,9,11,13,15,17,19,..., dimensions={0} | all-to-all | bytes 458752 | tf_op jit(solution)/shard_map/all_to_all | solution.py:664
  117.1 3.0 %collective-permute-start.24 = (bf16[16,56,128]{2,1,0:T(8,128)(2,1)S(1)}, bf16[16,56,128]{2,1,0:T(8,128)(2,1)S(1)}, u32[]{:S(2)}, u32[]{:S(2)}) collective-permute-start(bf16[16,56,128]{2,1,0:T(8,128)(2,1)S(1)} %all_to_all.16.refs_0_), channel_id=1, source_target_pairs={{0,1},{1,0},{2,3},{3,2},{4,5},{5,4},{6,7},{7,6},{8,9},{9,8},{10,11... | collective-permute-start | bytes 688136 | tf_op jit(solution)/shard_map/ppermute | solution.py:612
  121.2 2.9 %ffn.1 = (bf16[16,56,128]{2,1,0:T(8,128)(2,1)S(1)}, bf16[16,56,128]{2,1,0:T(8,128)(2,1)S(1)}) custom-call(bf16[16,56,128]{2,1,0:T(8,128)(2,1)S(1)} %all_to_all.16.refs_0_, bf16[16,56,128]{2,1,0:T(8,128)(2,1)S(1)} %collective-permute-done.24.refs_1_, bf16[7168,384]{1,0:T(8,128)(2,1)S(1)} %bitcast.7, bf16[7168,384]{1,0:T(8,128)(2,1)S(1)} %bitcast.9, ...), custom_call_target="tpu_custom_call" | custom-call | bytes 17000000 | tf_op jit(solution)/shard_map/ffn/pallas_call | solution.py:549
  124.6 1.1 collective-permute-done.25.other
  125.8 10.4 %all_to_all.17.got = bf16[16,56,128]{2,1,0:T(8,128)(2,1)S(1)} all-to-all(bf16[16,56,128]{2,1,0:T(8,128)(2,1)S(1)} %add.13), channel_id=1, replica_groups={{0,2,4,6,8,10,12,14,16,18,20,22,24,26,28,30},{1,3,5,7,9,11,13,15,17,19,..., dimensions={0} | all-to-all | bytes 458752 | tf_op jit(solution)/shard_map/all_to_all | solution.py:664
  (73 shorter events, 17.0 us)
Async XLA Ops:
  0.0 30.5 %collective-permute-start.10 = (bf16[8,576,128]{2,1,0:T(8,128)(2,1)}, bf16[8,576,128]{2,1,0:T(8,128)(2,1)S(1)}, u32[]{:S(2)}, u32[]{:S(2)}) collective-permute-start(bf16[8,576,128]{2,1,0:T(8,128)(2,1)} %refs_4_.3), channel_id=1, source_target_pairs={{96,0},{0,32},{32,64},{64,96},{97,1},{1,33},{33,65},{65,97},{98,2}... | collective-permute-start | bytes 3538952 | tf_op jit(solution)/shard_map/ppermute | solution.py:621
  2.5 30.2 %collective-permute-start.8 = (bf16[8,576,128]{2,1,0:T(8,128)(2,1)}, bf16[8,576,128]{2,1,0:T(8,128)(2,1)S(1)}, u32[]{:S(2)}, u32[]{:S(2)}) collective-permute-start(bf16[8,576,128]{2,1,0:T(8,128)(2,1)} %refs_4_.3), channel_id=1, source_target_pairs={{32,0},{64,32},{96,64},{0,96},{33,1},{65,33},{97,65},{1,97},{34,2}... | collective-permute-start | bytes 3538952 | tf_op jit(solution)/shard_map/ppermute | solution.py:620
  4.7 2.2 %collective-permute-start.1 = (bf16[576,128]{1,0:T(8,128)(2,1)}, bf16[576,128]{1,0:T(8,128)(2,1)S(1)}, u32[]{:S(2)}, u32[]{:S(2)}) collective-permute-start(bf16[576,128]{1,0:T(8,128)(2,1)} %bitcast.12), channel_id=1, source_target_pairs={{0,1},{1,0},{2,3},{3,2},{4,5},{5,4},{6,7},{7,6},{8,9},{9,8},{10,11... | collective-permute-start | bytes 442376 | tf_op jit(solution)/shard_map/ppermute | solution.py:612
  8.0 6.4 %collective-permute-start.4 = (bf16[1,576,128]{2,1,0:T(8,128)(2,1)S(1)}, bf16[1,576,128]{2,1,0:T(8,128)(2,1)S(1)}, u32[]{:S(2)}, u32[]{:S(2)}) collective-permute-start(bf16[1,576,128]{2,1,0:T(8,128)(2,1)S(1)} %turn.1.refs_0_), channel_id=1, source_target_pairs={{0,6},{1,25},{2,0},{3,27},{4,2},{5,29},{6,4},{7,31},{8,14},{9,1},{... | collective-permute-start | bytes 442376 | tf_op jit(solution)/shard_map/ppermute | solution.py:615
  10.8 5.8 %collective-permute-start.3 = (bf16[1,576,128]{2,1,0:T(8,128)(2,1)S(1)}, bf16[1,576,128]{2,1,0:T(8,128)(2,1)S(1)}, u32[]{:S(2)}, u32[]{:S(2)}) collective-permute-start(bf16[1,576,128]{2,1,0:T(8,128)(2,1)S(1)} %turn.1.refs_0_), channel_id=1, source_target_pairs={{0,4},{1,17},{2,6},{3,19},{4,0},{5,21},{6,2},{7,23},{8,12},{9,25},... | collective-permute-start | bytes 442376 | tf_op jit(solution)/shard_map/ppermute | solution.py:615
  11.1 7.0 %collective-permute-start.2 = (bf16[1,576,128]{2,1,0:T(8,128)(2,1)S(1)}, bf16[1,576,128]{2,1,0:T(8,128)(2,1)S(1)}, u32[]{:S(2)}, u32[]{:S(2)}) collective-permute-start(bf16[1,576,128]{2,1,0:T(8,128)(2,1)S(1)} %turn.1.refs_0_), channel_id=1, source_target_pairs={{0,2},{1,9},{2,4},{3,11},{4,6},{5,13},{6,0},{7,15},{8,10},{9,17},{... | collective-permute-start | bytes 442376 | tf_op jit(solution)/shard_map/ppermute | solution.py:615
  19.0 17.5 %collective-permute-start.7 = (bf16[4,576,128]{2,1,0:T(8,128)(2,1)S(1)}, bf16[4,576,128]{2,1,0:T(8,128)(2,1)S(1)}, u32[]{:S(2)}, u32[]{:S(2)}) collective-permute-start(bf16[4,576,128]{2,1,0:T(8,128)(2,1)S(1)} %join.1.refs_0_), channel_id=1, source_target_pairs={{0,24},{1,7},{2,26},{3,1},{4,28},{5,3},{6,30},{7,5},{8,0},{9,15},{... | collective-permute-start | bytes 1769480 | tf_op jit(solution)/shard_map/ppermute | solution.py:615
  21.5 15.5 %collective-permute-start.6 = (bf16[4,576,128]{2,1,0:T(8,128)(2,1)S(1)}, bf16[4,576,128]{2,1,0:T(8,128)(2,1)S(1)}, u32[]{:S(2)}, u32[]{:S(2)}) collective-permute-start(bf16[4,576,128]{2,1,0:T(8,128)(2,1)S(1)} %join.1.refs_0_), channel_id=1, source_target_pairs={{0,16},{1,5},{2,18},{3,7},{4,20},{5,1},{6,22},{7,3},{8,24},{9,13},... | collective-permute-start | bytes 1769480 | tf_op jit(solution)/shard_map/ppermute | solution.py:615
  22.0 16.4 %collective-permute-start.5 = (bf16[4,576,128]{2,1,0:T(8,128)(2,1)S(1)}, bf16[4,576,128]{2,1,0:T(8,128)(2,1)S(1)}, u32[]{:S(2)}, u32[]{:S(2)}) collective-permute-start(bf16[4,576,128]{2,1,0:T(8,128)(2,1)S(1)} %join.1.refs_0_), channel_id=1, source_target_pairs={{0,8},{1,3},{2,10},{3,5},{4,12},{5,7},{6,14},{7,1},{8,16},{9,11},{... | collective-permute-start | bytes 1769480 | tf_op jit(solution)/shard_map/ppermute | solution.py:615
  30.5 3.3 %collective-permute-start = (s32[1,128]{1,0:T(1,128)S(1)}, s32[1,128]{1,0:T(1,128)S(1)}, u32[]{:S(2)}, u32[]{:S(2)}) collective-permute-start(s32[1,128]{1,0:T(1,128)S(1)} %add_bitcast_fusion.code_own), channel_id=1, source_target_pairs={{0,1},{1,0},{2,3},{3,2},{4,5},{5,4},{6,7},{7,6},{8,9},{9,8},{10,11... | collective-permute-start | bytes 1544 | tf_op jit(solution)/shard_map/ppermute | solution.py:612
  32.7 16.6 %collective-permute-start.11 = (bf16[4,576,128]{2,1,0:T(8,128)(2,1)}, bf16[4,576,128]{2,1,0:T(8,128)(2,1)}, u32[]{:S(2)}, u32[]{:S(2)}) collective-permute-start(bf16[4,576,128]{2,1,0:T(8,128)(2,1)} %cut.3), channel_id=1, source_target_pairs={{96,0},{0,32},{32,64},{64,96},{97,1},{1,33},{33,65},{65,97},{98,2}... | collective-permute-start | bytes 1769480 | tf_op jit(solution)/shard_map/ppermute | solution.py:625
  33.8 16.3 %collective-permute-start.9 = (bf16[4,576,128]{2,1,0:T(8,128)(2,1)}, bf16[4,576,128]{2,1,0:T(8,128)(2,1)}, u32[]{:S(2)}, u32[]{:S(2)}) collective-permute-start(bf16[4,576,128]{2,1,0:T(8,128)(2,1)} %cut.2), channel_id=1, source_target_pairs={{32,0},{64,32},{96,64},{0,96},{33,1},{65,33},{97,65},{1,97},{34,2}... | collective-permute-start | bytes 1769480 | tf_op jit(solution)/shard_map/ppermute | solution.py:624
  36.5 14.8 %collective-permute-start.12 = (bf16[8,576,128]{2,1,0:T(8,128)(2,1)}, bf16[8,576,128]{2,1,0:T(8,128)(2,1)}, u32[]{:S(2)}, u32[]{:S(2)}) collective-permute-start(bf16[8,576,128]{2,1,0:T(8,128)(2,1)} %refs_4_.3), channel_id=1, source_target_pairs={{0,1},{1,0},{2,3},{3,2},{4,5},{5,4},{6,7},{7,6},{8,9},{9,8},{10,11... | collective-permute-start | bytes 3538952 | tf_op jit(solution)/shard_map/ppermute | solution.py:612
  37.1 14.8 %collective-permute-start.16 = (bf16[8,576,128]{2,1,0:T(8,128)(2,1)S(1)}, bf16[8,576,128]{2,1,0:T(8,128)(2,1)}, u32[]{:S(2)}, u32[]{:S(2)}) collective-permute-start(bf16[8,576,128]{2,1,0:T(8,128)(2,1)S(1)} %collective-permute-done.10.blocks.refs_8_), channel_id=1, source_target_pairs={{0,1},{1,0},{2,3},{3,2},{4,5},{5,4},{6,7},{7,6},{8,9},{9,8},{10,11... | collective-permute-start | bytes 3538952 | tf_op jit(solution)/shard_map/ppermute | solution.py:612
  38.5 14.3 %collective-permute-start.13 = (bf16[8,576,128]{2,1,0:T(8,128)(2,1)S(1)}, bf16[8,576,128]{2,1,0:T(8,128)(2,1)S(1)}, u32[]{:S(2)}, u32[]{:S(2)}) collective-permute-start(bf16[8,576,128]{2,1,0:T(8,128)(2,1)S(1)} %collective-permute-done.8.blocks.refs_5_), channel_id=1, source_target_pairs={{0,1},{1,0},{2,3},{3,2},{4,5},{5,4},{6,7},{7,6},{8,9},{9,8},{10,11... | collective-permute-start | bytes 3538952 | tf_op jit(solution)/shard_map/ppermute | solution.py:612
  49.3 2.6 %collective-permute-start.15 = (bf16[4,576,128]{2,1,0:T(8,128)(2,1)}, bf16[4,576,128]{2,1,0:T(8,128)(2,1)S(1)}, u32[]{:S(2)}, u32[]{:S(2)}) collective-permute-start(bf16[4,576,128]{2,1,0:T(8,128)(2,1)} %collective-permute-done.11.refs_7_), channel_id=1, source_target_pairs={{0,1},{1,0},{2,3},{3,2},{4,5},{5,4},{6,7},{7,6},{8,9},{9,8},{10,11... | collective-permute-start | bytes 1769480 | tf_op jit(solution)/shard_map/ppermute | solution.py:612
  50.1 2.7 %collective-permute-start.14 = (bf16[4,576,128]{2,1,0:T(8,128)(2,1)}, bf16[4,576,128]{2,1,0:T(8,128)(2,1)S(1)}, u32[]{:S(2)}, u32[]{:S(2)}) collective-permute-start(bf16[4,576,128]{2,1,0:T(8,128)(2,1)} %collective-permute-done.9.refs_6_), channel_id=1, source_target_pairs={{0,1},{1,0},{2,3},{3,2},{4,5},{5,4},{6,7},{7,6},{8,9},{9,8},{10,11... | collective-permute-start | bytes 1769480 | tf_op jit(solution)/shard_map/ppermute | solution.py:612
  61.5 10.1 %collective-permute-start.17 = (bf16[4,528,128]{2,1,0:T(8,128)(2,1)S(1)}, bf16[4,528,128]{2,1,0:T(8,128)(2,1)S(1)}, u32[]{:S(2)}, u32[]{:S(2)}) collective-permute-start(bf16[4,528,128]{2,1,0:T(8,128)(2,1)S(1)} %get-tuple-element.30), channel_id=1, source_target_pairs={{0,4},{1,17},{2,6},{3,19},{4,0},{5,21},{6,2},{7,23},{8,12},{9,25},... | collective-permute-start | bytes 1622024 | tf_op jit(solution)/shard_map/ppermute | solution.py:615
  64.5 12.9 %collective-permute-start.18 = (bf16[4,528,128]{2,1,0:T(8,128)(2,1)S(1)}, bf16[4,528,128]{2,1,0:T(8,128)(2,1)S(1)}, u32[]{:S(2)}, u32[]{:S(2)}) collective-permute-start(bf16[4,528,128]{2,1,0:T(8,128)(2,1)S(1)} %get-tuple-element.31), channel_id=1, source_target_pairs={{0,2},{1,9},{2,4},{3,11},{4,6},{5,13},{6,0},{7,15},{8,10},{9,17},{... | collective-permute-start | bytes 1622024 | tf_op jit(solution)/shard_map/ppermute | solution.py:615
  64.9 12.9 %collective-permute-start.19 = (bf16[4,528,128]{2,1,0:T(8,128)(2,1)S(1)}, bf16[4,528,128]{2,1,0:T(8,128)(2,1)S(1)}, u32[]{:S(2)}, u32[]{:S(2)}) collective-permute-start(bf16[4,528,128]{2,1,0:T(8,128)(2,1)S(1)} %get-tuple-element.32), channel_id=1, source_target_pairs={{0,6},{1,25},{2,0},{3,27},{4,2},{5,29},{6,4},{7,31},{8,14},{9,1},{... | collective-permute-start | bytes 1622024 | tf_op jit(solution)/shard_map/ppermute | solution.py:615
  67.2 54.0 %slice-start.2 = ((s8[5505024]{0:T(1024)(128)(4,1)}), s8[4194304]{0:T(1024)(128)(4,1)S(1)}, s32[]{:S(2)}) async-start(s8[5505024]{0:T(1024)(128)(4,1)} %bitcast.8), calls=%async_computation.5 | async-start | bytes 8388608
  67.2 54.0 %slice-start.4 = ((s8[5505024]{0:T(1024)(128)(4,1)}), s8[4194304]{0:T(1024)(128)(4,1)S(1)}, s32[]{:S(2)}) async-start(s8[5505024]{0:T(1024)(128)(4,1)} %bitcast.10), calls=%async_computation.7 | async-start | bytes 8388608
  70.4 50.8 %slice-start.3 = ((s8[5505024]{0:T(1024)(128)(4,1)}), s8[1310720]{0:T(1024)(128)(4,1)S(1)}, s32[]{:S(2)}) async-start(s8[5505024]{0:T(1024)(128)(4,1)} %bitcast.8), calls=%async_computation.6 | async-start | bytes 2621440
  70.5 50.7 %slice-start.5 = ((s8[5505024]{0:T(1024)(128)(4,1)}), s8[1310720]{0:T(1024)(128)(4,1)S(1)}, s32[]{:S(2)}) async-start(s8[5505024]{0:T(1024)(128)(4,1)} %bitcast.10), calls=%async_computation.8 | async-start | bytes 2621440
  78.8 5.7 %collective-permute-start.20 = (bf16[528,128]{1,0:T(8,128)(2,1)S(1)}, bf16[528,128]{1,0:T(8,128)(2,1)S(1)}, u32[]{:S(2)}, u32[]{:S(2)}) collective-permute-start(bf16[528,128]{1,0:T(8,128)(2,1)S(1)} %get-tuple-element.34), channel_id=1, source_target_pairs={{0,16},{1,5},{2,18},{3,7},{4,20},{5,1},{6,22},{7,3},{8,24},{9,13},... | collective-permute-start | bytes 405512 | tf_op jit(solution)/shard_map/ppermute | solution.py:615
  81.4 5.1 %collective-permute-start.21 = (bf16[528,128]{1,0:T(8,128)(2,1)S(1)}, bf16[528,128]{1,0:T(8,128)(2,1)S(1)}, u32[]{:S(2)}, u32[]{:S(2)}) collective-permute-start(bf16[528,128]{1,0:T(8,128)(2,1)S(1)} %get-tuple-element.35), channel_id=1, source_target_pairs={{0,8},{1,3},{2,10},{3,5},{4,12},{5,7},{6,14},{7,1},{8,16},{9,11},{... | collective-permute-start | bytes 405512 | tf_op jit(solution)/shard_map/ppermute | solution.py:615
  82.0 4.5 %collective-permute-start.22 = (bf16[528,128]{1,0:T(8,128)(2,1)S(1)}, bf16[528,128]{1,0:T(8,128)(2,1)S(1)}, u32[]{:S(2)}, u32[]{:S(2)}) collective-permute-start(bf16[528,128]{1,0:T(8,128)(2,1)S(1)} %get-tuple-element.36), channel_id=1, source_target_pairs={{0,24},{1,7},{2,26},{3,1},{4,28},{5,3},{6,30},{7,5},{8,0},{9,15},{... | collective-permute-start | bytes 405512 | tf_op jit(solution)/shard_map/ppermute | solution.py:615
  86.4 34.8 %slice-start = ((s8[5505024]{0:T(1024)(128)(4,1)}), s8[4194304]{0:T(1024)(128)(4,1)S(1)}, s32[]{:S(2)}) async-start(s8[5505024]{0:T(1024)(128)(4,1)} %bitcast.6), calls=%async_computation.3 | async-start | bytes 8388608
  86.5 34.8 %slice-start.1 = ((s8[5505024]{0:T(1024)(128)(4,1)}), s8[1310720]{0:T(1024)(128)(4,1)S(1)}, s32[]{:S(2)}) async-start(s8[5505024]{0:T(1024)(128)(4,1)} %bitcast.6), calls=%async_computation.4 | async-start | bytes 2621440
  88.6 4.2 %collective-permute-start.23 = (bf16[16,56,128]{2,1,0:T(8,128)(2,1)S(1)}, bf16[16,56,128]{2,1,0:T(8,128)(2,1)S(1)}, u32[]{:S(2)}, u32[]{:S(2)}) collective-permute-start(bf16[16,56,128]{2,1,0:T(8,128)(2,1)S(1)} %get-tuple-element.38), channel_id=1, source_target_pairs={{0,1},{1,0},{2,3},{3,2},{4,5},{5,4},{6,7},{7,6},{8,9},{9,8},{10,11... | collective-permute-start | bytes 688136 | tf_op jit(solution)/shard_map/ppermute | solution.py:612
  117.1 4.1 %collective-permute-start.24 = (bf16[16,56,128]{2,1,0:T(8,128)(2,1)S(1)}, bf16[16,56,128]{2,1,0:T(8,128)(2,1)S(1)}, u32[]{:S(2)}, u32[]{:S(2)}) collective-permute-start(bf16[16,56,128]{2,1,0:T(8,128)(2,1)S(1)} %all_to_all.16.refs_0_), channel_id=1, source_target_pairs={{0,1},{1,0},{2,3},{3,2},{4,5},{5,4},{6,7},{7,6},{8,9},{9,8},{10,11... | collective-permute-start | bytes 688136 | tf_op jit(solution)/shard_map/ppermute | solution.py:612
  124.1 1.6 %collective-permute-start.25 = (bf16[16,56,128]{2,1,0:T(8,128)(2,1)S(1)}, bf16[16,56,128]{2,1,0:T(8,128)(2,1)S(1)}, u32[]{:S(2)}, u32[]{:S(2)}) collective-permute-start(bf16[16,56,128]{2,1,0:T(8,128)(2,1)S(1)} %get-tuple-element.44), channel_id=1, source_target_pairs={{0,1},{1,0},{2,3},{3,2},{4,5},{5,4},{6,7},{7,6},{8,9},{9,8},{10,11... | collective-permute-start | bytes 688136 | tf_op jit(solution)/shard_map/ppermute | solution.py:612
  (10 other events, 122.2 us)
